TPU v7x, 512 devices: a whole 4x4x16 slice. The times are simulated.
512 devices in a mesh: section: 8 (over x, z_hi), tp: 64 (over z_lo, y, core).
Axes of the slice: x: 4, y: 4, z: 16 (z_hi: 2, z_lo: 8; z = z_hi * 8 + z_lo), core: 2. Of those that a mesh axis runs over, the one named last changes fastest.
Arguments:
- residual: bfloat16 [8, 512, 8192], P('section', 'tp'), may hold values from -300 to 300
- norm_gain: float32 [8, 8192], P('section'), may hold values from 0.1 to 1.9
- query_weight: bfloat16 [8, 8192, 8192], P('section', None, 'tp'), may hold values from -0.0625 to 0.0625
- kv_weight: bfloat16 [8, 8192, 2048], P('section', None, 'tp'), may hold values from -0.0625 to 0.0625
- resident_cache: bfloat16 [8, 8, 512, 256], P('section'), may hold values from -500 to 500
- block_start: int32 [8], P('section'), may hold values from 512 to 130560
- decode_owner: int32 [8, 8], P('section'), may hold values from 0 to 63
Outputs:
- attn_heads: bfloat16 [8, 512, 8192], P('section', None, 'tp')
- decode_kv: bfloat16 [8, 512, 8, 256], P('section', 'tp')
All inputs are finite; a program needn't handle non-finite values.
Results may differ from a plain program's by a relative error of at most 0.025.
Values may be sent and summed in bfloat16 or wider, within the bound.
No kernel may reach another device: no remote copies, remote signals or barrier semaphores. Data moves between devices by JAX's collectives and lax.ppermute only.
A program may use at most 64 MiB of HBM per device.

v0:
```python
import math

import jax
import jax.numpy as jnp
from jax import lax
from jax.sharding import PartitionSpec as P

HEADS = 64


rope_base = 500000.0
norm_eps = 1e-05
masked_score = -1e30


def passed_along(value, axis, steps):
    count = lax.axis_size(axis)
    pairs = [(source, (source + steps) % count) for source in range(count)]
    return lax.ppermute(value, axis, pairs)


def frequencies(head_dim):
    half_dim = head_dim // 2
    base_freqs = jnp.exp(
        jnp.arange(half_dim, dtype=jnp.float32) * (-2.0 * math.log(rope_base) / head_dim)
    )
    wavelength = 2.0 * math.pi / base_freqs
    smooth = (8192.0 / wavelength - 1.0) / 3.0
    blended = (1.0 - smooth) * base_freqs / 8.0 + smooth * base_freqs
    return jnp.where(
        wavelength < 2048.0, base_freqs, jnp.where(wavelength > 8192.0, base_freqs / 8.0, blended)
    )


def rotate(values, positions):
    half_dim = values.shape[-1] // 2
    freqs_table = frequencies(values.shape[-1])
    angles = positions.astype(jnp.float32)[:, None] * freqs_table[None, :]
    cosine = jnp.cos(angles)[:, None, :]
    sine_part = jnp.sin(angles)[:, None, :]
    first_half = values[..., :half_dim]
    second_half = values[..., half_dim:]
    return jnp.concatenate(
        [
            first_half * cosine - second_half * sine_part,
            second_half * cosine + first_half * sine_part,
        ],
        axis=-1,
    )


def normalize(rows_in, norm_scale):
    widened = rows_in.astype(jnp.float32)
    scale_row = lax.rsqrt(jnp.mean(widened * widened, axis=-1, keepdims=True) + norm_eps)
    return (widened * scale_row * norm_scale).astype(jnp.bfloat16)


def body(residual, norm_gain, query_weight, kv_weight, resident_cache, block_start, decode_owner):
    tp_count = lax.axis_size("tp")
    device_index = lax.axis_index("tp")
    query_cols = query_weight.shape[2]
    kv_heads = resident_cache.shape[1]
    resident_len = resident_cache.shape[2]
    head_dim = resident_cache.shape[3] // 2
    local_heads = query_cols // head_dim
    norm_scale = norm_gain[0]
    weight_query = query_weight[0]
    weight_kv = kv_weight[0]
    arriving = passed_along(residual, "section", 1)[0]
    normed = normalize(arriving, norm_scale)
    rows_in = lax.all_gather(normed, "tp", axis=0, tiled=True)
    projected = jnp.concatenate(
        [
            jnp.dot(rows_in, weight_query, preferred_element_type=jnp.float32),
            jnp.dot(rows_in, weight_kv, preferred_element_type=jnp.float32),
        ],
        axis=1,
    )
    token_count = projected.shape[0]
    positions = block_start[0] + jnp.arange(token_count, dtype=jnp.int32)
    query_rows = projected[:, :query_cols].reshape(token_count, local_heads, head_dim)
    query_rows = (rotate(query_rows, positions) * head_dim ** (-0.5)).astype(jnp.bfloat16)
    kv_local = projected[:, query_cols:].astype(jnp.bfloat16)
    kv_whole = lax.all_gather(kv_local, "tp", axis=1, tiled=True).reshape(
        token_count, kv_heads, 2 * head_dim
    )
    new_keys = rotate(kv_whole[:, :, :head_dim].astype(jnp.float32), positions).astype(jnp.bfloat16)
    new_kv = jnp.concatenate([new_keys, kv_whole[:, :, head_dim:]], axis=2)
    kv_group = device_index * local_heads // (HEADS // kv_heads)
    resident = lax.dynamic_index_in_dim(resident_cache[0], kv_group, 0, keepdims=False)
    fresh_rows = lax.dynamic_index_in_dim(new_kv, kv_group, 1, keepdims=False)
    key_rows = jnp.concatenate([resident[:, :head_dim], fresh_rows[:, :head_dim]], axis=0)
    value_rows = jnp.concatenate([resident[:, head_dim:], fresh_rows[:, head_dim:]], axis=0)
    scores = jnp.einsum("thd,sd->hts", query_rows, key_rows, preferred_element_type=jnp.float32)
    allowed = (
        jnp.arange(resident_len + token_count, dtype=jnp.int32)[None, :]
        <= resident_len + jnp.arange(token_count, dtype=jnp.int32)[:, None]
    )
    scores = jnp.where(allowed[None], scores, masked_score)
    row_max = jnp.max(scores, axis=2, keepdims=True)
    weights = jnp.exp(scores - row_max)
    probabilities = (weights / jnp.sum(weights, axis=2, keepdims=True)).astype(jnp.bfloat16)
    attended = jnp.einsum(
        "hts,sd->thd", probabilities, value_rows, preferred_element_type=jnp.float32
    )
    attn_heads = attended.reshape(token_count, query_cols).astype(jnp.bfloat16)[None]
    block_rows = token_count // tp_count
    first_rows = (device_index - decode_owner[0]) % tp_count * block_rows
    row_ids = first_rows[:, None] + jnp.arange(block_rows, dtype=jnp.int32)[None, :]
    picked = new_kv[row_ids, jnp.arange(kv_heads, dtype=jnp.int32)[:, None]]
    decode_kv = jnp.transpose(picked, (1, 0, 2))[None]
    return (attn_heads, decode_kv)


def solution(mesh):
    return jax.shard_map(
        body,
        mesh=mesh,
        in_specs=(
            P("section", "tp", None),
            P("section", None),
            P("section", None, "tp"),
            P("section", None, "tp"),
            P("section", None, None, None),
            P("section"),
            P("section", None),
        ),
        out_specs=(P("section", None, "tp"), P("section", "tp", None, None)),
        check_vma=False,
    )
```

profile of v0, /device:TPU:1, one launch (start us, length us, event | category | flops | bytes accessed | tf_op | source)
XLA Modules:
  0.0 314.5 jit_solution(17799190172012611802)
XLA Ops:
  7.2 0.0 copy-start
  7.2 0.0 all-gather.3.cloned.1.call-start
  7.2 16.4 %collective-permute-start = (bf16[1,8,8192]{2,1,0:T(8,128)(2,1)}, bf16[1,8,8192]{2,1,0:T(8,128)(2,1)S(1)}, u32[]{:S(2)}, u32[]{:S(2)}) collective-permute-start(bf16[1,8,8192]{2,1,0:T(8,128)(2,1)} %param.7), channel_id=1, source_target_pairs={{0,64},{64,128},{128,192},{192,256},{256,320},{320,384},{384,448},... | collective-permute-start | bytes 393224 | tf_op jit(solution)/shard_map/ppermute | solution.py:19
  23.6 5.0 %collective-permute-done = bf16[1,8,8192]{2,1,0:T(8,128)(2,1)S(1)} collective-permute-done((bf16[1,8,8192]{2,1,0:T(8,128)(2,1)}, bf16[1,8,8192]{2,1,0:T(8,128)(2,1)S(1)}, u32[]{:S(2)}, u32[]{:S(2)}) %collective-permute-start) | collective-permute-done | bytes 131104 | tf_op jit(solution)/shard_map/ppermute | solution.py:19
  28.7 0.2 fusion.9
  28.9 1.5 fusion.11
  30.4 0.0 all-gather.3.cloned.1.call-update
  30.4 0.0 copy-start.3
  30.4 0.0 all-gather.5.cloned.1.call-start
  30.5 135.7 %all-gather.3.cloned.1.call-done = bf16[512,8192]{1,0:T(8,128)(2,1)} async-done(((bf16[8,8192]{1,0:T(8,128)(2,1)}), bf16[512,8192]{1,0:T(8,128)(2,1)}) %all-gather.3.cloned.1.call-update) | async-done | bytes 8388624 | tf_op jit(solution)/shard_map/all_gather | solution.py:71
  166.2 6.7 %convolution_convert_fusion.1 = bf16[512,32]{0,1:T(8,128)(2,1)} fusion(bf16[512,8192]{1,0:T(8,128)(2,1)} %all-gather.3.cloned.1.call-done, bf16[1,8192,32]{1,2,0:T(8,128)(2,1)} %param.10), kind=kOutput, calls=%fused_computation.14 | convolution fusion | flops 268451840 | bytes 8945664 | tf_op jit(solution)/shard_map/dot_general | solution.py:75
  172.8 0.0 all-gather.5.cloned.1.call-update
  173.5 0.0 copy-done.3
  173.5 0.1 fusion.31
  173.6 0.1 reshape.279
  173.7 0.0 copy-done
  173.8 1.8 multiply_cosine_fusion
  175.6 6.9 %fusion.3 = f32[512,1,128]{0,2,1:T(8,128)S(1)} fusion(bf16[512,8192]{1,0:T(8,128)(2,1)} %all-gather.3.cloned.1.call-done, bf16[1,8192,128]{2,1,0:T(8,128)(2,1)} %param.9), kind=kOutput, calls=%fused_computation.11 | convolution fusion | flops 1073741824 | bytes 10747904 | tf_op jit(solution)/shard_map/dot_general | solution.py:74
  182.5 1.2 fusion.24
  183.7 105.6 %all-gather.5.cloned.1.call-done = bf16[512,2048]{0,1:T(8,128)(2,1)} async-done(((bf16[512,32]{0,1:T(8,128)(2,1)}), bf16[512,2048]{0,1:T(8,128)(2,1)}) %all-gather.5.cloned.1.call-update) | async-done | bytes 2097168 | tf_op jit(solution)/shard_map/all_gather | solution.py:84
  289.3 3.1 fusion.38
  292.4 1.7 copy.18
  294.1 1.5 convert_element_type.56
  295.6 1.7 copy.19
  297.3 3.1 subtract_convert_fusion
  300.4 1.0 pad_maximum_fusion
  301.4 0.0 copy-start.1
  301.4 1.3 copy-done.1
  302.7 0.0 copy-start.2
  302.7 0.5 constant_dynamic-slice_fusion
  303.3 1.6 gather_fusion
  304.9 0.6 copy.23
  305.5 0.1 fusion.39
  305.6 0.0 copy-done.2
  305.6 0.4 fusion.41
  306.0 0.4 fusion.2
  306.4 0.5 fusion.6
  306.9 0.8 copy.16
  (7 shorter events, 0.1 us)
Async XLA Ops:
  7.2 166.6 %copy-start = (bf16[1,8,512,256]{3,2,1,0:T(8,128)(2,1)S(1)}, bf16[1,8,512,256]{3,2,1,0:T(8,128)(2,1)}, u32[]{:S(2)}) copy-start(bf16[1,8,512,256]{3,2,1,0:T(8,128)(2,1)} %param.11) | copy-start | bytes 6291460
  7.2 159.0 %all-gather.3.cloned.1.call-start = ((), (), s32[]{:S(2)}) async-start(), calls=%async_computation | async-start | bytes 8519680 | tf_op jit(solution)/shard_map/all_gather | solution.py:71
  7.2 21.5 %collective-permute-start = (bf16[1,8,8192]{2,1,0:T(8,128)(2,1)}, bf16[1,8,8192]{2,1,0:T(8,128)(2,1)S(1)}, u32[]{:S(2)}, u32[]{:S(2)}) collective-permute-start(bf16[1,8,8192]{2,1,0:T(8,128)(2,1)} %param.7), channel_id=1, source_target_pairs={{0,64},{64,128},{128,192},{192,256},{256,320},{320,384},{384,448},... | collective-permute-start | bytes 393224 | tf_op jit(solution)/shard_map/ppermute | solution.py:19
  30.4 143.1 %copy-start.3 = (s32[1,8]{1,0:T(1,128)S(1)}, s32[1,8]{1,0:T(1,128)}, u32[]{:S(2)}) copy-start(s32[1,8]{1,0:T(1,128)} %param.13) | copy-start | bytes 100
  30.4 258.9 %all-gather.5.cloned.1.call-start = ((), (), s32[]{:S(2)}) async-start(), calls=%async_computation.1 | async-start | bytes 2129920 | tf_op jit(solution)/shard_map/all_gather | solution.py:84
  301.4 1.3 copy-start.1
  302.7 2.9 copy-start.2
Sparse Core Ops, SparseCore 0:
  30.5 135.5 all-gather.2
  173.0 116.2 all-gather.4
where the time goes:
time: 315 us
  waiting for transfers between devices  246 us (78%)
  starting transfers between devices  16.5 us (5%)
  between operations  14.8 us (5%)
  matrix products  14.5 us (5%)
  local copies, waits for them, and re-layouts  11.6 us (4%)
  other arithmetic  10.8 us (3%)
    all_gather x1, waiting for transfers between devices, body(): rows_in = lax.all_gather(normed, 'tp', axis=0, tiled=True)  136 us
    all_gather x1, waiting for transfers between devices, body(): lax.all_gather(kv_local, 'tp', axis=1, tiled=True)  106 us
    ppermute x1, starting transfers between devices, passed_along(): return lax.ppermute(value, axis, pairs)  16.4 us
    dot_general x1, matrix products, body(): jnp.dot(rows_in, weight_query, preferred_element_type=jnp.float32)  6.85 us
    dot_general x1, matrix products, body(): jnp.dot(rows_in, weight_kv, preferred_element_type=jnp.float32)  6.66 us
  transfers between devices with their start and end apart: 3, of which 3 were waited for; matrix products, arithmetic and copies ran while one was open for 3% of the time, Pallas kernels for 0%

commit v1 on v0

v1 whole, which is shorter than its diff:
```python
import math

import jax
import jax.numpy as jnp
from jax import lax
from jax.experimental import pallas as pl
from jax.experimental.pallas import tpu as pltpu
from jax.sharding import Mesh, PartitionSpec as P

BF = jnp.bfloat16
F32 = jnp.float32
rope_base = 500000.0
norm_eps = 1e-05
masked_score = -1e30

NZ, NY = 8, 4
ROWS = 16
TOKENS = 512
HD = 128


def frequencies(head_dim):
    half_dim = head_dim // 2
    base_freqs = jnp.exp(
        jnp.arange(half_dim, dtype=F32) * (-2.0 * math.log(rope_base) / head_dim)
    )
    wavelength = 2.0 * math.pi / base_freqs
    smooth = (8192.0 / wavelength - 1.0) / 3.0
    blended = (1.0 - smooth) * base_freqs / 8.0 + smooth * base_freqs
    return jnp.where(
        wavelength < 2048.0, base_freqs, jnp.where(wavelength > 8192.0, base_freqs / 8.0, blended)
    )


def along_y(value, k):
    return lax.ppermute(value, "y", [((i + k) % NY, i) for i in range(NY)])


def across_z(value, k):
    return lax.ppermute(value, "z", [(i, i ^ k) for i in range(NZ)])


def swap_core(value):
    return lax.ppermute(value, "c", [(0, 1), (1, 0)])


def place(slot, z0, y0):
    return ((z0 ^ (slot >> 2)) << 2) | ((y0 + (slot & 3)) & 3)


def tokens_of(row, z0, y0):
    return place(row >> 4, z0, y0) * ROWS + (row & 15)


def project_kernel(*refs):
    pieces = refs[:16]
    wq, wkv, own, send, x = refs[16:]
    for b in range(4):
        for k in range(4):
            for part in range(2):
                slot = (b + 4 * part) * 4 + k
                x[slot * ROWS : (slot + 1) * ROWS, :] = pieces[b * 4 + k][part]
    kv = lax.dot_general(
        x[...], wkv[...], (((1,), (1,)), ((), ())), preferred_element_type=F32
    )
    own[:, HD:] = kv
    send[:, HD:] = kv.astype(BF)
    q = jnp.dot(x[...], wq[...], preferred_element_type=F32)
    own[:, :HD] = q[:, :HD]
    send[:, :HD] = q[:, HD:].astype(BF)


def turn(v, cosine, sine):
    return v * cosine + pltpu.roll(v, HD // 2, 1) * sine


def kv_kernel(where, owner, own, got, cosine, sine, keys, values, blocks, held):
    z0, y0, c0 = where[0], where[1], where[2]
    raw = (own[:, HD:] + got[:, HD:].astype(F32)).astype(BF)
    k = turn(raw[:, :HD].astype(F32), cosine[...], sine[...]).astype(BF)
    v = raw[:, HD:]
    keys[...] = k
    values[...] = v
    for slot in range(32):
        to = pl.multiple_of(place(slot, z0, y0) * ROWS, ROWS)
        span = slice(slot * ROWS, (slot + 1) * ROWS)
        held[pl.ds(to, ROWS), :HD] = k[span].astype(F32)
        held[pl.ds(to, ROWS), HD:] = v[span].astype(F32)
    first = y0 * 2 + c0 - owner[z0] + 64
    for z in range(NZ):
        block = (first + z * 8) & 63
        blocks[z] = held[pl.ds(pl.multiple_of(block * 8, 8), 8), :].astype(BF)


def attend_kernel(where, own, got, cosine, sine, keys, values, resident, out):
    z0, y0 = where[0], where[1]
    q = own[:, :HD] + got[:, :HD].astype(F32)
    q = (turn(q, cosine[...], sine[...]) * HD ** (-0.5)).astype(BF)
    nt = (((1,), (1,)), ((), ()))
    old = lax.dot_general(q, resident[:, :HD], nt, preferred_element_type=F32)
    new = lax.dot_general(q, keys[...], nt, preferred_element_type=F32)
    token_q = tokens_of(lax.broadcasted_iota(jnp.int32, (TOKENS, 1), 0), z0, y0)
    token_k = tokens_of(lax.broadcasted_iota(jnp.int32, (1, TOKENS), 1), z0, y0)
    new = jnp.where(token_k <= token_q, new, masked_score)
    top = jnp.maximum(
        jnp.max(old, axis=1, keepdims=True), jnp.max(new, axis=1, keepdims=True)
    )
    old = jnp.exp(old - top)
    new = jnp.exp(new - top)
    total = jnp.sum(old, axis=1, keepdims=True) + jnp.sum(new, axis=1, keepdims=True)
    scale = 1.0 / total
    att = jnp.dot((old * scale).astype(BF), resident[:, HD:], preferred_element_type=F32)
    att = att + jnp.dot((new * scale).astype(BF), values[...], preferred_element_type=F32)
    att = att.astype(BF)
    for slot in range(32):
        to = pl.multiple_of(place(slot, z0, y0) * ROWS, ROWS)
        out[pl.ds(to, ROWS), :] = att[slot * ROWS : (slot + 1) * ROWS]


def kv_weight_kernel(where, gain, mine, one, two, three, out):
    y0 = where[1]
    for k, ref in enumerate((mine, one, two, three)):
        to = pl.multiple_of(((y0 + k) & 3) * 64, 64)
        out[pl.ds(to, 64), :] = (ref[...].astype(F32) * gain[...]).astype(BF)


VMEM = pl.BlockSpec(memory_space=pltpu.VMEM)
SMEM = pl.BlockSpec(memory_space=pltpu.SMEM)


def call(kernel, shapes, specs, scratch=(), flops=0, moved=0, exps=0):
    return pl.pallas_call(
        kernel,
        out_shape=shapes,
        in_specs=specs,
        out_specs=jax.tree.map(lambda _: VMEM, shapes),
        scratch_shapes=scratch,
        compiler_params=pltpu.CompilerParams(vmem_limit_bytes=40 * 2**20),
        cost_estimate=pl.CostEstimate(flops=flops, bytes_accessed=moved, transcendentals=exps),
    )


def shaped(*shape, dtype=BF):
    return jax.ShapeDtypeStruct(shape, dtype)


def body(residual, norm_gain, query_weight, kv_weight, resident_cache, block_start, decode_owner):
    z0, y0, c0 = (lax.axis_index(a).astype(jnp.int32) for a in ("z", "y", "c"))
    width = residual.shape[2]
    half = width // 2
    where = jnp.stack([z0, y0, c0])

    widened = residual[0].astype(F32)
    scale_row = lax.rsqrt(jnp.mean(widened * widened, axis=-1, keepdims=True) + norm_eps)
    rows = (widened * scale_row).astype(BF)
    kept = lax.dynamic_slice_in_dim(rows, c0 * half, half, 1)
    crossed = lax.dynamic_slice_in_dim(rows, (1 - c0) * half, half, 1)
    sections = lax.axis_size("s")
    straight = [(s * 2 + c, (s + 1) % sections * 2 + c) for s in range(sections) for c in (0, 1)]
    across = [(s * 2 + c, (s + 1) % sections * 2 + 1 - c) for s in range(sections) for c in (0, 1)]
    same = lax.ppermute(kept, ("s", "c"), straight)
    other = lax.ppermute(crossed, ("s", "c"), across)
    piece = jnp.where(c0 == 0, jnp.stack([same, other]), jnp.stack([other, same]))
    piece = piece.reshape(1, ROWS, half)

    gain = lax.dynamic_slice_in_dim(norm_gain[0], c0 * half, half, 0)
    wq_mine = lax.dynamic_slice_in_dim(query_weight[0], c0 * half, half, 0)
    wq_given = lax.dynamic_slice_in_dim(query_weight[0], (1 - c0) * half, half, 0)
    wq_got = swap_core(wq_given)
    wq = jnp.concatenate([wq_mine, wq_got], axis=1)
    wq = (wq.astype(F32) * gain[:, None]).astype(BF)
    wkv_t = kv_weight[0].T
    kv_mine = lax.dynamic_slice_in_dim(wkv_t, c0 * half, half, 1)
    kv_given = lax.dynamic_slice_in_dim(wkv_t, (1 - c0) * half, half, 1)
    kv_got = swap_core(kv_given)
    kv_chip = jnp.where(
        c0 == 0, jnp.concatenate([kv_mine, kv_got]), jnp.concatenate([kv_got, kv_mine])
    )
    kv_others = [along_y(kv_chip, k) for k in (1, 2, 3)]
    wkv = call(kv_weight_kernel, shaped(256, half), [SMEM] + [VMEM] * 5, moved=2**22)(
        where, gain[None], kv_chip, *kv_others
    )

    pair = jnp.concatenate([piece, across_z(piece, 4)])
    groups = [pair] + [across_z(pair, k) for k in (1, 2, 3)]
    pieces = [p if k == 0 else along_y(p, k) for p in groups for k in range(NY)]

    tokens = tokens_of(jnp.arange(TOKENS, dtype=jnp.int32), z0, y0)
    angles = (block_start[0] + tokens).astype(F32)[:, None] * frequencies(HD)[None, :]
    cosine, sine = jnp.cos(angles), jnp.sin(angles)
    cosine = jnp.concatenate([cosine, cosine], axis=1)
    sine = jnp.concatenate([-sine, sine], axis=1)

    own, send = call(
        project_kernel,
        (shaped(TOKENS, 3 * HD, dtype=F32), shaped(TOKENS, 3 * HD)),
        [VMEM] * 18,
        scratch=[pltpu.VMEM((TOKENS, half), BF)],
        flops=2 * TOKENS * half * 512,
        moved=9 * 2**20,
    )(*pieces, wq, wkv)
    got = swap_core(send)
    keys, values, blocks = call(
        kv_kernel,
        (shaped(TOKENS, HD), shaped(TOKENS, HD), shaped(NZ, 8, 2 * HD)),
        [SMEM, SMEM] + [VMEM] * 4,
        scratch=[pltpu.VMEM((TOKENS, 2 * HD), F32)],
        moved=2**21,
    )(where, decode_owner[0], own, got, cosine, sine)
    spread = lax.all_to_all(blocks, "z", 0, 0)
    decode_kv = jnp.transpose(spread, (1, 0, 2))[None]
    resident = lax.dynamic_index_in_dim(resident_cache[0], z0, 0, keepdims=False)
    attn = call(
        attend_kernel,
        shaped(TOKENS, HD),
        [SMEM] + [VMEM] * 7,
        flops=4 * TOKENS * 1024 * HD,
        moved=2**21,
        exps=TOKENS * 1024,
    )(where, own, got, cosine, sine, keys, values, resident)
    return attn[None], decode_kv


def solution(mesh):
    sections = mesh.shape["section"]
    fine = Mesh(mesh.devices.reshape(sections, NZ, NY, 2), ("s", "z", "y", "c"))
    tp = ("z", "y", "c")
    return jax.shard_map(
        body,
        mesh=fine,
        in_specs=(
            P("s", tp, None),
            P("s", None),
            P("s", None, tp),
            P("s", None, tp),
            P("s", None, None, None),
            P("s"),
            P("s", None),
        ),
        out_specs=(P("s", None, tp), P("s", tp, None, None)),
        check_vma=False,
    )
```

time: 315 us -> 193 us (0.61)
  waiting for transfers between devices: 246 us -> 68.9 us
  starting transfers between devices: 16.5 us -> 91.7 us
  matrix products: 14.5 us -> 0 us
  between operations: 14.8 us -> 1.87 us
  Pallas kernels: 0 us -> 9.63 us
  other arithmetic: 10.8 us -> 5.51 us
    all_gather x2 -> x0, waiting for transfers between devices: 241 us -> none  [the longest x1 136 us: body(): rows_in = lax.all_gather(normed, 'tp', axis=0, tiled=True)]
    ppermute x1 -> x24, starting transfers between devices: 16.4 us -> 86 us  [the longest x15 46.6 us: along_y(): return lax.ppermute(value, 'y', [((i + k) % NY, i) for i in range(NY)])]
    ppermute x1 -> x24, waiting for transfers between devices: 5.05 us -> 63.5 us  [the longest x15 31 us: along_y(): return lax.ppermute(value, 'y', [((i + k) % NY, i) for i in range(NY)])]
    dot_general x4 -> x0, matrix products: 14.5 us -> none  [the longest x1 6.85 us: body(): jnp.dot(rows_in, weight_query, preferred_element_type=jnp.float32)]
    pallas_call x0 -> x4, Pallas kernels: none -> 9.63 us  [the longest x1 4.31 us: body(): call(project_kernel, (shaped(TOKENS, 3 * HD, dtype=F32), shaped(TOKENS, 3...]
    unnamed x12 -> x49, local copies, waits for them, and re-layouts: 5.58 us -> 11.9 us
    all_to_all x0 -> x1, starting transfers between devices: none -> 5.67 us  [body(): spread = lax.all_to_all(blocks, 'z', 0, 0)]
    all_to_all x0 -> x1, waiting for transfers between devices: none -> 5.36 us  [body(): spread = lax.all_to_all(blocks, 'z', 0, 0)]
  transfers between devices with their start and end apart: 3 -> 25, of which waited for: 3 -> 10; matrix products, arithmetic and copies ran while one was open for 3% -> 3% of each run, Pallas kernels for 0% -> 2%
where the time goes in v1:
time: 193 us; the launch traced here: 192 us
  starting transfers between devices  91.7 us (48%)
  waiting for transfers between devices  68.9 us (36%)
  local copies, waits for them, and re-layouts  14.5 us (8%)
  Pallas kernels  9.63 us (5%)
  other arithmetic  5.51 us (3%)
    ppermute x15, starting transfers between devices, along_y(): return lax.ppermute(value, 'y', [((i + k) % NY, i) for i in range(NY)])  46.6 us
    ppermute x15, waiting for transfers between devices, along_y(): return lax.ppermute(value, 'y', [((i + k) % NY, i) for i in range(NY)])  31 us
    ppermute x4, waiting for transfers between devices, across_z(): return lax.ppermute(value, 'z', [(i, i ^ k) for i in range(NZ)])  16.6 us
    ppermute x1, starting transfers between devices, body(): same = lax.ppermute(kept, ('s', 'c'), straight)  16.3 us
    ppermute x1, waiting for transfers between devices, body(): other = lax.ppermute(crossed, ('s', 'c'), across)  13.9 us
    unnamed x49, local copies, waits for them, and re-layouts  11.9 us
    ppermute x4, starting transfers between devices, across_z(): return lax.ppermute(value, 'z', [(i, i ^ k) for i in range(NZ)])  11.6 us
    ppermute x3, starting transfers between devices, swap_core(): return lax.ppermute(value, 'c', [(0, 1), (1, 0)])  9.08 us
  transfers between devices with their start and end apart: 25, of which 10 were waited for; matrix products, arithmetic and copies ran while one was open for 3% of the time, Pallas kernels for 2%

profile of v1, /device:TPU:1, one launch (start us, length us, event | category | flops | bytes accessed | tf_op | source)
XLA Modules:
  0.0 192.1 jit_solution(11654886099873582514)
XLA Ops:
  0.7 1.2 fusion
  1.9 1.0 fusion.1
  2.9 16.3 %collective-permute-start = (bf16[8,4096]{1,0:T(8,128)(2,1)S(1)}, bf16[8,4096]{1,0:T(8,128)(2,1)S(1)}, u32[]{:S(2)}, u32[]{:S(2)}) collective-permute-start(bf16[8,4096]{1,0:T(8,128)(2,1)S(1)} %get-tuple-element.18), channel_id=1, source_target_pairs={{0,64},{1,65},{64,128},{65,129},{128,192},{129,193},{192,256},{193... | collective-permute-start | bytes 196616 | tf_op jit(solution)/shard_map/ppermute | solution.py:161
  19.2 2.5 %collective-permute-start.1 = (bf16[8,4096]{1,0:T(8,128)(2,1)S(1)}, bf16[8,4096]{1,0:T(8,128)(2,1)S(1)}, u32[]{:S(2)}, u32[]{:S(2)}) collective-permute-start(bf16[8,4096]{1,0:T(8,128)(2,1)S(1)} %get-tuple-element.19), channel_id=1, source_target_pairs={{0,65},{1,64},{64,129},{65,128},{128,193},{129,192},{192,257},{193... | collective-permute-start | bytes 196616 | tf_op jit(solution)/shard_map/ppermute | solution.py:162
  21.7 1.5 collective-permute-done
  23.2 13.9 %collective-permute-done.1 = bf16[8,4096]{1,0:T(8,128)(2,1)S(1)} collective-permute-done((bf16[8,4096]{1,0:T(8,128)(2,1)S(1)}, bf16[8,4096]{1,0:T(8,128)(2,1)S(1)}, u32[]{:S(2)}, u32[]{:S(2)}) %collective-permute-start.1) | collective-permute-done | bytes 65568 | tf_op jit(solution)/shard_map/ppermute | solution.py:162
  37.2 3.2 %collective-permute-start.2 = (bf16[1,16,4096]{2,1,0:T(8,128)(2,1)S(1)}, bf16[1,16,4096]{2,1,0:T(8,128)(2,1)S(1)}, u32[]{:S(2)}, u32[]{:S(2)}) collective-permute-start(bf16[1,16,4096]{2,1,0:T(8,128)(2,1)S(1)} %fusion.2), channel_id=1, source_target_pairs={{0,32},{8,40},{16,48},{24,56},{32,0},{40,8},{48,16},{56,24},{1,33}... | collective-permute-start | bytes 393224 | tf_op jit(solution)/shard_map/ppermute | solution.py:40
  40.4 1.1 dynamic-slice_bitcast_fusion.4
  41.4 3.0 %collective-permute-start.19 = (bf16[32,4096]{1,0:T(8,128)(2,1)S(1)}, bf16[32,4096]{1,0:T(8,128)(2,1)S(1)}, u32[]{:S(2)}, u32[]{:S(2)}) collective-permute-start(bf16[32,4096]{1,0:T(8,128)(2,1)S(1)} %get-tuple-element.17), channel_id=1, source_target_pairs={{0,1},{1,0},{2,3},{3,2},{4,5},{5,4},{6,7},{7,6},{8,9},{9,8},{10,11... | collective-permute-start | bytes 786440 | tf_op jit(solution)/shard_map/ppermute | solution.py:44
  44.4 11.6 %collective-permute-done.2 = bf16[1,16,4096]{2,1,0:T(8,128)(2,1)S(1)} collective-permute-done((bf16[1,16,4096]{2,1,0:T(8,128)(2,1)S(1)}, bf16[1,16,4096]{2,1,0:T(8,128)(2,1)S(1)}, u32[]{:S(2)}, u32[]{:S(2)}) %collective-permute-start.2) | collective-permute-done | bytes 131104 | tf_op jit(solution)/shard_map/ppermute | solution.py:40
  56.0 1.9 collective-permute-start.10
  57.9 3.7 %collective-permute-start.14 = (bf16[2,16,4096]{2,1,0:T(8,128)(2,1)S(1)}, bf16[2,16,4096]{2,1,0:T(8,128)(2,1)S(1)}, u32[]{:S(2)}, u32[]{:S(2)}) collective-permute-start(bf16[2,16,4096]{2,1,0:T(8,128)(2,1)S(1)} %pad_maximum_fusion.refs_0_), channel_id=1, source_target_pairs={{0,24},{8,16},{16,8},{24,0},{32,56},{40,48},{48,40},{56,32},{1,25}... | collective-permute-start | bytes 786440 | tf_op jit(solution)/shard_map/ppermute | solution.py:40
  61.7 2.7 %collective-permute-start.6 = (bf16[2,16,4096]{2,1,0:T(8,128)(2,1)S(1)}, bf16[2,16,4096]{2,1,0:T(8,128)(2,1)S(1)}, u32[]{:S(2)}, u32[]{:S(2)}) collective-permute-start(bf16[2,16,4096]{2,1,0:T(8,128)(2,1)S(1)} %pad_maximum_fusion.refs_0_), channel_id=1, source_target_pairs={{0,8},{8,0},{16,24},{24,16},{32,40},{40,32},{48,56},{56,48},{1,9},... | collective-permute-start | bytes 786440 | tf_op jit(solution)/shard_map/ppermute | solution.py:40
  64.4 5.9 %collective-permute-start.3 = (bf16[2,16,4096]{2,1,0:T(8,128)(2,1)S(1)}, bf16[2,16,4096]{2,1,0:T(8,128)(2,1)S(1)}, u32[]{:S(2)}, u32[]{:S(2)}) collective-permute-start(bf16[2,16,4096]{2,1,0:T(8,128)(2,1)S(1)} %pad_maximum_fusion.refs_0_), channel_id=1, source_target_pairs={{2,0},{4,2},{6,4},{0,6},{3,1},{5,3},{7,5},{1,7},{10,8},{12,10},{14... | collective-permute-start | bytes 786440 | tf_op jit(solution)/shard_map/ppermute | solution.py:36
  70.3 2.3 %collective-permute-start.4 = (bf16[2,16,4096]{2,1,0:T(8,128)(2,1)S(1)}, bf16[2,16,4096]{2,1,0:T(8,128)(2,1)S(1)}, u32[]{:S(2)}, u32[]{:S(2)}) collective-permute-start(bf16[2,16,4096]{2,1,0:T(8,128)(2,1)S(1)} %pad_maximum_fusion.refs_0_), channel_id=1, source_target_pairs={{4,0},{6,2},{0,4},{2,6},{5,1},{7,3},{1,5},{3,7},{12,8},{14,10},{8,... | collective-permute-start | bytes 786440 | tf_op jit(solution)/shard_map/ppermute | solution.py:36
  72.7 5.1 %collective-permute-done.10.refs_8_ = bf16[2,16,4096]{2,1,0:T(8,128)(2,1)S(1)} collective-permute-done((bf16[2,16,4096]{2,1,0:T(8,128)(2,1)S(1)}, bf16[2,16,4096]{2,1,0:T(8,128)(2,1)S(1)}, u32[]{:S(2)}, u32[]{:S(2)}) %collective-permute-start.10) | collective-permute-done | bytes 262176 | tf_op jit(solution)/shard_map/ppermute | solution.py:40
  77.8 4.6 %collective-permute-start.20 = (bf16[64,4096]{1,0:T(8,128)(2,1)S(1)}, bf16[64,4096]{1,0:T(8,128)(2,1)S(1)}, u32[]{:S(2)}, u32[]{:S(2)}) collective-permute-start(bf16[64,4096]{1,0:T(8,128)(2,1)S(1)} %maximum_select_fusion.mine), channel_id=1, source_target_pairs={{2,0},{4,2},{6,4},{0,6},{3,1},{5,3},{7,5},{1,7},{10,8},{12,10},{14... | collective-permute-start | bytes 1572872 | tf_op jit(solution)/shard_map/ppermute | solution.py:36
  82.4 2.3 %collective-permute-start.21 = (bf16[64,4096]{1,0:T(8,128)(2,1)S(1)}, bf16[64,4096]{1,0:T(8,128)(2,1)S(1)}, u32[]{:S(2)}, u32[]{:S(2)}) collective-permute-start(bf16[64,4096]{1,0:T(8,128)(2,1)S(1)} %maximum_select_fusion.mine), channel_id=1, source_target_pairs={{4,0},{6,2},{0,4},{2,6},{5,1},{7,3},{1,5},{3,7},{12,8},{14,10},{8,... | collective-permute-start | bytes 1572872 | tf_op jit(solution)/shard_map/ppermute | solution.py:36
  85.4 2.6 %collective-permute-start.22 = (bf16[64,4096]{1,0:T(8,128)(2,1)S(1)}, bf16[64,4096]{1,0:T(8,128)(2,1)S(1)}, u32[]{:S(2)}, u32[]{:S(2)}) collective-permute-start(bf16[64,4096]{1,0:T(8,128)(2,1)S(1)} %maximum_select_fusion.mine), channel_id=1, source_target_pairs={{6,0},{0,2},{2,4},{4,6},{7,1},{1,3},{3,5},{5,7},{14,8},{8,10},{10,... | collective-permute-start | bytes 1572872 | tf_op jit(solution)/shard_map/ppermute | solution.py:36
  88.0 1.5 dynamic-slice_bitcast_fusion.1
  90.2 3.3 %collective-permute-start.18 = (bf16[4096,128]{1,0:T(8,128)(2,1)}, bf16[4096,128]{1,0:T(8,128)(2,1)}, u32[]{:S(2)}, u32[]{:S(2)}) collective-permute-start(bf16[4096,128]{1,0:T(8,128)(2,1)} %get-tuple-element.15), channel_id=1, source_target_pairs={{0,1},{1,0},{2,3},{3,2},{4,5},{5,4},{6,7},{7,6},{8,9},{9,8},{10,11... | collective-permute-start | bytes 3145736 | tf_op jit(solution)/shard_map/ppermute | solution.py:44
  94.2 3.5 %collective-permute-start.5 = (bf16[2,16,4096]{2,1,0:T(8,128)(2,1)S(1)}, bf16[2,16,4096]{2,1,0:T(8,128)(2,1)S(1)}, u32[]{:S(2)}, u32[]{:S(2)}) collective-permute-start(bf16[2,16,4096]{2,1,0:T(8,128)(2,1)S(1)} %pad_maximum_fusion.refs_0_), channel_id=1, source_target_pairs={{6,0},{0,2},{2,4},{4,6},{7,1},{1,3},{3,5},{5,7},{14,8},{8,10},{10,... | collective-permute-start | bytes 786440 | tf_op jit(solution)/shard_map/ppermute | solution.py:36
  97.8 18.8 %collective-permute-done.5.refs_3_ = bf16[2,16,4096]{2,1,0:T(8,128)(2,1)S(1)} collective-permute-done((bf16[2,16,4096]{2,1,0:T(8,128)(2,1)S(1)}, bf16[2,16,4096]{2,1,0:T(8,128)(2,1)S(1)}, u32[]{:S(2)}, u32[]{:S(2)}) %collective-permute-start.5) | collective-permute-done | bytes 262176 | tf_op jit(solution)/shard_map/ppermute | solution.py:36
  117.2 1.9 collective-permute-start.11
  120.0 2.2 %collective-permute-start.12 = (bf16[2,16,4096]{2,1,0:T(8,128)(2,1)S(1)}, bf16[2,16,4096]{2,1,0:T(8,128)(2,1)}, u32[]{:S(2)}, u32[]{:S(2)}) collective-permute-start(bf16[2,16,4096]{2,1,0:T(8,128)(2,1)S(1)} %collective-permute-done.10.refs_8_), channel_id=1, source_target_pairs={{4,0},{6,2},{0,4},{2,6},{5,1},{7,3},{1,5},{3,7},{12,8},{14,10},{8,... | collective-permute-start | bytes 786440 | tf_op jit(solution)/shard_map/ppermute | solution.py:36
  123.0 3.0 %collective-permute-start.13 = (bf16[2,16,4096]{2,1,0:T(8,128)(2,1)S(1)}, bf16[2,16,4096]{2,1,0:T(8,128)(2,1)}, u32[]{:S(2)}, u32[]{:S(2)}) collective-permute-start(bf16[2,16,4096]{2,1,0:T(8,128)(2,1)S(1)} %collective-permute-done.10.refs_8_), channel_id=1, source_target_pairs={{6,0},{0,2},{2,4},{4,6},{7,1},{1,3},{3,5},{5,7},{14,8},{8,10},{10,... | collective-permute-start | bytes 786440 | tf_op jit(solution)/shard_map/ppermute | solution.py:36
  126.9 4.3 %collective-permute-start.15 = (bf16[2,16,4096]{2,1,0:T(8,128)(2,1)S(1)}, bf16[2,16,4096]{2,1,0:T(8,128)(2,1)}, u32[]{:S(2)}, u32[]{:S(2)}) collective-permute-start(bf16[2,16,4096]{2,1,0:T(8,128)(2,1)S(1)} %collective-permute-done.14.refs_12_), channel_id=1, source_target_pairs={{2,0},{4,2},{6,4},{0,6},{3,1},{5,3},{7,5},{1,7},{10,8},{12,10},{14... | collective-permute-start | bytes 786440 | tf_op jit(solution)/shard_map/ppermute | solution.py:36
  131.9 1.0 copy-done.2
  133.0 1.0 copy-done.4
  134.0 1.0 copy-done.6
  136.0 3.1 %collective-permute-start.16 = (bf16[2,16,4096]{2,1,0:T(8,128)(2,1)S(1)}, bf16[2,16,4096]{2,1,0:T(8,128)(2,1)S(1)}, u32[]{:S(2)}, u32[]{:S(2)}) collective-permute-start(bf16[2,16,4096]{2,1,0:T(8,128)(2,1)S(1)} %collective-permute-done.14.refs_12_), channel_id=1, source_target_pairs={{4,0},{6,2},{0,4},{2,6},{5,1},{7,3},{1,5},{3,7},{12,8},{14,10},{8,... | collective-permute-start | bytes 786440 | tf_op jit(solution)/shard_map/ppermute | solution.py:36
  139.1 2.8 %collective-permute-start.17 = (bf16[2,16,4096]{2,1,0:T(8,128)(2,1)S(1)}, bf16[2,16,4096]{2,1,0:T(8,128)(2,1)S(1)}, u32[]{:S(2)}, u32[]{:S(2)}) collective-permute-start(bf16[2,16,4096]{2,1,0:T(8,128)(2,1)S(1)} %collective-permute-done.14.refs_12_), channel_id=1, source_target_pairs={{6,0},{0,2},{2,4},{4,6},{7,1},{1,3},{3,5},{5,7},{14,8},{8,10},{10,... | collective-permute-start | bytes 786440 | tf_op jit(solution)/shard_map/ppermute | solution.py:36
  141.9 3.7 %collective-permute-start.7 = (bf16[2,16,4096]{2,1,0:T(8,128)(2,1)S(1)}, bf16[2,16,4096]{2,1,0:T(8,128)(2,1)S(1)}, u32[]{:S(2)}, u32[]{:S(2)}) collective-permute-start(bf16[2,16,4096]{2,1,0:T(8,128)(2,1)S(1)} %copy-done.10), channel_id=1, source_target_pairs={{2,0},{4,2},{6,4},{0,6},{3,1},{5,3},{7,5},{1,7},{10,8},{12,10},{14... | collective-permute-start | bytes 786440 | tf_op jit(solution)/shard_map/ppermute | solution.py:36
  145.6 2.5 %collective-permute-start.8 = (bf16[2,16,4096]{2,1,0:T(8,128)(2,1)S(1)}, bf16[2,16,4096]{2,1,0:T(8,128)(2,1)S(1)}, u32[]{:S(2)}, u32[]{:S(2)}) collective-permute-start(bf16[2,16,4096]{2,1,0:T(8,128)(2,1)S(1)} %copy-done.10), channel_id=1, source_target_pairs={{4,0},{6,2},{0,4},{2,6},{5,1},{7,3},{1,5},{3,7},{12,8},{14,10},{8,... | collective-permute-start | bytes 786440 | tf_op jit(solution)/shard_map/ppermute | solution.py:36
  148.1 1.9 %collective-permute-start.9 = (bf16[2,16,4096]{2,1,0:T(8,128)(2,1)S(1)}, bf16[2,16,4096]{2,1,0:T(8,128)(2,1)S(1)}, u32[]{:S(2)}, u32[]{:S(2)}) collective-permute-start(bf16[2,16,4096]{2,1,0:T(8,128)(2,1)S(1)} %copy-done.10), channel_id=1, source_target_pairs={{6,0},{0,2},{2,4},{4,6},{7,1},{1,3},{3,5},{5,7},{14,8},{8,10},{10,... | collective-permute-start | bytes 786440 | tf_op jit(solution)/shard_map/ppermute | solution.py:36
  150.1 1.8 multiply_convert_fusion.refs_16_
  152.0 1.6 collective-permute-done.17.refs_15_
  153.5 3.9 %collective-permute-done.8.refs_6_ = bf16[2,16,4096]{2,1,0:T(8,128)(2,1)S(1)} collective-permute-done((bf16[2,16,4096]{2,1,0:T(8,128)(2,1)S(1)}, bf16[2,16,4096]{2,1,0:T(8,128)(2,1)S(1)}, u32[]{:S(2)}, u32[]{:S(2)}) %collective-permute-start.8) | collective-permute-done | bytes 262176 | tf_op jit(solution)/shard_map/ppermute | solution.py:36
  157.5 6.7 %collective-permute-done.9.refs_7_ = bf16[2,16,4096]{2,1,0:T(8,128)(2,1)S(1)} collective-permute-done((bf16[2,16,4096]{2,1,0:T(8,128)(2,1)S(1)}, bf16[2,16,4096]{2,1,0:T(8,128)(2,1)S(1)}, u32[]{:S(2)}, u32[]{:S(2)}) %collective-permute-start.9) | collective-permute-done | bytes 262176 | tf_op jit(solution)/shard_map/ppermute | solution.py:36
  164.2 4.3 %shard_map.87 = (f32[512,384]{1,0:T(8,128)S(1)}, bf16[512,384]{1,0:T(8,128)(2,1)}) custom-call(bf16[2,16,4096]{2,1,0:T(8,128)(2,1)S(1)} %pad_maximum_fusion.refs_0_, bf16[2,16,4096]{2,1,0:T(8,128)(2,1)S(1)} %copy-done.12, bf16[2,16,4096]{2,1,0:T(8,128)(2,1)S(1)} %copy-done.14, bf16[2,16,4096]{2,1,0:T(8,128)(2,1)S(1)} %copy-done.16, ...), custom_call_target="tpu_custom_call" | custom-call | flops 2147483648 | bytes 9437184 | tf_op jit(solution)/shard_map/pallas_call | solution.py:194
  168.5 2.8 %collective-permute-start.23 = (bf16[512,384]{1,0:T(8,128)(2,1)}, bf16[512,384]{1,0:T(8,128)(2,1)}, u32[]{:S(2)}, u32[]{:S(2)}) collective-permute-start(bf16[512,384]{1,0:T(8,128)(2,1)} %get-tuple-element.8), channel_id=1, source_target_pairs={{0,1},{1,0},{2,3},{3,2},{4,5},{5,4},{6,7},{7,6},{8,9},{9,8},{10,11... | collective-permute-start | bytes 1179656 | tf_op jit(solution)/shard_map/ppermute | solution.py:44
  171.3 1.0 fusion.3
  173.0 1.2 shard_map.88
  175.4 5.7 %all-to-all-start = ((bf16[8,8,256]{2,1,0:T(8,128)(2,1)}), bf16[8,8,256]{2,1,0:T(8,128)(2,1)}, u32[]{:S(2)}, u32[]{:S(2)}) async-start(bf16[8,8,256]{2,1,0:T(8,128)(2,1)} %copy-done.19), calls=%async_computation | async-start | bytes 65536 | tf_op jit(solution)/shard_map/all_to_all | solution.py:210
  181.1 0.9 copy-done.18
  182.0 3.3 %shard_map.89 = bf16[512,128]{1,0:T(8,128)(2,1)} custom-call(s32[3]{0:T(128)S(1)} %pad_add_fusion.where, f32[512,384]{1,0:T(8,128)S(1)} %get-tuple-element.7.own, bf16[512,384]{1,0:T(8,128)(2,1)} %collective-permute-done.23.got, f32[512,128]{1,0:T(8,128)S(1)} %get-tuple-element.23.cosine, f32[512,128]{1,0:T(8,128)S(1)} %get-tuple-element.24.sine, ...), custom_call_target="tpu_custom_call" | custom-call | flops 268435456 | bytes 2097152 | tf_op jit(solution)/shard_map/pallas_call | solution.py:213
  185.3 5.4 %all-to-all-done = bf16[8,8,256]{2,1,0:T(8,128)(2,1)} async-done(((bf16[8,8,256]{2,1,0:T(8,128)(2,1)}), bf16[8,8,256]{2,1,0:T(8,128)(2,1)}, u32[]{:S(2)}, u32[]{:S(2)}) %all-to-all-start) | async-done | bytes 32800 | tf_op jit(solution)/shard_map/all_to_all | solution.py:210
  190.7 1.4 copy.9
  (72 shorter events, 8.4 us)
Async XLA Ops:
  0.6 180.5 %copy-start = (bf16[1,8,512,256]{3,2,1,0:T(8,128)(2,1)S(1)}, bf16[1,8,512,256]{3,2,1,0:T(8,128)(2,1)}, u32[]{:S(2)}) copy-start(bf16[1,8,512,256]{3,2,1,0:T(8,128)(2,1)} %param.11) | copy-start | bytes 6291460
  2.9 20.3 %collective-permute-start = (bf16[8,4096]{1,0:T(8,128)(2,1)S(1)}, bf16[8,4096]{1,0:T(8,128)(2,1)S(1)}, u32[]{:S(2)}, u32[]{:S(2)}) collective-permute-start(bf16[8,4096]{1,0:T(8,128)(2,1)S(1)} %get-tuple-element.18), channel_id=1, source_target_pairs={{0,64},{1,65},{64,128},{65,129},{128,192},{129,193},{192,256},{193... | collective-permute-start | bytes 196616 | tf_op jit(solution)/shard_map/ppermute | solution.py:161
  19.2 18.0 %collective-permute-start.1 = (bf16[8,4096]{1,0:T(8,128)(2,1)S(1)}, bf16[8,4096]{1,0:T(8,128)(2,1)S(1)}, u32[]{:S(2)}, u32[]{:S(2)}) collective-permute-start(bf16[8,4096]{1,0:T(8,128)(2,1)S(1)} %get-tuple-element.19), channel_id=1, source_target_pairs={{0,65},{1,64},{64,129},{65,128},{128,193},{129,192},{192,257},{193... | collective-permute-start | bytes 196616 | tf_op jit(solution)/shard_map/ppermute | solution.py:162
  21.7 66.3 %copy-start.22 = (bf16[1,8192,128]{2,1,0:T(8,128)(2,1)S(1)}, bf16[1,8192,128]{2,1,0:T(8,128)(2,1)}, u32[]{:S(2)}) copy-start(bf16[1,8192,128]{2,1,0:T(8,128)(2,1)} %param.9) | copy-start | bytes 6291460
  37.2 18.8 %collective-permute-start.2 = (bf16[1,16,4096]{2,1,0:T(8,128)(2,1)S(1)}, bf16[1,16,4096]{2,1,0:T(8,128)(2,1)S(1)}, u32[]{:S(2)}, u32[]{:S(2)}) collective-permute-start(bf16[1,16,4096]{2,1,0:T(8,128)(2,1)S(1)} %fusion.2), channel_id=1, source_target_pairs={{0,32},{8,40},{16,48},{24,56},{32,0},{40,8},{48,16},{56,24},{1,33}... | collective-permute-start | bytes 393224 | tf_op jit(solution)/shard_map/ppermute | solution.py:40
  41.4 28.9 %collective-permute-start.19 = (bf16[32,4096]{1,0:T(8,128)(2,1)S(1)}, bf16[32,4096]{1,0:T(8,128)(2,1)S(1)}, u32[]{:S(2)}, u32[]{:S(2)}) collective-permute-start(bf16[32,4096]{1,0:T(8,128)(2,1)S(1)} %get-tuple-element.17), channel_id=1, source_target_pairs={{0,1},{1,0},{2,3},{3,2},{4,5},{5,4},{6,7},{7,6},{8,9},{9,8},{10,11... | collective-permute-start | bytes 786440 | tf_op jit(solution)/shard_map/ppermute | solution.py:44
  56.0 21.8 %collective-permute-start.10 = (bf16[2,16,4096]{2,1,0:T(8,128)(2,1)S(1)}, bf16[2,16,4096]{2,1,0:T(8,128)(2,1)S(1)}, u32[]{:S(2)}, u32[]{:S(2)}) collective-permute-start(bf16[2,16,4096]{2,1,0:T(8,128)(2,1)S(1)} %pad_maximum_fusion.refs_0_), channel_id=1, source_target_pairs={{0,16},{8,24},{16,0},{24,8},{32,48},{40,56},{48,32},{56,40},{1,17}... | collective-permute-start | bytes 786440 | tf_op jit(solution)/shard_map/ppermute | solution.py:40
  57.9 24.5 %collective-permute-start.14 = (bf16[2,16,4096]{2,1,0:T(8,128)(2,1)S(1)}, bf16[2,16,4096]{2,1,0:T(8,128)(2,1)S(1)}, u32[]{:S(2)}, u32[]{:S(2)}) collective-permute-start(bf16[2,16,4096]{2,1,0:T(8,128)(2,1)S(1)} %pad_maximum_fusion.refs_0_), channel_id=1, source_target_pairs={{0,24},{8,16},{16,8},{24,0},{32,56},{40,48},{48,40},{56,32},{1,25}... | collective-permute-start | bytes 786440 | tf_op jit(solution)/shard_map/ppermute | solution.py:40
  61.7 23.0 %collective-permute-start.6 = (bf16[2,16,4096]{2,1,0:T(8,128)(2,1)S(1)}, bf16[2,16,4096]{2,1,0:T(8,128)(2,1)S(1)}, u32[]{:S(2)}, u32[]{:S(2)}) collective-permute-start(bf16[2,16,4096]{2,1,0:T(8,128)(2,1)S(1)} %pad_maximum_fusion.refs_0_), channel_id=1, source_target_pairs={{0,8},{8,0},{16,24},{24,16},{32,40},{40,32},{48,56},{56,48},{1,9},... | collective-permute-start | bytes 786440 | tf_op jit(solution)/shard_map/ppermute | solution.py:40
  64.4 25.1 %collective-permute-start.3 = (bf16[2,16,4096]{2,1,0:T(8,128)(2,1)S(1)}, bf16[2,16,4096]{2,1,0:T(8,128)(2,1)S(1)}, u32[]{:S(2)}, u32[]{:S(2)}) collective-permute-start(bf16[2,16,4096]{2,1,0:T(8,128)(2,1)S(1)} %pad_maximum_fusion.refs_0_), channel_id=1, source_target_pairs={{2,0},{4,2},{6,4},{0,6},{3,1},{5,3},{7,5},{1,7},{10,8},{12,10},{14... | collective-permute-start | bytes 786440 | tf_op jit(solution)/shard_map/ppermute | solution.py:36
  70.3 23.2 %collective-permute-start.4 = (bf16[2,16,4096]{2,1,0:T(8,128)(2,1)S(1)}, bf16[2,16,4096]{2,1,0:T(8,128)(2,1)S(1)}, u32[]{:S(2)}, u32[]{:S(2)}) collective-permute-start(bf16[2,16,4096]{2,1,0:T(8,128)(2,1)S(1)} %pad_maximum_fusion.refs_0_), channel_id=1, source_target_pairs={{4,0},{6,2},{0,4},{2,6},{5,1},{7,3},{1,5},{3,7},{12,8},{14,10},{8,... | collective-permute-start | bytes 786440 | tf_op jit(solution)/shard_map/ppermute | solution.py:36
  72.7 58.5 %copy-start.23 = (f32[1,8192]{1,0:T(1,128)S(1)}, f32[1,8192]{1,0:T(1,128)}, u32[]{:S(2)}) copy-start(f32[1,8192]{1,0:T(1,128)} %param.8) | copy-start | bytes 98308
  77.8 41.4 %collective-permute-start.20 = (bf16[64,4096]{1,0:T(8,128)(2,1)S(1)}, bf16[64,4096]{1,0:T(8,128)(2,1)S(1)}, u32[]{:S(2)}, u32[]{:S(2)}) collective-permute-start(bf16[64,4096]{1,0:T(8,128)(2,1)S(1)} %maximum_select_fusion.mine), channel_id=1, source_target_pairs={{2,0},{4,2},{6,4},{0,6},{3,1},{5,3},{7,5},{1,7},{10,8},{12,10},{14... | collective-permute-start | bytes 1572872 | tf_op jit(solution)/shard_map/ppermute | solution.py:36
  82.4 56.7 %copy-start.7 = (bf16[2,16,4096]{2,1,0:T(8,128)(2,1)}, bf16[2,16,4096]{2,1,0:T(8,128)(2,1)S(1)}, u32[]{:S(2)}) copy-start(bf16[2,16,4096]{2,1,0:T(8,128)(2,1)S(1)} %collective-permute-done.14.refs_12_) | copy-start | bytes 786436
  82.4 39.8 %collective-permute-start.21 = (bf16[64,4096]{1,0:T(8,128)(2,1)S(1)}, bf16[64,4096]{1,0:T(8,128)(2,1)S(1)}, u32[]{:S(2)}, u32[]{:S(2)}) collective-permute-start(bf16[64,4096]{1,0:T(8,128)(2,1)S(1)} %maximum_select_fusion.mine), channel_id=1, source_target_pairs={{4,0},{6,2},{0,4},{2,6},{5,1},{7,3},{1,5},{3,7},{12,8},{14,10},{8,... | collective-permute-start | bytes 1572872 | tf_op jit(solution)/shard_map/ppermute | solution.py:36
  84.7 0.7 copy-start.9
  85.4 40.7 %collective-permute-start.22 = (bf16[64,4096]{1,0:T(8,128)(2,1)S(1)}, bf16[64,4096]{1,0:T(8,128)(2,1)S(1)}, u32[]{:S(2)}, u32[]{:S(2)}) collective-permute-start(bf16[64,4096]{1,0:T(8,128)(2,1)S(1)} %maximum_select_fusion.mine), channel_id=1, source_target_pairs={{6,0},{0,2},{2,4},{4,6},{7,1},{1,3},{3,5},{5,7},{14,8},{8,10},{10,... | collective-permute-start | bytes 1572872 | tf_op jit(solution)/shard_map/ppermute | solution.py:36
  89.5 0.7 copy-start.11
  90.2 57.9 %collective-permute-start.18 = (bf16[4096,128]{1,0:T(8,128)(2,1)}, bf16[4096,128]{1,0:T(8,128)(2,1)}, u32[]{:S(2)}, u32[]{:S(2)}) collective-permute-start(bf16[4096,128]{1,0:T(8,128)(2,1)} %get-tuple-element.15), channel_id=1, source_target_pairs={{0,1},{1,0},{2,3},{3,2},{4,5},{5,4},{6,7},{7,6},{8,9},{9,8},{10,11... | collective-permute-start | bytes 3145736 | tf_op jit(solution)/shard_map/ppermute | solution.py:44
  93.6 0.7 copy-start.13
  94.2 22.3 %collective-permute-start.5 = (bf16[2,16,4096]{2,1,0:T(8,128)(2,1)S(1)}, bf16[2,16,4096]{2,1,0:T(8,128)(2,1)S(1)}, u32[]{:S(2)}, u32[]{:S(2)}) collective-permute-start(bf16[2,16,4096]{2,1,0:T(8,128)(2,1)S(1)} %pad_maximum_fusion.refs_0_), channel_id=1, source_target_pairs={{6,0},{0,2},{2,4},{4,6},{7,1},{1,3},{3,5},{5,7},{14,8},{8,10},{10,... | collective-permute-start | bytes 786440 | tf_op jit(solution)/shard_map/ppermute | solution.py:36
  116.5 0.7 copy-start.15
  117.2 18.7 %collective-permute-start.11 = (bf16[2,16,4096]{2,1,0:T(8,128)(2,1)S(1)}, bf16[2,16,4096]{2,1,0:T(8,128)(2,1)}, u32[]{:S(2)}, u32[]{:S(2)}) collective-permute-start(bf16[2,16,4096]{2,1,0:T(8,128)(2,1)S(1)} %collective-permute-done.10.refs_8_), channel_id=1, source_target_pairs={{2,0},{4,2},{6,4},{0,6},{3,1},{5,3},{7,5},{1,7},{10,8},{12,10},{14... | collective-permute-start | bytes 786440 | tf_op jit(solution)/shard_map/ppermute | solution.py:36
  119.2 0.8 copy-start.1
  120.0 19.1 %collective-permute-start.12 = (bf16[2,16,4096]{2,1,0:T(8,128)(2,1)S(1)}, bf16[2,16,4096]{2,1,0:T(8,128)(2,1)}, u32[]{:S(2)}, u32[]{:S(2)}) collective-permute-start(bf16[2,16,4096]{2,1,0:T(8,128)(2,1)S(1)} %collective-permute-done.10.refs_8_), channel_id=1, source_target_pairs={{4,0},{6,2},{0,4},{2,6},{5,1},{7,3},{1,5},{3,7},{12,8},{14,10},{8,... | collective-permute-start | bytes 786440 | tf_op jit(solution)/shard_map/ppermute | solution.py:36
  122.2 0.8 copy-start.3
  123.0 18.8 %collective-permute-start.13 = (bf16[2,16,4096]{2,1,0:T(8,128)(2,1)S(1)}, bf16[2,16,4096]{2,1,0:T(8,128)(2,1)}, u32[]{:S(2)}, u32[]{:S(2)}) collective-permute-start(bf16[2,16,4096]{2,1,0:T(8,128)(2,1)S(1)} %collective-permute-done.10.refs_8_), channel_id=1, source_target_pairs={{6,0},{0,2},{2,4},{4,6},{7,1},{1,3},{3,5},{5,7},{14,8},{8,10},{10,... | collective-permute-start | bytes 786440 | tf_op jit(solution)/shard_map/ppermute | solution.py:36
  126.1 0.8 copy-start.5
  126.9 18.8 %collective-permute-start.15 = (bf16[2,16,4096]{2,1,0:T(8,128)(2,1)S(1)}, bf16[2,16,4096]{2,1,0:T(8,128)(2,1)}, u32[]{:S(2)}, u32[]{:S(2)}) collective-permute-start(bf16[2,16,4096]{2,1,0:T(8,128)(2,1)S(1)} %collective-permute-done.14.refs_12_), channel_id=1, source_target_pairs={{2,0},{4,2},{6,4},{0,6},{3,1},{5,3},{7,5},{1,7},{10,8},{12,10},{14... | collective-permute-start | bytes 786440 | tf_op jit(solution)/shard_map/ppermute | solution.py:36
  131.9 1.0 copy-start.2
  133.0 1.0 copy-start.4
  134.0 1.0 copy-start.6
  135.1 6.8 %copy-start.10 = (bf16[2,16,4096]{2,1,0:T(8,128)(2,1)S(1)}, bf16[2,16,4096]{2,1,0:T(8,128)(2,1)}, u32[]{:S(2)}) copy-start(bf16[2,16,4096]{2,1,0:T(8,128)(2,1)} %copy-done.9) | copy-start | bytes 786436
  135.1 15.0 %copy-start.21 = (bf16[4096,128]{1,0:T(8,128)(2,1)S(1)}, bf16[4096,128]{1,0:T(8,128)(2,1)}, u32[]{:S(2)}) copy-start(bf16[4096,128]{1,0:T(8,128)(2,1)} %get-tuple-element.14) | copy-start | bytes 3145732
  136.0 16.0 %collective-permute-start.16 = (bf16[2,16,4096]{2,1,0:T(8,128)(2,1)S(1)}, bf16[2,16,4096]{2,1,0:T(8,128)(2,1)S(1)}, u32[]{:S(2)}, u32[]{:S(2)}) collective-permute-start(bf16[2,16,4096]{2,1,0:T(8,128)(2,1)S(1)} %collective-permute-done.14.refs_12_), channel_id=1, source_target_pairs={{4,0},{6,2},{0,4},{2,6},{5,1},{7,3},{1,5},{3,7},{12,8},{14,10},{8,... | collective-permute-start | bytes 786440 | tf_op jit(solution)/shard_map/ppermute | solution.py:36
  139.1 14.5 %collective-permute-start.17 = (bf16[2,16,4096]{2,1,0:T(8,128)(2,1)S(1)}, bf16[2,16,4096]{2,1,0:T(8,128)(2,1)S(1)}, u32[]{:S(2)}, u32[]{:S(2)}) collective-permute-start(bf16[2,16,4096]{2,1,0:T(8,128)(2,1)S(1)} %collective-permute-done.14.refs_12_), channel_id=1, source_target_pairs={{6,0},{0,2},{2,4},{4,6},{7,1},{1,3},{3,5},{5,7},{14,8},{8,10},{10,... | collective-permute-start | bytes 786440 | tf_op jit(solution)/shard_map/ppermute | solution.py:36
  141.9 11.7 %collective-permute-start.7 = (bf16[2,16,4096]{2,1,0:T(8,128)(2,1)S(1)}, bf16[2,16,4096]{2,1,0:T(8,128)(2,1)S(1)}, u32[]{:S(2)}, u32[]{:S(2)}) collective-permute-start(bf16[2,16,4096]{2,1,0:T(8,128)(2,1)S(1)} %copy-done.10), channel_id=1, source_target_pairs={{2,0},{4,2},{6,4},{0,6},{3,1},{5,3},{7,5},{1,7},{10,8},{12,10},{14... | collective-permute-start | bytes 786440 | tf_op jit(solution)/shard_map/ppermute | solution.py:36
  145.6 11.8 %collective-permute-start.8 = (bf16[2,16,4096]{2,1,0:T(8,128)(2,1)S(1)}, bf16[2,16,4096]{2,1,0:T(8,128)(2,1)S(1)}, u32[]{:S(2)}, u32[]{:S(2)}) collective-permute-start(bf16[2,16,4096]{2,1,0:T(8,128)(2,1)S(1)} %copy-done.10), channel_id=1, source_target_pairs={{4,0},{6,2},{0,4},{2,6},{5,1},{7,3},{1,5},{3,7},{12,8},{14,10},{8,... | collective-permute-start | bytes 786440 | tf_op jit(solution)/shard_map/ppermute | solution.py:36
  148.1 16.0 %collective-permute-start.9 = (bf16[2,16,4096]{2,1,0:T(8,128)(2,1)S(1)}, bf16[2,16,4096]{2,1,0:T(8,128)(2,1)S(1)}, u32[]{:S(2)}, u32[]{:S(2)}) collective-permute-start(bf16[2,16,4096]{2,1,0:T(8,128)(2,1)S(1)} %copy-done.10), channel_id=1, source_target_pairs={{6,0},{0,2},{2,4},{4,6},{7,1},{1,3},{3,5},{5,7},{14,8},{8,10},{10,... | collective-permute-start | bytes 786440 | tf_op jit(solution)/shard_map/ppermute | solution.py:36
  150.1 14.1 %copy-start.8 = (bf16[2,16,4096]{2,1,0:T(8,128)(2,1)S(1)}, bf16[2,16,4096]{2,1,0:T(8,128)(2,1)}, u32[]{:S(2)}) copy-start(bf16[2,16,4096]{2,1,0:T(8,128)(2,1)} %copy-done.7) | copy-start | bytes 786436
  150.1 14.1 %copy-start.12 = (bf16[2,16,4096]{2,1,0:T(8,128)(2,1)S(1)}, bf16[2,16,4096]{2,1,0:T(8,128)(2,1)}, u32[]{:S(2)}) copy-start(bf16[2,16,4096]{2,1,0:T(8,128)(2,1)} %copy-done.11) | copy-start | bytes 786436
  150.1 14.1 %copy-start.14 = (bf16[2,16,4096]{2,1,0:T(8,128)(2,1)S(1)}, bf16[2,16,4096]{2,1,0:T(8,128)(2,1)}, u32[]{:S(2)}) copy-start(bf16[2,16,4096]{2,1,0:T(8,128)(2,1)} %copy-done.13) | copy-start | bytes 786436
  150.1 14.1 %copy-start.16 = (bf16[2,16,4096]{2,1,0:T(8,128)(2,1)S(1)}, bf16[2,16,4096]{2,1,0:T(8,128)(2,1)}, u32[]{:S(2)}) copy-start(bf16[2,16,4096]{2,1,0:T(8,128)(2,1)} %copy-done.15) | copy-start | bytes 786436
  168.5 4.5 %copy-start.20 = (s32[1,8]{1,0:T(1,128)S(1)}, s32[1,8]{1,0:T(1,128)}, u32[]{:S(2)}) copy-start(s32[1,8]{1,0:T(1,128)} %param.13) | copy-start | bytes 100
  168.5 4.5 %collective-permute-start.23 = (bf16[512,384]{1,0:T(8,128)(2,1)}, bf16[512,384]{1,0:T(8,128)(2,1)}, u32[]{:S(2)}, u32[]{:S(2)}) collective-permute-start(bf16[512,384]{1,0:T(8,128)(2,1)} %get-tuple-element.8), channel_id=1, source_target_pairs={{0,1},{1,0},{2,3},{3,2},{4,5},{5,4},{6,7},{7,6},{8,9},{9,8},{10,11... | collective-permute-start | bytes 1179656 | tf_op jit(solution)/shard_map/ppermute | solution.py:44
  174.1 0.7 copy-start.17
  175.4 15.3 %all-to-all-start = ((bf16[8,8,256]{2,1,0:T(8,128)(2,1)}), bf16[8,8,256]{2,1,0:T(8,128)(2,1)}, u32[]{:S(2)}, u32[]{:S(2)}) async-start(bf16[8,8,256]{2,1,0:T(8,128)(2,1)} %copy-done.19), calls=%async_computation | async-start | bytes 65536 | tf_op jit(solution)/shard_map/all_to_all | solution.py:210
  181.1 0.9 copy-start.18
  (1 other events, 0.6 us)

commit v2 on v1

--- a/solution.py
+++ b/solution.py
@@ -45,7 +45,9 @@
 
 
 def place(slot, z0, y0):
-    return ((z0 ^ (slot >> 2)) << 2) | ((y0 + (slot & 3)) & 3)
+    group, k, part = slot >> 3, (slot >> 1) & 3, slot & 1
+    z = z0 ^ group ^ (group >> 1) ^ (4 * (1 - part))
+    return (z << 2) | ((y0 + k) & 3)
 
 
 def tokens_of(row, z0, y0):
@@ -53,30 +55,42 @@
 
 
 def project_kernel(*refs):
-    pieces = refs[:16]
-    wq, wkv, own, send, x = refs[16:]
-    for b in range(4):
-        for k in range(4):
-            for part in range(2):
-                slot = (b + 4 * part) * 4 + k
-                x[slot * ROWS : (slot + 1) * ROWS, :] = pieces[b * 4 + k][part]
-    kv = lax.dot_general(
-        x[...], wkv[...], (((1,), (1,)), ((), ())), preferred_element_type=F32
-    )
+    count = len(refs) - 6
+    pieces = refs[:count]
+    wq, wkv, own, send, x, sems = refs[count:]
+    copies = [
+        pltpu.make_async_copy(piece, x.at[2 * i : 2 * i + 2], sems.at[i])
+        for i, piece in enumerate(pieces)
+    ]
+    for copy in copies:
+        copy.start()
+    for copy in copies:
+        copy.wait()
+    rows = x[...].reshape(2 * ROWS * count, x.shape[2])
+    kv = lax.dot_general(rows, wkv[...], (((1,), (1,)), ((), ())), preferred_element_type=F32)
     own[:, HD:] = kv
     send[:, HD:] = kv.astype(BF)
-    q = jnp.dot(x[...], wq[...], preferred_element_type=F32)
+    q = jnp.dot(rows, wq[...], preferred_element_type=F32)
     own[:, :HD] = q[:, :HD]
     send[:, :HD] = q[:, HD:].astype(BF)
 
 
+def join_kernel(first, second, *rest):
+    pair = rest[-1]
+    pair[0] = first[0]
+    pair[1] = second[0]
+
+
 def turn(v, cosine, sine):
     return v * cosine + pltpu.roll(v, HD // 2, 1) * sine
 
 
-def kv_kernel(where, owner, own, got, cosine, sine, keys, values, blocks, held):
+def kv_kernel(
+    where, owner, own1, got1, own2, got2, cosine, sine, keys, values, blocks, held
+):
     z0, y0, c0 = where[0], where[1], where[2]
-    raw = (own[:, HD:] + got[:, HD:].astype(F32)).astype(BF)
+    raw = jnp.concatenate([o[:, HD:] + g[:, HD:].astype(F32) for o, g in ((own1, got1), (own2, got2))])
+    raw = raw.astype(BF)
     k = turn(raw[:, :HD].astype(F32), cosine[...], sine[...]).astype(BF)
     v = raw[:, HD:]
     keys[...] = k
@@ -92,9 +106,11 @@
         blocks[z] = held[pl.ds(pl.multiple_of(block * 8, 8), 8), :].astype(BF)
 
 
-def attend_kernel(where, own, got, cosine, sine, keys, values, resident, out):
+def attend_kernel(
+    where, own1, got1, own2, got2, cosine, sine, keys, values, resident, out
+):
     z0, y0 = where[0], where[1]
-    q = own[:, :HD] + got[:, :HD].astype(F32)
+    q = jnp.concatenate([o[:, :HD] + g[:, :HD].astype(F32) for o, g in ((own1, got1), (own2, got2))])
     q = (turn(q, cosine[...], sine[...]) * HD ** (-0.5)).astype(BF)
     nt = (((1,), (1,)), ((), ()))
     old = lax.dot_general(q, resident[:, :HD], nt, preferred_element_type=F32)
@@ -126,16 +142,17 @@
 
 VMEM = pl.BlockSpec(memory_space=pltpu.VMEM)
 SMEM = pl.BlockSpec(memory_space=pltpu.SMEM)
-
-
-def call(kernel, shapes, specs, scratch=(), flops=0, moved=0, exps=0):
+ANY = pl.BlockSpec(memory_space=pl.ANY)
+
+
+def call(kernel, shapes, specs, scratch=(), flops=0, moved=0, exps=0, limit=24):
     return pl.pallas_call(
         kernel,
         out_shape=shapes,
         in_specs=specs,
         out_specs=jax.tree.map(lambda _: VMEM, shapes),
         scratch_shapes=scratch,
-        compiler_params=pltpu.CompilerParams(vmem_limit_bytes=40 * 2**20),
+        compiler_params=pltpu.CompilerParams(vmem_limit_bytes=limit * 2**20),
         cost_estimate=pl.CostEstimate(flops=flops, bytes_accessed=moved, transcendentals=exps),
     )
 
@@ -156,10 +173,17 @@
     kept = lax.dynamic_slice_in_dim(rows, c0 * half, half, 1)
     crossed = lax.dynamic_slice_in_dim(rows, (1 - c0) * half, half, 1)
     sections = lax.axis_size("s")
-    straight = [(s * 2 + c, (s + 1) % sections * 2 + c) for s in range(sections) for c in (0, 1)]
-    across = [(s * 2 + c, (s + 1) % sections * 2 + 1 - c) for s in range(sections) for c in (0, 1)]
-    same = lax.ppermute(kept, ("s", "c"), straight)
-    other = lax.ppermute(crossed, ("s", "c"), across)
+    steps = [
+        [
+            ((s * NZ + z) * 2 + c, ((s + 1) % sections * NZ + (z ^ 4)) * 2 + (c ^ flip))
+            for s in range(sections)
+            for z in range(NZ)
+            for c in (0, 1)
+        ]
+        for flip in (0, 1)
+    ]
+    same = lax.ppermute(kept, ("s", "z", "c"), steps[0])
+    other = lax.ppermute(crossed, ("s", "z", "c"), steps[1])
     piece = jnp.where(c0 == 0, jnp.stack([same, other]), jnp.stack([other, same]))
     piece = piece.reshape(1, ROWS, half)
 
@@ -181,43 +205,54 @@
         where, gain[None], kv_chip, *kv_others
     )
 
-    pair = jnp.concatenate([piece, across_z(piece, 4)])
-    groups = [pair] + [across_z(pair, k) for k in (1, 2, 3)]
-    pieces = [p if k == 0 else along_y(p, k) for p in groups for k in range(NY)]
-
     tokens = tokens_of(jnp.arange(TOKENS, dtype=jnp.int32), z0, y0)
     angles = (block_start[0] + tokens).astype(F32)[:, None] * frequencies(HD)[None, :]
     cosine, sine = jnp.cos(angles), jnp.sin(angles)
     cosine = jnp.concatenate([cosine, cosine], axis=1)
     sine = jnp.concatenate([-sine, sine], axis=1)
 
-    own, send = call(
-        project_kernel,
-        (shaped(TOKENS, 3 * HD, dtype=F32), shaped(TOKENS, 3 * HD)),
-        [VMEM] * 18,
-        scratch=[pltpu.VMEM((TOKENS, half), BF)],
-        flops=2 * TOKENS * half * 512,
-        moved=9 * 2**20,
-    )(*pieces, wq, wkv)
-    got = swap_core(send)
+    pair = call(join_kernel, shaped(2, ROWS, half), [VMEM] * 2 + [ANY] * 4, moved=2**19)(
+        piece, across_z(piece, 4), wq, wkv, cosine, sine
+    )
+    groups = [pair] + [across_z(pair, k) for k in (1, 3, 2)]
+    pieces = [p if k == 0 else along_y(p, k) for p in groups for k in range(NY)]
+
+    def project(pieces):
+        tokens = len(pieces) * 2 * ROWS
+        return call(
+            project_kernel,
+            (shaped(tokens, 3 * HD, dtype=F32), shaped(tokens, 3 * HD)),
+            [ANY] * len(pieces) + [VMEM] * 2,
+            scratch=[
+                pltpu.VMEM((2 * len(pieces), ROWS, half), BF),
+                pltpu.SemaphoreType.DMA((len(pieces),)),
+            ],
+            flops=2 * tokens * half * 512,
+            moved=9 * 2**20,
+        )(*pieces, wq, wkv)
+
+    own1, send1 = project(pieces[:12])
+    got1 = swap_core(send1)
+    own2, send2 = project(pieces[12:])
+    got2 = swap_core(send2)
     keys, values, blocks = call(
         kv_kernel,
         (shaped(TOKENS, HD), shaped(TOKENS, HD), shaped(NZ, 8, 2 * HD)),
-        [SMEM, SMEM] + [VMEM] * 4,
+        [SMEM, SMEM] + [VMEM] * 6,
         scratch=[pltpu.VMEM((TOKENS, 2 * HD), F32)],
         moved=2**21,
-    )(where, decode_owner[0], own, got, cosine, sine)
+    )(where, decode_owner[0], own1, got1, own2, got2, cosine, sine)
     spread = lax.all_to_all(blocks, "z", 0, 0)
     decode_kv = jnp.transpose(spread, (1, 0, 2))[None]
     resident = lax.dynamic_index_in_dim(resident_cache[0], z0, 0, keepdims=False)
     attn = call(
         attend_kernel,
         shaped(TOKENS, HD),
-        [SMEM] + [VMEM] * 7,
+        [SMEM] + [VMEM] * 9,
         flops=4 * TOKENS * 1024 * HD,
         moved=2**21,
         exps=TOKENS * 1024,
-    )(where, own, got, cosine, sine, keys, values, resident)
+    )(where, own1, got1, own2, got2, cosine, sine, keys, values, resident)
     return attn[None], decode_kv
 
 

time: 193 us -> 160 us (0.83)
  waiting for transfers between devices: 68.9 us -> 30.9 us
  starting transfers between devices: 91.7 us -> 99.3 us
  local copies, waits for them, and re-layouts: 14.5 us -> 10.1 us
    ppermute x2, waiting for transfers between devices: 15.5 us -> 0.01 us  [the longest x1 0.01 us: body(): other = lax.ppermute(crossed, ('s', 'z', 'c'), steps[1])]
    ppermute x15, waiting for transfers between devices: 31 us -> 19.8 us  [along_y(): return lax.ppermute(value, 'y', [((i + k) % NY, i) for i in range(NY)])]
    ppermute x4, waiting for transfers between devices: 16.6 us -> 6.29 us  [across_z(): return lax.ppermute(value, 'z', [(i, i ^ k) for i in range(NZ)])]
    unnamed x49 -> x25, local copies, waits for them, and re-layouts: 11.9 us -> 6.29 us
    ppermute x3 -> x4, starting transfers between devices: 9.08 us -> 14.4 us  [swap_core(): return lax.ppermute(value, 'c', [(0, 1), (1, 0)])]
    ppermute x2, starting transfers between devices: 18.8 us -> 15.9 us  [the longest x1 13.8 us: body(): other = lax.ppermute(crossed, ('s', 'z', 'c'), steps[1])]
    all_to_all x1, starting transfers between devices: 5.67 us -> 8.38 us  [body(): spread = lax.all_to_all(blocks, 'z', 0, 0)]
    ppermute x4, starting transfers between devices: 11.6 us -> 13.7 us  [across_z(): return lax.ppermute(value, 'z', [(i, i ^ k) for i in range(NZ)])]
  transfers between devices with their start and end apart: 25 -> 26, of which waited for: 10 -> 7; matrix products, arithmetic and copies ran while one was open for 3% -> 5% of each run, Pallas kernels for 2% -> 6%
where the time goes in v2:
time: 160 us; the launch traced here: 159 us
  starting transfers between devices  99.3 us (62%)
  waiting for transfers between devices  30.9 us (19%)
  Pallas kernels  10.5 us (7%)
  local copies, waits for them, and re-layouts  10.1 us (6%)
  other arithmetic  6.38 us (4%)
  between operations  1.81 us (1%)
    ppermute x15, starting transfers between devices, along_y(): return lax.ppermute(value, 'y', [((i + k) % NY, i) for i in range(NY)])  46.9 us
    ppermute x15, waiting for transfers between devices, along_y(): return lax.ppermute(value, 'y', [((i + k) % NY, i) for i in range(NY)])  19.8 us
    ppermute x4, starting transfers between devices, swap_core(): return lax.ppermute(value, 'c', [(0, 1), (1, 0)])  14.4 us
    ppermute x1, starting transfers between devices, body(): other = lax.ppermute(crossed, ('s', 'z', 'c'), steps[1])  13.8 us
    ppermute x4, starting transfers between devices, across_z(): return lax.ppermute(value, 'z', [(i, i ^ k) for i in range(NZ)])  13.7 us
    all_to_all x1, starting transfers between devices, body(): spread = lax.all_to_all(blocks, 'z', 0, 0)  8.38 us
    ppermute x4, waiting for transfers between devices, across_z(): return lax.ppermute(value, 'z', [(i, i ^ k) for i in range(NZ)])  6.29 us
    unnamed x25, local copies, waits for them, and re-layouts  6.29 us
  transfers between devices with their start and end apart: 26, of which 7 were waited for; matrix products, arithmetic and copies ran while one was open for 5% of the time, Pallas kernels for 6%

profile of v2, /device:TPU:1, one launch (start us, length us, event | category | flops | bytes accessed | tf_op | source)
XLA Modules:
  0.0 158.9 jit_solution(13332521129016437875)
XLA Ops:
  0.7 1.2 fusion
  1.9 1.0 fusion.1
  3.5 13.8 %collective-permute-start.1 = (bf16[8,4096]{1,0:T(8,128)(2,1)}, bf16[8,4096]{1,0:T(8,128)(2,1)}, u32[]{:S(2)}, u32[]{:S(2)}) collective-permute-start(bf16[8,4096]{1,0:T(8,128)(2,1)} %get-tuple-element.23), channel_id=1, source_target_pairs={{0,97},{1,96},{8,105},{9,104},{16,113},{17,112},{24,121},{25,120},... | collective-permute-start | bytes 196616 | tf_op jit(solution)/shard_map/ppermute | solution.py:186
  17.4 2.1 %collective-permute-start = (bf16[8,4096]{1,0:T(8,128)(2,1)S(1)}, bf16[8,4096]{1,0:T(8,128)(2,1)}, u32[]{:S(2)}, u32[]{:S(2)}) collective-permute-start(bf16[8,4096]{1,0:T(8,128)(2,1)S(1)} %get-tuple-element.22), channel_id=1, source_target_pairs={{0,96},{1,97},{8,104},{9,105},{16,112},{17,113},{24,120},{25,121},... | collective-permute-start | bytes 196616 | tf_op jit(solution)/shard_map/ppermute | solution.py:185
  19.5 3.0 %dynamic-slice_bitcast_fusion.1 = (bf16[4096,128]{1,0:T(8,128)(2,1)}, bf16[4096,128]{1,0:T(8,128)(2,1)}) fusion(bf16[1,8192,128]{2,1,0:T(8,128)(2,1)} %param.9, s32[]{:T(128)S(6)} %select_n.57, s32[]{:T(128)S(6)} %select_n.58), kind=kLoop, calls=%fused_computation.2 | loop fusion | bytes 4194312 | tf_op jit(solution)/shard_map/dynamic_slice | solution.py:191
  22.5 2.3 %collective-permute-start.3 = (bf16[4096,128]{1,0:T(8,128)(2,1)}, bf16[4096,128]{1,0:T(8,128)(2,1)}, u32[]{:S(2)}, u32[]{:S(2)}) collective-permute-start(bf16[4096,128]{1,0:T(8,128)(2,1)} %get-tuple-element.19), channel_id=1, source_target_pairs={{0,1},{1,0},{2,3},{3,2},{4,5},{5,4},{6,7},{7,6},{8,9},{9,8},{10,11... | collective-permute-start | bytes 3145736 | tf_op jit(solution)/shard_map/ppermute | solution.py:44
  24.9 2.0 %collective-permute-start.4 = (bf16[32,4096]{1,0:T(8,128)(2,1)S(1)}, bf16[32,4096]{1,0:T(8,128)(2,1)S(1)}, u32[]{:S(2)}, u32[]{:S(2)}) collective-permute-start(bf16[32,4096]{1,0:T(8,128)(2,1)S(1)} %get-tuple-element.21), channel_id=1, source_target_pairs={{0,1},{1,0},{2,3},{3,2},{4,5},{5,4},{6,7},{7,6},{8,9},{9,8},{10,11... | collective-permute-start | bytes 786440 | tf_op jit(solution)/shard_map/ppermute | solution.py:44
  27.6 1.0 fusion.3
  28.9 4.6 %collective-permute-start.5 = (bf16[64,4096]{1,0:T(8,128)(2,1)S(1)}, bf16[64,4096]{1,0:T(8,128)(2,1)S(1)}, u32[]{:S(2)}, u32[]{:S(2)}) collective-permute-start(bf16[64,4096]{1,0:T(8,128)(2,1)S(1)} %maximum_select_fusion.mine), channel_id=1, source_target_pairs={{2,0},{4,2},{6,4},{0,6},{3,1},{5,3},{7,5},{1,7},{10,8},{12,10},{14... | collective-permute-start | bytes 1572872 | tf_op jit(solution)/shard_map/ppermute | solution.py:36
  33.6 2.3 %collective-permute-start.6 = (bf16[64,4096]{1,0:T(8,128)(2,1)S(1)}, bf16[64,4096]{1,0:T(8,128)(2,1)S(1)}, u32[]{:S(2)}, u32[]{:S(2)}) collective-permute-start(bf16[64,4096]{1,0:T(8,128)(2,1)S(1)} %maximum_select_fusion.mine), channel_id=1, source_target_pairs={{4,0},{6,2},{0,4},{2,6},{5,1},{7,3},{1,5},{3,7},{12,8},{14,10},{8,... | collective-permute-start | bytes 1572872 | tf_op jit(solution)/shard_map/ppermute | solution.py:36
  35.9 2.6 %collective-permute-start.7 = (bf16[64,4096]{1,0:T(8,128)(2,1)S(1)}, bf16[64,4096]{1,0:T(8,128)(2,1)S(1)}, u32[]{:S(2)}, u32[]{:S(2)}) collective-permute-start(bf16[64,4096]{1,0:T(8,128)(2,1)S(1)} %maximum_select_fusion.mine), channel_id=1, source_target_pairs={{6,0},{0,2},{2,4},{4,6},{7,1},{1,3},{3,5},{5,7},{14,8},{8,10},{10,... | collective-permute-start | bytes 1572872 | tf_op jit(solution)/shard_map/ppermute | solution.py:36
  38.6 1.0 fusion.2.first
  39.5 5.3 %collective-permute-start.2 = (bf16[1,16,4096]{2,1,0:T(8,128)(2,1)S(1)}, bf16[1,16,4096]{2,1,0:T(8,128)(2,1)S(1)}, u32[]{:S(2)}, u32[]{:S(2)}) collective-permute-start(bf16[1,16,4096]{2,1,0:T(8,128)(2,1)S(1)} %fusion.2.first), channel_id=1, source_target_pairs={{0,32},{8,40},{16,48},{24,56},{32,0},{40,8},{48,16},{56,24},{1,33}... | collective-permute-start | bytes 393224 | tf_op jit(solution)/shard_map/ppermute | solution.py:40
  44.9 10.7 %collective-permute-done.5.one = bf16[64,4096]{1,0:T(8,128)(2,1)S(1)} collective-permute-done((bf16[64,4096]{1,0:T(8,128)(2,1)S(1)}, bf16[64,4096]{1,0:T(8,128)(2,1)S(1)}, u32[]{:S(2)}, u32[]{:S(2)}) %collective-permute-start.5) | collective-permute-done | bytes 524320 | tf_op jit(solution)/shard_map/ppermute | solution.py:36
  55.6 6.5 %collective-permute-done.7.three = bf16[64,4096]{1,0:T(8,128)(2,1)S(1)} collective-permute-done((bf16[64,4096]{1,0:T(8,128)(2,1)S(1)}, bf16[64,4096]{1,0:T(8,128)(2,1)S(1)}, u32[]{:S(2)}, u32[]{:S(2)}) %collective-permute-start.7) | collective-permute-done | bytes 524320 | tf_op jit(solution)/shard_map/ppermute | solution.py:36
  62.1 0.9 shard_map.86.rest_1_.refs_13_.refs_5_
  63.0 1.8 %multiply_convert_fusion.rest_0_.refs_12_.refs_4_ = bf16[4096,256]{1,0:T(8,128)(2,1)S(1)} fusion(bf16[4096,128]{1,0:T(8,128)(2,1)} %collective-permute-done.3, bf16[4096,128]{1,0:T(8,128)(2,1)S(1)} %copy-done.9, f32[4096]{0:T(1024)S(1)} %bitcast.33), kind=kLoop, calls=%fused_computation | loop fusion | flops 6291456 | bytes 4210688 | tf_op jit(solution)/shard_map/convert_element_type | solution.py:195
  64.8 1.9 %collective-permute-start.8 = (bf16[2,16,4096]{2,1,0:T(8,128)(2,1)S(1)}, bf16[2,16,4096]{2,1,0:T(8,128)(2,1)S(1)}, u32[]{:S(2)}, u32[]{:S(2)}) collective-permute-start(bf16[2,16,4096]{2,1,0:T(8,128)(2,1)S(1)} %shard_map.87.refs_0_), channel_id=1, source_target_pairs={{2,0},{4,2},{6,4},{0,6},{3,1},{5,3},{7,5},{1,7},{10,8},{12,10},{14... | collective-permute-start | bytes 786440 | tf_op jit(solution)/shard_map/ppermute | solution.py:36
  66.7 2.6 %collective-permute-start.11 = (bf16[2,16,4096]{2,1,0:T(8,128)(2,1)S(1)}, bf16[2,16,4096]{2,1,0:T(8,128)(2,1)S(1)}, u32[]{:S(2)}, u32[]{:S(2)}) collective-permute-start(bf16[2,16,4096]{2,1,0:T(8,128)(2,1)S(1)} %shard_map.87.refs_0_), channel_id=1, source_target_pairs={{0,8},{8,0},{16,24},{24,16},{32,40},{40,32},{48,56},{56,48},{1,9},... | collective-permute-start | bytes 786440 | tf_op jit(solution)/shard_map/ppermute | solution.py:40
  69.4 2.3 %collective-permute-start.9 = (bf16[2,16,4096]{2,1,0:T(8,128)(2,1)S(1)}, bf16[2,16,4096]{2,1,0:T(8,128)(2,1)S(1)}, u32[]{:S(2)}, u32[]{:S(2)}) collective-permute-start(bf16[2,16,4096]{2,1,0:T(8,128)(2,1)S(1)} %shard_map.87.refs_0_), channel_id=1, source_target_pairs={{4,0},{6,2},{0,4},{2,6},{5,1},{7,3},{1,5},{3,7},{12,8},{14,10},{8,... | collective-permute-start | bytes 786440 | tf_op jit(solution)/shard_map/ppermute | solution.py:36
  71.7 3.0 %collective-permute-start.10 = (bf16[2,16,4096]{2,1,0:T(8,128)(2,1)S(1)}, bf16[2,16,4096]{2,1,0:T(8,128)(2,1)S(1)}, u32[]{:S(2)}, u32[]{:S(2)}) collective-permute-start(bf16[2,16,4096]{2,1,0:T(8,128)(2,1)S(1)} %shard_map.87.refs_0_), channel_id=1, source_target_pairs={{6,0},{0,2},{2,4},{4,6},{7,1},{1,3},{3,5},{5,7},{14,8},{8,10},{10,... | collective-permute-start | bytes 786440 | tf_op jit(solution)/shard_map/ppermute | solution.py:36
  74.7 3.5 %collective-permute-start.15 = (bf16[2,16,4096]{2,1,0:T(8,128)(2,1)S(1)}, bf16[2,16,4096]{2,1,0:T(8,128)(2,1)S(1)}, u32[]{:S(2)}, u32[]{:S(2)}) collective-permute-start(bf16[2,16,4096]{2,1,0:T(8,128)(2,1)S(1)} %shard_map.87.refs_0_), channel_id=1, source_target_pairs={{0,24},{8,16},{16,8},{24,0},{32,56},{40,48},{48,40},{56,32},{1,25}... | collective-permute-start | bytes 786440 | tf_op jit(solution)/shard_map/ppermute | solution.py:40
  78.3 2.2 %collective-permute-start.20 = (bf16[2,16,4096]{2,1,0:T(8,128)(2,1)S(1)}, bf16[2,16,4096]{2,1,0:T(8,128)(2,1)S(1)}, u32[]{:S(2)}, u32[]{:S(2)}) collective-permute-start(bf16[2,16,4096]{2,1,0:T(8,128)(2,1)S(1)} %shard_map.87.refs_0_), channel_id=1, source_target_pairs={{0,16},{8,24},{16,0},{24,8},{32,48},{40,56},{48,32},{56,40},{1,17}... | collective-permute-start | bytes 786440 | tf_op jit(solution)/shard_map/ppermute | solution.py:40
  80.5 4.3 %collective-permute-start.12 = (bf16[2,16,4096]{2,1,0:T(8,128)(2,1)S(1)}, bf16[2,16,4096]{2,1,0:T(8,128)(2,1)S(1)}, u32[]{:S(2)}, u32[]{:S(2)}) collective-permute-start(bf16[2,16,4096]{2,1,0:T(8,128)(2,1)S(1)} %collective-permute-done.11.refs_4_), channel_id=1, source_target_pairs={{2,0},{4,2},{6,4},{0,6},{3,1},{5,3},{7,5},{1,7},{10,8},{12,10},{14... | collective-permute-start | bytes 786440 | tf_op jit(solution)/shard_map/ppermute | solution.py:36
  84.8 3.1 %collective-permute-start.13 = (bf16[2,16,4096]{2,1,0:T(8,128)(2,1)S(1)}, bf16[2,16,4096]{2,1,0:T(8,128)(2,1)S(1)}, u32[]{:S(2)}, u32[]{:S(2)}) collective-permute-start(bf16[2,16,4096]{2,1,0:T(8,128)(2,1)S(1)} %collective-permute-done.11.refs_4_), channel_id=1, source_target_pairs={{4,0},{6,2},{0,4},{2,6},{5,1},{7,3},{1,5},{3,7},{12,8},{14,10},{8,... | collective-permute-start | bytes 786440 | tf_op jit(solution)/shard_map/ppermute | solution.py:36
  87.9 2.8 %collective-permute-start.14 = (bf16[2,16,4096]{2,1,0:T(8,128)(2,1)S(1)}, bf16[2,16,4096]{2,1,0:T(8,128)(2,1)S(1)}, u32[]{:S(2)}, u32[]{:S(2)}) collective-permute-start(bf16[2,16,4096]{2,1,0:T(8,128)(2,1)S(1)} %collective-permute-done.11.refs_4_), channel_id=1, source_target_pairs={{6,0},{0,2},{2,4},{4,6},{7,1},{1,3},{3,5},{5,7},{14,8},{8,10},{10,... | collective-permute-start | bytes 786440 | tf_op jit(solution)/shard_map/ppermute | solution.py:36
  90.7 3.7 %collective-permute-start.16 = (bf16[2,16,4096]{2,1,0:T(8,128)(2,1)S(1)}, bf16[2,16,4096]{2,1,0:T(8,128)(2,1)S(1)}, u32[]{:S(2)}, u32[]{:S(2)}) collective-permute-start(bf16[2,16,4096]{2,1,0:T(8,128)(2,1)S(1)} %collective-permute-done.15.refs_8_), channel_id=1, source_target_pairs={{2,0},{4,2},{6,4},{0,6},{3,1},{5,3},{7,5},{1,7},{10,8},{12,10},{14... | collective-permute-start | bytes 786440 | tf_op jit(solution)/shard_map/ppermute | solution.py:36
  94.4 6.3 %collective-permute-done.20.refs_0_ = bf16[2,16,4096]{2,1,0:T(8,128)(2,1)S(1)} collective-permute-done((bf16[2,16,4096]{2,1,0:T(8,128)(2,1)S(1)}, bf16[2,16,4096]{2,1,0:T(8,128)(2,1)S(1)}, u32[]{:S(2)}, u32[]{:S(2)}) %collective-permute-start.20) | collective-permute-done | bytes 262176 | tf_op jit(solution)/shard_map/ppermute | solution.py:40
  100.7 5.5 %collective-permute-start.17 = (bf16[2,16,4096]{2,1,0:T(8,128)(2,1)S(1)}, bf16[2,16,4096]{2,1,0:T(8,128)(2,1)S(1)}, u32[]{:S(2)}, u32[]{:S(2)}) collective-permute-start(bf16[2,16,4096]{2,1,0:T(8,128)(2,1)S(1)} %collective-permute-done.15.refs_8_), channel_id=1, source_target_pairs={{4,0},{6,2},{0,4},{2,6},{5,1},{7,3},{1,5},{3,7},{12,8},{14,10},{8,... | collective-permute-start | bytes 786440 | tf_op jit(solution)/shard_map/ppermute | solution.py:36
  106.2 1.9 %collective-permute-start.18 = (bf16[2,16,4096]{2,1,0:T(8,128)(2,1)S(1)}, bf16[2,16,4096]{2,1,0:T(8,128)(2,1)S(1)}, u32[]{:S(2)}, u32[]{:S(2)}) collective-permute-start(bf16[2,16,4096]{2,1,0:T(8,128)(2,1)S(1)} %collective-permute-done.15.refs_8_), channel_id=1, source_target_pairs={{6,0},{0,2},{2,4},{4,6},{7,1},{1,3},{3,5},{5,7},{14,8},{8,10},{10,... | collective-permute-start | bytes 786440 | tf_op jit(solution)/shard_map/ppermute | solution.py:36
  108.1 4.6 %collective-permute-start.21 = (bf16[2,16,4096]{2,1,0:T(8,128)(2,1)S(1)}, bf16[2,16,4096]{2,1,0:T(8,128)(2,1)S(1)}, u32[]{:S(2)}, u32[]{:S(2)}) collective-permute-start(bf16[2,16,4096]{2,1,0:T(8,128)(2,1)S(1)} %collective-permute-done.20.refs_0_), channel_id=1, source_target_pairs={{2,0},{4,2},{6,4},{0,6},{3,1},{5,3},{7,5},{1,7},{10,8},{12,10},{14... | collective-permute-start | bytes 786440 | tf_op jit(solution)/shard_map/ppermute | solution.py:36
  112.7 1.9 %collective-permute-start.22 = (bf16[2,16,4096]{2,1,0:T(8,128)(2,1)S(1)}, bf16[2,16,4096]{2,1,0:T(8,128)(2,1)S(1)}, u32[]{:S(2)}, u32[]{:S(2)}) collective-permute-start(bf16[2,16,4096]{2,1,0:T(8,128)(2,1)S(1)} %collective-permute-done.20.refs_0_), channel_id=1, source_target_pairs={{4,0},{6,2},{0,4},{2,6},{5,1},{7,3},{1,5},{3,7},{12,8},{14,10},{8,... | collective-permute-start | bytes 786440 | tf_op jit(solution)/shard_map/ppermute | solution.py:36
  114.6 2.5 %collective-permute-start.23 = (bf16[2,16,4096]{2,1,0:T(8,128)(2,1)S(1)}, bf16[2,16,4096]{2,1,0:T(8,128)(2,1)S(1)}, u32[]{:S(2)}, u32[]{:S(2)}) collective-permute-start(bf16[2,16,4096]{2,1,0:T(8,128)(2,1)S(1)} %collective-permute-done.20.refs_0_), channel_id=1, source_target_pairs={{6,0},{0,2},{2,4},{4,6},{7,1},{1,3},{3,5},{5,7},{14,8},{8,10},{10,... | collective-permute-start | bytes 786440 | tf_op jit(solution)/shard_map/ppermute | solution.py:36
  117.8 2.9 %shard_map.88 = (f32[384,384]{1,0:T(8,128)S(1)}, bf16[384,384]{1,0:T(8,128)(2,1)}) custom-call(bf16[2,16,4096]{2,1,0:T(8,128)(2,1)S(1)} %shard_map.87.refs_0_, bf16[2,16,4096]{2,1,0:T(8,128)(2,1)S(1)} %collective-permute-done.8.refs_1_, bf16[2,16,4096]{2,1,0:T(8,128)(2,1)S(1)} %collective-permute-done.9.refs_2_, ...), custom_call_target="tpu_custom_call" | custom-call | flops 1610612736 | bytes 9437184 | tf_op jit(solution)/shard_map/pallas_call | solution.py:222
  120.7 6.9 %collective-permute-start.19 = (bf16[384,384]{1,0:T(8,128)(2,1)}, bf16[384,384]{1,0:T(8,128)(2,1)S(1)}, u32[]{:S(2)}, u32[]{:S(2)}) collective-permute-start(bf16[384,384]{1,0:T(8,128)(2,1)} %get-tuple-element.10), channel_id=1, source_target_pairs={{0,1},{1,0},{2,3},{3,2},{4,5},{5,4},{6,7},{7,6},{8,9},{9,8},{10,11... | collective-permute-start | bytes 884744 | tf_op jit(solution)/shard_map/ppermute | solution.py:44
  127.6 1.9 %collective-permute-done.23.refs_3_ = bf16[2,16,4096]{2,1,0:T(8,128)(2,1)S(1)} collective-permute-done((bf16[2,16,4096]{2,1,0:T(8,128)(2,1)S(1)}, bf16[2,16,4096]{2,1,0:T(8,128)(2,1)S(1)}, u32[]{:S(2)}, u32[]{:S(2)}) %collective-permute-start.23) | collective-permute-done | bytes 262176 | tf_op jit(solution)/shard_map/ppermute | solution.py:36
  129.5 1.8 %shard_map.89 = (f32[128,384]{1,0:T(8,128)S(1)}, bf16[128,384]{1,0:T(8,128)(2,1)}) custom-call(bf16[2,16,4096]{2,1,0:T(8,128)(2,1)S(1)} %collective-permute-done.20.refs_0_, bf16[2,16,4096]{2,1,0:T(8,128)(2,1)S(1)} %collective-permute-done.21.refs_1_, bf16[2,16,4096]{2,1,0:T(8,128)(2,1)S(1)} %collective-permute-done.22.refs_2_, ...), custom_call_target="tpu_custom_call" | custom-call | flops 536870912 | bytes 9437184 | tf_op jit(solution)/shard_map/pallas_call | solution.py:222
  131.3 0.7 copy-done.1
  132.0 3.2 %collective-permute-start.24 = (bf16[128,384]{1,0:T(8,128)(2,1)}, bf16[128,384]{1,0:T(8,128)(2,1)}, u32[]{:S(2)}, u32[]{:S(2)}) collective-permute-start(bf16[128,384]{1,0:T(8,128)(2,1)} %get-tuple-element.12), channel_id=1, source_target_pairs={{0,1},{1,0},{2,3},{3,2},{4,5},{5,4},{6,7},{7,6},{8,9},{9,8},{10,11... | collective-permute-start | bytes 294920 | tf_op jit(solution)/shard_map/ppermute | solution.py:44
  135.3 1.3 collective-permute-done.24.got2
  136.5 0.9 copy-done.2
  137.5 1.7 %shard_map.90 = (bf16[512,128]{1,0:T(8,128)(2,1)S(1)}, bf16[512,128]{1,0:T(8,128)(2,1)S(1)}, bf16[8,8,256]{2,1,0:T(8,128)(2,1)}) custom-call(s32[3]{0:T(128)S(1)} %pad_add_fusion.where, s32[8]{0:T(128)S(1)} %bitcast.34, f32[384,384]{1,0:T(8,128)S(1)} %get-tuple-element.9.own1, bf16[384,384]{1,0:T(8,128)(2,1)S(1)} %collective-permute-done.19.got1, ...), custom_call_target="tpu_custom_call" | custom-call | bytes 2097152 | tf_op jit(solution)/shard_map/pallas_call | solution.py:238
  140.4 8.4 %all-to-all-start = ((bf16[8,8,256]{2,1,0:T(8,128)(2,1)}), bf16[8,8,256]{2,1,0:T(8,128)(2,1)S(1)}, u32[]{:S(2)}, u32[]{:S(2)}) async-start(bf16[8,8,256]{2,1,0:T(8,128)(2,1)} %get-tuple-element.15), calls=%async_computation | async-start | bytes 65536 | tf_op jit(solution)/shard_map/all_to_all | solution.py:245
  148.9 0.9 copy-done.3
  149.8 0.9 copy-done.5
  150.7 0.9 copy-done.7
  151.6 3.2 %shard_map.91 = bf16[512,128]{1,0:T(8,128)(2,1)} custom-call(s32[3]{0:T(128)S(1)} %pad_add_fusion.where, f32[384,384]{1,0:T(8,128)S(1)} %get-tuple-element.9.own1, bf16[384,384]{1,0:T(8,128)(2,1)S(1)} %collective-permute-done.19.got1, f32[128,384]{1,0:T(8,128)S(1)} %copy-done.3, bf16[128,384]{1,0:T(8,128)(2,1)} %collective-permute-done.24.got2, ...), custom_call_target="tpu_custom_call" | custom-call | flops 268435456 | bytes 2097152 | tf_op jit(solution)/shard_map/pallas_call | solution.py:248
  154.8 3.5 %all-to-all-done = bf16[8,8,256]{2,1,0:T(8,128)(2,1)S(1)} async-done(((bf16[8,8,256]{2,1,0:T(8,128)(2,1)}), bf16[8,8,256]{2,1,0:T(8,128)(2,1)S(1)}, u32[]{:S(2)}, u32[]{:S(2)}) %all-to-all-start) | async-done | bytes 32800 | tf_op jit(solution)/shard_map/all_to_all | solution.py:245
  (51 shorter events, 3.8 us)
Async XLA Ops:
  0.6 148.2 %copy-start = (bf16[1,8,512,256]{3,2,1,0:T(8,128)(2,1)S(1)}, bf16[1,8,512,256]{3,2,1,0:T(8,128)(2,1)}, u32[]{:S(2)}) copy-start(bf16[1,8,512,256]{3,2,1,0:T(8,128)(2,1)} %param.11) | copy-start | bytes 6291460
  3.5 32.3 %collective-permute-start.1 = (bf16[8,4096]{1,0:T(8,128)(2,1)}, bf16[8,4096]{1,0:T(8,128)(2,1)}, u32[]{:S(2)}, u32[]{:S(2)}) collective-permute-start(bf16[8,4096]{1,0:T(8,128)(2,1)} %get-tuple-element.23), channel_id=1, source_target_pairs={{0,97},{1,96},{8,105},{9,104},{16,113},{17,112},{24,121},{25,120},... | collective-permute-start | bytes 196616 | tf_op jit(solution)/shard_map/ppermute | solution.py:186
  17.4 7.4 %copy-start.10 = (bf16[1,8192,32]{1,2,0:T(8,128)(2,1)S(1)}, bf16[1,8192,32]{1,2,0:T(8,128)(2,1)}, u32[]{:S(2)}) copy-start(bf16[1,8192,32]{1,2,0:T(8,128)(2,1)} %param.10) | copy-start | bytes 1572868
  17.4 9.5 %copy-start.11 = (f32[1,8192]{1,0:T(1,128)S(1)}, f32[1,8192]{1,0:T(1,128)}, u32[]{:S(2)}) copy-start(f32[1,8192]{1,0:T(1,128)} %param.8) | copy-start | bytes 98308
  17.4 21.2 %collective-permute-start = (bf16[8,4096]{1,0:T(8,128)(2,1)S(1)}, bf16[8,4096]{1,0:T(8,128)(2,1)}, u32[]{:S(2)}, u32[]{:S(2)}) collective-permute-start(bf16[8,4096]{1,0:T(8,128)(2,1)S(1)} %get-tuple-element.22), channel_id=1, source_target_pairs={{0,96},{1,97},{8,104},{9,105},{16,112},{17,113},{24,120},{25,121},... | collective-permute-start | bytes 196616 | tf_op jit(solution)/shard_map/ppermute | solution.py:185
  22.5 40.5 %collective-permute-start.3 = (bf16[4096,128]{1,0:T(8,128)(2,1)}, bf16[4096,128]{1,0:T(8,128)(2,1)}, u32[]{:S(2)}, u32[]{:S(2)}) collective-permute-start(bf16[4096,128]{1,0:T(8,128)(2,1)} %get-tuple-element.19), channel_id=1, source_target_pairs={{0,1},{1,0},{2,3},{3,2},{4,5},{5,4},{6,7},{7,6},{8,9},{9,8},{10,11... | collective-permute-start | bytes 3145736 | tf_op jit(solution)/shard_map/ppermute | solution.py:44
  24.9 4.0 %collective-permute-start.4 = (bf16[32,4096]{1,0:T(8,128)(2,1)S(1)}, bf16[32,4096]{1,0:T(8,128)(2,1)S(1)}, u32[]{:S(2)}, u32[]{:S(2)}) collective-permute-start(bf16[32,4096]{1,0:T(8,128)(2,1)S(1)} %get-tuple-element.21), channel_id=1, source_target_pairs={{0,1},{1,0},{2,3},{3,2},{4,5},{5,4},{6,7},{7,6},{8,9},{9,8},{10,11... | collective-permute-start | bytes 786440 | tf_op jit(solution)/shard_map/ppermute | solution.py:44
  28.9 26.6 %collective-permute-start.5 = (bf16[64,4096]{1,0:T(8,128)(2,1)S(1)}, bf16[64,4096]{1,0:T(8,128)(2,1)S(1)}, u32[]{:S(2)}, u32[]{:S(2)}) collective-permute-start(bf16[64,4096]{1,0:T(8,128)(2,1)S(1)} %maximum_select_fusion.mine), channel_id=1, source_target_pairs={{2,0},{4,2},{6,4},{0,6},{3,1},{5,3},{7,5},{1,7},{10,8},{12,10},{14... | collective-permute-start | bytes 1572872 | tf_op jit(solution)/shard_map/ppermute | solution.py:36
  33.6 22.0 %collective-permute-start.6 = (bf16[64,4096]{1,0:T(8,128)(2,1)S(1)}, bf16[64,4096]{1,0:T(8,128)(2,1)S(1)}, u32[]{:S(2)}, u32[]{:S(2)}) collective-permute-start(bf16[64,4096]{1,0:T(8,128)(2,1)S(1)} %maximum_select_fusion.mine), channel_id=1, source_target_pairs={{4,0},{6,2},{0,4},{2,6},{5,1},{7,3},{1,5},{3,7},{12,8},{14,10},{8,... | collective-permute-start | bytes 1572872 | tf_op jit(solution)/shard_map/ppermute | solution.py:36
  35.9 26.2 %collective-permute-start.7 = (bf16[64,4096]{1,0:T(8,128)(2,1)S(1)}, bf16[64,4096]{1,0:T(8,128)(2,1)S(1)}, u32[]{:S(2)}, u32[]{:S(2)}) collective-permute-start(bf16[64,4096]{1,0:T(8,128)(2,1)S(1)} %maximum_select_fusion.mine), channel_id=1, source_target_pairs={{6,0},{0,2},{2,4},{4,6},{7,1},{1,3},{3,5},{5,7},{14,8},{8,10},{10,... | collective-permute-start | bytes 1572872 | tf_op jit(solution)/shard_map/ppermute | solution.py:36
  39.5 23.4 %copy-start.9 = (bf16[4096,128]{1,0:T(8,128)(2,1)S(1)}, bf16[4096,128]{1,0:T(8,128)(2,1)}, u32[]{:S(2)}) copy-start(bf16[4096,128]{1,0:T(8,128)(2,1)} %get-tuple-element.18) | copy-start | bytes 3145732
  39.5 25.2 %collective-permute-start.2 = (bf16[1,16,4096]{2,1,0:T(8,128)(2,1)S(1)}, bf16[1,16,4096]{2,1,0:T(8,128)(2,1)S(1)}, u32[]{:S(2)}, u32[]{:S(2)}) collective-permute-start(bf16[1,16,4096]{2,1,0:T(8,128)(2,1)S(1)} %fusion.2.first), channel_id=1, source_target_pairs={{0,32},{8,40},{16,48},{24,56},{32,0},{40,8},{48,16},{56,24},{1,33}... | collective-permute-start | bytes 393224 | tf_op jit(solution)/shard_map/ppermute | solution.py:40
  64.8 13.4 %collective-permute-start.8 = (bf16[2,16,4096]{2,1,0:T(8,128)(2,1)S(1)}, bf16[2,16,4096]{2,1,0:T(8,128)(2,1)S(1)}, u32[]{:S(2)}, u32[]{:S(2)}) collective-permute-start(bf16[2,16,4096]{2,1,0:T(8,128)(2,1)S(1)} %shard_map.87.refs_0_), channel_id=1, source_target_pairs={{2,0},{4,2},{6,4},{0,6},{3,1},{5,3},{7,5},{1,7},{10,8},{12,10},{14... | collective-permute-start | bytes 786440 | tf_op jit(solution)/shard_map/ppermute | solution.py:36
  66.7 13.7 %collective-permute-start.11 = (bf16[2,16,4096]{2,1,0:T(8,128)(2,1)S(1)}, bf16[2,16,4096]{2,1,0:T(8,128)(2,1)S(1)}, u32[]{:S(2)}, u32[]{:S(2)}) collective-permute-start(bf16[2,16,4096]{2,1,0:T(8,128)(2,1)S(1)} %shard_map.87.refs_0_), channel_id=1, source_target_pairs={{0,8},{8,0},{16,24},{24,16},{32,40},{40,32},{48,56},{56,48},{1,9},... | collective-permute-start | bytes 786440 | tf_op jit(solution)/shard_map/ppermute | solution.py:40
  69.4 15.4 %collective-permute-start.9 = (bf16[2,16,4096]{2,1,0:T(8,128)(2,1)S(1)}, bf16[2,16,4096]{2,1,0:T(8,128)(2,1)S(1)}, u32[]{:S(2)}, u32[]{:S(2)}) collective-permute-start(bf16[2,16,4096]{2,1,0:T(8,128)(2,1)S(1)} %shard_map.87.refs_0_), channel_id=1, source_target_pairs={{4,0},{6,2},{0,4},{2,6},{5,1},{7,3},{1,5},{3,7},{12,8},{14,10},{8,... | collective-permute-start | bytes 786440 | tf_op jit(solution)/shard_map/ppermute | solution.py:36
  71.7 16.2 %collective-permute-start.10 = (bf16[2,16,4096]{2,1,0:T(8,128)(2,1)S(1)}, bf16[2,16,4096]{2,1,0:T(8,128)(2,1)S(1)}, u32[]{:S(2)}, u32[]{:S(2)}) collective-permute-start(bf16[2,16,4096]{2,1,0:T(8,128)(2,1)S(1)} %shard_map.87.refs_0_), channel_id=1, source_target_pairs={{6,0},{0,2},{2,4},{4,6},{7,1},{1,3},{3,5},{5,7},{14,8},{8,10},{10,... | collective-permute-start | bytes 786440 | tf_op jit(solution)/shard_map/ppermute | solution.py:36
  74.7 16.0 %collective-permute-start.15 = (bf16[2,16,4096]{2,1,0:T(8,128)(2,1)S(1)}, bf16[2,16,4096]{2,1,0:T(8,128)(2,1)S(1)}, u32[]{:S(2)}, u32[]{:S(2)}) collective-permute-start(bf16[2,16,4096]{2,1,0:T(8,128)(2,1)S(1)} %shard_map.87.refs_0_), channel_id=1, source_target_pairs={{0,24},{8,16},{16,8},{24,0},{32,56},{40,48},{48,40},{56,32},{1,25}... | collective-permute-start | bytes 786440 | tf_op jit(solution)/shard_map/ppermute | solution.py:40
  78.3 22.4 %collective-permute-start.20 = (bf16[2,16,4096]{2,1,0:T(8,128)(2,1)S(1)}, bf16[2,16,4096]{2,1,0:T(8,128)(2,1)S(1)}, u32[]{:S(2)}, u32[]{:S(2)}) collective-permute-start(bf16[2,16,4096]{2,1,0:T(8,128)(2,1)S(1)} %shard_map.87.refs_0_), channel_id=1, source_target_pairs={{0,16},{8,24},{16,0},{24,8},{32,48},{40,56},{48,32},{56,40},{1,17}... | collective-permute-start | bytes 786440 | tf_op jit(solution)/shard_map/ppermute | solution.py:40
  80.5 25.7 %collective-permute-start.12 = (bf16[2,16,4096]{2,1,0:T(8,128)(2,1)S(1)}, bf16[2,16,4096]{2,1,0:T(8,128)(2,1)S(1)}, u32[]{:S(2)}, u32[]{:S(2)}) collective-permute-start(bf16[2,16,4096]{2,1,0:T(8,128)(2,1)S(1)} %collective-permute-done.11.refs_4_), channel_id=1, source_target_pairs={{2,0},{4,2},{6,4},{0,6},{3,1},{5,3},{7,5},{1,7},{10,8},{12,10},{14... | collective-permute-start | bytes 786440 | tf_op jit(solution)/shard_map/ppermute | solution.py:36
  84.8 23.3 %collective-permute-start.13 = (bf16[2,16,4096]{2,1,0:T(8,128)(2,1)S(1)}, bf16[2,16,4096]{2,1,0:T(8,128)(2,1)S(1)}, u32[]{:S(2)}, u32[]{:S(2)}) collective-permute-start(bf16[2,16,4096]{2,1,0:T(8,128)(2,1)S(1)} %collective-permute-done.11.refs_4_), channel_id=1, source_target_pairs={{4,0},{6,2},{0,4},{2,6},{5,1},{7,3},{1,5},{3,7},{12,8},{14,10},{8,... | collective-permute-start | bytes 786440 | tf_op jit(solution)/shard_map/ppermute | solution.py:36
  87.9 24.8 %collective-permute-start.14 = (bf16[2,16,4096]{2,1,0:T(8,128)(2,1)S(1)}, bf16[2,16,4096]{2,1,0:T(8,128)(2,1)S(1)}, u32[]{:S(2)}, u32[]{:S(2)}) collective-permute-start(bf16[2,16,4096]{2,1,0:T(8,128)(2,1)S(1)} %collective-permute-done.11.refs_4_), channel_id=1, source_target_pairs={{6,0},{0,2},{2,4},{4,6},{7,1},{1,3},{3,5},{5,7},{14,8},{8,10},{10,... | collective-permute-start | bytes 786440 | tf_op jit(solution)/shard_map/ppermute | solution.py:36
  90.7 24.0 %collective-permute-start.16 = (bf16[2,16,4096]{2,1,0:T(8,128)(2,1)S(1)}, bf16[2,16,4096]{2,1,0:T(8,128)(2,1)S(1)}, u32[]{:S(2)}, u32[]{:S(2)}) collective-permute-start(bf16[2,16,4096]{2,1,0:T(8,128)(2,1)S(1)} %collective-permute-done.15.refs_8_), channel_id=1, source_target_pairs={{2,0},{4,2},{6,4},{0,6},{3,1},{5,3},{7,5},{1,7},{10,8},{12,10},{14... | collective-permute-start | bytes 786440 | tf_op jit(solution)/shard_map/ppermute | solution.py:36
  100.7 16.4 %collective-permute-start.17 = (bf16[2,16,4096]{2,1,0:T(8,128)(2,1)S(1)}, bf16[2,16,4096]{2,1,0:T(8,128)(2,1)S(1)}, u32[]{:S(2)}, u32[]{:S(2)}) collective-permute-start(bf16[2,16,4096]{2,1,0:T(8,128)(2,1)S(1)} %collective-permute-done.15.refs_8_), channel_id=1, source_target_pairs={{4,0},{6,2},{0,4},{2,6},{5,1},{7,3},{1,5},{3,7},{12,8},{14,10},{8,... | collective-permute-start | bytes 786440 | tf_op jit(solution)/shard_map/ppermute | solution.py:36
  106.2 11.6 %collective-permute-start.18 = (bf16[2,16,4096]{2,1,0:T(8,128)(2,1)S(1)}, bf16[2,16,4096]{2,1,0:T(8,128)(2,1)S(1)}, u32[]{:S(2)}, u32[]{:S(2)}) collective-permute-start(bf16[2,16,4096]{2,1,0:T(8,128)(2,1)S(1)} %collective-permute-done.15.refs_8_), channel_id=1, source_target_pairs={{6,0},{0,2},{2,4},{4,6},{7,1},{1,3},{3,5},{5,7},{14,8},{8,10},{10,... | collective-permute-start | bytes 786440 | tf_op jit(solution)/shard_map/ppermute | solution.py:36
  108.1 19.5 %collective-permute-start.21 = (bf16[2,16,4096]{2,1,0:T(8,128)(2,1)S(1)}, bf16[2,16,4096]{2,1,0:T(8,128)(2,1)S(1)}, u32[]{:S(2)}, u32[]{:S(2)}) collective-permute-start(bf16[2,16,4096]{2,1,0:T(8,128)(2,1)S(1)} %collective-permute-done.20.refs_0_), channel_id=1, source_target_pairs={{2,0},{4,2},{6,4},{0,6},{3,1},{5,3},{7,5},{1,7},{10,8},{12,10},{14... | collective-permute-start | bytes 786440 | tf_op jit(solution)/shard_map/ppermute | solution.py:36
  112.7 14.9 %collective-permute-start.22 = (bf16[2,16,4096]{2,1,0:T(8,128)(2,1)S(1)}, bf16[2,16,4096]{2,1,0:T(8,128)(2,1)S(1)}, u32[]{:S(2)}, u32[]{:S(2)}) collective-permute-start(bf16[2,16,4096]{2,1,0:T(8,128)(2,1)S(1)} %collective-permute-done.20.refs_0_), channel_id=1, source_target_pairs={{4,0},{6,2},{0,4},{2,6},{5,1},{7,3},{1,5},{3,7},{12,8},{14,10},{8,... | collective-permute-start | bytes 786440 | tf_op jit(solution)/shard_map/ppermute | solution.py:36
  114.6 14.8 %collective-permute-start.23 = (bf16[2,16,4096]{2,1,0:T(8,128)(2,1)S(1)}, bf16[2,16,4096]{2,1,0:T(8,128)(2,1)S(1)}, u32[]{:S(2)}, u32[]{:S(2)}) collective-permute-start(bf16[2,16,4096]{2,1,0:T(8,128)(2,1)S(1)} %collective-permute-done.20.refs_0_), channel_id=1, source_target_pairs={{6,0},{0,2},{2,4},{4,6},{7,1},{1,3},{3,5},{5,7},{14,8},{8,10},{10,... | collective-permute-start | bytes 786440 | tf_op jit(solution)/shard_map/ppermute | solution.py:36
  120.7 15.8 %copy-start.8 = (s32[1,8]{1,0:T(1,128)S(1)}, s32[1,8]{1,0:T(1,128)}, u32[]{:S(2)}) copy-start(s32[1,8]{1,0:T(1,128)} %param.13) | copy-start | bytes 100
  120.7 15.8 %collective-permute-start.19 = (bf16[384,384]{1,0:T(8,128)(2,1)}, bf16[384,384]{1,0:T(8,128)(2,1)S(1)}, u32[]{:S(2)}, u32[]{:S(2)}) collective-permute-start(bf16[384,384]{1,0:T(8,128)(2,1)} %get-tuple-element.10), channel_id=1, source_target_pairs={{0,1},{1,0},{2,3},{3,2},{4,5},{5,4},{6,7},{7,6},{8,9},{9,8},{10,11... | collective-permute-start | bytes 884744 | tf_op jit(solution)/shard_map/ppermute | solution.py:44
  131.3 0.7 copy-start.1
  132.0 4.5 %collective-permute-start.24 = (bf16[128,384]{1,0:T(8,128)(2,1)}, bf16[128,384]{1,0:T(8,128)(2,1)}, u32[]{:S(2)}, u32[]{:S(2)}) collective-permute-start(bf16[128,384]{1,0:T(8,128)(2,1)} %get-tuple-element.12), channel_id=1, source_target_pairs={{0,1},{1,0},{2,3},{3,2},{4,5},{5,4},{6,7},{7,6},{8,9},{9,8},{10,11... | collective-permute-start | bytes 294920 | tf_op jit(solution)/shard_map/ppermute | solution.py:44
  136.5 0.9 copy-start.2
  139.1 0.7 copy-start.4
  139.8 0.7 copy-start.6
  140.4 17.9 %all-to-all-start = ((bf16[8,8,256]{2,1,0:T(8,128)(2,1)}), bf16[8,8,256]{2,1,0:T(8,128)(2,1)S(1)}, u32[]{:S(2)}, u32[]{:S(2)}) async-start(bf16[8,8,256]{2,1,0:T(8,128)(2,1)} %get-tuple-element.15), calls=%async_computation | async-start | bytes 65536 | tf_op jit(solution)/shard_map/all_to_all | solution.py:245
  148.8 0.9 copy-start.3
  149.8 0.9 copy-start.5
  150.7 0.9 copy-start.7

commit v3 on v2

v3 whole, which is shorter than its diff:
```python
import math

import jax
import jax.numpy as jnp
from jax import lax
from jax.experimental import pallas as pl
from jax.experimental.pallas import tpu as pltpu
from jax.sharding import Mesh, PartitionSpec as P

BF = jnp.bfloat16
F32 = jnp.float32
rope_base = 500000.0
norm_eps = 1e-05
masked_score = -1e30

NZ, NY = 8, 4
ROWS = 16
TOKENS = 512
HD = 128


def frequencies(head_dim):
    half_dim = head_dim // 2
    base_freqs = jnp.exp(
        jnp.arange(half_dim, dtype=F32) * (-2.0 * math.log(rope_base) / head_dim)
    )
    wavelength = 2.0 * math.pi / base_freqs
    smooth = (8192.0 / wavelength - 1.0) / 3.0
    blended = (1.0 - smooth) * base_freqs / 8.0 + smooth * base_freqs
    return jnp.where(
        wavelength < 2048.0, base_freqs, jnp.where(wavelength > 8192.0, base_freqs / 8.0, blended)
    )


def along_y(value, k):
    return lax.ppermute(value, "y", [((i + k) % NY, i) for i in range(NY)])


def across_z(value, k):
    return lax.ppermute(value, "z", [(i, i ^ k) for i in range(NZ)])


def swap_core(value):
    return lax.ppermute(value, "c", [(0, 1), (1, 0)])


def place(slot, z0, y0):
    batch, k, i = slot >> 4, (slot >> 2) & 3, slot & 3
    z = z0 ^ i ^ (4 * (1 - batch))
    return (z << 2) | ((k + y0) & 3)


def slot_of(chip, z0, y0):
    far = (chip >> 2) ^ z0
    return ((1 - (far >> 2)) << 4) | (((chip - y0) & 3) << 2) | (far & 3)


def tokens_of(row, z0, y0):
    return place(row >> 4, z0, y0) * ROWS + (row & 15)


def project_kernel(*refs):
    *pieces, wq_far, wkv_far, _, own, send, x, wq, wkv, sems = refs
    count = len(pieces)
    copies = [
        pltpu.make_async_copy(wq_far, wq, sems.at[count]),
        pltpu.make_async_copy(wkv_far, wkv, sems.at[count + 1]),
    ]
    at = 0
    for i, piece in enumerate(pieces):
        slots = piece.shape[0]
        copies.append(pltpu.make_async_copy(piece, x.at[at : at + slots], sems.at[i]))
        at += slots
    for copy in copies:
        copy.start()
    for copy in copies:
        copy.wait()
    rows = x[...].reshape(-1, x.shape[-1])
    kv = lax.dot_general(rows, wkv[...], (((1,), (1,)), ((), ())), preferred_element_type=F32)
    own[:, HD:] = kv
    send[:, HD:] = kv.astype(BF)
    q = jnp.dot(rows, wq[...], preferred_element_type=F32)
    own[:, :HD] = q[:, :HD]
    send[:, :HD] = q[:, HD:].astype(BF)


def join_kernel(one, two, three, four, passed, *rest):
    batch, kept = rest[-2:]
    for i, piece in enumerate((one, two, three, four)):
        batch[i] = piece[...]
    kept[...] = passed[...]


def turn(v, cosine, sine):
    return v * cosine + pltpu.roll(v, HD // 2, 1) * sine


def pick_kernel(where, owner, own1, own2, blocks, held):
    z0, y0 = where[0], where[1]
    rows = own1.shape[0]
    held[:rows] = own1[:, HD:]
    held[rows:] = own2[:, HD:]
    for z in range(NZ):
        for c in (0, 1):
            block = (z * 8 + y0 * 2 + c - owner[z0]) & 63
            row = slot_of(block >> 1, z0, y0) * ROWS + (block & 1) * 8
            blocks[2 * z + c] = held[pl.ds(pl.multiple_of(row, 8), 8), :]


def decode_kernel(got, cosine, sine, out):
    for g in range(NZ):
        raw = (got[2 * g] + got[2 * g + 1]).astype(BF)
        out[g, :, :HD] = turn(raw[:, :HD].astype(F32), cosine[g], sine[g]).astype(BF)
        out[g, :, HD:] = raw[:, HD:]


def attend_kernel(where, own1, got1, own2, got2, cosine, sine, resident, out):
    z0, y0 = where[0], where[1]
    halves = ((own1, got1), (own2, got2))
    raw = jnp.concatenate([o[:, HD:] + g[:, HD:].astype(F32) for o, g in halves]).astype(BF)
    keys = turn(raw[:, :HD].astype(F32), cosine[...], sine[...]).astype(BF)
    q = jnp.concatenate([o[:, :HD] + g[:, :HD].astype(F32) for o, g in halves])
    q = (turn(q, cosine[...], sine[...]) * HD ** (-0.5)).astype(BF)
    nt = (((1,), (1,)), ((), ()))
    old = lax.dot_general(q, resident[:, :HD], nt, preferred_element_type=F32)
    new = lax.dot_general(q, keys, nt, preferred_element_type=F32)
    token_q = tokens_of(lax.broadcasted_iota(jnp.int32, (TOKENS, 1), 0), z0, y0)
    token_k = tokens_of(lax.broadcasted_iota(jnp.int32, (1, TOKENS), 1), z0, y0)
    new = jnp.where(token_k <= token_q, new, masked_score)
    top = jnp.maximum(
        jnp.max(old, axis=1, keepdims=True), jnp.max(new, axis=1, keepdims=True)
    )
    old = jnp.exp(old - top)
    new = jnp.exp(new - top)
    total = jnp.sum(old, axis=1, keepdims=True) + jnp.sum(new, axis=1, keepdims=True)
    scale = 1.0 / total
    att = jnp.dot((old * scale).astype(BF), resident[:, HD:], preferred_element_type=F32)
    att = att + jnp.dot((new * scale).astype(BF), raw[:, HD:], preferred_element_type=F32)
    att = att.astype(BF)
    for slot in range(32):
        to = pl.multiple_of(place(slot, z0, y0) * ROWS, ROWS)
        out[pl.ds(to, ROWS), :] = att[slot * ROWS : (slot + 1) * ROWS]


def kv_weight_kernel(gain, given, out):
    out[...] = (given[...].astype(F32) * gain[...]).astype(BF)


VMEM = pl.BlockSpec(memory_space=pltpu.VMEM)
SMEM = pl.BlockSpec(memory_space=pltpu.SMEM)
HBM = pl.BlockSpec(memory_space=pltpu.HBM)


def call(kernel, shapes, specs, scratch=(), flops=0, moved=0, exps=0, limit=24):
    return pl.pallas_call(
        kernel,
        out_shape=shapes,
        in_specs=specs,
        out_specs=jax.tree.map(lambda _: VMEM, shapes),
        scratch_shapes=scratch,
        compiler_params=pltpu.CompilerParams(vmem_limit_bytes=limit * 2**20),
        cost_estimate=pl.CostEstimate(flops=flops, bytes_accessed=moved, transcendentals=exps),
    )


def shaped(*shape, dtype=BF):
    return jax.ShapeDtypeStruct(shape, dtype)


def body(residual, norm_gain, query_weight, kv_weight, resident_cache, block_start, decode_owner):
    z0, y0, c0 = (lax.axis_index(a).astype(jnp.int32) for a in ("z", "y", "c"))
    width = residual.shape[2]
    half = width // 2
    where = jnp.stack([z0, y0, c0])

    widened = residual[0].astype(F32)
    scale_row = lax.rsqrt(jnp.mean(widened * widened, axis=-1, keepdims=True) + norm_eps)
    rows = (widened * scale_row).astype(BF)
    kept = lax.dynamic_slice_in_dim(rows, c0 * half, half, 1)
    crossed = lax.dynamic_slice_in_dim(rows, (1 - c0) * half, half, 1)
    sections = lax.axis_size("s")
    steps = [
        [
            ((s * NZ + z) * 2 + c, ((s + 1) % sections * NZ + (z ^ 4)) * 2 + (c ^ flip))
            for s in range(sections)
            for z in range(NZ)
            for c in (0, 1)
        ]
        for flip in (0, 1)
    ]
    same = lax.ppermute(kept, ("s", "z", "c"), steps[0])
    other = lax.ppermute(crossed, ("s", "z", "c"), steps[1])
    piece = jnp.where(c0 == 0, jnp.stack([same, other]), jnp.stack([other, same]))
    piece = piece.reshape(ROWS, half)

    gain = lax.dynamic_slice_in_dim(norm_gain[0], c0 * half, half, 0)
    wq = jnp.concatenate(
        [
            lax.dynamic_slice_in_dim(w, c0 * half, half, 0)
            for w in (query_weight[0], swap_core(query_weight[0]))
        ],
        axis=1,
    )
    wq = (wq.astype(F32) * gain[:, None]).astype(BF)
    kv_halves = jnp.transpose(kv_weight[0].T.reshape(32, 2, half), (1, 0, 2))
    kv_halves = jnp.broadcast_to(kv_halves, (NY, 2, 32, half)).reshape(NY * 2, 32, half)
    wkv = lax.all_to_all(kv_halves, ("y", "c"), 0, 0).reshape(256, half)
    wkv = call(kv_weight_kernel, shaped(256, half), [VMEM] * 2, moved=2**22)(gain[None], wkv)

    def join(one, passed, *after):
        pieces = [one] + [across_z(one, k) for k in (1, 2, 3)]
        return call(
            join_kernel,
            (shaped(4, ROWS, half), shaped(*passed.shape)),
            [VMEM] * 5 + [HBM] * len(after),
            moved=2**20,
            limit=4,
        )(*pieces, passed, *after)

    def everywhere(batch):
        return [batch] + [along_y(batch, k) for k in (1, 2, 3)]

    batch1, second = join(piece, across_z(piece, 4))
    late = (second[0, 0] > 3e38).astype(jnp.int32)

    def tables(tokens):
        angles = (block_start[0] + late + tokens).astype(F32)[..., None] * frequencies(HD)
        cosine, sine = jnp.cos(angles), jnp.sin(angles)
        return jnp.concatenate([cosine, cosine], -1), jnp.concatenate([-sine, sine], -1)

    blocks = (z0 * 8 + y0 * 2 + c0 - decode_owner[0]) & 63
    decode_tokens = (blocks * 8)[:, None] + jnp.arange(8, dtype=jnp.int32)
    row_tokens = tokens_of(jnp.arange(TOKENS, dtype=jnp.int32), z0, y0)
    cosine, sine = tables(row_tokens)
    decode_cosine, decode_sine = tables(decode_tokens)

    batch2, _ = join(second, jnp.zeros((16, HD), BF), wkv, wq, cosine, sine, decode_cosine, decode_sine)
    batch1, batch2 = everywhere(batch1), everywhere(batch2)

    def project(pieces, earlier, weight):
        slots = sum(p.shape[0] for p in pieces)
        tokens = slots * ROWS
        return call(
            project_kernel,
            (shaped(tokens, 3 * HD, dtype=F32), shaped(tokens, 3 * HD)),
            [HBM] * (len(pieces) + 3),
            scratch=[
                pltpu.VMEM((slots, ROWS, half), BF),
                pltpu.VMEM((half, 2 * HD), BF),
                pltpu.VMEM((2 * HD, half), BF),
                pltpu.SemaphoreType.DMA((len(pieces) + 2,)),
            ],
            flops=2 * tokens * half * 512 * weight,
            moved=9 * 2**20,
        )(*pieces, wq, wkv, earlier)

    own1, send1 = project(batch1, wkv, 100)
    got1 = swap_core(send1)
    own2, send2 = project(batch2, got1, 1)
    got2 = swap_core(send2)
    blocks = call(
        pick_kernel,
        shaped(NZ * 2, 8, 2 * HD, dtype=F32),
        [SMEM, SMEM] + [VMEM] * 2,
        scratch=[pltpu.VMEM((TOKENS, 2 * HD), F32)],
        moved=2**20,
        limit=4,
    )(where, decode_owner[0], own1, own2)
    blocks = lax.all_to_all(blocks, ("z", "c"), 0, 0)
    decode_kv = call(decode_kernel, shaped(NZ, 8, 2 * HD), [VMEM] * 3, moved=2**18, limit=4)(
        blocks, decode_cosine, decode_sine
    )
    decode_kv = jnp.transpose(decode_kv, (1, 0, 2))[None]
    resident = lax.dynamic_index_in_dim(resident_cache[0], z0, 0, keepdims=False)
    attn = call(
        attend_kernel,
        shaped(TOKENS, HD),
        [SMEM] + [VMEM] * 7,
        flops=4 * TOKENS * 1024 * HD,
        moved=2**21,
        exps=TOKENS * 1024,
    )(where, own1, got1, own2, got2, cosine, sine, resident)
    return attn[None], decode_kv


def solution(mesh):
    sections = mesh.shape["section"]
    fine = Mesh(mesh.devices.reshape(sections, NZ, NY, 2), ("s", "z", "y", "c"))
    tp = ("z", "y", "c")
    return jax.shard_map(
        body,
        mesh=fine,
        in_specs=(
            P("s", tp, None),
            P("s", None),
            P("s", None, tp),
            P("s", None, tp),
            P("s", None, None, None),
            P("s"),
            P("s", None),
        ),
        out_specs=(P("s", None, tp), P("s", tp, None, None)),
        check_vma=False,
    )
```

time: 160 us -> 153 us (0.956)
  waiting for transfers between devices: 30.9 us -> 25.5 us
  starting transfers between devices: 99.3 us -> 95 us
  Pallas kernels: 10.5 us -> 12.3 us
  local copies, waits for them, and re-layouts: 10.1 us -> 11.9 us
  other arithmetic: 6.38 us -> 4.64 us
    ppermute x15 -> x6, starting transfers between devices: 46.9 us -> 19.1 us  [along_y(): return lax.ppermute(value, 'y', [((i + k) % NY, i) for i in range(NY)])]
    ppermute x4 -> x7, starting transfers between devices: 13.7 us -> 34.1 us  [across_z(): return lax.ppermute(value, 'z', [(i, i ^ k) for i in range(NZ)])]
    all_to_all x1 -> x2, starting transfers between devices: 8.38 us -> 16.6 us  [the longest x1 12 us: body(): blocks = lax.all_to_all(blocks, ('z', 'c'), 0, 0)]
    ppermute x15 -> x6, waiting for transfers between devices: 19.8 us -> 13 us  [along_y(): return lax.ppermute(value, 'y', [((i + k) % NY, i) for i in range(NY)])]
    ppermute x4 -> x3, starting transfers between devices: 14.4 us -> 9.49 us  [swap_core(): return lax.ppermute(value, 'c', [(0, 1), (1, 0)])]
    unnamed x25, local copies, waits for them, and re-layouts: 6.29 us -> 4.41 us
    pallas_call x4 -> x6, Pallas kernels: 5.76 us -> 7.42 us  [the longest x1 3.22 us: body(): call(attend_kernel, shaped(TOKENS, HD), [SMEM] + [VMEM] * 7, flops=4 * TO...]
    broadcast_in_dim x0 -> x2, local copies, waits for them, and re-layouts: none -> 1.63 us  [the longest x1 1.62 us: body(): jnp.broadcast_to(kv_halves, (NY, 2, 32, half)).reshape(NY * 2, 32, half)]
  transfers between devices with their start and end apart: 26 -> 20, of which waited for: 7 -> 6; matrix products, arithmetic and copies ran while one was open for 5% -> 7% of each run, Pallas kernels for 6% -> 6%
where the time goes in v3:
time: 153 us; the launch traced here: 152 us
  starting transfers between devices  95 us (62%)
  waiting for transfers between devices  25.5 us (17%)
  Pallas kernels  12.3 us (8%)
  local copies, waits for them, and re-layouts  11.9 us (8%)
  other arithmetic  4.64 us (3%)
  between operations  2.39 us (2%)
    ppermute x7, starting transfers between devices, across_z(): return lax.ppermute(value, 'z', [(i, i ^ k) for i in range(NZ)])  34.1 us
    ppermute x6, starting transfers between devices, along_y(): return lax.ppermute(value, 'y', [((i + k) % NY, i) for i in range(NY)])  19.1 us
    ppermute x1, starting transfers between devices, body(): other = lax.ppermute(crossed, ('s', 'z', 'c'), steps[1])  13.8 us
    ppermute x6, waiting for transfers between devices, along_y(): return lax.ppermute(value, 'y', [((i + k) % NY, i) for i in range(NY)])  13 us
    all_to_all x1, starting transfers between devices, body(): blocks = lax.all_to_all(blocks, ('z', 'c'), 0, 0)  12 us
    ppermute x3, starting transfers between devices, swap_core(): return lax.ppermute(value, 'c', [(0, 1), (1, 0)])  9.49 us
    ppermute x7, waiting for transfers between devices, across_z(): return lax.ppermute(value, 'z', [(i, i ^ k) for i in range(NZ)])  5.75 us
    pallas_call x2, Pallas kernels, project(): call(project_kernel, (shaped(tokens, 3 * HD, dtype=F32), shaped(tokens, 3...  4.87 us
  transfers between devices with their start and end apart: 20, of which 6 were waited for; matrix products, arithmetic and copies ran while one was open for 7% of the time, Pallas kernels for 6%

profile of v3, /device:TPU:1, one launch (start us, length us, event | category | flops | bytes accessed | tf_op | source)
XLA Modules:
  0.0 151.8 jit_solution(1366875246857009249)
XLA Ops:
  0.7 1.2 fusion
  1.9 1.0 fusion.1
  2.9 13.8 %collective-permute-start.1 = (bf16[8,4096]{1,0:T(8,128)(2,1)S(1)}, bf16[8,4096]{1,0:T(8,128)(2,1)S(1)}, u32[]{:S(2)}, u32[]{:S(2)}) collective-permute-start(bf16[8,4096]{1,0:T(8,128)(2,1)S(1)} %get-tuple-element.19), channel_id=1, source_target_pairs={{0,97},{1,96},{8,105},{9,104},{16,113},{17,112},{24,121},{25,120},... | collective-permute-start | bytes 196616 | tf_op jit(solution)/shard_map/ppermute | solution.py:192
  16.8 1.9 %collective-permute-start = (bf16[8,4096]{1,0:T(8,128)(2,1)S(1)}, bf16[8,4096]{1,0:T(8,128)(2,1)S(1)}, u32[]{:S(2)}, u32[]{:S(2)}) collective-permute-start(bf16[8,4096]{1,0:T(8,128)(2,1)S(1)} %get-tuple-element.18), channel_id=1, source_target_pairs={{0,96},{1,97},{8,104},{9,105},{16,112},{17,113},{24,120},{25,121},... | collective-permute-start | bytes 196616 | tf_op jit(solution)/shard_map/ppermute | solution.py:191
  18.7 2.3 %collective-permute-start.9 = (bf16[8192,128]{1,0:T(8,128)(2,1)}, bf16[8192,128]{1,0:T(8,128)(2,1)}, u32[]{:S(2)}, u32[]{:S(2)}) collective-permute-start(bf16[8192,128]{1,0:T(8,128)(2,1)} %bitcast.37), channel_id=1, source_target_pairs={{0,1},{1,0},{2,3},{3,2},{4,5},{5,4},{6,7},{7,6},{8,9},{9,8},{10,11... | collective-permute-start | bytes 6291464 | tf_op jit(solution)/shard_map/ppermute | solution.py:44
  21.0 1.4 reshape.130
  22.7 1.6 %broadcast_in_dim.8 = bf16[4,2,32,4096]{3,2,1,0:T(8,128)(2,1)} broadcast(bf16[2,32,4096]{2,1,0:T(8,128)(2,1)S(1)} %copy.9), dimensions={1,2,3} | broadcast | bytes 2621440 | tf_op jit(solution)/shard_map/broadcast_in_dim | solution.py:206
  24.4 4.6 %all-to-all-start = ((bf16[8,32,4096]{2,1,0:T(8,128)(2,1)}), bf16[8,32,4096]{2,1,0:T(8,128)(2,1)}, u32[]{:S(2)}, u32[]{:S(2)}) async-start(bf16[8,32,4096]{2,1,0:T(8,128)(2,1)} %bitcast.35), calls=%async_computation | async-start | bytes 4194304 | tf_op jit(solution)/shard_map/all_to_all | solution.py:207
  29.0 2.3 %dynamic-slice_bitcast_fusion = bf16[4096,128]{1,0:T(8,128)(2,1)} fusion(bf16[1,8192,128]{2,1,0:T(8,128)(2,1)} %param.9, s32[]{:T(128)S(6)} %select_n.55), kind=kLoop, calls=%fused_computation.1 | loop fusion | bytes 2097156 | tf_op jit(solution)/shard_map/dynamic_slice | solution.py:199
  31.3 2.6 %collective-permute-start.2 = (bf16[16,4096]{1,0:T(8,128)(2,1)S(1)}, bf16[16,4096]{1,0:T(8,128)(2,1)S(1)}, u32[]{:S(2)}, u32[]{:S(2)}) collective-permute-start(bf16[16,4096]{1,0:T(8,128)(2,1)S(1)} %fusion.2.one), channel_id=1, source_target_pairs={{0,8},{8,0},{16,24},{24,16},{32,40},{40,32},{48,56},{56,48},{1,9},... | collective-permute-start | bytes 393224 | tf_op jit(solution)/shard_map/ppermute | solution.py:40
  34.0 4.5 %collective-permute-start.3 = (bf16[16,4096]{1,0:T(8,128)(2,1)S(1)}, bf16[16,4096]{1,0:T(8,128)(2,1)S(1)}, u32[]{:S(2)}, u32[]{:S(2)}) collective-permute-start(bf16[16,4096]{1,0:T(8,128)(2,1)S(1)} %fusion.2.one), channel_id=1, source_target_pairs={{0,16},{8,24},{16,0},{24,8},{32,48},{40,56},{48,32},{56,40},{1,17}... | collective-permute-start | bytes 393224 | tf_op jit(solution)/shard_map/ppermute | solution.py:40
  38.5 2.1 %collective-permute-start.4 = (bf16[16,4096]{1,0:T(8,128)(2,1)S(1)}, bf16[16,4096]{1,0:T(8,128)(2,1)S(1)}, u32[]{:S(2)}, u32[]{:S(2)}) collective-permute-start(bf16[16,4096]{1,0:T(8,128)(2,1)S(1)} %fusion.2.one), channel_id=1, source_target_pairs={{0,24},{8,16},{16,8},{24,0},{32,56},{40,48},{48,40},{56,32},{1,25}... | collective-permute-start | bytes 393224 | tf_op jit(solution)/shard_map/ppermute | solution.py:40
  40.6 6.6 %collective-permute-start.5 = (bf16[16,4096]{1,0:T(8,128)(2,1)S(1)}, bf16[16,4096]{1,0:T(8,128)(2,1)S(1)}, u32[]{:S(2)}, u32[]{:S(2)}) collective-permute-start(bf16[16,4096]{1,0:T(8,128)(2,1)S(1)} %fusion.2.one), channel_id=1, source_target_pairs={{0,32},{8,40},{16,48},{24,56},{32,0},{40,8},{48,16},{56,24},{1,33}... | collective-permute-start | bytes 393224 | tf_op jit(solution)/shard_map/ppermute | solution.py:40
  47.9 2.5 %collective-permute-done.5.passed = bf16[16,4096]{1,0:T(8,128)(2,1)S(1)} collective-permute-done((bf16[16,4096]{1,0:T(8,128)(2,1)S(1)}, bf16[16,4096]{1,0:T(8,128)(2,1)S(1)}, u32[]{:S(2)}, u32[]{:S(2)}) %collective-permute-start.5) | collective-permute-done | bytes 131104 | tf_op jit(solution)/shard_map/ppermute | solution.py:40
  50.4 0.9 shard_map.86
  51.3 4.5 %collective-permute-start.6 = (bf16[4,16,4096]{2,1,0:T(8,128)(2,1)}, bf16[4,16,4096]{2,1,0:T(8,128)(2,1)}, u32[]{:S(2)}, u32[]{:S(2)}) collective-permute-start(bf16[4,16,4096]{2,1,0:T(8,128)(2,1)} %get-tuple-element.9.refs_0_), channel_id=1, source_target_pairs={{2,0},{4,2},{6,4},{0,6},{3,1},{5,3},{7,5},{1,7},{10,8},{12,10},{14... | collective-permute-start | bytes 1572872 | tf_op jit(solution)/shard_map/ppermute | solution.py:36
  55.8 2.5 %collective-permute-start.7 = (bf16[4,16,4096]{2,1,0:T(8,128)(2,1)}, bf16[4,16,4096]{2,1,0:T(8,128)(2,1)}, u32[]{:S(2)}, u32[]{:S(2)}) collective-permute-start(bf16[4,16,4096]{2,1,0:T(8,128)(2,1)} %get-tuple-element.9.refs_0_), channel_id=1, source_target_pairs={{4,0},{6,2},{0,4},{2,6},{5,1},{7,3},{1,5},{3,7},{12,8},{14,10},{8,... | collective-permute-start | bytes 1572872 | tf_op jit(solution)/shard_map/ppermute | solution.py:36
  58.3 2.5 %collective-permute-start.8 = (bf16[4,16,4096]{2,1,0:T(8,128)(2,1)}, bf16[4,16,4096]{2,1,0:T(8,128)(2,1)}, u32[]{:S(2)}, u32[]{:S(2)}) collective-permute-start(bf16[4,16,4096]{2,1,0:T(8,128)(2,1)} %get-tuple-element.9.refs_0_), channel_id=1, source_target_pairs={{6,0},{0,2},{2,4},{4,6},{7,1},{1,3},{3,5},{5,7},{14,8},{8,10},{10,... | collective-permute-start | bytes 1572872 | tf_op jit(solution)/shard_map/ppermute | solution.py:36
  60.8 12.2 %collective-permute-start.11 = (bf16[16,4096]{1,0:T(8,128)(2,1)S(1)}, bf16[16,4096]{1,0:T(8,128)(2,1)S(1)}, u32[]{:S(2)}, u32[]{:S(2)}) collective-permute-start(bf16[16,4096]{1,0:T(8,128)(2,1)S(1)} %get-tuple-element.12.one), channel_id=1, source_target_pairs={{0,8},{8,0},{16,24},{24,16},{32,40},{40,32},{48,56},{56,48},{1,9},... | collective-permute-start | bytes 393224 | tf_op jit(solution)/shard_map/ppermute | solution.py:40
  73.0 0.5 slice.3
  74.6 1.0 fusion.3
  75.8 1.9 %shard_map.87.refs_5_.refs_6_.rest_0_ = bf16[256,4096]{1,0:T(8,128)(2,1)S(1)} custom-call(f32[1,4096]{1,0:T(1,128)S(1)} %constant_dynamic-slice_fusion.gain, bf16[256,4096]{1,0:T(8,128)(2,1)} %bitcast.15.given), custom_call_target="tpu_custom_call" | custom-call | bytes 4194304 | tf_op jit(solution)/shard_map/pallas_call | solution.py:208
  77.8 2.1 %collective-permute-start.12 = (bf16[16,4096]{1,0:T(8,128)(2,1)S(1)}, bf16[16,4096]{1,0:T(8,128)(2,1)S(1)}, u32[]{:S(2)}, u32[]{:S(2)}) collective-permute-start(bf16[16,4096]{1,0:T(8,128)(2,1)S(1)} %get-tuple-element.12.one), channel_id=1, source_target_pairs={{0,16},{8,24},{16,0},{24,8},{32,48},{40,56},{48,32},{56,40},{1,17}... | collective-permute-start | bytes 393224 | tf_op jit(solution)/shard_map/ppermute | solution.py:40
  79.8 1.3 constant_dynamic-slice_fusion.1
  81.1 4.0 %collective-permute-start.13 = (bf16[16,4096]{1,0:T(8,128)(2,1)S(1)}, bf16[16,4096]{1,0:T(8,128)(2,1)S(1)}, u32[]{:S(2)}, u32[]{:S(2)}) collective-permute-start(bf16[16,4096]{1,0:T(8,128)(2,1)S(1)} %get-tuple-element.12.one), channel_id=1, source_target_pairs={{0,24},{8,16},{16,8},{24,0},{32,56},{40,48},{48,40},{56,32},{1,25}... | collective-permute-start | bytes 393224 | tf_op jit(solution)/shard_map/ppermute | solution.py:40
  85.1 0.7 multiply_convert_fusion.refs_4_.rest_1_
  85.9 3.3 %collective-permute-done.12.three = bf16[16,4096]{1,0:T(8,128)(2,1)S(1)} collective-permute-done((bf16[16,4096]{1,0:T(8,128)(2,1)S(1)}, bf16[16,4096]{1,0:T(8,128)(2,1)S(1)}, u32[]{:S(2)}, u32[]{:S(2)}) %collective-permute-start.12) | collective-permute-done | bytes 131104 | tf_op jit(solution)/shard_map/ppermute | solution.py:40
  89.2 0.6 shard_map.89
  89.8 3.8 %collective-permute-start.14 = (bf16[4,16,4096]{2,1,0:T(8,128)(2,1)S(1)}, bf16[4,16,4096]{2,1,0:T(8,128)(2,1)S(1)}, u32[]{:S(2)}, u32[]{:S(2)}) collective-permute-start(bf16[4,16,4096]{2,1,0:T(8,128)(2,1)S(1)} %get-tuple-element.13.refs_0_), channel_id=1, source_target_pairs={{2,0},{4,2},{6,4},{0,6},{3,1},{5,3},{7,5},{1,7},{10,8},{12,10},{14... | collective-permute-start | bytes 1572872 | tf_op jit(solution)/shard_map/ppermute | solution.py:36
  93.6 3.9 %collective-permute-start.15 = (bf16[4,16,4096]{2,1,0:T(8,128)(2,1)S(1)}, bf16[4,16,4096]{2,1,0:T(8,128)(2,1)S(1)}, u32[]{:S(2)}, u32[]{:S(2)}) collective-permute-start(bf16[4,16,4096]{2,1,0:T(8,128)(2,1)S(1)} %get-tuple-element.13.refs_0_), channel_id=1, source_target_pairs={{4,0},{6,2},{0,4},{2,6},{5,1},{7,3},{1,5},{3,7},{12,8},{14,10},{8,... | collective-permute-start | bytes 1572872 | tf_op jit(solution)/shard_map/ppermute | solution.py:36
  97.5 1.9 %collective-permute-start.16 = (bf16[4,16,4096]{2,1,0:T(8,128)(2,1)S(1)}, bf16[4,16,4096]{2,1,0:T(8,128)(2,1)S(1)}, u32[]{:S(2)}, u32[]{:S(2)}) collective-permute-start(bf16[4,16,4096]{2,1,0:T(8,128)(2,1)S(1)} %get-tuple-element.13.refs_0_), channel_id=1, source_target_pairs={{6,0},{0,2},{2,4},{4,6},{7,1},{1,3},{3,5},{5,7},{14,8},{8,10},{10,... | collective-permute-start | bytes 1572872 | tf_op jit(solution)/shard_map/ppermute | solution.py:36
  99.5 3.1 %shard_map.88 = (f32[256,384]{1,0:T(8,128)S(1)}, bf16[256,384]{1,0:T(8,128)(2,1)S(1)}) custom-call(bf16[4,16,4096]{2,1,0:T(8,128)(2,1)} %get-tuple-element.9.refs_0_, bf16[4,16,4096]{2,1,0:T(8,128)(2,1)} %collective-permute-done.6.refs_1_, bf16[4,16,4096]{2,1,0:T(8,128)(2,1)} %collective-permute-done.7.refs_2_, ...), custom_call_target="tpu_custom_call" | custom-call | flops 107374182400 | bytes 9437184 | tf_op jit(solution)/shard_map/pallas_call | solution.py:243
  102.6 5.2 %collective-permute-start.10 = (bf16[256,384]{1,0:T(8,128)(2,1)S(1)}, bf16[256,384]{1,0:T(8,128)(2,1)S(1)}, u32[]{:S(2)}, u32[]{:S(2)}) collective-permute-start(bf16[256,384]{1,0:T(8,128)(2,1)S(1)} %get-tuple-element.11), channel_id=1, source_target_pairs={{0,1},{1,0},{2,3},{3,2},{4,5},{5,4},{6,7},{7,6},{8,9},{9,8},{10,11... | collective-permute-start | bytes 589832 | tf_op jit(solution)/shard_map/ppermute | solution.py:44
  107.8 1.0 collective-permute-done.10.refs_6_.got1
  108.8 13.0 %collective-permute-done.16.refs_3_ = bf16[4,16,4096]{2,1,0:T(8,128)(2,1)S(1)} collective-permute-done((bf16[4,16,4096]{2,1,0:T(8,128)(2,1)S(1)}, bf16[4,16,4096]{2,1,0:T(8,128)(2,1)S(1)}, u32[]{:S(2)}, u32[]{:S(2)}) %collective-permute-start.16) | collective-permute-done | bytes 524320 | tf_op jit(solution)/shard_map/ppermute | solution.py:36
  121.8 1.8 %shard_map.90 = (f32[256,384]{1,0:T(8,128)S(1)}, bf16[256,384]{1,0:T(8,128)(2,1)S(1)}) custom-call(bf16[4,16,4096]{2,1,0:T(8,128)(2,1)S(1)} %get-tuple-element.13.refs_0_, bf16[4,16,4096]{2,1,0:T(8,128)(2,1)S(1)} %collective-permute-done.14.refs_1_, bf16[4,16,4096]{2,1,0:T(8,128)(2,1)S(1)} %collective-permute-done.15.refs_2_, ...), custom_call_target="tpu_custom_call" | custom-call | flops 1073741824 | bytes 9437184 | tf_op jit(solution)/shard_map/pallas_call | solution.py:243
  123.6 0.7 copy-done.9
  124.2 0.7 shard_map.92
  124.9 0.6 copy-done.3
  125.5 12.0 %all-to-all-start.1 = ((f32[16,8,256]{2,1,0:T(8,128)}), f32[16,8,256]{2,1,0:T(8,128)S(1)}, u32[]{:S(2)}, u32[]{:S(2)}) async-start(f32[16,8,256]{2,1,0:T(8,128)} %copy-done.3), calls=%async_computation.1 | async-start | bytes 262144 | tf_op jit(solution)/shard_map/all_to_all | solution.py:269
  137.5 2.0 %collective-permute-start.17 = (bf16[256,384]{1,0:T(8,128)(2,1)}, bf16[256,384]{1,0:T(8,128)(2,1)}, u32[]{:S(2)}, u32[]{:S(2)}) collective-permute-start(bf16[256,384]{1,0:T(8,128)(2,1)} %copy-done.9), channel_id=1, source_target_pairs={{0,1},{1,0},{2,3},{3,2},{4,5},{5,4},{6,7},{7,6},{8,9},{9,8},{10,11... | collective-permute-start | bytes 589832 | tf_op jit(solution)/shard_map/ppermute | solution.py:44
  139.6 1.6 %collective-permute-done.17.got2 = bf16[256,384]{1,0:T(8,128)(2,1)} collective-permute-done((bf16[256,384]{1,0:T(8,128)(2,1)}, bf16[256,384]{1,0:T(8,128)(2,1)}, u32[]{:S(2)}, u32[]{:S(2)}) %collective-permute-start.17) | collective-permute-done | bytes 196640 | tf_op jit(solution)/shard_map/ppermute | solution.py:44
  141.2 0.9 copy-done.2
  142.1 3.2 %shard_map.91 = bf16[512,128]{1,0:T(8,128)(2,1)} custom-call(s32[3]{0:T(128)S(1)} %pad_add_fusion.where, f32[256,384]{1,0:T(8,128)S(1)} %get-tuple-element.10.own1, bf16[256,384]{1,0:T(8,128)(2,1)S(1)} %copy-done.2, f32[256,384]{1,0:T(8,128)S(1)} %get-tuple-element.14.own2, bf16[256,384]{1,0:T(8,128)(2,1)} %collective-permute-done.17.got2, ...), custom_call_target="tpu_custom_call" | custom-call | flops 268435456 | bytes 2097152 | tf_op jit(solution)/shard_map/pallas_call | solution.py:275
  145.3 4.2 %all-to-all-done.1.got = f32[16,8,256]{2,1,0:T(8,128)S(1)} async-done(((f32[16,8,256]{2,1,0:T(8,128)}), f32[16,8,256]{2,1,0:T(8,128)S(1)}, u32[]{:S(2)}, u32[]{:S(2)}) %all-to-all-start.1) | async-done | bytes 131104 | tf_op jit(solution)/shard_map/all_to_all | solution.py:269
  149.5 0.8 copy-done.5
  150.3 0.8 copy-done.7
  151.1 0.6 copy.10
  (49 shorter events, 1.2 us)
Async XLA Ops:
  0.6 138.9 %copy-start = (bf16[1,8,512,256]{3,2,1,0:T(8,128)(2,1)S(1)}, bf16[1,8,512,256]{3,2,1,0:T(8,128)(2,1)}, u32[]{:S(2)}) copy-start(bf16[1,8,512,256]{3,2,1,0:T(8,128)(2,1)} %param.11) | copy-start | bytes 6291460
  2.9 28.4 %collective-permute-start.1 = (bf16[8,4096]{1,0:T(8,128)(2,1)S(1)}, bf16[8,4096]{1,0:T(8,128)(2,1)S(1)}, u32[]{:S(2)}, u32[]{:S(2)}) collective-permute-start(bf16[8,4096]{1,0:T(8,128)(2,1)S(1)} %get-tuple-element.19), channel_id=1, source_target_pairs={{0,97},{1,96},{8,105},{9,104},{16,113},{17,112},{24,121},{25,120},... | collective-permute-start | bytes 196616 | tf_op jit(solution)/shard_map/ppermute | solution.py:192
  16.8 14.5 %collective-permute-start = (bf16[8,4096]{1,0:T(8,128)(2,1)S(1)}, bf16[8,4096]{1,0:T(8,128)(2,1)S(1)}, u32[]{:S(2)}, u32[]{:S(2)}) collective-permute-start(bf16[8,4096]{1,0:T(8,128)(2,1)S(1)} %get-tuple-element.18), channel_id=1, source_target_pairs={{0,96},{1,97},{8,104},{9,105},{16,112},{17,113},{24,120},{25,121},... | collective-permute-start | bytes 196616 | tf_op jit(solution)/shard_map/ppermute | solution.py:191
  18.7 59.0 %collective-permute-start.9 = (bf16[8192,128]{1,0:T(8,128)(2,1)}, bf16[8192,128]{1,0:T(8,128)(2,1)}, u32[]{:S(2)}, u32[]{:S(2)}) collective-permute-start(bf16[8192,128]{1,0:T(8,128)(2,1)} %bitcast.37), channel_id=1, source_target_pairs={{0,1},{1,0},{2,3},{3,2},{4,5},{5,4},{6,7},{7,6},{8,9},{9,8},{10,11... | collective-permute-start | bytes 6291464 | tf_op jit(solution)/shard_map/ppermute | solution.py:44
  24.4 51.4 %all-to-all-start = ((bf16[8,32,4096]{2,1,0:T(8,128)(2,1)}), bf16[8,32,4096]{2,1,0:T(8,128)(2,1)}, u32[]{:S(2)}, u32[]{:S(2)}) async-start(bf16[8,32,4096]{2,1,0:T(8,128)(2,1)} %bitcast.35), calls=%async_computation | async-start | bytes 4194304 | tf_op jit(solution)/shard_map/all_to_all | solution.py:207
  29.0 2.3 %copy-start.11 = (f32[1,8192]{1,0:T(1,128)S(1)}, f32[1,8192]{1,0:T(1,128)}, u32[]{:S(2)}) copy-start(f32[1,8192]{1,0:T(1,128)} %param.8) | copy-start | bytes 98308
  29.0 18.2 %copy-start.8 = (s32[1,8]{1,0:T(1,128)S(1)}, s32[1,8]{1,0:T(1,128)}, u32[]{:S(2)}) copy-start(s32[1,8]{1,0:T(1,128)} %param.13) | copy-start | bytes 100
  31.3 16.6 %collective-permute-start.2 = (bf16[16,4096]{1,0:T(8,128)(2,1)S(1)}, bf16[16,4096]{1,0:T(8,128)(2,1)S(1)}, u32[]{:S(2)}, u32[]{:S(2)}) collective-permute-start(bf16[16,4096]{1,0:T(8,128)(2,1)S(1)} %fusion.2.one), channel_id=1, source_target_pairs={{0,8},{8,0},{16,24},{24,16},{32,40},{40,32},{48,56},{56,48},{1,9},... | collective-permute-start | bytes 393224 | tf_op jit(solution)/shard_map/ppermute | solution.py:40
  34.0 14.0 %collective-permute-start.3 = (bf16[16,4096]{1,0:T(8,128)(2,1)S(1)}, bf16[16,4096]{1,0:T(8,128)(2,1)S(1)}, u32[]{:S(2)}, u32[]{:S(2)}) collective-permute-start(bf16[16,4096]{1,0:T(8,128)(2,1)S(1)} %fusion.2.one), channel_id=1, source_target_pairs={{0,16},{8,24},{16,0},{24,8},{32,48},{40,56},{48,32},{56,40},{1,17}... | collective-permute-start | bytes 393224 | tf_op jit(solution)/shard_map/ppermute | solution.py:40
  38.5 9.4 %collective-permute-start.4 = (bf16[16,4096]{1,0:T(8,128)(2,1)S(1)}, bf16[16,4096]{1,0:T(8,128)(2,1)S(1)}, u32[]{:S(2)}, u32[]{:S(2)}) collective-permute-start(bf16[16,4096]{1,0:T(8,128)(2,1)S(1)} %fusion.2.one), channel_id=1, source_target_pairs={{0,24},{8,16},{16,8},{24,0},{32,56},{40,48},{48,40},{56,32},{1,25}... | collective-permute-start | bytes 393224 | tf_op jit(solution)/shard_map/ppermute | solution.py:40
  40.6 9.8 %collective-permute-start.5 = (bf16[16,4096]{1,0:T(8,128)(2,1)S(1)}, bf16[16,4096]{1,0:T(8,128)(2,1)S(1)}, u32[]{:S(2)}, u32[]{:S(2)}) collective-permute-start(bf16[16,4096]{1,0:T(8,128)(2,1)S(1)} %fusion.2.one), channel_id=1, source_target_pairs={{0,32},{8,40},{16,48},{24,56},{32,0},{40,8},{48,16},{56,24},{1,33}... | collective-permute-start | bytes 393224 | tf_op jit(solution)/shard_map/ppermute | solution.py:40
  51.3 46.2 %collective-permute-start.6 = (bf16[4,16,4096]{2,1,0:T(8,128)(2,1)}, bf16[4,16,4096]{2,1,0:T(8,128)(2,1)}, u32[]{:S(2)}, u32[]{:S(2)}) collective-permute-start(bf16[4,16,4096]{2,1,0:T(8,128)(2,1)} %get-tuple-element.9.refs_0_), channel_id=1, source_target_pairs={{2,0},{4,2},{6,4},{0,6},{3,1},{5,3},{7,5},{1,7},{10,8},{12,10},{14... | collective-permute-start | bytes 1572872 | tf_op jit(solution)/shard_map/ppermute | solution.py:36
  55.8 43.6 %collective-permute-start.7 = (bf16[4,16,4096]{2,1,0:T(8,128)(2,1)}, bf16[4,16,4096]{2,1,0:T(8,128)(2,1)}, u32[]{:S(2)}, u32[]{:S(2)}) collective-permute-start(bf16[4,16,4096]{2,1,0:T(8,128)(2,1)} %get-tuple-element.9.refs_0_), channel_id=1, source_target_pairs={{4,0},{6,2},{0,4},{2,6},{5,1},{7,3},{1,5},{3,7},{12,8},{14,10},{8,... | collective-permute-start | bytes 1572872 | tf_op jit(solution)/shard_map/ppermute | solution.py:36
  58.3 41.2 %collective-permute-start.8 = (bf16[4,16,4096]{2,1,0:T(8,128)(2,1)}, bf16[4,16,4096]{2,1,0:T(8,128)(2,1)}, u32[]{:S(2)}, u32[]{:S(2)}) collective-permute-start(bf16[4,16,4096]{2,1,0:T(8,128)(2,1)} %get-tuple-element.9.refs_0_), channel_id=1, source_target_pairs={{6,0},{0,2},{2,4},{4,6},{7,1},{1,3},{3,5},{5,7},{14,8},{8,10},{10,... | collective-permute-start | bytes 1572872 | tf_op jit(solution)/shard_map/ppermute | solution.py:36
  60.8 20.3 %collective-permute-start.11 = (bf16[16,4096]{1,0:T(8,128)(2,1)S(1)}, bf16[16,4096]{1,0:T(8,128)(2,1)S(1)}, u32[]{:S(2)}, u32[]{:S(2)}) collective-permute-start(bf16[16,4096]{1,0:T(8,128)(2,1)S(1)} %get-tuple-element.12.one), channel_id=1, source_target_pairs={{0,8},{8,0},{16,24},{24,16},{32,40},{40,32},{48,56},{56,48},{1,9},... | collective-permute-start | bytes 393224 | tf_op jit(solution)/shard_map/ppermute | solution.py:40
  74.6 14.6 %copy-start.4 = (f32[8,8,128]{2,1,0:T(8,128)}, f32[8,8,128]{2,1,0:T(8,128)S(1)}, u32[]{:S(2)}) copy-start(f32[8,8,128]{2,1,0:T(8,128)S(1)} %get-tuple-element.28.rest_4_.cosine) | copy-start | bytes 98308
  74.6 14.6 %copy-start.6 = (f32[8,8,128]{2,1,0:T(8,128)}, f32[8,8,128]{2,1,0:T(8,128)S(1)}, u32[]{:S(2)}) copy-start(f32[8,8,128]{2,1,0:T(8,128)S(1)} %get-tuple-element.29.rest_5_.sine) | copy-start | bytes 98308
  77.7 7.4 %copy-start.10 = (bf16[4096,128]{1,0:T(8,128)(2,1)S(1)}, bf16[4096,128]{1,0:T(8,128)(2,1)}, u32[]{:S(2)}) copy-start(bf16[4096,128]{1,0:T(8,128)(2,1)} %dynamic-slice_bitcast_fusion) | copy-start | bytes 3145732
  77.8 11.4 %collective-permute-start.12 = (bf16[16,4096]{1,0:T(8,128)(2,1)S(1)}, bf16[16,4096]{1,0:T(8,128)(2,1)S(1)}, u32[]{:S(2)}, u32[]{:S(2)}) collective-permute-start(bf16[16,4096]{1,0:T(8,128)(2,1)S(1)} %get-tuple-element.12.one), channel_id=1, source_target_pairs={{0,16},{8,24},{16,0},{24,8},{32,48},{40,56},{48,32},{56,40},{1,17}... | collective-permute-start | bytes 393224 | tf_op jit(solution)/shard_map/ppermute | solution.py:40
  81.1 8.0 %collective-permute-start.13 = (bf16[16,4096]{1,0:T(8,128)(2,1)S(1)}, bf16[16,4096]{1,0:T(8,128)(2,1)S(1)}, u32[]{:S(2)}, u32[]{:S(2)}) collective-permute-start(bf16[16,4096]{1,0:T(8,128)(2,1)S(1)} %get-tuple-element.12.one), channel_id=1, source_target_pairs={{0,24},{8,16},{16,8},{24,0},{32,56},{40,48},{48,40},{56,32},{1,25}... | collective-permute-start | bytes 393224 | tf_op jit(solution)/shard_map/ppermute | solution.py:40
  89.8 19.0 %collective-permute-start.14 = (bf16[4,16,4096]{2,1,0:T(8,128)(2,1)S(1)}, bf16[4,16,4096]{2,1,0:T(8,128)(2,1)S(1)}, u32[]{:S(2)}, u32[]{:S(2)}) collective-permute-start(bf16[4,16,4096]{2,1,0:T(8,128)(2,1)S(1)} %get-tuple-element.13.refs_0_), channel_id=1, source_target_pairs={{2,0},{4,2},{6,4},{0,6},{3,1},{5,3},{7,5},{1,7},{10,8},{12,10},{14... | collective-permute-start | bytes 1572872 | tf_op jit(solution)/shard_map/ppermute | solution.py:36
  93.6 15.2 %collective-permute-start.15 = (bf16[4,16,4096]{2,1,0:T(8,128)(2,1)S(1)}, bf16[4,16,4096]{2,1,0:T(8,128)(2,1)S(1)}, u32[]{:S(2)}, u32[]{:S(2)}) collective-permute-start(bf16[4,16,4096]{2,1,0:T(8,128)(2,1)S(1)} %get-tuple-element.13.refs_0_), channel_id=1, source_target_pairs={{4,0},{6,2},{0,4},{2,6},{5,1},{7,3},{1,5},{3,7},{12,8},{14,10},{8,... | collective-permute-start | bytes 1572872 | tf_op jit(solution)/shard_map/ppermute | solution.py:36
  97.5 24.3 %collective-permute-start.16 = (bf16[4,16,4096]{2,1,0:T(8,128)(2,1)S(1)}, bf16[4,16,4096]{2,1,0:T(8,128)(2,1)S(1)}, u32[]{:S(2)}, u32[]{:S(2)}) collective-permute-start(bf16[4,16,4096]{2,1,0:T(8,128)(2,1)S(1)} %get-tuple-element.13.refs_0_), channel_id=1, source_target_pairs={{6,0},{0,2},{2,4},{4,6},{7,1},{1,3},{3,5},{5,7},{14,8},{8,10},{10,... | collective-permute-start | bytes 1572872 | tf_op jit(solution)/shard_map/ppermute | solution.py:36
  102.6 6.2 %collective-permute-start.10 = (bf16[256,384]{1,0:T(8,128)(2,1)S(1)}, bf16[256,384]{1,0:T(8,128)(2,1)S(1)}, u32[]{:S(2)}, u32[]{:S(2)}) collective-permute-start(bf16[256,384]{1,0:T(8,128)(2,1)S(1)} %get-tuple-element.11), channel_id=1, source_target_pairs={{0,1},{1,0},{2,3},{3,2},{4,5},{5,4},{6,7},{7,6},{8,9},{9,8},{10,11... | collective-permute-start | bytes 589832 | tf_op jit(solution)/shard_map/ppermute | solution.py:44
  108.8 14.7 %copy-start.1 = (bf16[256,384]{1,0:T(8,128)(2,1)}, bf16[256,384]{1,0:T(8,128)(2,1)S(1)}, u32[]{:S(2)}) copy-start(bf16[256,384]{1,0:T(8,128)(2,1)S(1)} %collective-permute-done.10.refs_6_.got1) | copy-start | bytes 589828
  123.5 0.7 copy-start.9
  124.9 0.6 copy-start.3
  125.5 24.0 %all-to-all-start.1 = ((f32[16,8,256]{2,1,0:T(8,128)}), f32[16,8,256]{2,1,0:T(8,128)S(1)}, u32[]{:S(2)}, u32[]{:S(2)}) async-start(f32[16,8,256]{2,1,0:T(8,128)} %copy-done.3), calls=%async_computation.1 | async-start | bytes 262144 | tf_op jit(solution)/shard_map/all_to_all | solution.py:269
  137.5 3.7 %collective-permute-start.17 = (bf16[256,384]{1,0:T(8,128)(2,1)}, bf16[256,384]{1,0:T(8,128)(2,1)}, u32[]{:S(2)}, u32[]{:S(2)}) collective-permute-start(bf16[256,384]{1,0:T(8,128)(2,1)} %copy-done.9), channel_id=1, source_target_pairs={{0,1},{1,0},{2,3},{3,2},{4,5},{5,4},{6,7},{7,6},{8,9},{9,8},{10,11... | collective-permute-start | bytes 589832 | tf_op jit(solution)/shard_map/ppermute | solution.py:44
  141.2 0.9 copy-start.2
  149.5 0.8 copy-start.5
  150.3 0.8 copy-start.7

commit v4 on v3

--- a/solution.py
+++ b/solution.py
@@ -46,25 +46,29 @@
 
 def place(slot, z0, y0):
     batch, k, i = slot >> 4, (slot >> 2) & 3, slot & 3
-    z = z0 ^ i ^ (4 * (1 - batch))
+    z = z0 ^ (batch << 1) ^ (i >> 1) ^ (4 * (1 - (i & 1)))
     return (z << 2) | ((k + y0) & 3)
 
 
 def slot_of(chip, z0, y0):
     far = (chip >> 2) ^ z0
-    return ((1 - (far >> 2)) << 4) | (((chip - y0) & 3) << 2) | (far & 3)
+    i = ((far & 1) << 1) | (1 - (far >> 2))
+    return (((far >> 1) & 1) << 4) | (((chip - y0) & 3) << 2) | i
 
 
 def tokens_of(row, z0, y0):
     return place(row >> 4, z0, y0) * ROWS + (row & 15)
 
 
-def project_kernel(*refs):
-    *pieces, wq_far, wkv_far, _, own, send, x, wq, wkv, sems = refs
+def project_kernel(where, *refs):
+    *pieces, wq_mine, wq_other, wkv_far, _, own, send, x, wq, wkv, sems = refs
     count = len(pieces)
+    half = x.shape[-1]
+    rows = pl.ds(pl.multiple_of(where[2] * half, half), half)
     copies = [
-        pltpu.make_async_copy(wq_far, wq, sems.at[count]),
-        pltpu.make_async_copy(wkv_far, wkv, sems.at[count + 1]),
+        pltpu.make_async_copy(wq_mine.at[rows], wq.at[:, :HD], sems.at[count]),
+        pltpu.make_async_copy(wq_other.at[rows], wq.at[:, HD:], sems.at[count + 1]),
+        pltpu.make_async_copy(wkv_far, wkv, sems.at[count + 2]),
     ]
     at = 0
     for i, piece in enumerate(pieces):
@@ -84,11 +88,10 @@
     send[:, :HD] = q[:, HD:].astype(BF)
 
 
-def join_kernel(one, two, three, four, passed, *rest):
-    batch, kept = rest[-2:]
-    for i, piece in enumerate((one, two, three, four)):
-        batch[i] = piece[...]
-    kept[...] = passed[...]
+def join_kernel(one, two, *rest):
+    batch = rest[-1]
+    batch[:2] = one[...]
+    batch[2:] = two[...]
 
 
 def turn(v, cosine, sine):
@@ -140,10 +143,6 @@
     for slot in range(32):
         to = pl.multiple_of(place(slot, z0, y0) * ROWS, ROWS)
         out[pl.ds(to, ROWS), :] = att[slot * ROWS : (slot + 1) * ROWS]
-
-
-def kv_weight_kernel(gain, given, out):
-    out[...] = (given[...].astype(F32) * gain[...]).astype(BF)
 
 
 VMEM = pl.BlockSpec(memory_space=pltpu.VMEM)
@@ -191,37 +190,27 @@
     same = lax.ppermute(kept, ("s", "z", "c"), steps[0])
     other = lax.ppermute(crossed, ("s", "z", "c"), steps[1])
     piece = jnp.where(c0 == 0, jnp.stack([same, other]), jnp.stack([other, same]))
-    piece = piece.reshape(ROWS, half)
-
     gain = lax.dynamic_slice_in_dim(norm_gain[0], c0 * half, half, 0)
-    wq = jnp.concatenate(
-        [
-            lax.dynamic_slice_in_dim(w, c0 * half, half, 0)
-            for w in (query_weight[0], swap_core(query_weight[0]))
-        ],
-        axis=1,
-    )
-    wq = (wq.astype(F32) * gain[:, None]).astype(BF)
+    piece = (piece.reshape(ROWS, half).astype(F32) * gain[None]).astype(BF)
+
+    wq_other = swap_core(query_weight[0])
     kv_halves = jnp.transpose(kv_weight[0].T.reshape(32, 2, half), (1, 0, 2))
     kv_halves = jnp.broadcast_to(kv_halves, (NY, 2, 32, half)).reshape(NY * 2, 32, half)
     wkv = lax.all_to_all(kv_halves, ("y", "c"), 0, 0).reshape(256, half)
-    wkv = call(kv_weight_kernel, shaped(256, half), [VMEM] * 2, moved=2**22)(gain[None], wkv)
-
-    def join(one, passed, *after):
-        pieces = [one] + [across_z(one, k) for k in (1, 2, 3)]
+
+    pair = jnp.stack([piece, across_z(piece, 4)])
+
+    def join(one, two, *after):
         return call(
             join_kernel,
-            (shaped(4, ROWS, half), shaped(*passed.shape)),
-            [VMEM] * 5 + [HBM] * len(after),
+            shaped(4, ROWS, half),
+            [VMEM] * 2 + [HBM] * len(after),
             moved=2**20,
             limit=4,
-        )(*pieces, passed, *after)
-
-    def everywhere(batch):
-        return [batch] + [along_y(batch, k) for k in (1, 2, 3)]
-
-    batch1, second = join(piece, across_z(piece, 4))
-    late = (second[0, 0] > 3e38).astype(jnp.int32)
+        )(one, two, *after)
+
+    batch1 = join(pair, across_z(pair, 1), wq_other)
+    late = (batch1[0, 0, 0] > 3e38).astype(jnp.int32)
 
     def tables(tokens):
         angles = (block_start[0] + late + tokens).astype(F32)[..., None] * frequencies(HD)
@@ -234,8 +223,11 @@
     cosine, sine = tables(row_tokens)
     decode_cosine, decode_sine = tables(decode_tokens)
 
-    batch2, _ = join(second, jnp.zeros((16, HD), BF), wkv, wq, cosine, sine, decode_cosine, decode_sine)
-    batch1, batch2 = everywhere(batch1), everywhere(batch2)
+    made = (wkv, cosine, sine, decode_cosine, decode_sine)
+    batch2 = join(across_z(pair, 2), across_z(pair, 3), *made)
+    batch1, batch2 = (
+        [batch] + [along_y(batch, k) for k in (1, 2, 3)] for batch in (batch1, batch2)
+    )
 
     def project(pieces, earlier, weight):
         slots = sum(p.shape[0] for p in pieces)
@@ -243,16 +235,16 @@
         return call(
             project_kernel,
             (shaped(tokens, 3 * HD, dtype=F32), shaped(tokens, 3 * HD)),
-            [HBM] * (len(pieces) + 3),
+            [SMEM] + [HBM] * (len(pieces) + 4),
             scratch=[
                 pltpu.VMEM((slots, ROWS, half), BF),
                 pltpu.VMEM((half, 2 * HD), BF),
                 pltpu.VMEM((2 * HD, half), BF),
-                pltpu.SemaphoreType.DMA((len(pieces) + 2,)),
+                pltpu.SemaphoreType.DMA((len(pieces) + 3,)),
             ],
             flops=2 * tokens * half * 512 * weight,
             moved=9 * 2**20,
-        )(*pieces, wq, wkv, earlier)
+        )(where, *pieces, query_weight[0], wq_other, wkv, earlier)
 
     own1, send1 = project(batch1, wkv, 100)
     got1 = swap_core(send1)

time: 153 us -> 147 us (0.961)
  starting transfers between devices: 95 us -> 75.6 us
  waiting for transfers between devices: 25.5 us -> 41.6 us
  local copies, waits for them, and re-layouts: 11.9 us -> 8.34 us
    ppermute x7 -> x4, starting transfers between devices: 34.1 us -> 17.2 us  [across_z(): return lax.ppermute(value, 'z', [(i, i ^ k) for i in range(NZ)])]
    ppermute x7 -> x4, waiting for transfers between devices: 5.75 us -> 19.7 us  [across_z(): return lax.ppermute(value, 'z', [(i, i ^ k) for i in range(NZ)])]
    all_to_all x1, starting transfers between devices: 12 us -> 8.09 us  [body(): blocks = lax.all_to_all(blocks, ('z', 'c'), 0, 0)]
    dynamic_slice x3 -> x1, local copies, waits for them, and re-layouts: 3.6 us -> 0.02 us  [body(): crossed = lax.dynamic_slice_in_dim(rows, (1 - c0) * half, half, 1)]
    pallas_call x2, Pallas kernels: 4.87 us -> 8.35 us  [project(): call(project_kernel, (shaped(tokens, 3 * HD, dtype=F32), shaped(tokens, 3...]
    ppermute x6, waiting for transfers between devices: 13 us -> 16.1 us  [along_y(): return lax.ppermute(value, 'y', [((i + k) % NY, i) for i in range(NY)])]
    ppermute x6, starting transfers between devices: 19.1 us -> 21.4 us  [along_y(): return lax.ppermute(value, 'y', [((i + k) % NY, i) for i in range(NY)])]
    pallas_call x3 -> x2, Pallas kernels: 3.46 us -> 1.25 us  [join(): call(join_kernel, shaped(4, ROWS, half), [VMEM] * 2 + [HBM] * len(after),...]
  transfers between devices with their start and end apart: 20 -> 17, of which waited for: 6 -> 9; matrix products, arithmetic and copies ran while one was open for 7% -> 4% of each run, Pallas kernels for 6% -> 6%
where the time goes in v4:
time: 147 us; the launch traced here: 145 us
  starting transfers between devices  75.6 us (51%)
  waiting for transfers between devices  41.6 us (28%)
  Pallas kernels  13.6 us (9%)
  local copies, waits for them, and re-layouts  8.34 us (6%)
  other arithmetic  4.01 us (3%)
  between operations  2.33 us (2%)
    ppermute x6, starting transfers between devices, along_y(): return lax.ppermute(value, 'y', [((i + k) % NY, i) for i in range(NY)])  21.4 us
    ppermute x4, waiting for transfers between devices, across_z(): return lax.ppermute(value, 'z', [(i, i ^ k) for i in range(NZ)])  19.7 us
    ppermute x4, starting transfers between devices, across_z(): return lax.ppermute(value, 'z', [(i, i ^ k) for i in range(NZ)])  17.2 us
    ppermute x6, waiting for transfers between devices, along_y(): return lax.ppermute(value, 'y', [((i + k) % NY, i) for i in range(NY)])  16.1 us
    ppermute x1, starting transfers between devices, body(): other = lax.ppermute(crossed, ('s', 'z', 'c'), steps[1])  13.8 us
    pallas_call x2, Pallas kernels, project(): call(project_kernel, (shaped(tokens, 3 * HD, dtype=F32), shaped(tokens, 3...  8.35 us
    ppermute x3, starting transfers between devices, swap_core(): return lax.ppermute(value, 'c', [(0, 1), (1, 0)])  8.13 us
    all_to_all x1, starting transfers between devices, body(): blocks = lax.all_to_all(blocks, ('z', 'c'), 0, 0)  8.09 us
  transfers between devices with their start and end apart: 17, of which 9 were waited for; matrix products, arithmetic and copies ran while one was open for 4% of the time, Pallas kernels for 6%

profile of v4, /device:TPU:1, one launch (start us, length us, event | category | flops | bytes accessed | tf_op | source)
XLA Modules:
  0.0 145.5 jit_solution(4928277265104525270)
XLA Ops:
  0.7 1.2 fusion.4
  1.9 1.0 fusion.5
  2.9 13.8 %collective-permute-start.1 = (bf16[8,4096]{1,0:T(8,128)(2,1)S(1)}, bf16[8,4096]{1,0:T(8,128)(2,1)S(1)}, u32[]{:S(2)}, u32[]{:S(2)}) collective-permute-start(bf16[8,4096]{1,0:T(8,128)(2,1)S(1)} %get-tuple-element.12), channel_id=1, source_target_pairs={{0,97},{1,96},{8,105},{9,104},{16,113},{17,112},{24,121},{25,120},... | collective-permute-start | bytes 196616 | tf_op jit(solution)/shard_map/ppermute | solution.py:191
  16.8 1.9 %collective-permute-start = (bf16[8,4096]{1,0:T(8,128)(2,1)S(1)}, bf16[8,4096]{1,0:T(8,128)(2,1)S(1)}, u32[]{:S(2)}, u32[]{:S(2)}) collective-permute-start(bf16[8,4096]{1,0:T(8,128)(2,1)S(1)} %get-tuple-element.13), channel_id=1, source_target_pairs={{0,96},{1,97},{8,104},{9,105},{16,112},{17,113},{24,120},{25,121},... | collective-permute-start | bytes 196616 | tf_op jit(solution)/shard_map/ppermute | solution.py:190
  18.7 1.4 reshape.187
  20.1 0.3 copy.9
  20.4 1.6 %broadcast_in_dim.6 = bf16[4,2,32,4096]{3,2,1,0:T(8,128)(2,1)} broadcast(bf16[2,32,4096]{2,1,0:T(8,128)(2,1)S(1)} %copy.9), dimensions={1,2,3} | broadcast | bytes 2621440 | tf_op jit(solution)/shard_map/broadcast_in_dim | solution.py:198
  22.1 5.0 %all-to-all-start = ((bf16[8,32,4096]{2,1,0:T(8,128)(2,1)}), bf16[8,32,4096]{2,1,0:T(8,128)(2,1)}, u32[]{:S(2)}, u32[]{:S(2)}) async-start(bf16[8,32,4096]{2,1,0:T(8,128)(2,1)} %bitcast.46), calls=%async_computation | async-start | bytes 4194304 | tf_op jit(solution)/shard_map/all_to_all | solution.py:199
  27.0 1.9 %collective-permute-start.4 = (bf16[8192,128]{1,0:T(8,128)(2,1)}, bf16[8192,128]{1,0:T(8,128)(2,1)}, u32[]{:S(2)}, u32[]{:S(2)}) collective-permute-start(bf16[8192,128]{1,0:T(8,128)(2,1)} %bitcast.41), channel_id=1, source_target_pairs={{0,1},{1,0},{2,3},{3,2},{4,5},{5,4},{6,7},{7,6},{8,9},{9,8},{10,11... | collective-permute-start | bytes 6291464 | tf_op jit(solution)/shard_map/ppermute | solution.py:44
  29.1 8.8 %collective-permute-start.2 = (bf16[16,4096]{1,0:T(8,128)(2,1)S(1)}, bf16[16,4096]{1,0:T(8,128)(2,1)S(1)}, u32[]{:S(2)}, u32[]{:S(2)}) collective-permute-start(bf16[16,4096]{1,0:T(8,128)(2,1)S(1)} %fusion.3), channel_id=1, source_target_pairs={{0,32},{8,40},{16,48},{24,56},{32,0},{40,8},{48,16},{56,24},{1,33}... | collective-permute-start | bytes 393224 | tf_op jit(solution)/shard_map/ppermute | solution.py:40
  38.0 12.2 %collective-permute-done.2 = bf16[16,4096]{1,0:T(8,128)(2,1)S(1)} collective-permute-done((bf16[16,4096]{1,0:T(8,128)(2,1)S(1)}, bf16[16,4096]{1,0:T(8,128)(2,1)S(1)}, u32[]{:S(2)}, u32[]{:S(2)}) %collective-permute-start.2) | collective-permute-done | bytes 131104 | tf_op jit(solution)/shard_map/ppermute | solution.py:40
  50.2 1.9 %collective-permute-start.3 = (bf16[2,16,4096]{2,1,0:T(8,128)(2,1)S(1)}, bf16[2,16,4096]{2,1,0:T(8,128)(2,1)S(1)}, u32[]{:S(2)}, u32[]{:S(2)}) collective-permute-start(bf16[2,16,4096]{2,1,0:T(8,128)(2,1)S(1)} %pad_maximum_fusion.one), channel_id=1, source_target_pairs={{0,8},{8,0},{16,24},{24,16},{32,40},{40,32},{48,56},{56,48},{1,9},... | collective-permute-start | bytes 786440 | tf_op jit(solution)/shard_map/ppermute | solution.py:40
  52.9 1.9 %collective-permute-start.10 = (bf16[2,16,4096]{2,1,0:T(8,128)(2,1)S(1)}, bf16[2,16,4096]{2,1,0:T(8,128)(2,1)}, u32[]{:S(2)}, u32[]{:S(2)}) collective-permute-start(bf16[2,16,4096]{2,1,0:T(8,128)(2,1)S(1)} %pad_maximum_fusion.one), channel_id=1, source_target_pairs={{0,24},{8,16},{16,8},{24,0},{32,56},{40,48},{48,40},{56,32},{1,25}... | collective-permute-start | bytes 786440 | tf_op jit(solution)/shard_map/ppermute | solution.py:40
  54.8 4.5 %collective-permute-start.9 = (bf16[2,16,4096]{2,1,0:T(8,128)(2,1)S(1)}, bf16[2,16,4096]{2,1,0:T(8,128)(2,1)}, u32[]{:S(2)}, u32[]{:S(2)}) collective-permute-start(bf16[2,16,4096]{2,1,0:T(8,128)(2,1)S(1)} %pad_maximum_fusion.one), channel_id=1, source_target_pairs={{0,16},{8,24},{16,0},{24,8},{32,48},{40,56},{48,32},{56,40},{1,17}... | collective-permute-start | bytes 786440 | tf_op jit(solution)/shard_map/ppermute | solution.py:40
  59.3 5.0 %collective-permute-done.3.two = bf16[2,16,4096]{2,1,0:T(8,128)(2,1)S(1)} collective-permute-done((bf16[2,16,4096]{2,1,0:T(8,128)(2,1)S(1)}, bf16[2,16,4096]{2,1,0:T(8,128)(2,1)S(1)}, u32[]{:S(2)}, u32[]{:S(2)}) %collective-permute-start.3) | collective-permute-done | bytes 262176 | tf_op jit(solution)/shard_map/ppermute | solution.py:40
  64.4 0.5 slice.4
  65.0 3.2 %collective-permute-start.7 = (bf16[4,16,4096]{2,1,0:T(8,128)(2,1)S(1)}, bf16[4,16,4096]{2,1,0:T(8,128)(2,1)}, u32[]{:S(2)}, u32[]{:S(2)}) collective-permute-start(bf16[4,16,4096]{2,1,0:T(8,128)(2,1)S(1)} %shard_map.86.refs_0_), channel_id=1, source_target_pairs={{6,0},{0,2},{2,4},{4,6},{7,1},{1,3},{3,5},{5,7},{14,8},{8,10},{10,... | collective-permute-start | bytes 1572872 | tf_op jit(solution)/shard_map/ppermute | solution.py:36
  68.2 4.5 %collective-permute-start.6 = (bf16[4,16,4096]{2,1,0:T(8,128)(2,1)S(1)}, bf16[4,16,4096]{2,1,0:T(8,128)(2,1)}, u32[]{:S(2)}, u32[]{:S(2)}) collective-permute-start(bf16[4,16,4096]{2,1,0:T(8,128)(2,1)S(1)} %shard_map.86.refs_0_), channel_id=1, source_target_pairs={{4,0},{6,2},{0,4},{2,6},{5,1},{7,3},{1,5},{3,7},{12,8},{14,10},{8,... | collective-permute-start | bytes 1572872 | tf_op jit(solution)/shard_map/ppermute | solution.py:36
  72.7 3.0 %collective-permute-start.5 = (bf16[4,16,4096]{2,1,0:T(8,128)(2,1)S(1)}, bf16[4,16,4096]{2,1,0:T(8,128)(2,1)}, u32[]{:S(2)}, u32[]{:S(2)}) collective-permute-start(bf16[4,16,4096]{2,1,0:T(8,128)(2,1)S(1)} %shard_map.86.refs_0_), channel_id=1, source_target_pairs={{2,0},{4,2},{6,4},{0,6},{3,1},{5,3},{7,5},{1,7},{10,8},{12,10},{14... | collective-permute-start | bytes 1572872 | tf_op jit(solution)/shard_map/ppermute | solution.py:36
  76.3 1.0 fusion.6
  77.4 0.2 fusion.7
  77.6 0.1 pad_maximum_fusion.3
  77.7 0.2 pad_maximum_fusion.1
  77.9 2.5 %collective-permute-done.9.one = bf16[2,16,4096]{2,1,0:T(8,128)(2,1)} collective-permute-done((bf16[2,16,4096]{2,1,0:T(8,128)(2,1)S(1)}, bf16[2,16,4096]{2,1,0:T(8,128)(2,1)}, u32[]{:S(2)}, u32[]{:S(2)}) %collective-permute-start.9) | collective-permute-done | bytes 262176 | tf_op jit(solution)/shard_map/ppermute | solution.py:40
  80.5 1.2 shard_map.88.refs_0_
  81.7 3.2 %collective-permute-start.13 = (bf16[4,16,4096]{2,1,0:T(8,128)(2,1)S(1)}, bf16[4,16,4096]{2,1,0:T(8,128)(2,1)S(1)}, u32[]{:S(2)}, u32[]{:S(2)}) collective-permute-start(bf16[4,16,4096]{2,1,0:T(8,128)(2,1)S(1)} %shard_map.88.refs_0_), channel_id=1, source_target_pairs={{6,0},{0,2},{2,4},{4,6},{7,1},{1,3},{3,5},{5,7},{14,8},{8,10},{10,... | collective-permute-start | bytes 1572872 | tf_op jit(solution)/shard_map/ppermute | solution.py:36
  84.9 4.5 %collective-permute-start.12 = (bf16[4,16,4096]{2,1,0:T(8,128)(2,1)S(1)}, bf16[4,16,4096]{2,1,0:T(8,128)(2,1)S(1)}, u32[]{:S(2)}, u32[]{:S(2)}) collective-permute-start(bf16[4,16,4096]{2,1,0:T(8,128)(2,1)S(1)} %shard_map.88.refs_0_), channel_id=1, source_target_pairs={{4,0},{6,2},{0,4},{2,6},{5,1},{7,3},{1,5},{3,7},{12,8},{14,10},{8,... | collective-permute-start | bytes 1572872 | tf_op jit(solution)/shard_map/ppermute | solution.py:36
  89.5 3.0 %collective-permute-start.11 = (bf16[4,16,4096]{2,1,0:T(8,128)(2,1)S(1)}, bf16[4,16,4096]{2,1,0:T(8,128)(2,1)S(1)}, u32[]{:S(2)}, u32[]{:S(2)}) collective-permute-start(bf16[4,16,4096]{2,1,0:T(8,128)(2,1)S(1)} %shard_map.88.refs_0_), channel_id=1, source_target_pairs={{2,0},{4,2},{6,4},{0,6},{3,1},{5,3},{7,5},{1,7},{10,8},{12,10},{14... | collective-permute-start | bytes 1572872 | tf_op jit(solution)/shard_map/ppermute | solution.py:36
  92.5 4.4 %collective-permute-done.5.refs_1_ = bf16[4,16,4096]{2,1,0:T(8,128)(2,1)} collective-permute-done((bf16[4,16,4096]{2,1,0:T(8,128)(2,1)S(1)}, bf16[4,16,4096]{2,1,0:T(8,128)(2,1)}, u32[]{:S(2)}, u32[]{:S(2)}) %collective-permute-start.5) | collective-permute-done | bytes 524320 | tf_op jit(solution)/shard_map/ppermute | solution.py:36
  96.8 4.4 %shard_map.87 = (f32[256,384]{1,0:T(8,128)S(1)}, bf16[256,384]{1,0:T(8,128)(2,1)S(1)}) custom-call(s32[3]{0:T(128)S(1)} %pad_add_fusion.where, bf16[4,16,4096]{2,1,0:T(8,128)(2,1)S(1)} %shard_map.86.refs_0_, bf16[4,16,4096]{2,1,0:T(8,128)(2,1)} %collective-permute-done.5.refs_1_, bf16[4,16,4096]{2,1,0:T(8,128)(2,1)} %collective-permute-done.6.refs_2_, ...), custom_call_target="tpu_custom_call" | custom-call | flops 107374182400 | bytes 9437184 | tf_op jit(solution)/shard_map/pallas_call | solution.py:235
  101.2 4.2 %collective-permute-start.8 = (bf16[256,384]{1,0:T(8,128)(2,1)S(1)}, bf16[256,384]{1,0:T(8,128)(2,1)S(1)}, u32[]{:S(2)}, u32[]{:S(2)}) collective-permute-start(bf16[256,384]{1,0:T(8,128)(2,1)S(1)} %get-tuple-element.7), channel_id=1, source_target_pairs={{0,1},{1,0},{2,3},{3,2},{4,5},{5,4},{6,7},{7,6},{8,9},{9,8},{10,11... | collective-permute-start | bytes 589832 | tf_op jit(solution)/shard_map/ppermute | solution.py:44
  105.4 2.6 %collective-permute-done.13.refs_3_ = bf16[4,16,4096]{2,1,0:T(8,128)(2,1)S(1)} collective-permute-done((bf16[4,16,4096]{2,1,0:T(8,128)(2,1)S(1)}, bf16[4,16,4096]{2,1,0:T(8,128)(2,1)S(1)}, u32[]{:S(2)}, u32[]{:S(2)}) %collective-permute-start.13) | collective-permute-done | bytes 524320 | tf_op jit(solution)/shard_map/ppermute | solution.py:36
  108.0 6.4 %collective-permute-done.12.refs_2_ = bf16[4,16,4096]{2,1,0:T(8,128)(2,1)S(1)} collective-permute-done((bf16[4,16,4096]{2,1,0:T(8,128)(2,1)S(1)}, bf16[4,16,4096]{2,1,0:T(8,128)(2,1)S(1)}, u32[]{:S(2)}, u32[]{:S(2)}) %collective-permute-start.12) | collective-permute-done | bytes 524320 | tf_op jit(solution)/shard_map/ppermute | solution.py:36
  114.4 2.7 %collective-permute-done.11.refs_1_ = bf16[4,16,4096]{2,1,0:T(8,128)(2,1)S(1)} collective-permute-done((bf16[4,16,4096]{2,1,0:T(8,128)(2,1)S(1)}, bf16[4,16,4096]{2,1,0:T(8,128)(2,1)S(1)}, u32[]{:S(2)}, u32[]{:S(2)}) %collective-permute-start.11) | collective-permute-done | bytes 524320 | tf_op jit(solution)/shard_map/ppermute | solution.py:36
  117.1 4.0 %shard_map.89 = (f32[256,384]{1,0:T(8,128)S(1)}, bf16[256,384]{1,0:T(8,128)(2,1)S(1)}) custom-call(s32[3]{0:T(128)S(1)} %pad_add_fusion.where, bf16[4,16,4096]{2,1,0:T(8,128)(2,1)S(1)} %shard_map.88.refs_0_, bf16[4,16,4096]{2,1,0:T(8,128)(2,1)S(1)} %collective-permute-done.11.refs_1_, bf16[4,16,4096]{2,1,0:T(8,128)(2,1)S(1)} %collective-permute-done.12.refs_2_, ...), custom_call_target="tpu_custom_call" | custom-call | flops 1073741824 | bytes 9437184 | tf_op jit(solution)/shard_map/pallas_call | solution.py:235
  121.2 0.7 copy-done.10
  121.8 0.7 shard_map.91
  122.5 0.6 copy-done.4
  123.2 8.1 %all-to-all-start.1 = ((f32[16,8,256]{2,1,0:T(8,128)}), f32[16,8,256]{2,1,0:T(8,128)S(1)}, u32[]{:S(2)}, u32[]{:S(2)}) async-start(f32[16,8,256]{2,1,0:T(8,128)} %copy-done.4), calls=%async_computation.1 | async-start | bytes 262144 | tf_op jit(solution)/shard_map/all_to_all | solution.py:261
  131.2 2.0 %collective-permute-start.14 = (bf16[256,384]{1,0:T(8,128)(2,1)}, bf16[256,384]{1,0:T(8,128)(2,1)}, u32[]{:S(2)}, u32[]{:S(2)}) collective-permute-start(bf16[256,384]{1,0:T(8,128)(2,1)} %copy-done.10), channel_id=1, source_target_pairs={{0,1},{1,0},{2,3},{3,2},{4,5},{5,4},{6,7},{7,6},{8,9},{9,8},{10,11... | collective-permute-start | bytes 589832 | tf_op jit(solution)/shard_map/ppermute | solution.py:44
  133.3 1.6 %collective-permute-done.14.got2 = bf16[256,384]{1,0:T(8,128)(2,1)} collective-permute-done((bf16[256,384]{1,0:T(8,128)(2,1)}, bf16[256,384]{1,0:T(8,128)(2,1)}, u32[]{:S(2)}, u32[]{:S(2)}) %collective-permute-start.14) | collective-permute-done | bytes 196640 | tf_op jit(solution)/shard_map/ppermute | solution.py:44
  134.9 0.9 copy-done.3
  135.8 3.2 %shard_map.90 = bf16[512,128]{1,0:T(8,128)(2,1)} custom-call(s32[3]{0:T(128)S(1)} %pad_add_fusion.where, f32[256,384]{1,0:T(8,128)S(1)} %get-tuple-element.6.own1, bf16[256,384]{1,0:T(8,128)(2,1)S(1)} %copy-done.3, f32[256,384]{1,0:T(8,128)S(1)} %get-tuple-element.8.own2, bf16[256,384]{1,0:T(8,128)(2,1)} %collective-permute-done.14.got2, ...), custom_call_target="tpu_custom_call" | custom-call | flops 268435456 | bytes 2097152 | tf_op jit(solution)/shard_map/pallas_call | solution.py:267
  139.1 4.2 %all-to-all-done.1.got = f32[16,8,256]{2,1,0:T(8,128)S(1)} async-done(((f32[16,8,256]{2,1,0:T(8,128)}), f32[16,8,256]{2,1,0:T(8,128)S(1)}, u32[]{:S(2)}, u32[]{:S(2)}) %all-to-all-start.1) | async-done | bytes 131104 | tf_op jit(solution)/shard_map/all_to_all | solution.py:261
  143.3 0.8 copy-done.6
  144.0 0.8 copy-done.8
  144.8 0.1 shard_map.92
  144.9 0.6 copy.10
  (40 shorter events, 0.5 us)
Async XLA Ops:
  0.6 132.6 %copy-start = (bf16[1,8,512,256]{3,2,1,0:T(8,128)(2,1)S(1)}, bf16[1,8,512,256]{3,2,1,0:T(8,128)(2,1)}, u32[]{:S(2)}) copy-start(bf16[1,8,512,256]{3,2,1,0:T(8,128)(2,1)} %param.11) | copy-start | bytes 6291460
  2.9 26.1 %collective-permute-start.1 = (bf16[8,4096]{1,0:T(8,128)(2,1)S(1)}, bf16[8,4096]{1,0:T(8,128)(2,1)S(1)}, u32[]{:S(2)}, u32[]{:S(2)}) collective-permute-start(bf16[8,4096]{1,0:T(8,128)(2,1)S(1)} %get-tuple-element.12), channel_id=1, source_target_pairs={{0,97},{1,96},{8,105},{9,104},{16,113},{17,112},{24,121},{25,120},... | collective-permute-start | bytes 196616 | tf_op jit(solution)/shard_map/ppermute | solution.py:191
  16.8 12.3 %collective-permute-start = (bf16[8,4096]{1,0:T(8,128)(2,1)S(1)}, bf16[8,4096]{1,0:T(8,128)(2,1)S(1)}, u32[]{:S(2)}, u32[]{:S(2)}) collective-permute-start(bf16[8,4096]{1,0:T(8,128)(2,1)S(1)} %get-tuple-element.13), channel_id=1, source_target_pairs={{0,96},{1,97},{8,104},{9,105},{16,112},{17,113},{24,120},{25,121},... | collective-permute-start | bytes 196616 | tf_op jit(solution)/shard_map/ppermute | solution.py:190
  22.0 6.9 %copy-start.11 = (f32[1,8192]{1,0:T(1,128)S(1)}, f32[1,8192]{1,0:T(1,128)}, u32[]{:S(2)}) copy-start(f32[1,8192]{1,0:T(1,128)} %param.8) | copy-start | bytes 98308
  22.0 30.8 %copy-start.9 = (s32[1,8]{1,0:T(1,128)S(1)}, s32[1,8]{1,0:T(1,128)}, u32[]{:S(2)}) copy-start(s32[1,8]{1,0:T(1,128)} %param.13) | copy-start | bytes 100
  22.1 58.4 %all-to-all-start = ((bf16[8,32,4096]{2,1,0:T(8,128)(2,1)}), bf16[8,32,4096]{2,1,0:T(8,128)(2,1)}, u32[]{:S(2)}, u32[]{:S(2)}) async-start(bf16[8,32,4096]{2,1,0:T(8,128)(2,1)} %bitcast.46), calls=%async_computation | async-start | bytes 4194304 | tf_op jit(solution)/shard_map/all_to_all | solution.py:199
  27.0 37.3 %collective-permute-start.4 = (bf16[8192,128]{1,0:T(8,128)(2,1)}, bf16[8192,128]{1,0:T(8,128)(2,1)}, u32[]{:S(2)}, u32[]{:S(2)}) collective-permute-start(bf16[8192,128]{1,0:T(8,128)(2,1)} %bitcast.41), channel_id=1, source_target_pairs={{0,1},{1,0},{2,3},{3,2},{4,5},{5,4},{6,7},{7,6},{8,9},{9,8},{10,11... | collective-permute-start | bytes 6291464 | tf_op jit(solution)/shard_map/ppermute | solution.py:44
  29.1 21.1 %collective-permute-start.2 = (bf16[16,4096]{1,0:T(8,128)(2,1)S(1)}, bf16[16,4096]{1,0:T(8,128)(2,1)S(1)}, u32[]{:S(2)}, u32[]{:S(2)}) collective-permute-start(bf16[16,4096]{1,0:T(8,128)(2,1)S(1)} %fusion.3), channel_id=1, source_target_pairs={{0,32},{8,40},{16,48},{24,56},{32,0},{40,8},{48,16},{56,24},{1,33}... | collective-permute-start | bytes 393224 | tf_op jit(solution)/shard_map/ppermute | solution.py:40
  50.2 14.2 %collective-permute-start.3 = (bf16[2,16,4096]{2,1,0:T(8,128)(2,1)S(1)}, bf16[2,16,4096]{2,1,0:T(8,128)(2,1)S(1)}, u32[]{:S(2)}, u32[]{:S(2)}) collective-permute-start(bf16[2,16,4096]{2,1,0:T(8,128)(2,1)S(1)} %pad_maximum_fusion.one), channel_id=1, source_target_pairs={{0,8},{8,0},{16,24},{24,16},{32,40},{40,32},{48,56},{56,48},{1,9},... | collective-permute-start | bytes 786440 | tf_op jit(solution)/shard_map/ppermute | solution.py:40
  52.9 25.1 %collective-permute-start.10 = (bf16[2,16,4096]{2,1,0:T(8,128)(2,1)S(1)}, bf16[2,16,4096]{2,1,0:T(8,128)(2,1)}, u32[]{:S(2)}, u32[]{:S(2)}) collective-permute-start(bf16[2,16,4096]{2,1,0:T(8,128)(2,1)S(1)} %pad_maximum_fusion.one), channel_id=1, source_target_pairs={{0,24},{8,16},{16,8},{24,0},{32,56},{40,48},{48,40},{56,32},{1,25}... | collective-permute-start | bytes 786440 | tf_op jit(solution)/shard_map/ppermute | solution.py:40
  54.8 25.7 %collective-permute-start.9 = (bf16[2,16,4096]{2,1,0:T(8,128)(2,1)S(1)}, bf16[2,16,4096]{2,1,0:T(8,128)(2,1)}, u32[]{:S(2)}, u32[]{:S(2)}) collective-permute-start(bf16[2,16,4096]{2,1,0:T(8,128)(2,1)S(1)} %pad_maximum_fusion.one), channel_id=1, source_target_pairs={{0,16},{8,24},{16,0},{24,8},{32,48},{40,56},{48,32},{56,40},{1,17}... | collective-permute-start | bytes 786440 | tf_op jit(solution)/shard_map/ppermute | solution.py:40
  65.0 24.5 %collective-permute-start.7 = (bf16[4,16,4096]{2,1,0:T(8,128)(2,1)S(1)}, bf16[4,16,4096]{2,1,0:T(8,128)(2,1)}, u32[]{:S(2)}, u32[]{:S(2)}) collective-permute-start(bf16[4,16,4096]{2,1,0:T(8,128)(2,1)S(1)} %shard_map.86.refs_0_), channel_id=1, source_target_pairs={{6,0},{0,2},{2,4},{4,6},{7,1},{1,3},{3,5},{5,7},{14,8},{8,10},{10,... | collective-permute-start | bytes 1572872 | tf_op jit(solution)/shard_map/ppermute | solution.py:36
  68.2 24.3 %collective-permute-start.6 = (bf16[4,16,4096]{2,1,0:T(8,128)(2,1)S(1)}, bf16[4,16,4096]{2,1,0:T(8,128)(2,1)}, u32[]{:S(2)}, u32[]{:S(2)}) collective-permute-start(bf16[4,16,4096]{2,1,0:T(8,128)(2,1)S(1)} %shard_map.86.refs_0_), channel_id=1, source_target_pairs={{4,0},{6,2},{0,4},{2,6},{5,1},{7,3},{1,5},{3,7},{12,8},{14,10},{8,... | collective-permute-start | bytes 1572872 | tf_op jit(solution)/shard_map/ppermute | solution.py:36
  72.7 24.1 %collective-permute-start.5 = (bf16[4,16,4096]{2,1,0:T(8,128)(2,1)S(1)}, bf16[4,16,4096]{2,1,0:T(8,128)(2,1)}, u32[]{:S(2)}, u32[]{:S(2)}) collective-permute-start(bf16[4,16,4096]{2,1,0:T(8,128)(2,1)S(1)} %shard_map.86.refs_0_), channel_id=1, source_target_pairs={{2,0},{4,2},{6,4},{0,6},{3,1},{5,3},{7,5},{1,7},{10,8},{12,10},{14... | collective-permute-start | bytes 1572872 | tf_op jit(solution)/shard_map/ppermute | solution.py:36
  77.7 4.0 %copy-start.5 = (f32[8,8,128]{2,1,0:T(8,128)}, f32[8,8,128]{2,1,0:T(8,128)S(1)}, u32[]{:S(2)}) copy-start(f32[8,8,128]{2,1,0:T(8,128)S(1)} %get-tuple-element.22.rest_3_.cosine) | copy-start | bytes 98308
  77.7 4.0 %copy-start.7 = (f32[8,8,128]{2,1,0:T(8,128)}, f32[8,8,128]{2,1,0:T(8,128)S(1)}, u32[]{:S(2)}) copy-start(f32[8,8,128]{2,1,0:T(8,128)S(1)} %get-tuple-element.23.rest_4_.sine) | copy-start | bytes 98308
  80.5 16.3 %copy-start.1 = (bf16[1,8192,128]{2,1,0:T(8,128)(2,1)S(1)}, bf16[1,8192,128]{2,1,0:T(8,128)(2,1)}, u32[]{:S(2)}) copy-start(bf16[1,8192,128]{2,1,0:T(8,128)(2,1)} %param.9) | copy-start | bytes 6291460
  81.7 26.3 %collective-permute-start.13 = (bf16[4,16,4096]{2,1,0:T(8,128)(2,1)S(1)}, bf16[4,16,4096]{2,1,0:T(8,128)(2,1)S(1)}, u32[]{:S(2)}, u32[]{:S(2)}) collective-permute-start(bf16[4,16,4096]{2,1,0:T(8,128)(2,1)S(1)} %shard_map.88.refs_0_), channel_id=1, source_target_pairs={{6,0},{0,2},{2,4},{4,6},{7,1},{1,3},{3,5},{5,7},{14,8},{8,10},{10,... | collective-permute-start | bytes 1572872 | tf_op jit(solution)/shard_map/ppermute | solution.py:36
  84.9 29.5 %collective-permute-start.12 = (bf16[4,16,4096]{2,1,0:T(8,128)(2,1)S(1)}, bf16[4,16,4096]{2,1,0:T(8,128)(2,1)S(1)}, u32[]{:S(2)}, u32[]{:S(2)}) collective-permute-start(bf16[4,16,4096]{2,1,0:T(8,128)(2,1)S(1)} %shard_map.88.refs_0_), channel_id=1, source_target_pairs={{4,0},{6,2},{0,4},{2,6},{5,1},{7,3},{1,5},{3,7},{12,8},{14,10},{8,... | collective-permute-start | bytes 1572872 | tf_op jit(solution)/shard_map/ppermute | solution.py:36
  89.5 27.7 %collective-permute-start.11 = (bf16[4,16,4096]{2,1,0:T(8,128)(2,1)S(1)}, bf16[4,16,4096]{2,1,0:T(8,128)(2,1)S(1)}, u32[]{:S(2)}, u32[]{:S(2)}) collective-permute-start(bf16[4,16,4096]{2,1,0:T(8,128)(2,1)S(1)} %shard_map.88.refs_0_), channel_id=1, source_target_pairs={{2,0},{4,2},{6,4},{0,6},{3,1},{5,3},{7,5},{1,7},{10,8},{12,10},{14... | collective-permute-start | bytes 1572872 | tf_op jit(solution)/shard_map/ppermute | solution.py:36
  101.2 16.0 %collective-permute-start.8 = (bf16[256,384]{1,0:T(8,128)(2,1)S(1)}, bf16[256,384]{1,0:T(8,128)(2,1)S(1)}, u32[]{:S(2)}, u32[]{:S(2)}) collective-permute-start(bf16[256,384]{1,0:T(8,128)(2,1)S(1)} %get-tuple-element.7), channel_id=1, source_target_pairs={{0,1},{1,0},{2,3},{3,2},{4,5},{5,4},{6,7},{7,6},{8,9},{9,8},{10,11... | collective-permute-start | bytes 589832 | tf_op jit(solution)/shard_map/ppermute | solution.py:44
  117.1 4.0 %copy-start.2 = (bf16[256,384]{1,0:T(8,128)(2,1)}, bf16[256,384]{1,0:T(8,128)(2,1)S(1)}, u32[]{:S(2)}) copy-start(bf16[256,384]{1,0:T(8,128)(2,1)S(1)} %collective-permute-done.8.refs_7_.got1) | copy-start | bytes 589828
  121.1 0.7 copy-start.10
  122.5 0.7 copy-start.4
  123.2 20.1 %all-to-all-start.1 = ((f32[16,8,256]{2,1,0:T(8,128)}), f32[16,8,256]{2,1,0:T(8,128)S(1)}, u32[]{:S(2)}, u32[]{:S(2)}) async-start(f32[16,8,256]{2,1,0:T(8,128)} %copy-done.4), calls=%async_computation.1 | async-start | bytes 262144 | tf_op jit(solution)/shard_map/all_to_all | solution.py:261
  131.2 3.7 %collective-permute-start.14 = (bf16[256,384]{1,0:T(8,128)(2,1)}, bf16[256,384]{1,0:T(8,128)(2,1)}, u32[]{:S(2)}, u32[]{:S(2)}) collective-permute-start(bf16[256,384]{1,0:T(8,128)(2,1)} %copy-done.10), channel_id=1, source_target_pairs={{0,1},{1,0},{2,3},{3,2},{4,5},{5,4},{6,7},{7,6},{8,9},{9,8},{10,11... | collective-permute-start | bytes 589832 | tf_op jit(solution)/shard_map/ppermute | solution.py:44
  134.9 0.9 copy-start.3
  143.3 0.8 copy-start.6
  144.0 0.8 copy-start.8

commit v5 on v4

--- a/solution.py
+++ b/solution.py
@@ -45,36 +45,29 @@
 
 
 def place(slot, z0, y0):
-    batch, k, i = slot >> 4, (slot >> 2) & 3, slot & 3
-    z = z0 ^ (batch << 1) ^ (i >> 1) ^ (4 * (1 - (i & 1)))
+    inner = (slot >= 8) & (slot < 24)
+    k = jnp.where(inner, (slot - 8) >> 2, (slot >> 1) & 3)
+    step = jnp.where(inner, 1 + (slot & 2), jnp.where(slot < 8, 0, 2))
+    z = z0 ^ step ^ (4 * (1 - (slot & 1)))
     return (z << 2) | ((k + y0) & 3)
 
 
 def slot_of(chip, z0, y0):
     far = (chip >> 2) ^ z0
-    i = ((far & 1) << 1) | (1 - (far >> 2))
-    return (((far >> 1) & 1) << 4) | (((chip - y0) & 3) << 2) | i
+    step, part, k = far & 3, 1 - (far >> 2), (chip - y0) & 3
+    outer = jnp.where(step == 0, 0, 24) + 2 * k + part
+    return jnp.where((step & 1) == 1, 8 + 4 * k + (step & 2) + part, outer)
 
 
 def tokens_of(row, z0, y0):
     return place(row >> 4, z0, y0) * ROWS + (row & 15)
 
 
-def project_kernel(where, *refs):
-    *pieces, wq_mine, wq_other, wkv_far, _, own, send, x, wq, wkv, sems = refs
-    count = len(pieces)
-    half = x.shape[-1]
-    rows = pl.ds(pl.multiple_of(where[2] * half, half), half)
-    copies = [
-        pltpu.make_async_copy(wq_mine.at[rows], wq.at[:, :HD], sems.at[count]),
-        pltpu.make_async_copy(wq_other.at[rows], wq.at[:, HD:], sems.at[count + 1]),
-        pltpu.make_async_copy(wkv_far, wkv, sems.at[count + 2]),
+def project(pieces, copies, wq, wkv, own, send, x, sems):
+    copies += [
+        pltpu.make_async_copy(piece, x.at[at : at + piece.shape[0]], sems.at[i])
+        for i, (piece, at) in enumerate(pieces)
     ]
-    at = 0
-    for i, piece in enumerate(pieces):
-        slots = piece.shape[0]
-        copies.append(pltpu.make_async_copy(piece, x.at[at : at + slots], sems.at[i]))
-        at += slots
     for copy in copies:
         copy.start()
     for copy in copies:
@@ -88,10 +81,30 @@
     send[:, :HD] = q[:, HD:].astype(BF)
 
 
+def first_kernel(where, *refs):
+    *pieces, wq_mine, wq_other, wkv_far, own, send, wq, x, wkv, sems = refs
+    half = x.shape[-1]
+    rows = pl.ds(pl.multiple_of(where[2] * half, half), half)
+    copies = [
+        pltpu.make_async_copy(wq_mine.at[rows], wq.at[:, :HD], sems.at[8]),
+        pltpu.make_async_copy(wq_other.at[rows], wq.at[:, HD:], sems.at[9]),
+        pltpu.make_async_copy(wkv_far, wkv, sems.at[10]),
+    ]
+    places = [2 * k for k in range(NY)] + [8 + 4 * k for k in range(NY)]
+    project(list(zip(pieces, places)), copies, wq, wkv, own, send, x, sems)
+
+
+def second_kernel(*refs):
+    pieces, (wq, wkv), (own, send, x, sems) = refs[:NY], refs[NY : NY + 2], refs[-4:]
+    places = [2 * k for k in range(NY)]
+    project(list(zip(pieces, places)), [], wq, wkv, own, send, x, sems)
+
+
 def join_kernel(one, two, *rest):
     batch = rest[-1]
-    batch[:2] = one[...]
-    batch[2:] = two[...]
+    count = one.shape[0]
+    batch[:count] = one[...]
+    batch[count:] = two[...]
 
 
 def turn(v, cosine, sine):
@@ -110,11 +123,13 @@
             blocks[2 * z + c] = held[pl.ds(pl.multiple_of(row, 8), 8), :]
 
 
-def decode_kernel(got, cosine, sine, out):
+def decode_kernel(got, tables, out):
+    heads = []
     for g in range(NZ):
-        raw = (got[2 * g] + got[2 * g + 1]).astype(BF)
-        out[g, :, :HD] = turn(raw[:, :HD].astype(F32), cosine[g], sine[g]).astype(BF)
-        out[g, :, HD:] = raw[:, HD:]
+        raw = (got[2 * g] + got[2 * g + 1]).astype(BF).astype(F32)
+        k = turn(raw[:, :HD], tables[g, :, :HD], tables[g, :, HD:])
+        heads.append(jnp.concatenate([k, raw[:, HD:]], axis=1))
+    out[...] = jnp.stack(heads, axis=1).astype(BF)
 
 
 def attend_kernel(where, own1, got1, own2, got2, cosine, sine, resident, out):
@@ -198,18 +213,22 @@
     kv_halves = jnp.broadcast_to(kv_halves, (NY, 2, 32, half)).reshape(NY * 2, 32, half)
     wkv = lax.all_to_all(kv_halves, ("y", "c"), 0, 0).reshape(256, half)
 
-    pair = jnp.stack([piece, across_z(piece, 4)])
-
     def join(one, two, *after):
         return call(
             join_kernel,
-            shaped(4, ROWS, half),
+            shaped(one.shape[0] + two.shape[0], ROWS, half),
             [VMEM] * 2 + [HBM] * len(after),
             moved=2**20,
             limit=4,
         )(one, two, *after)
 
-    batch1 = join(pair, across_z(pair, 1), wq_other)
+    def everywhere(batch):
+        return [batch] + [along_y(batch, k) for k in (1, 2, 3)]
+
+    piece = piece[None]
+    second = across_z(piece, 4)
+    pair = jnp.concatenate([piece, second])
+    batch1 = join(across_z(pair, 1), across_z(pair, 3), wq_other, wkv)
     late = (batch1[0, 0, 0] > 3e38).astype(jnp.int32)
 
     def tables(tokens):
@@ -221,34 +240,35 @@
     decode_tokens = (blocks * 8)[:, None] + jnp.arange(8, dtype=jnp.int32)
     row_tokens = tokens_of(jnp.arange(TOKENS, dtype=jnp.int32), z0, y0)
     cosine, sine = tables(row_tokens)
-    decode_cosine, decode_sine = tables(decode_tokens)
-
-    made = (wkv, cosine, sine, decode_cosine, decode_sine)
-    batch2 = join(across_z(pair, 2), across_z(pair, 3), *made)
-    batch1, batch2 = (
-        [batch] + [along_y(batch, k) for k in (1, 2, 3)] for batch in (batch1, batch2)
-    )
-
-    def project(pieces, earlier, weight):
-        slots = sum(p.shape[0] for p in pieces)
-        tokens = slots * ROWS
-        return call(
-            project_kernel,
-            (shaped(tokens, 3 * HD, dtype=F32), shaped(tokens, 3 * HD)),
-            [SMEM] + [HBM] * (len(pieces) + 4),
-            scratch=[
-                pltpu.VMEM((slots, ROWS, half), BF),
-                pltpu.VMEM((half, 2 * HD), BF),
-                pltpu.VMEM((2 * HD, half), BF),
-                pltpu.SemaphoreType.DMA((len(pieces) + 3,)),
-            ],
-            flops=2 * tokens * half * 512 * weight,
-            moved=9 * 2**20,
-        )(where, *pieces, query_weight[0], wq_other, wkv, earlier)
-
-    own1, send1 = project(batch1, wkv, 100)
+    decode_tables = jnp.concatenate(tables(decode_tokens), -1)
+
+    pieces1 = everywhere(pair) + everywhere(batch1)
+    pieces2 = everywhere(across_z(pair, 2))
+
+    def projected(rows):
+        return shaped(rows, 3 * HD, dtype=F32), shaped(rows, 3 * HD)
+
+    own1, send1, wq = call(
+        first_kernel,
+        (*projected(384), shaped(half, 2 * HD)),
+        [SMEM] + [HBM] * 11,
+        scratch=[
+            pltpu.VMEM((24, ROWS, half), BF),
+            pltpu.VMEM((2 * HD, half), BF),
+            pltpu.SemaphoreType.DMA((11,)),
+        ],
+        flops=200 * 384 * half * 512,
+        moved=9 * 2**20,
+    )(where, *pieces1, query_weight[0], wq_other, wkv)
     got1 = swap_core(send1)
-    own2, send2 = project(batch2, got1, 1)
+    own2, send2 = call(
+        second_kernel,
+        projected(128),
+        [HBM] * 4 + [VMEM] * 2 + [HBM] * 4,
+        scratch=[pltpu.VMEM((8, ROWS, half), BF), pltpu.SemaphoreType.DMA((4,))],
+        flops=2 * 128 * half * 512,
+        moved=9 * 2**20,
+    )(*pieces2, wq, wkv, got1, cosine, sine, decode_tables)
     got2 = swap_core(send2)
     blocks = call(
         pick_kernel,
@@ -259,10 +279,9 @@
         limit=4,
     )(where, decode_owner[0], own1, own2)
     blocks = lax.all_to_all(blocks, ("z", "c"), 0, 0)
-    decode_kv = call(decode_kernel, shaped(NZ, 8, 2 * HD), [VMEM] * 3, moved=2**18, limit=4)(
-        blocks, decode_cosine, decode_sine
-    )
-    decode_kv = jnp.transpose(decode_kv, (1, 0, 2))[None]
+    decode_kv = call(decode_kernel, shaped(8, NZ, 2 * HD), [VMEM] * 2, moved=2**18, limit=4)(
+        blocks, decode_tables
+    )
     resident = lax.dynamic_index_in_dim(resident_cache[0], z0, 0, keepdims=False)
     attn = call(
         attend_kernel,
@@ -272,7 +291,7 @@
         moved=2**21,
         exps=TOKENS * 1024,
     )(where, own1, got1, own2, got2, cosine, sine, resident)
-    return attn[None], decode_kv
+    return attn[None], decode_kv[None]
 
 
 def solution(mesh):

time: 147 us -> 153 us (1.041)
  starting transfers between devices: 75.6 us -> 82.2 us
  waiting for transfers between devices: 41.6 us -> 37.3 us
  local copies, waits for them, and re-layouts: 8.34 us -> 10.3 us
    ppermute x6 -> x9, waiting for transfers between devices: 16.1 us -> 7.37 us  [along_y(): return lax.ppermute(value, 'y', [((i + k) % NY, i) for i in range(NY)])]
    ppermute x6 -> x9, starting transfers between devices: 21.4 us -> 26.9 us  [along_y(): return lax.ppermute(value, 'y', [((i + k) % NY, i) for i in range(NY)])]
    ppermute x4, waiting for transfers between devices: 19.7 us -> 23.7 us  [across_z(): return lax.ppermute(value, 'z', [(i, i ^ k) for i in range(NZ)])]
    unnamed x25 -> x38, local copies, waits for them, and re-layouts: 4.41 us -> 6.31 us
    pallas_call x5 -> x4, Pallas kernels: 9.68 us -> 10.7 us  [the longest x1 5.11 us: body(): call(first_kernel, (*projected(384), shaped(half, 2 * HD)), [SMEM] + [HBM...]
  transfers between devices with their start and end apart: 17 -> 20, of which waited for: 9 -> 7; matrix products, arithmetic and copies ran while one was open for 4% -> 5% of each run, Pallas kernels for 6% -> 5%
where the time goes in v5:
time: 153 us; the launch traced here: 152 us
  starting transfers between devices  82.2 us (54%)
  waiting for transfers between devices  37.3 us (24%)
  Pallas kernels  14.3 us (9%)
  local copies, waits for them, and re-layouts  10.3 us (7%)
  other arithmetic  5.49 us (4%)
  between operations  2.43 us (2%)
    ppermute x9, starting transfers between devices, along_y(): return lax.ppermute(value, 'y', [((i + k) % NY, i) for i in range(NY)])  26.9 us
    ppermute x4, waiting for transfers between devices, across_z(): return lax.ppermute(value, 'z', [(i, i ^ k) for i in range(NZ)])  23.7 us
    ppermute x4, starting transfers between devices, across_z(): return lax.ppermute(value, 'z', [(i, i ^ k) for i in range(NZ)])  17.6 us
    ppermute x1, starting transfers between devices, body(): other = lax.ppermute(crossed, ('s', 'z', 'c'), steps[1])  13.8 us
    all_to_all x1, starting transfers between devices, body(): blocks = lax.all_to_all(blocks, ('z', 'c'), 0, 0)  9.22 us
    ppermute x3, starting transfers between devices, swap_core(): return lax.ppermute(value, 'c', [(0, 1), (1, 0)])  7.97 us
    ppermute x9, waiting for transfers between devices, along_y(): return lax.ppermute(value, 'y', [((i + k) % NY, i) for i in range(NY)])  7.37 us
    unnamed x38, local copies, waits for them, and re-layouts  6.31 us
  transfers between devices with their start and end apart: 20, of which 7 were waited for; matrix products, arithmetic and copies ran while one was open for 5% of the time, Pallas kernels for 5%

profile of v5, /device:TPU:1, one launch (start us, length us, event | category | flops | bytes accessed | tf_op | source)
XLA Modules:
  0.0 152.0 jit_solution(4715262132146155847)
XLA Ops:
  0.7 1.2 fusion
  1.9 1.0 fusion.1
  2.9 13.8 %collective-permute-start.1 = (bf16[8,4096]{1,0:T(8,128)(2,1)S(1)}, bf16[8,4096]{1,0:T(8,128)(2,1)S(1)}, u32[]{:S(2)}, u32[]{:S(2)}) collective-permute-start(bf16[8,4096]{1,0:T(8,128)(2,1)S(1)} %get-tuple-element.13), channel_id=1, source_target_pairs={{0,97},{1,96},{8,105},{9,104},{16,113},{17,112},{24,121},{25,120},... | collective-permute-start | bytes 196616 | tf_op jit(solution)/shard_map/ppermute | solution.py:206
  16.8 1.9 %collective-permute-start = (bf16[8,4096]{1,0:T(8,128)(2,1)S(1)}, bf16[8,4096]{1,0:T(8,128)(2,1)S(1)}, u32[]{:S(2)}, u32[]{:S(2)}) collective-permute-start(bf16[8,4096]{1,0:T(8,128)(2,1)S(1)} %get-tuple-element.12), channel_id=1, source_target_pairs={{0,96},{1,97},{8,104},{9,105},{16,112},{17,113},{24,120},{25,121},... | collective-permute-start | bytes 196616 | tf_op jit(solution)/shard_map/ppermute | solution.py:205
  18.7 2.3 %collective-permute-start.8 = (bf16[8192,128]{1,0:T(8,128)(2,1)}, bf16[8192,128]{1,0:T(8,128)(2,1)}, u32[]{:S(2)}, u32[]{:S(2)}) collective-permute-start(bf16[8192,128]{1,0:T(8,128)(2,1)} %bitcast.32), channel_id=1, source_target_pairs={{0,1},{1,0},{2,3},{3,2},{4,5},{5,4},{6,7},{7,6},{8,9},{9,8},{10,11... | collective-permute-start | bytes 6291464 | tf_op jit(solution)/shard_map/ppermute | solution.py:44
  21.0 1.4 reshape.189
  22.4 0.3 copy.9
  22.7 1.6 %broadcast_in_dim.12 = bf16[4,2,32,4096]{3,2,1,0:T(8,128)(2,1)} broadcast(bf16[2,32,4096]{2,1,0:T(8,128)(2,1)S(1)} %copy.9), dimensions={1,2,3} | broadcast | bytes 2621440 | tf_op jit(solution)/shard_map/broadcast_in_dim | solution.py:213
  24.4 4.7 %all-to-all-start = ((bf16[8,32,4096]{2,1,0:T(8,128)(2,1)}), bf16[8,32,4096]{2,1,0:T(8,128)(2,1)}, u32[]{:S(2)}, u32[]{:S(2)}) async-start(bf16[8,32,4096]{2,1,0:T(8,128)(2,1)} %bitcast.34), calls=%async_computation | async-start | bytes 4194304 | tf_op jit(solution)/shard_map/all_to_all | solution.py:214
  29.2 8.7 %collective-permute-start.2 = (bf16[1,16,4096]{2,1,0:T(8,128)(2,1)S(1)}, bf16[1,16,4096]{2,1,0:T(8,128)(2,1)S(1)}, u32[]{:S(2)}, u32[]{:S(2)}) collective-permute-start(bf16[1,16,4096]{2,1,0:T(8,128)(2,1)S(1)} %fusion.2), channel_id=1, source_target_pairs={{0,32},{8,40},{16,48},{24,56},{32,0},{40,8},{48,16},{56,24},{1,33}... | collective-permute-start | bytes 393224 | tf_op jit(solution)/shard_map/ppermute | solution.py:40
  38.0 12.2 %collective-permute-done.2 = bf16[1,16,4096]{2,1,0:T(8,128)(2,1)S(1)} collective-permute-done((bf16[1,16,4096]{2,1,0:T(8,128)(2,1)S(1)}, bf16[1,16,4096]{2,1,0:T(8,128)(2,1)S(1)}, u32[]{:S(2)}, u32[]{:S(2)}) %collective-permute-start.2) | collective-permute-done | bytes 131104 | tf_op jit(solution)/shard_map/ppermute | solution.py:40
  50.2 1.9 %collective-permute-start.6 = (bf16[2,16,4096]{2,1,0:T(8,128)(2,1)S(1)}, bf16[2,16,4096]{2,1,0:T(8,128)(2,1)S(1)}, u32[]{:S(2)}, u32[]{:S(2)}) collective-permute-start(bf16[2,16,4096]{2,1,0:T(8,128)(2,1)S(1)} %pad_maximum_fusion.refs_0_), channel_id=1, source_target_pairs={{0,8},{8,0},{16,24},{24,16},{32,40},{40,32},{48,56},{56,48},{1,9},... | collective-permute-start | bytes 786440 | tf_op jit(solution)/shard_map/ppermute | solution.py:40
  52.1 1.9 %collective-permute-start.7 = (bf16[2,16,4096]{2,1,0:T(8,128)(2,1)S(1)}, bf16[2,16,4096]{2,1,0:T(8,128)(2,1)S(1)}, u32[]{:S(2)}, u32[]{:S(2)}) collective-permute-start(bf16[2,16,4096]{2,1,0:T(8,128)(2,1)S(1)} %pad_maximum_fusion.refs_0_), channel_id=1, source_target_pairs={{0,24},{8,16},{16,8},{24,0},{32,56},{40,48},{48,40},{56,32},{1,25}... | collective-permute-start | bytes 786440 | tf_op jit(solution)/shard_map/ppermute | solution.py:40
  54.1 4.6 %collective-permute-start.3 = (bf16[2,16,4096]{2,1,0:T(8,128)(2,1)S(1)}, bf16[2,16,4096]{2,1,0:T(8,128)(2,1)}, u32[]{:S(2)}, u32[]{:S(2)}) collective-permute-start(bf16[2,16,4096]{2,1,0:T(8,128)(2,1)S(1)} %pad_maximum_fusion.refs_0_), channel_id=1, source_target_pairs={{2,0},{4,2},{6,4},{0,6},{3,1},{5,3},{7,5},{1,7},{10,8},{12,10},{14... | collective-permute-start | bytes 786440 | tf_op jit(solution)/shard_map/ppermute | solution.py:36
  58.8 2.3 %collective-permute-start.4 = (bf16[2,16,4096]{2,1,0:T(8,128)(2,1)S(1)}, bf16[2,16,4096]{2,1,0:T(8,128)(2,1)}, u32[]{:S(2)}, u32[]{:S(2)}) collective-permute-start(bf16[2,16,4096]{2,1,0:T(8,128)(2,1)S(1)} %pad_maximum_fusion.refs_0_), channel_id=1, source_target_pairs={{4,0},{6,2},{0,4},{2,6},{5,1},{7,3},{1,5},{3,7},{12,8},{14,10},{8,... | collective-permute-start | bytes 786440 | tf_op jit(solution)/shard_map/ppermute | solution.py:36
  61.8 3.5 %collective-permute-done.6.one = bf16[2,16,4096]{2,1,0:T(8,128)(2,1)S(1)} collective-permute-done((bf16[2,16,4096]{2,1,0:T(8,128)(2,1)S(1)}, bf16[2,16,4096]{2,1,0:T(8,128)(2,1)S(1)}, u32[]{:S(2)}, u32[]{:S(2)}) %collective-permute-start.6) | collective-permute-done | bytes 262176 | tf_op jit(solution)/shard_map/ppermute | solution.py:40
  65.3 4.6 %collective-permute-start.9 = (bf16[4,16,4096]{2,1,0:T(8,128)(2,1)S(1)}, bf16[4,16,4096]{2,1,0:T(8,128)(2,1)}, u32[]{:S(2)}, u32[]{:S(2)}) collective-permute-start(bf16[4,16,4096]{2,1,0:T(8,128)(2,1)S(1)} %shard_map.86.refs_4_), channel_id=1, source_target_pairs={{2,0},{4,2},{6,4},{0,6},{3,1},{5,3},{7,5},{1,7},{10,8},{12,10},{14... | collective-permute-start | bytes 1572872 | tf_op jit(solution)/shard_map/ppermute | solution.py:36
  69.9 2.2 %collective-permute-start.10 = (bf16[4,16,4096]{2,1,0:T(8,128)(2,1)S(1)}, bf16[4,16,4096]{2,1,0:T(8,128)(2,1)}, u32[]{:S(2)}, u32[]{:S(2)}) collective-permute-start(bf16[4,16,4096]{2,1,0:T(8,128)(2,1)S(1)} %shard_map.86.refs_4_), channel_id=1, source_target_pairs={{4,0},{6,2},{0,4},{2,6},{5,1},{7,3},{1,5},{3,7},{12,8},{14,10},{8,... | collective-permute-start | bytes 1572872 | tf_op jit(solution)/shard_map/ppermute | solution.py:36
  72.1 2.7 %collective-permute-start.11 = (bf16[4,16,4096]{2,1,0:T(8,128)(2,1)S(1)}, bf16[4,16,4096]{2,1,0:T(8,128)(2,1)}, u32[]{:S(2)}, u32[]{:S(2)}) collective-permute-start(bf16[4,16,4096]{2,1,0:T(8,128)(2,1)S(1)} %shard_map.86.refs_4_), channel_id=1, source_target_pairs={{6,0},{0,2},{2,4},{4,6},{7,1},{1,3},{3,5},{5,7},{14,8},{8,10},{10,... | collective-permute-start | bytes 1572872 | tf_op jit(solution)/shard_map/ppermute | solution.py:36
  74.8 0.6 slice.4
  76.0 0.7 add_convert_fusion
  76.7 3.5 %collective-permute-start.5 = (bf16[2,16,4096]{2,1,0:T(8,128)(2,1)S(1)}, bf16[2,16,4096]{2,1,0:T(8,128)(2,1)S(1)}, u32[]{:S(2)}, u32[]{:S(2)}) collective-permute-start(bf16[2,16,4096]{2,1,0:T(8,128)(2,1)S(1)} %pad_maximum_fusion.refs_0_), channel_id=1, source_target_pairs={{6,0},{0,2},{2,4},{4,6},{7,1},{1,3},{3,5},{5,7},{14,8},{8,10},{10,... | collective-permute-start | bytes 786440 | tf_op jit(solution)/shard_map/ppermute | solution.py:36
  80.2 5.0 %collective-permute-start.13 = (bf16[2,16,4096]{2,1,0:T(8,128)(2,1)S(1)}, bf16[2,16,4096]{2,1,0:T(8,128)(2,1)}, u32[]{:S(2)}, u32[]{:S(2)}) collective-permute-start(bf16[2,16,4096]{2,1,0:T(8,128)(2,1)S(1)} %pad_maximum_fusion.refs_0_), channel_id=1, source_target_pairs={{0,16},{8,24},{16,0},{24,8},{32,48},{40,56},{48,32},{56,40},{1,17}... | collective-permute-start | bytes 786440 | tf_op jit(solution)/shard_map/ppermute | solution.py:40
  85.3 1.9 %fusion.4 = (f32[512,64]{1,0:T(8,128)}, f32[512,64]{1,0:T(8,128)}, f32[512,64]{1,0:T(8,128)}) fusion(f32[64]{0:T(128)S(1)} %compare_select_fusion.1, f32[512]{0:T(512)S(1)} %add_convert_fusion.1), kind=kLoop, calls=%fused_computation.14 | loop fusion | flops 65536 | bytes 395520 | tf_op jit(solution)/shard_map/neg | solution.py:237
  87.2 8.1 %collective-permute-done.13.refs_0_ = bf16[2,16,4096]{2,1,0:T(8,128)(2,1)} collective-permute-done((bf16[2,16,4096]{2,1,0:T(8,128)(2,1)S(1)}, bf16[2,16,4096]{2,1,0:T(8,128)(2,1)}, u32[]{:S(2)}, u32[]{:S(2)}) %collective-permute-start.13) | collective-permute-done | bytes 262176 | tf_op jit(solution)/shard_map/ppermute | solution.py:40
  95.2 3.0 %collective-permute-start.14 = (bf16[2,16,4096]{2,1,0:T(8,128)(2,1)}, bf16[2,16,4096]{2,1,0:T(8,128)(2,1)}, u32[]{:S(2)}, u32[]{:S(2)}) collective-permute-start(bf16[2,16,4096]{2,1,0:T(8,128)(2,1)} %collective-permute-done.13.refs_0_), channel_id=1, source_target_pairs={{2,0},{4,2},{6,4},{0,6},{3,1},{5,3},{7,5},{1,7},{10,8},{12,10},{14... | collective-permute-start | bytes 786440 | tf_op jit(solution)/shard_map/ppermute | solution.py:36
  98.2 5.8 %collective-permute-done.5.refs_3_ = bf16[2,16,4096]{2,1,0:T(8,128)(2,1)S(1)} collective-permute-done((bf16[2,16,4096]{2,1,0:T(8,128)(2,1)S(1)}, bf16[2,16,4096]{2,1,0:T(8,128)(2,1)S(1)}, u32[]{:S(2)}, u32[]{:S(2)}) %collective-permute-start.5) | collective-permute-done | bytes 262176 | tf_op jit(solution)/shard_map/ppermute | solution.py:36
  104.0 2.1 %collective-permute-start.15 = (bf16[2,16,4096]{2,1,0:T(8,128)(2,1)}, bf16[2,16,4096]{2,1,0:T(8,128)(2,1)}, u32[]{:S(2)}, u32[]{:S(2)}) collective-permute-start(bf16[2,16,4096]{2,1,0:T(8,128)(2,1)} %collective-permute-done.13.refs_0_), channel_id=1, source_target_pairs={{4,0},{6,2},{0,4},{2,6},{5,1},{7,3},{1,5},{3,7},{12,8},{14,10},{8,... | collective-permute-start | bytes 786440 | tf_op jit(solution)/shard_map/ppermute | solution.py:36
  106.2 1.9 %collective-permute-start.16 = (bf16[2,16,4096]{2,1,0:T(8,128)(2,1)}, bf16[2,16,4096]{2,1,0:T(8,128)(2,1)}, u32[]{:S(2)}, u32[]{:S(2)}) collective-permute-start(bf16[2,16,4096]{2,1,0:T(8,128)(2,1)} %collective-permute-done.13.refs_0_), channel_id=1, source_target_pairs={{6,0},{0,2},{2,4},{4,6},{7,1},{1,3},{3,5},{5,7},{14,8},{8,10},{10,... | collective-permute-start | bytes 786440 | tf_op jit(solution)/shard_map/ppermute | solution.py:36
  108.1 0.9 copy-done.7
  109.1 1.6 %copy-done.10 = bf16[1,8192,128]{2,1,0:T(8,128)(2,1)S(1)} copy-done((bf16[1,8192,128]{2,1,0:T(8,128)(2,1)S(1)}, bf16[1,8192,128]{2,1,0:T(8,128)(2,1)}, u32[]{:S(2)}) %copy-start.10) | copy-done | bytes 2097176
  110.7 5.1 %shard_map.87 = (f32[384,384]{1,0:T(8,128)S(1)}, bf16[384,384]{1,0:T(8,128)(2,1)S(1)}, bf16[4096,256]{1,0:T(8,128)(2,1)S(1)}) custom-call(s32[3]{0:T(128)S(1)} %pad_add_fusion.where, bf16[2,16,4096]{2,1,0:T(8,128)(2,1)S(1)} %copy-done.7, bf16[2,16,4096]{2,1,0:T(8,128)(2,1)} %collective-permute-done.3.refs_1_, ...), custom_call_target="tpu_custom_call" | custom-call | flops 161061273600 | bytes 9437184 | tf_op jit(solution)/shard_map/pallas_call | solution.py:251
  115.8 3.6 %collective-permute-start.12 = (bf16[384,384]{1,0:T(8,128)(2,1)S(1)}, bf16[384,384]{1,0:T(8,128)(2,1)S(1)}, u32[]{:S(2)}, u32[]{:S(2)}) collective-permute-start(bf16[384,384]{1,0:T(8,128)(2,1)S(1)} %get-tuple-element.8), channel_id=1, source_target_pairs={{0,1},{1,0},{2,3},{3,2},{4,5},{5,4},{6,7},{7,6},{8,9},{9,8},{10,11... | collective-permute-start | bytes 884744 | tf_op jit(solution)/shard_map/ppermute | solution.py:44
  119.8 0.2 pad_maximum_fusion.1
  120.0 1.5 %collective-permute-done.16.refs_3_ = bf16[2,16,4096]{2,1,0:T(8,128)(2,1)} collective-permute-done((bf16[2,16,4096]{2,1,0:T(8,128)(2,1)}, bf16[2,16,4096]{2,1,0:T(8,128)(2,1)}, u32[]{:S(2)}, u32[]{:S(2)}) %collective-permute-start.16) | collective-permute-done | bytes 262176 | tf_op jit(solution)/shard_map/ppermute | solution.py:36
  121.6 3.9 %shard_map.88 = (f32[128,384]{1,0:T(8,128)S(1)}, bf16[128,384]{1,0:T(8,128)(2,1)S(1)}) custom-call(bf16[2,16,4096]{2,1,0:T(8,128)(2,1)} %collective-permute-done.13.refs_0_, bf16[2,16,4096]{2,1,0:T(8,128)(2,1)} %collective-permute-done.14.refs_1_, bf16[2,16,4096]{2,1,0:T(8,128)(2,1)} %collective-permute-done.15.refs_2_, ...), custom_call_target="tpu_custom_call" | custom-call | flops 536870912 | bytes 9437184 | tf_op jit(solution)/shard_map/pallas_call | solution.py:264
  125.5 0.6 copy-done.11
  126.1 0.7 shard_map.90
  126.8 0.7 copy-done.1
  127.5 0.6 copy-done.5
  128.2 9.2 %all-to-all-start.1 = ((f32[16,8,256]{2,1,0:T(8,128)}), f32[16,8,256]{2,1,0:T(8,128)}, u32[]{:S(2)}, u32[]{:S(2)}) async-start(f32[16,8,256]{2,1,0:T(8,128)} %copy-done.5), calls=%async_computation.1 | async-start | bytes 262144 | tf_op jit(solution)/shard_map/all_to_all | solution.py:281
  137.4 2.1 %collective-permute-start.17 = (bf16[128,384]{1,0:T(8,128)(2,1)}, bf16[128,384]{1,0:T(8,128)(2,1)S(1)}, u32[]{:S(2)}, u32[]{:S(2)}) collective-permute-start(bf16[128,384]{1,0:T(8,128)(2,1)} %copy-done.11), channel_id=1, source_target_pairs={{0,1},{1,0},{2,3},{3,2},{4,5},{5,4},{6,7},{7,6},{8,9},{9,8},{10,11... | collective-permute-start | bytes 294920 | tf_op jit(solution)/shard_map/ppermute | solution.py:44
  139.5 1.3 collective-permute-done.17.got2
  140.8 0.9 copy-done.2
  141.7 2.9 %shard_map.89 = bf16[512,128]{1,0:T(8,128)(2,1)} custom-call(s32[3]{0:T(128)S(1)} %pad_add_fusion.where, f32[384,384]{1,0:T(8,128)S(1)} %get-tuple-element.7.own1, bf16[384,384]{1,0:T(8,128)(2,1)S(1)} %collective-permute-done.12.refs_6_.got1, f32[128,384]{1,0:T(8,128)S(1)} %copy-done.2, bf16[128,384]{1,0:T(8,128)(2,1)S(1)} %collective-permute-done.17.got2, ...), custom_call_target="tpu_custom_call" | custom-call | flops 268435456 | bytes 2097152 | tf_op jit(solution)/shard_map/pallas_call | solution.py:286
  144.6 4.9 %all-to-all-done.1.got = f32[16,8,256]{2,1,0:T(8,128)} async-done(((f32[16,8,256]{2,1,0:T(8,128)}), f32[16,8,256]{2,1,0:T(8,128)}, u32[]{:S(2)}, u32[]{:S(2)}) %all-to-all-start.1) | async-done | bytes 131104 | tf_op jit(solution)/shard_map/all_to_all | solution.py:281
  149.5 0.8 copy-done.4
  150.4 1.6 %shard_map.91 = bf16[8,8,256]{2,1,0:T(8,128)(2,1)} custom-call(f32[16,8,256]{2,1,0:T(8,128)} %all-to-all-done.1.got, f32[8,8,256]{2,1,0:T(8,128)S(1)} %copy-done.4), custom_call_target="tpu_custom_call" | custom-call | bytes 262144 | tf_op jit(solution)/shard_map/pallas_call | solution.py:282
  (57 shorter events, 0.7 us)
Async XLA Ops:
  0.6 138.8 %copy-start = (bf16[1,8,512,256]{3,2,1,0:T(8,128)(2,1)S(1)}, bf16[1,8,512,256]{3,2,1,0:T(8,128)(2,1)}, u32[]{:S(2)}) copy-start(bf16[1,8,512,256]{3,2,1,0:T(8,128)(2,1)} %param.11) | copy-start | bytes 6291460
  2.9 26.2 %collective-permute-start.1 = (bf16[8,4096]{1,0:T(8,128)(2,1)S(1)}, bf16[8,4096]{1,0:T(8,128)(2,1)S(1)}, u32[]{:S(2)}, u32[]{:S(2)}) collective-permute-start(bf16[8,4096]{1,0:T(8,128)(2,1)S(1)} %get-tuple-element.13), channel_id=1, source_target_pairs={{0,97},{1,96},{8,105},{9,104},{16,113},{17,112},{24,121},{25,120},... | collective-permute-start | bytes 196616 | tf_op jit(solution)/shard_map/ppermute | solution.py:206
  16.8 12.4 %collective-permute-start = (bf16[8,4096]{1,0:T(8,128)(2,1)S(1)}, bf16[8,4096]{1,0:T(8,128)(2,1)S(1)}, u32[]{:S(2)}, u32[]{:S(2)}) collective-permute-start(bf16[8,4096]{1,0:T(8,128)(2,1)S(1)} %get-tuple-element.12), channel_id=1, source_target_pairs={{0,96},{1,97},{8,104},{9,105},{16,112},{17,113},{24,120},{25,121},... | collective-permute-start | bytes 196616 | tf_op jit(solution)/shard_map/ppermute | solution.py:205
  18.7 46.5 %collective-permute-start.8 = (bf16[8192,128]{1,0:T(8,128)(2,1)}, bf16[8192,128]{1,0:T(8,128)(2,1)}, u32[]{:S(2)}, u32[]{:S(2)}) collective-permute-start(bf16[8192,128]{1,0:T(8,128)(2,1)} %bitcast.32), channel_id=1, source_target_pairs={{0,1},{1,0},{2,3},{3,2},{4,5},{5,4},{6,7},{7,6},{8,9},{9,8},{10,11... | collective-permute-start | bytes 6291464 | tf_op jit(solution)/shard_map/ppermute | solution.py:44
  24.4 4.8 %copy-start.16 = (f32[1,8192]{1,0:T(1,128)S(1)}, f32[1,8192]{1,0:T(1,128)}, u32[]{:S(2)}) copy-start(f32[1,8192]{1,0:T(1,128)} %param.8) | copy-start | bytes 98308
  24.4 29.7 %copy-start.8 = (s32[1,8]{1,0:T(1,128)S(1)}, s32[1,8]{1,0:T(1,128)}, u32[]{:S(2)}) copy-start(s32[1,8]{1,0:T(1,128)} %param.13) | copy-start | bytes 100
  24.4 40.8 %all-to-all-start = ((bf16[8,32,4096]{2,1,0:T(8,128)(2,1)}), bf16[8,32,4096]{2,1,0:T(8,128)(2,1)}, u32[]{:S(2)}, u32[]{:S(2)}) async-start(bf16[8,32,4096]{2,1,0:T(8,128)(2,1)} %bitcast.34), calls=%async_computation | async-start | bytes 4194304 | tf_op jit(solution)/shard_map/all_to_all | solution.py:214
  29.2 21.0 %collective-permute-start.2 = (bf16[1,16,4096]{2,1,0:T(8,128)(2,1)S(1)}, bf16[1,16,4096]{2,1,0:T(8,128)(2,1)S(1)}, u32[]{:S(2)}, u32[]{:S(2)}) collective-permute-start(bf16[1,16,4096]{2,1,0:T(8,128)(2,1)S(1)} %fusion.2), channel_id=1, source_target_pairs={{0,32},{8,40},{16,48},{24,56},{32,0},{40,8},{48,16},{56,24},{1,33}... | collective-permute-start | bytes 393224 | tf_op jit(solution)/shard_map/ppermute | solution.py:40
  50.2 30.0 %copy-start.6 = (bf16[2,16,4096]{2,1,0:T(8,128)(2,1)}, bf16[2,16,4096]{2,1,0:T(8,128)(2,1)S(1)}, u32[]{:S(2)}) copy-start(bf16[2,16,4096]{2,1,0:T(8,128)(2,1)S(1)} %pad_maximum_fusion.refs_0_) | copy-start | bytes 786436
  50.2 15.0 %collective-permute-start.6 = (bf16[2,16,4096]{2,1,0:T(8,128)(2,1)S(1)}, bf16[2,16,4096]{2,1,0:T(8,128)(2,1)S(1)}, u32[]{:S(2)}, u32[]{:S(2)}) collective-permute-start(bf16[2,16,4096]{2,1,0:T(8,128)(2,1)S(1)} %pad_maximum_fusion.refs_0_), channel_id=1, source_target_pairs={{0,8},{8,0},{16,24},{24,16},{32,40},{40,32},{48,56},{56,48},{1,9},... | collective-permute-start | bytes 786440 | tf_op jit(solution)/shard_map/ppermute | solution.py:40
  52.1 13.1 %collective-permute-start.7 = (bf16[2,16,4096]{2,1,0:T(8,128)(2,1)S(1)}, bf16[2,16,4096]{2,1,0:T(8,128)(2,1)S(1)}, u32[]{:S(2)}, u32[]{:S(2)}) collective-permute-start(bf16[2,16,4096]{2,1,0:T(8,128)(2,1)S(1)} %pad_maximum_fusion.refs_0_), channel_id=1, source_target_pairs={{0,24},{8,16},{16,8},{24,0},{32,56},{40,48},{48,40},{56,32},{1,25}... | collective-permute-start | bytes 786440 | tf_op jit(solution)/shard_map/ppermute | solution.py:40
  54.1 31.2 %copy-start.17 = (f32[64]{0:T(128)}, f32[64]{0:T(128)S(1)}, u32[]{:S(2)}) copy-start(f32[64]{0:T(128)S(1)} %compare_select_fusion.1) | copy-start | bytes 772
  54.1 22.6 %collective-permute-start.3 = (bf16[2,16,4096]{2,1,0:T(8,128)(2,1)S(1)}, bf16[2,16,4096]{2,1,0:T(8,128)(2,1)}, u32[]{:S(2)}, u32[]{:S(2)}) collective-permute-start(bf16[2,16,4096]{2,1,0:T(8,128)(2,1)S(1)} %pad_maximum_fusion.refs_0_), channel_id=1, source_target_pairs={{2,0},{4,2},{6,4},{0,6},{3,1},{5,3},{7,5},{1,7},{10,8},{12,10},{14... | collective-permute-start | bytes 786440 | tf_op jit(solution)/shard_map/ppermute | solution.py:36
  58.8 21.4 %collective-permute-start.4 = (bf16[2,16,4096]{2,1,0:T(8,128)(2,1)S(1)}, bf16[2,16,4096]{2,1,0:T(8,128)(2,1)}, u32[]{:S(2)}, u32[]{:S(2)}) collective-permute-start(bf16[2,16,4096]{2,1,0:T(8,128)(2,1)S(1)} %pad_maximum_fusion.refs_0_), channel_id=1, source_target_pairs={{4,0},{6,2},{0,4},{2,6},{5,1},{7,3},{1,5},{3,7},{12,8},{14,10},{8,... | collective-permute-start | bytes 786440 | tf_op jit(solution)/shard_map/ppermute | solution.py:36
  65.3 40.9 %collective-permute-start.9 = (bf16[4,16,4096]{2,1,0:T(8,128)(2,1)S(1)}, bf16[4,16,4096]{2,1,0:T(8,128)(2,1)}, u32[]{:S(2)}, u32[]{:S(2)}) collective-permute-start(bf16[4,16,4096]{2,1,0:T(8,128)(2,1)S(1)} %shard_map.86.refs_4_), channel_id=1, source_target_pairs={{2,0},{4,2},{6,4},{0,6},{3,1},{5,3},{7,5},{1,7},{10,8},{12,10},{14... | collective-permute-start | bytes 1572872 | tf_op jit(solution)/shard_map/ppermute | solution.py:36
  69.9 38.2 %collective-permute-start.10 = (bf16[4,16,4096]{2,1,0:T(8,128)(2,1)S(1)}, bf16[4,16,4096]{2,1,0:T(8,128)(2,1)}, u32[]{:S(2)}, u32[]{:S(2)}) collective-permute-start(bf16[4,16,4096]{2,1,0:T(8,128)(2,1)S(1)} %shard_map.86.refs_4_), channel_id=1, source_target_pairs={{4,0},{6,2},{0,4},{2,6},{5,1},{7,3},{1,5},{3,7},{12,8},{14,10},{8,... | collective-permute-start | bytes 1572872 | tf_op jit(solution)/shard_map/ppermute | solution.py:36
  72.1 36.0 %collective-permute-start.11 = (bf16[4,16,4096]{2,1,0:T(8,128)(2,1)S(1)}, bf16[4,16,4096]{2,1,0:T(8,128)(2,1)}, u32[]{:S(2)}, u32[]{:S(2)}) collective-permute-start(bf16[4,16,4096]{2,1,0:T(8,128)(2,1)S(1)} %shard_map.86.refs_4_), channel_id=1, source_target_pairs={{6,0},{0,2},{2,4},{4,6},{7,1},{1,3},{3,5},{5,7},{14,8},{8,10},{10,... | collective-permute-start | bytes 1572872 | tf_op jit(solution)/shard_map/ppermute | solution.py:36
  76.7 27.3 %collective-permute-start.5 = (bf16[2,16,4096]{2,1,0:T(8,128)(2,1)S(1)}, bf16[2,16,4096]{2,1,0:T(8,128)(2,1)S(1)}, u32[]{:S(2)}, u32[]{:S(2)}) collective-permute-start(bf16[2,16,4096]{2,1,0:T(8,128)(2,1)S(1)} %pad_maximum_fusion.refs_0_), channel_id=1, source_target_pairs={{6,0},{0,2},{2,4},{4,6},{7,1},{1,3},{3,5},{5,7},{14,8},{8,10},{10,... | collective-permute-start | bytes 786440 | tf_op jit(solution)/shard_map/ppermute | solution.py:36
  80.2 15.0 %collective-permute-start.13 = (bf16[2,16,4096]{2,1,0:T(8,128)(2,1)S(1)}, bf16[2,16,4096]{2,1,0:T(8,128)(2,1)}, u32[]{:S(2)}, u32[]{:S(2)}) collective-permute-start(bf16[2,16,4096]{2,1,0:T(8,128)(2,1)S(1)} %pad_maximum_fusion.refs_0_), channel_id=1, source_target_pairs={{0,16},{8,24},{16,0},{24,8},{32,48},{40,56},{48,32},{56,40},{1,17}... | collective-permute-start | bytes 786440 | tf_op jit(solution)/shard_map/ppermute | solution.py:40
  95.2 24.8 %collective-permute-start.14 = (bf16[2,16,4096]{2,1,0:T(8,128)(2,1)}, bf16[2,16,4096]{2,1,0:T(8,128)(2,1)}, u32[]{:S(2)}, u32[]{:S(2)}) collective-permute-start(bf16[2,16,4096]{2,1,0:T(8,128)(2,1)} %collective-permute-done.13.refs_0_), channel_id=1, source_target_pairs={{2,0},{4,2},{6,4},{0,6},{3,1},{5,3},{7,5},{1,7},{10,8},{12,10},{14... | collective-permute-start | bytes 786440 | tf_op jit(solution)/shard_map/ppermute | solution.py:36
  104.0 16.0 %collective-permute-start.15 = (bf16[2,16,4096]{2,1,0:T(8,128)(2,1)}, bf16[2,16,4096]{2,1,0:T(8,128)(2,1)}, u32[]{:S(2)}, u32[]{:S(2)}) collective-permute-start(bf16[2,16,4096]{2,1,0:T(8,128)(2,1)} %collective-permute-done.13.refs_0_), channel_id=1, source_target_pairs={{4,0},{6,2},{0,4},{2,6},{5,1},{7,3},{1,5},{3,7},{12,8},{14,10},{8,... | collective-permute-start | bytes 786440 | tf_op jit(solution)/shard_map/ppermute | solution.py:36
  106.2 15.4 %collective-permute-start.16 = (bf16[2,16,4096]{2,1,0:T(8,128)(2,1)}, bf16[2,16,4096]{2,1,0:T(8,128)(2,1)}, u32[]{:S(2)}, u32[]{:S(2)}) collective-permute-start(bf16[2,16,4096]{2,1,0:T(8,128)(2,1)} %collective-permute-done.13.refs_0_), channel_id=1, source_target_pairs={{6,0},{0,2},{2,4},{4,6},{7,1},{1,3},{3,5},{5,7},{14,8},{8,10},{10,... | collective-permute-start | bytes 786440 | tf_op jit(solution)/shard_map/ppermute | solution.py:36
  108.1 1.0 copy-start.7
  109.1 1.6 %copy-start.10 = (bf16[1,8192,128]{2,1,0:T(8,128)(2,1)S(1)}, bf16[1,8192,128]{2,1,0:T(8,128)(2,1)}, u32[]{:S(2)}) copy-start(bf16[1,8192,128]{2,1,0:T(8,128)(2,1)} %param.9) | copy-start | bytes 6291460
  110.7 8.8 %copy-start.15 = (f32[8,8]{1,0:T(8,128)S(1)}, f32[8,8]{1,0:T(8,128)}, u32[]{:S(2)}) copy-start(f32[8,8]{1,0:T(8,128)} %add_convert_fusion) | copy-start | bytes 772
  110.7 8.8 %copy-start.18 = (f32[64]{0:T(128)S(1)}, f32[64]{0:T(128)}, u32[]{:S(2)}) copy-start(f32[64]{0:T(128)} %copy-done.17) | copy-start | bytes 772
  110.7 9.1 %copy-start.12 = (f32[512,64]{1,0:T(8,128)S(1)}, f32[512,64]{1,0:T(8,128)}, u32[]{:S(2)}) copy-start(f32[512,64]{1,0:T(8,128)} %get-tuple-element.17) | copy-start | bytes 393220
  110.7 9.1 %copy-start.13 = (f32[512,64]{1,0:T(8,128)S(1)}, f32[512,64]{1,0:T(8,128)}, u32[]{:S(2)}) copy-start(f32[512,64]{1,0:T(8,128)} %get-tuple-element.18) | copy-start | bytes 393220
  110.7 9.1 %copy-start.14 = (f32[512,64]{1,0:T(8,128)S(1)}, f32[512,64]{1,0:T(8,128)}, u32[]{:S(2)}) copy-start(f32[512,64]{1,0:T(8,128)} %get-tuple-element.19) | copy-start | bytes 393220
  115.8 5.8 %collective-permute-start.12 = (bf16[384,384]{1,0:T(8,128)(2,1)S(1)}, bf16[384,384]{1,0:T(8,128)(2,1)S(1)}, u32[]{:S(2)}, u32[]{:S(2)}) collective-permute-start(bf16[384,384]{1,0:T(8,128)(2,1)S(1)} %get-tuple-element.8), channel_id=1, source_target_pairs={{0,1},{1,0},{2,3},{3,2},{4,5},{5,4},{6,7},{7,6},{8,9},{9,8},{10,11... | collective-permute-start | bytes 884744 | tf_op jit(solution)/shard_map/ppermute | solution.py:44
  119.7 5.7 %copy-start.3 = (f32[8,8,256]{2,1,0:T(8,128)}, f32[8,8,256]{2,1,0:T(8,128)S(1)}, u32[]{:S(2)}) copy-start(f32[8,8,256]{2,1,0:T(8,128)S(1)} %pad_maximum_fusion.3.refs_9_.tables) | copy-start | bytes 196612
  121.6 4.6 %copy-start.9 = (s32[1,8]{1,0:T(1,128)S(1)}, s32[1,8]{1,0:T(1,128)}, u32[]{:S(2)}) copy-start(s32[1,8]{1,0:T(1,128)} %param.13) | copy-start | bytes 100
  125.5 0.6 copy-start.11
  126.8 0.7 copy-start.1
  127.5 0.7 copy-start.5
  128.2 21.4 %all-to-all-start.1 = ((f32[16,8,256]{2,1,0:T(8,128)}), f32[16,8,256]{2,1,0:T(8,128)}, u32[]{:S(2)}, u32[]{:S(2)}) async-start(f32[16,8,256]{2,1,0:T(8,128)} %copy-done.5), calls=%async_computation.1 | async-start | bytes 262144 | tf_op jit(solution)/shard_map/all_to_all | solution.py:281
  137.4 3.4 %collective-permute-start.17 = (bf16[128,384]{1,0:T(8,128)(2,1)}, bf16[128,384]{1,0:T(8,128)(2,1)S(1)}, u32[]{:S(2)}, u32[]{:S(2)}) collective-permute-start(bf16[128,384]{1,0:T(8,128)(2,1)} %copy-done.11), channel_id=1, source_target_pairs={{0,1},{1,0},{2,3},{3,2},{4,5},{5,4},{6,7},{7,6},{8,9},{9,8},{10,11... | collective-permute-start | bytes 294920 | tf_op jit(solution)/shard_map/ppermute | solution.py:44
  140.8 0.9 copy-start.2
  149.5 0.8 copy-start.4

commit v6 on v4

--- a/solution.py
+++ b/solution.py
@@ -60,21 +60,14 @@
     return place(row >> 4, z0, y0) * ROWS + (row & 15)
 
 
-def project_kernel(where, *refs):
-    *pieces, wq_mine, wq_other, wkv_far, _, own, send, x, wq, wkv, sems = refs
-    count = len(pieces)
-    half = x.shape[-1]
-    rows = pl.ds(pl.multiple_of(where[2] * half, half), half)
-    copies = [
-        pltpu.make_async_copy(wq_mine.at[rows], wq.at[:, :HD], sems.at[count]),
-        pltpu.make_async_copy(wq_other.at[rows], wq.at[:, HD:], sems.at[count + 1]),
-        pltpu.make_async_copy(wkv_far, wkv, sems.at[count + 2]),
+PLACES = (0, 4, 8, 10, 12)
+
+
+def project(pieces, copies, wq, wkv, own, send, x, sems):
+    copies += [
+        pltpu.make_async_copy(piece, x.at[at : at + piece.shape[0]], sems.at[i])
+        for i, (piece, at) in enumerate(zip(pieces, PLACES))
     ]
-    at = 0
-    for i, piece in enumerate(pieces):
-        slots = piece.shape[0]
-        copies.append(pltpu.make_async_copy(piece, x.at[at : at + slots], sems.at[i]))
-        at += slots
     for copy in copies:
         copy.start()
     for copy in copies:
@@ -88,21 +81,25 @@
     send[:, :HD] = q[:, HD:].astype(BF)
 
 
-def join_kernel(one, two, *rest):
-    batch = rest[-1]
-    batch[:2] = one[...]
-    batch[2:] = two[...]
-
-
-def turn(v, cosine, sine):
-    return v * cosine + pltpu.roll(v, HD // 2, 1) * sine
-
-
-def pick_kernel(where, owner, own1, own2, blocks, held):
+def first_kernel(where, *refs):
+    *pieces, wq_mine, wq_other, wkv_far, own, send, wq, wkv, x, sems = refs
+    half = x.shape[-1]
+    rows = pl.ds(pl.multiple_of(where[2] * half, half), half)
+    copies = [
+        pltpu.make_async_copy(wq_mine.at[rows], wq.at[:, :HD], sems.at[5]),
+        pltpu.make_async_copy(wq_other, wq.at[:, HD:], sems.at[6]),
+        pltpu.make_async_copy(wkv_far, wkv, sems.at[7]),
+    ]
+    project(pieces, copies, wq, wkv, own, send, x, sems)
+
+
+def second_kernel(where, owner, *refs):
+    pieces, (wq, wkv, first), (own, send, blocks, x, held, sems) = refs[:5], refs[5:8], refs[8:]
+    project(pieces, [], wq, wkv, own, send, x, sems)
     z0, y0 = where[0], where[1]
-    rows = own1.shape[0]
-    held[:rows] = own1[:, HD:]
-    held[rows:] = own2[:, HD:]
+    rows = own.shape[0]
+    held[:rows] = first[:, HD:]
+    held[rows:] = own[:, HD:]
     for z in range(NZ):
         for c in (0, 1):
             block = (z * 8 + y0 * 2 + c - owner[z0]) & 63
@@ -110,10 +107,34 @@
             blocks[2 * z + c] = held[pl.ds(pl.multiple_of(row, 8), 8), :]
 
 
-def decode_kernel(got, cosine, sine, out):
+def spread_kernel(kv, out, sems):
+    half = out.shape[-1]
+    copies = [
+        pltpu.make_async_copy(kv.at[:, pl.ds((i & 1) * half, half)], out.at[i], sems.at[i])
+        for i in range(NY * 2)
+    ]
+    for copy in copies:
+        copy.start()
+    for copy in copies:
+        copy.wait()
+
+
+def join_kernel(one, two, *rest):
+    batch = rest[-1]
+    batch[:2] = one[...]
+    batch[2:] = two[...]
+
+
+def turn(v, cosine, sine):
+    return v * cosine + pltpu.roll(v, HD // 2, 1) * sine
+
+
+def decode_kernel(got, tables, out):
     for g in range(NZ):
         raw = (got[2 * g] + got[2 * g + 1]).astype(BF)
-        out[g, :, :HD] = turn(raw[:, :HD].astype(F32), cosine[g], sine[g]).astype(BF)
+        out[g, :, :HD] = turn(
+            raw[:, :HD].astype(F32), tables[g, :, :HD], tables[g, :, HD:]
+        ).astype(BF)
         out[g, :, HD:] = raw[:, HD:]
 
 
@@ -150,12 +171,12 @@
 HBM = pl.BlockSpec(memory_space=pltpu.HBM)
 
 
-def call(kernel, shapes, specs, scratch=(), flops=0, moved=0, exps=0, limit=24):
+def call(kernel, shapes, specs, scratch=(), flops=0, moved=0, exps=0, limit=24, out=VMEM):
     return pl.pallas_call(
         kernel,
         out_shape=shapes,
         in_specs=specs,
-        out_specs=jax.tree.map(lambda _: VMEM, shapes),
+        out_specs=jax.tree.map(lambda _: out, shapes),
         scratch_shapes=scratch,
         compiler_params=pltpu.CompilerParams(vmem_limit_bytes=limit * 2**20),
         cost_estimate=pl.CostEstimate(flops=flops, bytes_accessed=moved, transcendentals=exps),
@@ -193,9 +214,12 @@
     gain = lax.dynamic_slice_in_dim(norm_gain[0], c0 * half, half, 0)
     piece = (piece.reshape(ROWS, half).astype(F32) * gain[None]).astype(BF)
 
-    wq_other = swap_core(query_weight[0])
-    kv_halves = jnp.transpose(kv_weight[0].T.reshape(32, 2, half), (1, 0, 2))
-    kv_halves = jnp.broadcast_to(kv_halves, (NY, 2, 32, half)).reshape(NY * 2, 32, half)
+    arrived = (piece[0, 0] > 3e38).astype(jnp.int32)
+    wq_other = swap_core(
+        lax.dynamic_slice_in_dim(query_weight[0], (1 - c0) * half + arrived, half, 0)
+    )
+    kv_halves = call(spread_kernel, shaped(NY * 2, 32, half), [HBM], moved=2**22, limit=4,
+        scratch=[pltpu.SemaphoreType.DMA((NY * 2,))], out=HBM)(kv_weight[0].T)
     wkv = lax.all_to_all(kv_halves, ("y", "c"), 0, 0).reshape(256, half)
 
     pair = jnp.stack([piece, across_z(piece, 4)])
@@ -221,46 +245,38 @@
     decode_tokens = (blocks * 8)[:, None] + jnp.arange(8, dtype=jnp.int32)
     row_tokens = tokens_of(jnp.arange(TOKENS, dtype=jnp.int32), z0, y0)
     cosine, sine = tables(row_tokens)
-    decode_cosine, decode_sine = tables(decode_tokens)
-
-    made = (wkv, cosine, sine, decode_cosine, decode_sine)
-    batch2 = join(across_z(pair, 2), across_z(pair, 3), *made)
-    batch1, batch2 = (
-        [batch] + [along_y(batch, k) for k in (1, 2, 3)] for batch in (batch1, batch2)
-    )
-
-    def project(pieces, earlier, weight):
-        slots = sum(p.shape[0] for p in pieces)
-        tokens = slots * ROWS
-        return call(
-            project_kernel,
-            (shaped(tokens, 3 * HD, dtype=F32), shaped(tokens, 3 * HD)),
-            [SMEM] + [HBM] * (len(pieces) + 4),
-            scratch=[
-                pltpu.VMEM((slots, ROWS, half), BF),
-                pltpu.VMEM((half, 2 * HD), BF),
-                pltpu.VMEM((2 * HD, half), BF),
-                pltpu.SemaphoreType.DMA((len(pieces) + 3,)),
-            ],
-            flops=2 * tokens * half * 512 * weight,
-            moved=9 * 2**20,
-        )(where, *pieces, query_weight[0], wq_other, wkv, earlier)
-
-    own1, send1 = project(batch1, wkv, 100)
+    decode_tables = jnp.concatenate(tables(decode_tokens), -1)
+
+    batch2 = join(across_z(pair, 2), across_z(pair, 3), wkv, cosine, sine, decode_tables)
+
+    def everywhere(batch):
+        after, before = along_y(batch, 1), along_y(batch, 3)
+        return [batch, after, along_y(before[:2], 3), along_y(after[2:], 1), before]
+
+    rows = TOKENS // 2
+    projected = (shaped(rows, 3 * HD, dtype=F32), shaped(rows, 3 * HD))
+    scratch = pltpu.VMEM((rows // ROWS, ROWS, half), BF)
+    own1, send1, *weights = call(
+        first_kernel,
+        (*projected, shaped(half, 2 * HD), shaped(2 * HD, half)),
+        [SMEM] + [HBM] * 8,
+        scratch=[scratch, pltpu.SemaphoreType.DMA((8,))],
+        flops=200 * rows * half * 512,
+        moved=9 * 2**20,
+    )(where, *everywhere(batch1), query_weight[0], wq_other, wkv)
     got1 = swap_core(send1)
-    own2, send2 = project(batch2, got1, 1)
+    own2, send2, blocks = call(
+        second_kernel,
+        (*projected, shaped(NZ * 2, 8, 2 * HD, dtype=F32)),
+        [SMEM, SMEM] + [HBM] * 5 + [VMEM] * 3,
+        scratch=[scratch, pltpu.VMEM((TOKENS, 2 * HD), F32), pltpu.SemaphoreType.DMA((5,))],
+        flops=2 * rows * half * 512,
+        moved=9 * 2**20,
+    )(where, decode_owner[0], *everywhere(batch2), *weights, own1)
     got2 = swap_core(send2)
-    blocks = call(
-        pick_kernel,
-        shaped(NZ * 2, 8, 2 * HD, dtype=F32),
-        [SMEM, SMEM] + [VMEM] * 2,
-        scratch=[pltpu.VMEM((TOKENS, 2 * HD), F32)],
-        moved=2**20,
-        limit=4,
-    )(where, decode_owner[0], own1, own2)
     blocks = lax.all_to_all(blocks, ("z", "c"), 0, 0)
-    decode_kv = call(decode_kernel, shaped(NZ, 8, 2 * HD), [VMEM] * 3, moved=2**18, limit=4)(
-        blocks, decode_cosine, decode_sine
+    decode_kv = call(decode_kernel, shaped(NZ, 8, 2 * HD), [VMEM] * 2, moved=2**18, limit=4)(
+        blocks, decode_tables
     )
     decode_kv = jnp.transpose(decode_kv, (1, 0, 2))[None]
     resident = lax.dynamic_index_in_dim(resident_cache[0], z0, 0, keepdims=False)

time: 147 us -> 135 us (0.918)
  waiting for transfers between devices: 41.6 us -> 16.5 us
  starting transfers between devices: 75.6 us -> 84.3 us
  local copies, waits for them, and re-layouts: 8.34 us -> 11.8 us
    ppermute x6 -> x8, waiting for transfers between devices: 16.1 us -> 3.02 us  [along_y(): return lax.ppermute(value, 'y', [((i + k) % NY, i) for i in range(NY)])]
    ppermute x4, waiting for transfers between devices: 19.7 us -> 7.9 us  [across_z(): return lax.ppermute(value, 'z', [(i, i ^ k) for i in range(NZ)])]
    ppermute x1, starting transfers between devices: 13.8 us -> 2.48 us  [body(): other = lax.ppermute(crossed, ('s', 'z', 'c'), steps[1])]
    ppermute x1, starting transfers between devices: 1.92 us -> 13.3 us  [body(): same = lax.ppermute(kept, ('s', 'z', 'c'), steps[0])]
    ppermute x6 -> x8, starting transfers between devices: 21.4 us -> 26.1 us  [along_y(): return lax.ppermute(value, 'y', [((i + k) % NY, i) for i in range(NY)])]
    all_to_all x1, starting transfers between devices: 8.09 us -> 11.6 us  [body(): blocks = lax.all_to_all(blocks, ('z', 'c'), 0, 0)]
    dynamic_slice x0 -> x1, local copies, waits for them, and re-layouts: none -> 2.54 us  [body(): lax.dynamic_slice_in_dim(query_weight[0], (1 - c0) * half + arrived, half...]
    slice x0 -> x5, local copies, waits for them, and re-layouts: none -> 2.49 us  [the longest x4 1.97 us: everywhere(): return [batch, after, along_y(before[:2], 3), along_y(after[2:], 1), before]]
  transfers between devices with their start and end apart: 17 -> 19, of which waited for: 9 -> 8; matrix products, arithmetic and copies ran while one was open for 4% -> 7% of each run, Pallas kernels for 6% -> 8%
where the time goes in v6:
time: 135 us; the launch traced here: 134 us
  starting transfers between devices  84.3 us (62%)
  waiting for transfers between devices  16.5 us (12%)
  Pallas kernels  13.7 us (10%)
  local copies, waits for them, and re-layouts  11.8 us (9%)
  other arithmetic  4.92 us (4%)
  between operations  3.03 us (2%)
    ppermute x8, starting transfers between devices, along_y(): return lax.ppermute(value, 'y', [((i + k) % NY, i) for i in range(NY)])  26.1 us
    ppermute x4, starting transfers between devices, across_z(): return lax.ppermute(value, 'z', [(i, i ^ k) for i in range(NZ)])  18.6 us
    ppermute x1, starting transfers between devices, body(): same = lax.ppermute(kept, ('s', 'z', 'c'), steps[0])  13.3 us
    all_to_all x1, starting transfers between devices, body(): blocks = lax.all_to_all(blocks, ('z', 'c'), 0, 0)  11.6 us
    ppermute x4, waiting for transfers between devices, across_z(): return lax.ppermute(value, 'z', [(i, i ^ k) for i in range(NZ)])  7.9 us
    ppermute x3, starting transfers between devices, swap_core(): return lax.ppermute(value, 'c', [(0, 1), (1, 0)])  7.15 us
    unnamed x25, local copies, waits for them, and re-layouts  5.44 us
    all_to_all x1, starting transfers between devices, body(): wkv = lax.all_to_all(kv_halves, ('y', 'c'), 0, 0).reshape(256, half)  4.99 us
  transfers between devices with their start and end apart: 19, of which 8 were waited for; matrix products, arithmetic and copies ran while one was open for 7% of the time, Pallas kernels for 8%

profile of v6, /device:TPU:1, one launch (start us, length us, event | category | flops | bytes accessed | tf_op | source)
XLA Modules:
  0.0 134.2 jit_solution(4260689642452298993)
XLA Ops:
  0.7 1.2 fusion.4
  1.9 1.0 fusion.5
  2.9 13.3 %collective-permute-start = (bf16[8,4096]{1,0:T(8,128)(2,1)S(1)}, bf16[8,4096]{1,0:T(8,128)(2,1)S(1)}, u32[]{:S(2)}, u32[]{:S(2)}) collective-permute-start(bf16[8,4096]{1,0:T(8,128)(2,1)S(1)} %get-tuple-element.19), channel_id=1, source_target_pairs={{0,96},{1,97},{8,104},{9,105},{16,112},{17,113},{24,120},{25,121},... | collective-permute-start | bytes 196616 | tf_op jit(solution)/shard_map/ppermute | solution.py:211
  16.2 2.5 %collective-permute-start.1 = (bf16[8,4096]{1,0:T(8,128)(2,1)S(1)}, bf16[8,4096]{1,0:T(8,128)(2,1)S(1)}, u32[]{:S(2)}, u32[]{:S(2)}) collective-permute-start(bf16[8,4096]{1,0:T(8,128)(2,1)S(1)} %get-tuple-element.18), channel_id=1, source_target_pairs={{0,97},{1,96},{8,105},{9,104},{16,113},{17,112},{24,121},{25,120},... | collective-permute-start | bytes 196616 | tf_op jit(solution)/shard_map/ppermute | solution.py:212
  18.7 1.0 copy-done.4
  19.7 0.2 shard_map.87
  20.0 1.3 copy-done.1
  21.3 5.0 %all-to-all-start = ((bf16[8,32,4096]{2,1,0:T(8,128)(2,1)}), bf16[8,32,4096]{2,1,0:T(8,128)(2,1)}, u32[]{:S(2)}, u32[]{:S(2)}) async-start(bf16[8,32,4096]{2,1,0:T(8,128)(2,1)} %copy-done.1), calls=%async_computation | async-start | bytes 4194304 | tf_op jit(solution)/shard_map/all_to_all | solution.py:223
  26.3 2.2 %collective-permute-done.1 = bf16[8,4096]{1,0:T(8,128)(2,1)S(1)} collective-permute-done((bf16[8,4096]{1,0:T(8,128)(2,1)S(1)}, bf16[8,4096]{1,0:T(8,128)(2,1)S(1)}, u32[]{:S(2)}, u32[]{:S(2)}) %collective-permute-start.1) | collective-permute-done | bytes 65568 | tf_op jit(solution)/shard_map/ppermute | solution.py:212
  28.6 9.4 %collective-permute-start.2 = (bf16[16,4096]{1,0:T(8,128)(2,1)S(1)}, bf16[16,4096]{1,0:T(8,128)(2,1)}, u32[]{:S(2)}, u32[]{:S(2)}) collective-permute-start(bf16[16,4096]{1,0:T(8,128)(2,1)S(1)} %fusion.3), channel_id=1, source_target_pairs={{0,32},{8,40},{16,48},{24,56},{32,0},{40,8},{48,16},{56,24},{1,33}... | collective-permute-start | bytes 393224 | tf_op jit(solution)/shard_map/ppermute | solution.py:40
  38.0 0.5 slice.24
  39.2 2.5 %dynamic-slice_bitcast_fusion = bf16[4096,128]{1,0:T(8,128)(2,1)} fusion(bf16[1,8192,128]{2,1,0:T(8,128)(2,1)} %param.9, s32[]{:T(128)S(6)} %select_n.65), kind=kLoop, calls=%fused_computation | loop fusion | bytes 2097156 | tf_op jit(solution)/shard_map/dynamic_slice | solution.py:219
  41.7 2.8 %collective-permute-start.4 = (bf16[4096,128]{1,0:T(8,128)(2,1)}, bf16[4096,128]{1,0:T(8,128)(2,1)S(1)}, u32[]{:S(2)}, u32[]{:S(2)}) collective-permute-start(bf16[4096,128]{1,0:T(8,128)(2,1)} %dynamic-slice_bitcast_fusion), channel_id=1, source_target_pairs={{0,1},{1,0},{2,3},{3,2},{4,5},{5,4},{6,7},{7,6},{8,9},{9,8},{10,11... | collective-permute-start | bytes 3145736 | tf_op jit(solution)/shard_map/ppermute | solution.py:44
  44.6 5.7 %collective-permute-done.2 = bf16[16,4096]{1,0:T(8,128)(2,1)} collective-permute-done((bf16[16,4096]{1,0:T(8,128)(2,1)S(1)}, bf16[16,4096]{1,0:T(8,128)(2,1)}, u32[]{:S(2)}, u32[]{:S(2)}) %collective-permute-start.2) | collective-permute-done | bytes 131104 | tf_op jit(solution)/shard_map/ppermute | solution.py:40
  50.3 0.9 pad_maximum_fusion.one
  51.2 1.9 %collective-permute-start.3 = (bf16[2,16,4096]{2,1,0:T(8,128)(2,1)S(1)}, bf16[2,16,4096]{2,1,0:T(8,128)(2,1)}, u32[]{:S(2)}, u32[]{:S(2)}) collective-permute-start(bf16[2,16,4096]{2,1,0:T(8,128)(2,1)S(1)} %pad_maximum_fusion.one), channel_id=1, source_target_pairs={{0,8},{8,0},{16,24},{24,16},{32,40},{40,32},{48,56},{56,48},{1,9},... | collective-permute-start | bytes 786440 | tf_op jit(solution)/shard_map/ppermute | solution.py:40
  53.9 1.9 %collective-permute-start.10 = (bf16[2,16,4096]{2,1,0:T(8,128)(2,1)S(1)}, bf16[2,16,4096]{2,1,0:T(8,128)(2,1)}, u32[]{:S(2)}, u32[]{:S(2)}) collective-permute-start(bf16[2,16,4096]{2,1,0:T(8,128)(2,1)S(1)} %pad_maximum_fusion.one), channel_id=1, source_target_pairs={{0,16},{8,24},{16,0},{24,8},{32,48},{40,56},{48,32},{56,40},{1,17}... | collective-permute-start | bytes 786440 | tf_op jit(solution)/shard_map/ppermute | solution.py:40
  55.8 5.4 %collective-permute-start.11 = (bf16[2,16,4096]{2,1,0:T(8,128)(2,1)S(1)}, bf16[2,16,4096]{2,1,0:T(8,128)(2,1)}, u32[]{:S(2)}, u32[]{:S(2)}) collective-permute-start(bf16[2,16,4096]{2,1,0:T(8,128)(2,1)S(1)} %pad_maximum_fusion.one), channel_id=1, source_target_pairs={{0,24},{8,16},{16,8},{24,0},{32,56},{40,48},{48,40},{56,32},{1,25}... | collective-permute-start | bytes 786440 | tf_op jit(solution)/shard_map/ppermute | solution.py:40
  61.2 0.6 collective-permute-done.3.two
  61.9 1.9 %shard_map.86.refs_0_ = bf16[4,16,4096]{2,1,0:T(8,128)(2,1)} custom-call(bf16[2,16,4096]{2,1,0:T(8,128)(2,1)S(1)} %pad_maximum_fusion.one, bf16[2,16,4096]{2,1,0:T(8,128)(2,1)} %collective-permute-done.3.two, bf16[4096,128]{1,0:T(8,128)(2,1)S(1)} %collective-permute-done.4.rest_0_.refs_6_), custom_call_target="tpu_custom_call" | custom-call | bytes 1048576 | tf_op jit(solution)/shard_map/pallas_call | solution.py:228
  63.8 4.6 %collective-permute-start.5 = (bf16[4,16,4096]{2,1,0:T(8,128)(2,1)}, bf16[4,16,4096]{2,1,0:T(8,128)(2,1)}, u32[]{:S(2)}, u32[]{:S(2)}) collective-permute-start(bf16[4,16,4096]{2,1,0:T(8,128)(2,1)} %shard_map.86.refs_0_), channel_id=1, source_target_pairs={{2,0},{4,2},{6,4},{0,6},{3,1},{5,3},{7,5},{1,7},{10,8},{12,10},{14... | collective-permute-start | bytes 1572872 | tf_op jit(solution)/shard_map/ppermute | solution.py:36
  68.4 1.9 %collective-permute-start.6 = (bf16[4,16,4096]{2,1,0:T(8,128)(2,1)}, bf16[4,16,4096]{2,1,0:T(8,128)(2,1)}, u32[]{:S(2)}, u32[]{:S(2)}) collective-permute-start(bf16[4,16,4096]{2,1,0:T(8,128)(2,1)} %shard_map.86.refs_0_), channel_id=1, source_target_pairs={{6,0},{0,2},{2,4},{4,6},{7,1},{1,3},{3,5},{5,7},{14,8},{8,10},{10,... | collective-permute-start | bytes 1572872 | tf_op jit(solution)/shard_map/ppermute | solution.py:36
  70.4 1.3 slice.27
  72.4 1.0 fusion.6
  73.9 1.6 %collective-permute-done.10.one = bf16[2,16,4096]{2,1,0:T(8,128)(2,1)} collective-permute-done((bf16[2,16,4096]{2,1,0:T(8,128)(2,1)S(1)}, bf16[2,16,4096]{2,1,0:T(8,128)(2,1)}, u32[]{:S(2)}, u32[]{:S(2)}) %collective-permute-start.10) | collective-permute-done | bytes 262176 | tf_op jit(solution)/shard_map/ppermute | solution.py:40
  75.5 1.2 shard_map.89.refs_0_
  76.7 3.2 %collective-permute-start.13 = (bf16[4,16,4096]{2,1,0:T(8,128)(2,1)S(1)}, bf16[4,16,4096]{2,1,0:T(8,128)(2,1)S(1)}, u32[]{:S(2)}, u32[]{:S(2)}) collective-permute-start(bf16[4,16,4096]{2,1,0:T(8,128)(2,1)S(1)} %shard_map.89.refs_0_), channel_id=1, source_target_pairs={{6,0},{0,2},{2,4},{4,6},{7,1},{1,3},{3,5},{5,7},{14,8},{8,10},{10,... | collective-permute-start | bytes 1572872 | tf_op jit(solution)/shard_map/ppermute | solution.py:36
  79.9 3.4 %collective-permute-start.12 = (bf16[4,16,4096]{2,1,0:T(8,128)(2,1)S(1)}, bf16[4,16,4096]{2,1,0:T(8,128)(2,1)S(1)}, u32[]{:S(2)}, u32[]{:S(2)}) collective-permute-start(bf16[4,16,4096]{2,1,0:T(8,128)(2,1)S(1)} %shard_map.89.refs_0_), channel_id=1, source_target_pairs={{2,0},{4,2},{6,4},{0,6},{3,1},{5,3},{7,5},{1,7},{10,8},{12,10},{14... | collective-permute-start | bytes 1572872 | tf_op jit(solution)/shard_map/ppermute | solution.py:36
  83.3 0.4 collective-permute-done.6.refs_4_
  83.7 1.0 slice.25
  84.7 1.9 %collective-permute-start.7 = (bf16[2,16,4096]{2,1,0:T(8,128)(2,1)S(1)}, bf16[2,16,4096]{2,1,0:T(8,128)(2,1)S(1)}, u32[]{:S(2)}, u32[]{:S(2)}) collective-permute-start(bf16[2,16,4096]{2,1,0:T(8,128)(2,1)S(1)} %slice.25), channel_id=1, source_target_pairs={{6,0},{0,2},{2,4},{4,6},{7,1},{1,3},{3,5},{5,7},{14,8},{8,10},{10,... | collective-permute-start | bytes 786440 | tf_op jit(solution)/shard_map/ppermute | solution.py:36
  86.6 1.0 slice.26
  87.6 4.6 %collective-permute-start.8 = (bf16[2,16,4096]{2,1,0:T(8,128)(2,1)S(1)}, bf16[2,16,4096]{2,1,0:T(8,128)(2,1)S(1)}, u32[]{:S(2)}, u32[]{:S(2)}) collective-permute-start(bf16[2,16,4096]{2,1,0:T(8,128)(2,1)S(1)} %slice.26), channel_id=1, source_target_pairs={{2,0},{4,2},{6,4},{0,6},{3,1},{5,3},{7,5},{1,7},{10,8},{12,10},{14... | collective-permute-start | bytes 786440 | tf_op jit(solution)/shard_map/ppermute | solution.py:36
  92.2 2.6 %collective-permute-done.13.refs_4_ = bf16[4,16,4096]{2,1,0:T(8,128)(2,1)S(1)} collective-permute-done((bf16[4,16,4096]{2,1,0:T(8,128)(2,1)S(1)}, bf16[4,16,4096]{2,1,0:T(8,128)(2,1)S(1)}, u32[]{:S(2)}, u32[]{:S(2)}) %collective-permute-start.13) | collective-permute-done | bytes 524320 | tf_op jit(solution)/shard_map/ppermute | solution.py:36
  94.8 1.9 %collective-permute-start.14 = (bf16[2,16,4096]{2,1,0:T(8,128)(2,1)S(1)}, bf16[2,16,4096]{2,1,0:T(8,128)(2,1)S(1)}, u32[]{:S(2)}, u32[]{:S(2)}) collective-permute-start(bf16[2,16,4096]{2,1,0:T(8,128)(2,1)S(1)} %slice.28), channel_id=1, source_target_pairs={{6,0},{0,2},{2,4},{4,6},{7,1},{1,3},{3,5},{5,7},{14,8},{8,10},{10,... | collective-permute-start | bytes 786440 | tf_op jit(solution)/shard_map/ppermute | solution.py:36
  96.8 4.6 %collective-permute-start.15 = (bf16[2,16,4096]{2,1,0:T(8,128)(2,1)S(1)}, bf16[2,16,4096]{2,1,0:T(8,128)(2,1)S(1)}, u32[]{:S(2)}, u32[]{:S(2)}) collective-permute-start(bf16[2,16,4096]{2,1,0:T(8,128)(2,1)S(1)} %slice.29), channel_id=1, source_target_pairs={{2,0},{4,2},{6,4},{0,6},{3,1},{5,3},{7,5},{1,7},{10,8},{12,10},{14... | collective-permute-start | bytes 786440 | tf_op jit(solution)/shard_map/ppermute | solution.py:36
  101.4 4.2 %shard_map.88 = (f32[256,384]{1,0:T(8,128)S(1)}, bf16[256,384]{1,0:T(8,128)(2,1)S(1)}, bf16[4096,256]{1,0:T(8,128)(2,1)S(1)}, bf16[256,4096]{1,0:T(8,128)(2,1)S(1)}) custom-call(s32[3]{0:T(128)S(1)} %pad_add_fusion.where, bf16[4,16,4096]{2,1,0:T(8,128)(2,1)} %shard_map.86.refs_0_, bf16[4,16,4096]{2,1,0:T(8,128)(2,1)} %collective-permute-done.5.refs_1_, ...), custom_call_target="tpu_custom_call" | custom-call | flops 107374182400 | bytes 9437184 | tf_op jit(solution)/shard_map/pallas_call | solution.py:259
  105.7 2.7 %shard_map.90 = (f32[256,384]{1,0:T(8,128)S(1)}, bf16[256,384]{1,0:T(8,128)(2,1)S(1)}, f32[16,8,256]{2,1,0:T(8,128)}) custom-call(s32[3]{0:T(128)S(1)} %pad_add_fusion.where, s32[8]{0:T(128)S(1)} %bitcast.45, bf16[4,16,4096]{2,1,0:T(8,128)(2,1)S(1)} %shard_map.89.refs_0_, bf16[4,16,4096]{2,1,0:T(8,128)(2,1)S(1)} %collective-permute-done.12.refs_1_, ...), custom_call_target="tpu_custom_call" | custom-call | flops 1073741824 | bytes 9437184 | tf_op jit(solution)/shard_map/pallas_call | solution.py:268
  108.4 0.7 copy-done.6
  109.2 0.7 copy-done.10
  109.9 11.6 %all-to-all-start.1 = ((f32[16,8,256]{2,1,0:T(8,128)}), f32[16,8,256]{2,1,0:T(8,128)S(1)}, u32[]{:S(2)}, u32[]{:S(2)}) async-start(f32[16,8,256]{2,1,0:T(8,128)} %get-tuple-element.15), calls=%async_computation.1 | async-start | bytes 262144 | tf_op jit(solution)/shard_map/all_to_all | solution.py:277
  121.5 2.0 %collective-permute-start.9 = (bf16[256,384]{1,0:T(8,128)(2,1)}, bf16[256,384]{1,0:T(8,128)(2,1)S(1)}, u32[]{:S(2)}, u32[]{:S(2)}) collective-permute-start(bf16[256,384]{1,0:T(8,128)(2,1)} %copy-done.9), channel_id=1, source_target_pairs={{0,1},{1,0},{2,3},{3,2},{4,5},{5,4},{6,7},{7,6},{8,9},{9,8},{10,11... | collective-permute-start | bytes 589832 | tf_op jit(solution)/shard_map/ppermute | solution.py:44
  123.5 2.3 %collective-permute-start.16 = (bf16[256,384]{1,0:T(8,128)(2,1)}, bf16[256,384]{1,0:T(8,128)(2,1)}, u32[]{:S(2)}, u32[]{:S(2)}) collective-permute-start(bf16[256,384]{1,0:T(8,128)(2,1)} %copy-done.10), channel_id=1, source_target_pairs={{0,1},{1,0},{2,3},{3,2},{4,5},{5,4},{6,7},{7,6},{8,9},{9,8},{10,11... | collective-permute-start | bytes 589832 | tf_op jit(solution)/shard_map/ppermute | solution.py:44
  125.9 1.3 collective-permute-done.16.got2
  127.2 1.0 copy-done.7
  128.2 3.3 %shard_map.91 = bf16[512,128]{1,0:T(8,128)(2,1)} custom-call(s32[3]{0:T(128)S(1)} %pad_add_fusion.where, f32[256,384]{1,0:T(8,128)S(1)} %get-tuple-element.9.refs_7_.own1, bf16[256,384]{1,0:T(8,128)(2,1)S(1)} %collective-permute-done.9.got1, f32[256,384]{1,0:T(8,128)S(1)} %copy-done.7, bf16[256,384]{1,0:T(8,128)(2,1)} %collective-permute-done.16.got2, ...), custom_call_target="tpu_custom_call" | custom-call | flops 268435456 | bytes 2097152 | tf_op jit(solution)/shard_map/pallas_call | solution.py:283
  131.5 2.0 %all-to-all-done.1.got = f32[16,8,256]{2,1,0:T(8,128)S(1)} async-done(((f32[16,8,256]{2,1,0:T(8,128)}), f32[16,8,256]{2,1,0:T(8,128)S(1)}, u32[]{:S(2)}, u32[]{:S(2)}) %all-to-all-start.1) | async-done | bytes 131104 | tf_op jit(solution)/shard_map/all_to_all | solution.py:277
  133.6 0.6 copy.9
  (47 shorter events, 1.0 us)
Async XLA Ops:
  0.6 125.2 %copy-start = (bf16[1,8,512,256]{3,2,1,0:T(8,128)(2,1)S(1)}, bf16[1,8,512,256]{3,2,1,0:T(8,128)(2,1)}, u32[]{:S(2)}) copy-start(bf16[1,8,512,256]{3,2,1,0:T(8,128)(2,1)} %param.11) | copy-start | bytes 6291460
  2.9 23.4 %collective-permute-start = (bf16[8,4096]{1,0:T(8,128)(2,1)S(1)}, bf16[8,4096]{1,0:T(8,128)(2,1)S(1)}, u32[]{:S(2)}, u32[]{:S(2)}) collective-permute-start(bf16[8,4096]{1,0:T(8,128)(2,1)S(1)} %get-tuple-element.19), channel_id=1, source_target_pairs={{0,96},{1,97},{8,104},{9,105},{16,112},{17,113},{24,120},{25,121},... | collective-permute-start | bytes 196616 | tf_op jit(solution)/shard_map/ppermute | solution.py:211
  16.2 12.4 %collective-permute-start.1 = (bf16[8,4096]{1,0:T(8,128)(2,1)S(1)}, bf16[8,4096]{1,0:T(8,128)(2,1)S(1)}, u32[]{:S(2)}, u32[]{:S(2)}) collective-permute-start(bf16[8,4096]{1,0:T(8,128)(2,1)S(1)} %get-tuple-element.18), channel_id=1, source_target_pairs={{0,97},{1,96},{8,105},{9,104},{16,113},{17,112},{24,121},{25,120},... | collective-permute-start | bytes 196616 | tf_op jit(solution)/shard_map/ppermute | solution.py:212
  18.7 1.0 copy-start.4
  20.0 1.3 copy-start.1
  21.3 5.0 %copy-start.11 = (f32[1,8192]{1,0:T(1,128)S(1)}, f32[1,8192]{1,0:T(1,128)}, u32[]{:S(2)}) copy-start(f32[1,8192]{1,0:T(1,128)} %param.8) | copy-start | bytes 98308
  21.3 54.1 %all-to-all-start = ((bf16[8,32,4096]{2,1,0:T(8,128)(2,1)}), bf16[8,32,4096]{2,1,0:T(8,128)(2,1)}, u32[]{:S(2)}, u32[]{:S(2)}) async-start(bf16[8,32,4096]{2,1,0:T(8,128)(2,1)} %copy-done.1), calls=%async_computation | async-start | bytes 4194304 | tf_op jit(solution)/shard_map/all_to_all | solution.py:223
  26.3 27.5 %copy-start.8 = (s32[1,8]{1,0:T(1,128)S(1)}, s32[1,8]{1,0:T(1,128)}, u32[]{:S(2)}) copy-start(s32[1,8]{1,0:T(1,128)} %param.13) | copy-start | bytes 100
  28.6 21.7 %collective-permute-start.2 = (bf16[16,4096]{1,0:T(8,128)(2,1)S(1)}, bf16[16,4096]{1,0:T(8,128)(2,1)}, u32[]{:S(2)}, u32[]{:S(2)}) collective-permute-start(bf16[16,4096]{1,0:T(8,128)(2,1)S(1)} %fusion.3), channel_id=1, source_target_pairs={{0,32},{8,40},{16,48},{24,56},{32,0},{40,8},{48,16},{56,24},{1,33}... | collective-permute-start | bytes 393224 | tf_op jit(solution)/shard_map/ppermute | solution.py:40
  41.7 20.2 %collective-permute-start.4 = (bf16[4096,128]{1,0:T(8,128)(2,1)}, bf16[4096,128]{1,0:T(8,128)(2,1)S(1)}, u32[]{:S(2)}, u32[]{:S(2)}) collective-permute-start(bf16[4096,128]{1,0:T(8,128)(2,1)} %dynamic-slice_bitcast_fusion), channel_id=1, source_target_pairs={{0,1},{1,0},{2,3},{3,2},{4,5},{5,4},{6,7},{7,6},{8,9},{9,8},{10,11... | collective-permute-start | bytes 3145736 | tf_op jit(solution)/shard_map/ppermute | solution.py:44
  51.2 10.6 %collective-permute-start.3 = (bf16[2,16,4096]{2,1,0:T(8,128)(2,1)S(1)}, bf16[2,16,4096]{2,1,0:T(8,128)(2,1)}, u32[]{:S(2)}, u32[]{:S(2)}) collective-permute-start(bf16[2,16,4096]{2,1,0:T(8,128)(2,1)S(1)} %pad_maximum_fusion.one), channel_id=1, source_target_pairs={{0,8},{8,0},{16,24},{24,16},{32,40},{40,32},{48,56},{56,48},{1,9},... | collective-permute-start | bytes 786440 | tf_op jit(solution)/shard_map/ppermute | solution.py:40
  53.9 21.6 %collective-permute-start.10 = (bf16[2,16,4096]{2,1,0:T(8,128)(2,1)S(1)}, bf16[2,16,4096]{2,1,0:T(8,128)(2,1)}, u32[]{:S(2)}, u32[]{:S(2)}) collective-permute-start(bf16[2,16,4096]{2,1,0:T(8,128)(2,1)S(1)} %pad_maximum_fusion.one), channel_id=1, source_target_pairs={{0,16},{8,24},{16,0},{24,8},{32,48},{40,56},{48,32},{56,40},{1,17}... | collective-permute-start | bytes 786440 | tf_op jit(solution)/shard_map/ppermute | solution.py:40
  55.8 19.7 %collective-permute-start.11 = (bf16[2,16,4096]{2,1,0:T(8,128)(2,1)S(1)}, bf16[2,16,4096]{2,1,0:T(8,128)(2,1)}, u32[]{:S(2)}, u32[]{:S(2)}) collective-permute-start(bf16[2,16,4096]{2,1,0:T(8,128)(2,1)S(1)} %pad_maximum_fusion.one), channel_id=1, source_target_pairs={{0,24},{8,16},{16,8},{24,0},{32,56},{40,48},{48,40},{56,32},{1,25}... | collective-permute-start | bytes 786440 | tf_op jit(solution)/shard_map/ppermute | solution.py:40
  61.9 11.8 %copy-start.2 = (bf16[4096,128]{1,0:T(8,128)(2,1)}, bf16[4096,128]{1,0:T(8,128)(2,1)S(1)}, u32[]{:S(2)}) copy-start(bf16[4096,128]{1,0:T(8,128)(2,1)S(1)} %collective-permute-done.4.rest_0_.refs_6_) | copy-start | bytes 3145732
  63.8 22.8 %collective-permute-start.5 = (bf16[4,16,4096]{2,1,0:T(8,128)(2,1)}, bf16[4,16,4096]{2,1,0:T(8,128)(2,1)}, u32[]{:S(2)}, u32[]{:S(2)}) collective-permute-start(bf16[4,16,4096]{2,1,0:T(8,128)(2,1)} %shard_map.86.refs_0_), channel_id=1, source_target_pairs={{2,0},{4,2},{6,4},{0,6},{3,1},{5,3},{7,5},{1,7},{10,8},{12,10},{14... | collective-permute-start | bytes 1572872 | tf_op jit(solution)/shard_map/ppermute | solution.py:36
  68.4 15.2 %collective-permute-start.6 = (bf16[4,16,4096]{2,1,0:T(8,128)(2,1)}, bf16[4,16,4096]{2,1,0:T(8,128)(2,1)}, u32[]{:S(2)}, u32[]{:S(2)}) collective-permute-start(bf16[4,16,4096]{2,1,0:T(8,128)(2,1)} %shard_map.86.refs_0_), channel_id=1, source_target_pairs={{6,0},{0,2},{2,4},{4,6},{7,1},{1,3},{3,5},{5,7},{14,8},{8,10},{10,... | collective-permute-start | bytes 1572872 | tf_op jit(solution)/shard_map/ppermute | solution.py:36
  75.5 26.0 %copy-start.3 = (bf16[4096,128]{1,0:T(8,128)(2,1)S(1)}, bf16[4096,128]{1,0:T(8,128)(2,1)}, u32[]{:S(2)}) copy-start(bf16[4096,128]{1,0:T(8,128)(2,1)} %copy-done.2) | copy-start | bytes 3145732
  75.5 26.0 %copy-start.5 = (bf16[1,8192,128]{2,1,0:T(8,128)(2,1)S(1)}, bf16[1,8192,128]{2,1,0:T(8,128)(2,1)}, u32[]{:S(2)}) copy-start(bf16[1,8192,128]{2,1,0:T(8,128)(2,1)} %param.9) | copy-start | bytes 6291460
  76.7 18.1 %collective-permute-start.13 = (bf16[4,16,4096]{2,1,0:T(8,128)(2,1)S(1)}, bf16[4,16,4096]{2,1,0:T(8,128)(2,1)S(1)}, u32[]{:S(2)}, u32[]{:S(2)}) collective-permute-start(bf16[4,16,4096]{2,1,0:T(8,128)(2,1)S(1)} %shard_map.89.refs_0_), channel_id=1, source_target_pairs={{6,0},{0,2},{2,4},{4,6},{7,1},{1,3},{3,5},{5,7},{14,8},{8,10},{10,... | collective-permute-start | bytes 1572872 | tf_op jit(solution)/shard_map/ppermute | solution.py:36
  79.9 16.9 %collective-permute-start.12 = (bf16[4,16,4096]{2,1,0:T(8,128)(2,1)S(1)}, bf16[4,16,4096]{2,1,0:T(8,128)(2,1)S(1)}, u32[]{:S(2)}, u32[]{:S(2)}) collective-permute-start(bf16[4,16,4096]{2,1,0:T(8,128)(2,1)S(1)} %shard_map.89.refs_0_), channel_id=1, source_target_pairs={{2,0},{4,2},{6,4},{0,6},{3,1},{5,3},{7,5},{1,7},{10,8},{12,10},{14... | collective-permute-start | bytes 1572872 | tf_op jit(solution)/shard_map/ppermute | solution.py:36
  84.7 16.7 %collective-permute-start.7 = (bf16[2,16,4096]{2,1,0:T(8,128)(2,1)S(1)}, bf16[2,16,4096]{2,1,0:T(8,128)(2,1)S(1)}, u32[]{:S(2)}, u32[]{:S(2)}) collective-permute-start(bf16[2,16,4096]{2,1,0:T(8,128)(2,1)S(1)} %slice.25), channel_id=1, source_target_pairs={{6,0},{0,2},{2,4},{4,6},{7,1},{1,3},{3,5},{5,7},{14,8},{8,10},{10,... | collective-permute-start | bytes 786440 | tf_op jit(solution)/shard_map/ppermute | solution.py:36
  87.6 13.8 %collective-permute-start.8 = (bf16[2,16,4096]{2,1,0:T(8,128)(2,1)S(1)}, bf16[2,16,4096]{2,1,0:T(8,128)(2,1)S(1)}, u32[]{:S(2)}, u32[]{:S(2)}) collective-permute-start(bf16[2,16,4096]{2,1,0:T(8,128)(2,1)S(1)} %slice.26), channel_id=1, source_target_pairs={{2,0},{4,2},{6,4},{0,6},{3,1},{5,3},{7,5},{1,7},{10,8},{12,10},{14... | collective-permute-start | bytes 786440 | tf_op jit(solution)/shard_map/ppermute | solution.py:36
  94.8 10.9 %collective-permute-start.14 = (bf16[2,16,4096]{2,1,0:T(8,128)(2,1)S(1)}, bf16[2,16,4096]{2,1,0:T(8,128)(2,1)S(1)}, u32[]{:S(2)}, u32[]{:S(2)}) collective-permute-start(bf16[2,16,4096]{2,1,0:T(8,128)(2,1)S(1)} %slice.28), channel_id=1, source_target_pairs={{6,0},{0,2},{2,4},{4,6},{7,1},{1,3},{3,5},{5,7},{14,8},{8,10},{10,... | collective-permute-start | bytes 786440 | tf_op jit(solution)/shard_map/ppermute | solution.py:36
  96.8 8.9 %collective-permute-start.15 = (bf16[2,16,4096]{2,1,0:T(8,128)(2,1)S(1)}, bf16[2,16,4096]{2,1,0:T(8,128)(2,1)S(1)}, u32[]{:S(2)}, u32[]{:S(2)}) collective-permute-start(bf16[2,16,4096]{2,1,0:T(8,128)(2,1)S(1)} %slice.29), channel_id=1, source_target_pairs={{2,0},{4,2},{6,4},{0,6},{3,1},{5,3},{7,5},{1,7},{10,8},{12,10},{14... | collective-permute-start | bytes 786440 | tf_op jit(solution)/shard_map/ppermute | solution.py:36
  105.7 2.7 %copy-start.9 = (bf16[256,384]{1,0:T(8,128)(2,1)}, bf16[256,384]{1,0:T(8,128)(2,1)S(1)}, u32[]{:S(2)}) copy-start(bf16[256,384]{1,0:T(8,128)(2,1)S(1)} %get-tuple-element.10) | copy-start | bytes 589828
  108.4 0.7 copy-start.6
  109.2 0.7 copy-start.10
  109.9 23.6 %all-to-all-start.1 = ((f32[16,8,256]{2,1,0:T(8,128)}), f32[16,8,256]{2,1,0:T(8,128)S(1)}, u32[]{:S(2)}, u32[]{:S(2)}) async-start(f32[16,8,256]{2,1,0:T(8,128)} %get-tuple-element.15), calls=%async_computation.1 | async-start | bytes 262144 | tf_op jit(solution)/shard_map/all_to_all | solution.py:277
  121.5 4.4 %collective-permute-start.9 = (bf16[256,384]{1,0:T(8,128)(2,1)}, bf16[256,384]{1,0:T(8,128)(2,1)S(1)}, u32[]{:S(2)}, u32[]{:S(2)}) collective-permute-start(bf16[256,384]{1,0:T(8,128)(2,1)} %copy-done.9), channel_id=1, source_target_pairs={{0,1},{1,0},{2,3},{3,2},{4,5},{5,4},{6,7},{7,6},{8,9},{9,8},{10,11... | collective-permute-start | bytes 589832 | tf_op jit(solution)/shard_map/ppermute | solution.py:44
  123.5 3.7 %collective-permute-start.16 = (bf16[256,384]{1,0:T(8,128)(2,1)}, bf16[256,384]{1,0:T(8,128)(2,1)}, u32[]{:S(2)}, u32[]{:S(2)}) collective-permute-start(bf16[256,384]{1,0:T(8,128)(2,1)} %copy-done.10), channel_id=1, source_target_pairs={{0,1},{1,0},{2,3},{3,2},{4,5},{5,4},{6,7},{7,6},{8,9},{9,8},{10,11... | collective-permute-start | bytes 589832 | tf_op jit(solution)/shard_map/ppermute | solution.py:44
  127.2 1.0 copy-start.7

commit v7 on v6

--- a/solution.py
+++ b/solution.py
@@ -63,19 +63,21 @@
 PLACES = (0, 4, 8, 10, 12)
 
 
-def project(pieces, copies, wq, wkv, own, send, x, sems):
-    copies += [
+def project(pieces, early, late, wq, wkv, own, send, x, sems):
+    early += [
         pltpu.make_async_copy(piece, x.at[at : at + piece.shape[0]], sems.at[i])
         for i, (piece, at) in enumerate(zip(pieces, PLACES))
     ]
-    for copy in copies:
+    for copy in early + late:
         copy.start()
-    for copy in copies:
+    for copy in early:
         copy.wait()
     rows = x[...].reshape(-1, x.shape[-1])
     kv = lax.dot_general(rows, wkv[...], (((1,), (1,)), ((), ())), preferred_element_type=F32)
     own[:, HD:] = kv
     send[:, HD:] = kv.astype(BF)
+    for copy in late:
+        copy.wait()
     q = jnp.dot(rows, wq[...], preferred_element_type=F32)
     own[:, :HD] = q[:, :HD]
     send[:, :HD] = q[:, HD:].astype(BF)
@@ -85,20 +87,21 @@
     *pieces, wq_mine, wq_other, wkv_far, own, send, wq, wkv, x, sems = refs
     half = x.shape[-1]
     rows = pl.ds(pl.multiple_of(where[2] * half, half), half)
-    copies = [
+    early = [pltpu.make_async_copy(wkv_far, wkv, sems.at[7])]
+    late = [
         pltpu.make_async_copy(wq_mine.at[rows], wq.at[:, :HD], sems.at[5]),
         pltpu.make_async_copy(wq_other, wq.at[:, HD:], sems.at[6]),
-        pltpu.make_async_copy(wkv_far, wkv, sems.at[7]),
     ]
-    project(pieces, copies, wq, wkv, own, send, x, sems)
+    project(pieces, early, late, wq, wkv, own, send, x, sems)
 
 
 def second_kernel(where, owner, *refs):
-    pieces, (wq, wkv, first), (own, send, blocks, x, held, sems) = refs[:5], refs[5:8], refs[8:]
-    project(pieces, [], wq, wkv, own, send, x, sems)
+    pieces, (wq, wkv, own1, send1), (own, send, blocks, x, held, sems) = refs[:5], refs[5:9], refs[9:]
+    rows = own.shape[0]
+    send[:rows] = send1[...]
+    project(pieces, [], [], wq, wkv, own, send.at[rows:], x, sems)
     z0, y0 = where[0], where[1]
-    rows = own.shape[0]
-    held[:rows] = first[:, HD:]
+    held[:rows] = own1[:, HD:]
     held[rows:] = own[:, HD:]
     for z in range(NZ):
         for c in (0, 1):
@@ -120,9 +123,10 @@
 
 
 def join_kernel(one, two, *rest):
-    batch = rest[-1]
+    batch, zero = rest[-2:]
     batch[:2] = one[...]
     batch[2:] = two[...]
+    zero[0] = 0
 
 
 def turn(v, cosine, sine):
@@ -138,12 +142,12 @@
         out[g, :, HD:] = raw[:, HD:]
 
 
-def attend_kernel(where, own1, got1, own2, got2, cosine, sine, resident, out):
+def attend_kernel(where, own1, own2, got, cosine, sine, resident, out):
     z0, y0 = where[0], where[1]
-    halves = ((own1, got1), (own2, got2))
-    raw = jnp.concatenate([o[:, HD:] + g[:, HD:].astype(F32) for o, g in halves]).astype(BF)
+    own = jnp.concatenate([own1[...], own2[...]])
+    raw = (own[:, HD:] + got[:, HD:].astype(F32)).astype(BF)
     keys = turn(raw[:, :HD].astype(F32), cosine[...], sine[...]).astype(BF)
-    q = jnp.concatenate([o[:, :HD] + g[:, :HD].astype(F32) for o, g in halves])
+    q = own[:, :HD] + got[:, :HD].astype(F32)
     q = (turn(q, cosine[...], sine[...]) * HD ** (-0.5)).astype(BF)
     nt = (((1,), (1,)), ((), ()))
     old = lax.dot_general(q, resident[:, :HD], nt, preferred_element_type=F32)
@@ -176,7 +180,7 @@
         kernel,
         out_shape=shapes,
         in_specs=specs,
-        out_specs=jax.tree.map(lambda _: out, shapes),
+        out_specs=jax.tree.map(lambda shape: SMEM if shape.shape == (1,) else out, shapes),
         scratch_shapes=scratch,
         compiler_params=pltpu.CompilerParams(vmem_limit_bytes=limit * 2**20),
         cost_estimate=pl.CostEstimate(flops=flops, bytes_accessed=moved, transcendentals=exps),
@@ -227,17 +231,16 @@
     def join(one, two, *after):
         return call(
             join_kernel,
-            shaped(4, ROWS, half),
+            (shaped(4, ROWS, half), shaped(1, dtype=jnp.int32)),
             [VMEM] * 2 + [HBM] * len(after),
             moved=2**20,
             limit=4,
         )(one, two, *after)
 
-    batch1 = join(pair, across_z(pair, 1), wq_other)
-    late = (batch1[0, 0, 0] > 3e38).astype(jnp.int32)
+    batch1, late = join(pair, across_z(pair, 1), wq_other, wkv)
 
     def tables(tokens):
-        angles = (block_start[0] + late + tokens).astype(F32)[..., None] * frequencies(HD)
+        angles = (block_start[0] + late[0] + tokens).astype(F32)[..., None] * frequencies(HD)
         cosine, sine = jnp.cos(angles), jnp.sin(angles)
         return jnp.concatenate([cosine, cosine], -1), jnp.concatenate([-sine, sine], -1)
 
@@ -247,7 +250,7 @@
     cosine, sine = tables(row_tokens)
     decode_tables = jnp.concatenate(tables(decode_tokens), -1)
 
-    batch2 = join(across_z(pair, 2), across_z(pair, 3), wkv, cosine, sine, decode_tables)
+    batch2, _ = join(across_z(pair, 2), across_z(pair, 3), cosine, sine, decode_tables)
 
     def everywhere(batch):
         after, before = along_y(batch, 1), along_y(batch, 3)
@@ -264,16 +267,15 @@
         flops=200 * rows * half * 512,
         moved=9 * 2**20,
     )(where, *everywhere(batch1), query_weight[0], wq_other, wkv)
-    got1 = swap_core(send1)
-    own2, send2, blocks = call(
+    own2, send, blocks = call(
         second_kernel,
-        (*projected, shaped(NZ * 2, 8, 2 * HD, dtype=F32)),
-        [SMEM, SMEM] + [HBM] * 5 + [VMEM] * 3,
+        (projected[0], shaped(TOKENS, 3 * HD), shaped(NZ * 2, 8, 2 * HD, dtype=F32)),
+        [SMEM, SMEM] + [HBM] * 5 + [VMEM] * 4,
         scratch=[scratch, pltpu.VMEM((TOKENS, 2 * HD), F32), pltpu.SemaphoreType.DMA((5,))],
         flops=2 * rows * half * 512,
         moved=9 * 2**20,
-    )(where, decode_owner[0], *everywhere(batch2), *weights, own1)
-    got2 = swap_core(send2)
+    )(where, decode_owner[0], *everywhere(batch2), *weights, own1, send1)
+    got = swap_core(send)
     blocks = lax.all_to_all(blocks, ("z", "c"), 0, 0)
     decode_kv = call(decode_kernel, shaped(NZ, 8, 2 * HD), [VMEM] * 2, moved=2**18, limit=4)(
         blocks, decode_tables
@@ -283,11 +285,11 @@
     attn = call(
         attend_kernel,
         shaped(TOKENS, HD),
-        [SMEM] + [VMEM] * 7,
+        [SMEM] + [VMEM] * 6,
         flops=4 * TOKENS * 1024 * HD,
         moved=2**21,
         exps=TOKENS * 1024,
-    )(where, own1, got1, own2, got2, cosine, sine, resident)
+    )(where, own1, own2, got, cosine, sine, resident)
     return attn[None], decode_kv
 
 

time: 135 us -> 134 us (level)
  waiting for transfers between devices: 16.5 us -> 22.3 us
  local copies, waits for them, and re-layouts: 11.8 us -> 8.66 us
  Pallas kernels: 13.7 us -> 12.2 us
  starting transfers between devices: 84.3 us -> 82.9 us
    ppermute x4, waiting for transfers between devices: 7.9 us -> 10.4 us  [across_z(): return lax.ppermute(value, 'z', [(i, i ^ k) for i in range(NZ)])]
    ppermute x3 -> x2, starting transfers between devices: 7.15 us -> 4.85 us  [swap_core(): return lax.ppermute(value, 'c', [(0, 1), (1, 0)])]
    pallas_call x4, Pallas kernels: 9.15 us -> 7.18 us  [the longest x1 3.35 us: body(): call(attend_kernel, shaped(TOKENS, HD), [SMEM] + [VMEM] * 6, flops=4 * TO...]
    slice x4, local copies, waits for them, and re-layouts: 1.97 us -> 0.07 us  [everywhere(): return [batch, after, along_y(before[:2], 3), along_y(after[2:], 1), before]]
    all_to_all x1, waiting for transfers between devices: 2.03 us -> 3.73 us  [body(): blocks = lax.all_to_all(blocks, ('z', 'c'), 0, 0)]
    unnamed x25 -> x19, local copies, waits for them, and re-layouts: 5.44 us -> 5.52 us
  transfers between devices with their start and end apart: 19 -> 18, of which waited for: 8 -> 7; matrix products, arithmetic and copies ran while one was open for 7% -> 4% of each run, Pallas kernels for 8% -> 7%
where the time goes in v7:
time: 134 us; the launch traced here: 133 us
  starting transfers between devices  82.9 us (62%)
  waiting for transfers between devices  22.3 us (17%)
  Pallas kernels  12.2 us (9%)
  local copies, waits for them, and re-layouts  8.66 us (6%)
  other arithmetic  4.02 us (3%)
  between operations  2.94 us (2%)
    ppermute x8, starting transfers between devices, along_y(): return lax.ppermute(value, 'y', [((i + k) % NY, i) for i in range(NY)])  26.1 us
    ppermute x4, starting transfers between devices, across_z(): return lax.ppermute(value, 'z', [(i, i ^ k) for i in range(NZ)])  18.6 us
    ppermute x1, starting transfers between devices, body(): same = lax.ppermute(kept, ('s', 'z', 'c'), steps[0])  13.3 us
    all_to_all x1, starting transfers between devices, body(): blocks = lax.all_to_all(blocks, ('z', 'c'), 0, 0)  12.6 us
    ppermute x4, waiting for transfers between devices, across_z(): return lax.ppermute(value, 'z', [(i, i ^ k) for i in range(NZ)])  10.4 us
    unnamed x19, local copies, waits for them, and re-layouts  5.52 us
    all_to_all x1, starting transfers between devices, body(): wkv = lax.all_to_all(kv_halves, ('y', 'c'), 0, 0).reshape(256, half)  4.99 us
    ppermute x2, starting transfers between devices, swap_core(): return lax.ppermute(value, 'c', [(0, 1), (1, 0)])  4.85 us
  transfers between devices with their start and end apart: 18, of which 7 were waited for; matrix products, arithmetic and copies ran while one was open for 4% of the time, Pallas kernels for 7%

profile of v7, /device:TPU:1, one launch (start us, length us, event | category | flops | bytes accessed | tf_op | source)
XLA Modules:
  0.0 133.0 jit_solution(13630130676267154124)
XLA Ops:
  0.7 1.2 fusion.4
  1.9 1.0 fusion.5
  2.9 13.3 %collective-permute-start = (bf16[8,4096]{1,0:T(8,128)(2,1)S(1)}, bf16[8,4096]{1,0:T(8,128)(2,1)S(1)}, u32[]{:S(2)}, u32[]{:S(2)}) collective-permute-start(bf16[8,4096]{1,0:T(8,128)(2,1)S(1)} %get-tuple-element.25), channel_id=1, source_target_pairs={{0,96},{1,97},{8,104},{9,105},{16,112},{17,113},{24,120},{25,121},... | collective-permute-start | bytes 196616 | tf_op jit(solution)/shard_map/ppermute | solution.py:215
  16.2 2.5 %collective-permute-start.1 = (bf16[8,4096]{1,0:T(8,128)(2,1)S(1)}, bf16[8,4096]{1,0:T(8,128)(2,1)S(1)}, u32[]{:S(2)}, u32[]{:S(2)}) collective-permute-start(bf16[8,4096]{1,0:T(8,128)(2,1)S(1)} %get-tuple-element.24), channel_id=1, source_target_pairs={{0,97},{1,96},{8,105},{9,104},{16,113},{17,112},{24,121},{25,120},... | collective-permute-start | bytes 196616 | tf_op jit(solution)/shard_map/ppermute | solution.py:216
  18.7 1.0 copy-done.2
  19.7 0.2 shard_map.86
  20.0 1.3 copy-done.1
  21.3 5.0 %all-to-all-start = ((bf16[8,32,4096]{2,1,0:T(8,128)(2,1)}), bf16[8,32,4096]{2,1,0:T(8,128)(2,1)}, u32[]{:S(2)}, u32[]{:S(2)}) async-start(bf16[8,32,4096]{2,1,0:T(8,128)(2,1)} %copy-done.1), calls=%async_computation | async-start | bytes 4194304 | tf_op jit(solution)/shard_map/all_to_all | solution.py:227
  26.3 2.2 %collective-permute-done.1 = bf16[8,4096]{1,0:T(8,128)(2,1)S(1)} collective-permute-done((bf16[8,4096]{1,0:T(8,128)(2,1)S(1)}, bf16[8,4096]{1,0:T(8,128)(2,1)S(1)}, u32[]{:S(2)}, u32[]{:S(2)}) %collective-permute-start.1) | collective-permute-done | bytes 65568 | tf_op jit(solution)/shard_map/ppermute | solution.py:216
  28.6 9.3 %collective-permute-start.2 = (bf16[16,4096]{1,0:T(8,128)(2,1)S(1)}, bf16[16,4096]{1,0:T(8,128)(2,1)S(1)}, u32[]{:S(2)}, u32[]{:S(2)}) collective-permute-start(bf16[16,4096]{1,0:T(8,128)(2,1)S(1)} %fusion.3), channel_id=1, source_target_pairs={{0,32},{8,40},{16,48},{24,56},{32,0},{40,8},{48,16},{56,24},{1,33}... | collective-permute-start | bytes 393224 | tf_op jit(solution)/shard_map/ppermute | solution.py:40
  38.0 0.5 slice.20
  39.2 2.5 %dynamic-slice_bitcast_fusion = bf16[4096,128]{1,0:T(8,128)(2,1)} fusion(bf16[1,8192,128]{2,1,0:T(8,128)(2,1)} %param.9, s32[]{:T(128)S(6)} %select_n.65), kind=kLoop, calls=%fused_computation | loop fusion | bytes 2097156 | tf_op jit(solution)/shard_map/dynamic_slice | solution.py:223
  41.7 2.8 %collective-permute-start.4 = (bf16[4096,128]{1,0:T(8,128)(2,1)}, bf16[4096,128]{1,0:T(8,128)(2,1)}, u32[]{:S(2)}, u32[]{:S(2)}) collective-permute-start(bf16[4096,128]{1,0:T(8,128)(2,1)} %dynamic-slice_bitcast_fusion), channel_id=1, source_target_pairs={{0,1},{1,0},{2,3},{3,2},{4,5},{5,4},{6,7},{7,6},{8,9},{9,8},{10,11... | collective-permute-start | bytes 3145736 | tf_op jit(solution)/shard_map/ppermute | solution.py:44
  44.6 5.6 %collective-permute-done.2 = bf16[16,4096]{1,0:T(8,128)(2,1)S(1)} collective-permute-done((bf16[16,4096]{1,0:T(8,128)(2,1)S(1)}, bf16[16,4096]{1,0:T(8,128)(2,1)S(1)}, u32[]{:S(2)}, u32[]{:S(2)}) %collective-permute-start.2) | collective-permute-done | bytes 131104 | tf_op jit(solution)/shard_map/ppermute | solution.py:40
  50.2 1.9 %collective-permute-start.3 = (bf16[2,16,4096]{2,1,0:T(8,128)(2,1)S(1)}, bf16[2,16,4096]{2,1,0:T(8,128)(2,1)S(1)}, u32[]{:S(2)}, u32[]{:S(2)}) collective-permute-start(bf16[2,16,4096]{2,1,0:T(8,128)(2,1)S(1)} %pad_maximum_fusion.one), channel_id=1, source_target_pairs={{0,8},{8,0},{16,24},{24,16},{32,40},{40,32},{48,56},{56,48},{1,9},... | collective-permute-start | bytes 786440 | tf_op jit(solution)/shard_map/ppermute | solution.py:40
  52.9 1.9 %collective-permute-start.9 = (bf16[2,16,4096]{2,1,0:T(8,128)(2,1)S(1)}, bf16[2,16,4096]{2,1,0:T(8,128)(2,1)S(1)}, u32[]{:S(2)}, u32[]{:S(2)}) collective-permute-start(bf16[2,16,4096]{2,1,0:T(8,128)(2,1)S(1)} %pad_maximum_fusion.one), channel_id=1, source_target_pairs={{0,16},{8,24},{16,0},{24,8},{32,48},{40,56},{48,32},{56,40},{1,17}... | collective-permute-start | bytes 786440 | tf_op jit(solution)/shard_map/ppermute | solution.py:40
  54.8 5.4 %collective-permute-start.10 = (bf16[2,16,4096]{2,1,0:T(8,128)(2,1)S(1)}, bf16[2,16,4096]{2,1,0:T(8,128)(2,1)S(1)}, u32[]{:S(2)}, u32[]{:S(2)}) collective-permute-start(bf16[2,16,4096]{2,1,0:T(8,128)(2,1)S(1)} %pad_maximum_fusion.one), channel_id=1, source_target_pairs={{0,24},{8,16},{16,8},{24,0},{32,56},{40,48},{48,40},{56,32},{1,25}... | collective-permute-start | bytes 786440 | tf_op jit(solution)/shard_map/ppermute | solution.py:40
  60.2 0.5 collective-permute-done.3.two
  60.7 0.6 shard_map.87
  61.3 4.6 %collective-permute-start.5 = (bf16[4,16,4096]{2,1,0:T(8,128)(2,1)S(1)}, bf16[4,16,4096]{2,1,0:T(8,128)(2,1)S(1)}, u32[]{:S(2)}, u32[]{:S(2)}) collective-permute-start(bf16[4,16,4096]{2,1,0:T(8,128)(2,1)S(1)} %get-tuple-element.12.refs_0_), channel_id=1, source_target_pairs={{2,0},{4,2},{6,4},{0,6},{3,1},{5,3},{7,5},{1,7},{10,8},{12,10},{14... | collective-permute-start | bytes 1572872 | tf_op jit(solution)/shard_map/ppermute | solution.py:36
  66.0 1.9 %collective-permute-start.6 = (bf16[4,16,4096]{2,1,0:T(8,128)(2,1)S(1)}, bf16[4,16,4096]{2,1,0:T(8,128)(2,1)S(1)}, u32[]{:S(2)}, u32[]{:S(2)}) collective-permute-start(bf16[4,16,4096]{2,1,0:T(8,128)(2,1)S(1)} %get-tuple-element.12.refs_0_), channel_id=1, source_target_pairs={{6,0},{0,2},{2,4},{4,6},{7,1},{1,3},{3,5},{5,7},{14,8},{8,10},{10,... | collective-permute-start | bytes 1572872 | tf_op jit(solution)/shard_map/ppermute | solution.py:36
  68.5 0.1 add_convert_fusion
  68.5 1.0 fusion.6
  69.5 0.2 multiply_cosine_fusion.1
  69.7 0.1 pad_maximum_fusion.3.rest_2_.tables
  69.9 0.2 pad_maximum_fusion.1
  70.1 4.3 %collective-permute-done.9.one = bf16[2,16,4096]{2,1,0:T(8,128)(2,1)S(1)} collective-permute-done((bf16[2,16,4096]{2,1,0:T(8,128)(2,1)S(1)}, bf16[2,16,4096]{2,1,0:T(8,128)(2,1)S(1)}, u32[]{:S(2)}, u32[]{:S(2)}) %collective-permute-start.9) | collective-permute-done | bytes 262176 | tf_op jit(solution)/shard_map/ppermute | solution.py:40
  74.3 0.6 shard_map.89
  74.9 3.2 %collective-permute-start.12 = (bf16[4,16,4096]{2,1,0:T(8,128)(2,1)S(1)}, bf16[4,16,4096]{2,1,0:T(8,128)(2,1)S(1)}, u32[]{:S(2)}, u32[]{:S(2)}) collective-permute-start(bf16[4,16,4096]{2,1,0:T(8,128)(2,1)S(1)} %get-tuple-element.15.refs_0_), channel_id=1, source_target_pairs={{6,0},{0,2},{2,4},{4,6},{7,1},{1,3},{3,5},{5,7},{14,8},{8,10},{10,... | collective-permute-start | bytes 1572872 | tf_op jit(solution)/shard_map/ppermute | solution.py:36
  78.1 3.4 %collective-permute-start.11 = (bf16[4,16,4096]{2,1,0:T(8,128)(2,1)S(1)}, bf16[4,16,4096]{2,1,0:T(8,128)(2,1)S(1)}, u32[]{:S(2)}, u32[]{:S(2)}) collective-permute-start(bf16[4,16,4096]{2,1,0:T(8,128)(2,1)S(1)} %get-tuple-element.15.refs_0_), channel_id=1, source_target_pairs={{2,0},{4,2},{6,4},{0,6},{3,1},{5,3},{7,5},{1,7},{10,8},{12,10},{14... | collective-permute-start | bytes 1572872 | tf_op jit(solution)/shard_map/ppermute | solution.py:36
  81.5 1.9 %collective-permute-start.7 = (bf16[2,16,4096]{2,1,0:T(8,128)(2,1)S(1)}, bf16[2,16,4096]{2,1,0:T(8,128)(2,1)S(1)}, u32[]{:S(2)}, u32[]{:S(2)}) collective-permute-start(bf16[2,16,4096]{2,1,0:T(8,128)(2,1)S(1)} %slice.21), channel_id=1, source_target_pairs={{6,0},{0,2},{2,4},{4,6},{7,1},{1,3},{3,5},{5,7},{14,8},{8,10},{10,... | collective-permute-start | bytes 786440 | tf_op jit(solution)/shard_map/ppermute | solution.py:36
  83.5 4.6 %collective-permute-start.8 = (bf16[2,16,4096]{2,1,0:T(8,128)(2,1)S(1)}, bf16[2,16,4096]{2,1,0:T(8,128)(2,1)S(1)}, u32[]{:S(2)}, u32[]{:S(2)}) collective-permute-start(bf16[2,16,4096]{2,1,0:T(8,128)(2,1)S(1)} %slice.22), channel_id=1, source_target_pairs={{2,0},{4,2},{6,4},{0,6},{3,1},{5,3},{7,5},{1,7},{10,8},{12,10},{14... | collective-permute-start | bytes 786440 | tf_op jit(solution)/shard_map/ppermute | solution.py:36
  88.1 0.1 pad_add_fusion.where
  88.1 4.0 %collective-permute-done.12.refs_4_ = bf16[4,16,4096]{2,1,0:T(8,128)(2,1)S(1)} collective-permute-done((bf16[4,16,4096]{2,1,0:T(8,128)(2,1)S(1)}, bf16[4,16,4096]{2,1,0:T(8,128)(2,1)S(1)}, u32[]{:S(2)}, u32[]{:S(2)}) %collective-permute-start.12) | collective-permute-done | bytes 524320 | tf_op jit(solution)/shard_map/ppermute | solution.py:36
  92.1 1.9 %collective-permute-start.13 = (bf16[2,16,4096]{2,1,0:T(8,128)(2,1)S(1)}, bf16[2,16,4096]{2,1,0:T(8,128)(2,1)S(1)}, u32[]{:S(2)}, u32[]{:S(2)}) collective-permute-start(bf16[2,16,4096]{2,1,0:T(8,128)(2,1)S(1)} %slice.23), channel_id=1, source_target_pairs={{6,0},{0,2},{2,4},{4,6},{7,1},{1,3},{3,5},{5,7},{14,8},{8,10},{10,... | collective-permute-start | bytes 786440 | tf_op jit(solution)/shard_map/ppermute | solution.py:36
  94.1 4.6 %collective-permute-start.14 = (bf16[2,16,4096]{2,1,0:T(8,128)(2,1)S(1)}, bf16[2,16,4096]{2,1,0:T(8,128)(2,1)S(1)}, u32[]{:S(2)}, u32[]{:S(2)}) collective-permute-start(bf16[2,16,4096]{2,1,0:T(8,128)(2,1)S(1)} %slice.24), channel_id=1, source_target_pairs={{2,0},{4,2},{6,4},{0,6},{3,1},{5,3},{7,5},{1,7},{10,8},{12,10},{14... | collective-permute-start | bytes 786440 | tf_op jit(solution)/shard_map/ppermute | solution.py:36
  98.7 4.7 %shard_map.88 = (f32[256,384]{1,0:T(8,128)S(1)}, bf16[256,384]{1,0:T(8,128)(2,1)S(1)}, bf16[4096,256]{1,0:T(8,128)(2,1)S(1)}, bf16[256,4096]{1,0:T(8,128)(2,1)S(1)}) custom-call(s32[3]{0:T(128)S(1)} %pad_add_fusion.where, bf16[4,16,4096]{2,1,0:T(8,128)(2,1)S(1)} %get-tuple-element.12.refs_0_, bf16[4,16,4096]{2,1,0:T(8,128)(2,1)S(1)} %collective-permute-done.5.refs_1_, ...), custom_call_target="tpu_custom_call" | custom-call | flops 107374182400 | bytes 9437184 | tf_op jit(solution)/shard_map/pallas_call | solution.py:262
  103.5 2.7 %shard_map.90 = (f32[256,384]{1,0:T(8,128)S(1)}, bf16[512,384]{1,0:T(8,128)(2,1)S(1)}, f32[16,8,256]{2,1,0:T(8,128)}) custom-call(s32[3]{0:T(128)S(1)} %pad_add_fusion.where, s32[8]{0:T(128)S(1)} %bitcast.43, bf16[4,16,4096]{2,1,0:T(8,128)(2,1)S(1)} %get-tuple-element.15.refs_0_, bf16[4,16,4096]{2,1,0:T(8,128)(2,1)S(1)} %collective-permute-done.11.refs_1_, ...), custom_call_target="tpu_custom_call" | custom-call | flops 1073741824 | bytes 9437184 | tf_op jit(solution)/shard_map/pallas_call | solution.py:270
  106.2 0.7 copy-done.4
  106.9 0.8 copy-done.7
  107.7 12.6 %all-to-all-start.1 = ((f32[16,8,256]{2,1,0:T(8,128)}), f32[16,8,256]{2,1,0:T(8,128)S(1)}, u32[]{:S(2)}, u32[]{:S(2)}) async-start(f32[16,8,256]{2,1,0:T(8,128)} %get-tuple-element.21), calls=%async_computation.1 | async-start | bytes 262144 | tf_op jit(solution)/shard_map/all_to_all | solution.py:279
  120.3 2.0 %collective-permute-start.15 = (bf16[512,384]{1,0:T(8,128)(2,1)}, bf16[512,384]{1,0:T(8,128)(2,1)}, u32[]{:S(2)}, u32[]{:S(2)}) collective-permute-start(bf16[512,384]{1,0:T(8,128)(2,1)} %copy-done.7), channel_id=1, source_target_pairs={{0,1},{1,0},{2,3},{3,2},{4,5},{5,4},{6,7},{7,6},{8,9},{9,8},{10,11... | collective-permute-start | bytes 1179656 | tf_op jit(solution)/shard_map/ppermute | solution.py:44
  122.3 1.9 %collective-permute-done.15.got = bf16[512,384]{1,0:T(8,128)(2,1)} collective-permute-done((bf16[512,384]{1,0:T(8,128)(2,1)}, bf16[512,384]{1,0:T(8,128)(2,1)}, u32[]{:S(2)}, u32[]{:S(2)}) %collective-permute-start.15) | collective-permute-done | bytes 393248 | tf_op jit(solution)/shard_map/ppermute | solution.py:44
  124.2 1.0 copy-done.5
  125.2 3.3 %shard_map.91 = bf16[512,128]{1,0:T(8,128)(2,1)} custom-call(s32[3]{0:T(128)S(1)} %pad_add_fusion.where, f32[256,384]{1,0:T(8,128)S(1)} %get-tuple-element.13.refs_7_.own1, f32[256,384]{1,0:T(8,128)S(1)} %copy-done.5, bf16[512,384]{1,0:T(8,128)(2,1)} %collective-permute-done.15.got, f32[512,128]{1,0:T(8,128)S(1)} %get-tuple-element.32.rest_0_.cosine, ...), custom_call_target="tpu_custom_call" | custom-call | flops 268435456 | bytes 2097152 | tf_op jit(solution)/shard_map/pallas_call | solution.py:285
  128.6 3.7 %all-to-all-done.1.got = f32[16,8,256]{2,1,0:T(8,128)S(1)} async-done(((f32[16,8,256]{2,1,0:T(8,128)}), f32[16,8,256]{2,1,0:T(8,128)S(1)}, u32[]{:S(2)}, u32[]{:S(2)}) %all-to-all-start.1) | async-done | bytes 131104 | tf_op jit(solution)/shard_map/all_to_all | solution.py:279
  132.3 0.1 shard_map.92
  132.4 0.6 copy.9
  (38 shorter events, 0.3 us)
Async XLA Ops:
  0.6 121.7 %copy-start = (bf16[1,8,512,256]{3,2,1,0:T(8,128)(2,1)S(1)}, bf16[1,8,512,256]{3,2,1,0:T(8,128)(2,1)}, u32[]{:S(2)}) copy-start(bf16[1,8,512,256]{3,2,1,0:T(8,128)(2,1)} %param.11) | copy-start | bytes 6291460
  2.9 23.4 %collective-permute-start = (bf16[8,4096]{1,0:T(8,128)(2,1)S(1)}, bf16[8,4096]{1,0:T(8,128)(2,1)S(1)}, u32[]{:S(2)}, u32[]{:S(2)}) collective-permute-start(bf16[8,4096]{1,0:T(8,128)(2,1)S(1)} %get-tuple-element.25), channel_id=1, source_target_pairs={{0,96},{1,97},{8,104},{9,105},{16,112},{17,113},{24,120},{25,121},... | collective-permute-start | bytes 196616 | tf_op jit(solution)/shard_map/ppermute | solution.py:215
  16.2 12.4 %collective-permute-start.1 = (bf16[8,4096]{1,0:T(8,128)(2,1)S(1)}, bf16[8,4096]{1,0:T(8,128)(2,1)S(1)}, u32[]{:S(2)}, u32[]{:S(2)}) collective-permute-start(bf16[8,4096]{1,0:T(8,128)(2,1)S(1)} %get-tuple-element.24), channel_id=1, source_target_pairs={{0,97},{1,96},{8,105},{9,104},{16,113},{17,112},{24,121},{25,120},... | collective-permute-start | bytes 196616 | tf_op jit(solution)/shard_map/ppermute | solution.py:216
  18.7 1.0 copy-start.2
  20.0 1.3 %copy-start.1 = (bf16[8,32,4096]{2,1,0:T(8,128)(2,1)}, bf16[8,32,4096]{2,1,0:T(8,128)(2,1)S(1)}, u32[]{:S(2)}) copy-start(bf16[8,32,4096]{2,1,0:T(8,128)(2,1)S(1)} %shard_map.86) | copy-start | bytes 6291460
  21.3 5.0 %copy-start.8 = (f32[1,8192]{1,0:T(1,128)S(1)}, f32[1,8192]{1,0:T(1,128)}, u32[]{:S(2)}) copy-start(f32[1,8192]{1,0:T(1,128)} %param.8) | copy-start | bytes 98308
  21.3 39.4 %all-to-all-start = ((bf16[8,32,4096]{2,1,0:T(8,128)(2,1)}), bf16[8,32,4096]{2,1,0:T(8,128)(2,1)}, u32[]{:S(2)}, u32[]{:S(2)}) async-start(bf16[8,32,4096]{2,1,0:T(8,128)(2,1)} %copy-done.1), calls=%async_computation | async-start | bytes 4194304 | tf_op jit(solution)/shard_map/all_to_all | solution.py:227
  26.3 26.5 %copy-start.6 = (s32[1,8]{1,0:T(1,128)S(1)}, s32[1,8]{1,0:T(1,128)}, u32[]{:S(2)}) copy-start(s32[1,8]{1,0:T(1,128)} %param.13) | copy-start | bytes 100
  28.6 21.6 %collective-permute-start.2 = (bf16[16,4096]{1,0:T(8,128)(2,1)S(1)}, bf16[16,4096]{1,0:T(8,128)(2,1)S(1)}, u32[]{:S(2)}, u32[]{:S(2)}) collective-permute-start(bf16[16,4096]{1,0:T(8,128)(2,1)S(1)} %fusion.3), channel_id=1, source_target_pairs={{0,32},{8,40},{16,48},{24,56},{32,0},{40,8},{48,16},{56,24},{1,33}... | collective-permute-start | bytes 393224 | tf_op jit(solution)/shard_map/ppermute | solution.py:40
  41.7 19.1 %collective-permute-start.4 = (bf16[4096,128]{1,0:T(8,128)(2,1)}, bf16[4096,128]{1,0:T(8,128)(2,1)}, u32[]{:S(2)}, u32[]{:S(2)}) collective-permute-start(bf16[4096,128]{1,0:T(8,128)(2,1)} %dynamic-slice_bitcast_fusion), channel_id=1, source_target_pairs={{0,1},{1,0},{2,3},{3,2},{4,5},{5,4},{6,7},{7,6},{8,9},{9,8},{10,11... | collective-permute-start | bytes 3145736 | tf_op jit(solution)/shard_map/ppermute | solution.py:44
  50.2 10.5 %collective-permute-start.3 = (bf16[2,16,4096]{2,1,0:T(8,128)(2,1)S(1)}, bf16[2,16,4096]{2,1,0:T(8,128)(2,1)S(1)}, u32[]{:S(2)}, u32[]{:S(2)}) collective-permute-start(bf16[2,16,4096]{2,1,0:T(8,128)(2,1)S(1)} %pad_maximum_fusion.one), channel_id=1, source_target_pairs={{0,8},{8,0},{16,24},{24,16},{32,40},{40,32},{48,56},{56,48},{1,9},... | collective-permute-start | bytes 786440 | tf_op jit(solution)/shard_map/ppermute | solution.py:40
  52.9 21.5 %collective-permute-start.9 = (bf16[2,16,4096]{2,1,0:T(8,128)(2,1)S(1)}, bf16[2,16,4096]{2,1,0:T(8,128)(2,1)S(1)}, u32[]{:S(2)}, u32[]{:S(2)}) collective-permute-start(bf16[2,16,4096]{2,1,0:T(8,128)(2,1)S(1)} %pad_maximum_fusion.one), channel_id=1, source_target_pairs={{0,16},{8,24},{16,0},{24,8},{32,48},{40,56},{48,32},{56,40},{1,17}... | collective-permute-start | bytes 786440 | tf_op jit(solution)/shard_map/ppermute | solution.py:40
  54.8 19.6 %collective-permute-start.10 = (bf16[2,16,4096]{2,1,0:T(8,128)(2,1)S(1)}, bf16[2,16,4096]{2,1,0:T(8,128)(2,1)S(1)}, u32[]{:S(2)}, u32[]{:S(2)}) collective-permute-start(bf16[2,16,4096]{2,1,0:T(8,128)(2,1)S(1)} %pad_maximum_fusion.one), channel_id=1, source_target_pairs={{0,24},{8,16},{16,8},{24,0},{32,56},{40,48},{48,40},{56,32},{1,25}... | collective-permute-start | bytes 786440 | tf_op jit(solution)/shard_map/ppermute | solution.py:40
  61.3 22.1 %collective-permute-start.5 = (bf16[4,16,4096]{2,1,0:T(8,128)(2,1)S(1)}, bf16[4,16,4096]{2,1,0:T(8,128)(2,1)S(1)}, u32[]{:S(2)}, u32[]{:S(2)}) collective-permute-start(bf16[4,16,4096]{2,1,0:T(8,128)(2,1)S(1)} %get-tuple-element.12.refs_0_), channel_id=1, source_target_pairs={{2,0},{4,2},{6,4},{0,6},{3,1},{5,3},{7,5},{1,7},{10,8},{12,10},{14... | collective-permute-start | bytes 1572872 | tf_op jit(solution)/shard_map/ppermute | solution.py:36
  66.0 15.5 %collective-permute-start.6 = (bf16[4,16,4096]{2,1,0:T(8,128)(2,1)S(1)}, bf16[4,16,4096]{2,1,0:T(8,128)(2,1)S(1)}, u32[]{:S(2)}, u32[]{:S(2)}) collective-permute-start(bf16[4,16,4096]{2,1,0:T(8,128)(2,1)S(1)} %get-tuple-element.12.refs_0_), channel_id=1, source_target_pairs={{6,0},{0,2},{2,4},{4,6},{7,1},{1,3},{3,5},{5,7},{14,8},{8,10},{10,... | collective-permute-start | bytes 1572872 | tf_op jit(solution)/shard_map/ppermute | solution.py:36
  69.8 28.9 %copy-start.3 = (bf16[1,8192,128]{2,1,0:T(8,128)(2,1)S(1)}, bf16[1,8192,128]{2,1,0:T(8,128)(2,1)}, u32[]{:S(2)}) copy-start(bf16[1,8192,128]{2,1,0:T(8,128)(2,1)} %param.9) | copy-start | bytes 6291460
  74.9 17.2 %collective-permute-start.12 = (bf16[4,16,4096]{2,1,0:T(8,128)(2,1)S(1)}, bf16[4,16,4096]{2,1,0:T(8,128)(2,1)S(1)}, u32[]{:S(2)}, u32[]{:S(2)}) collective-permute-start(bf16[4,16,4096]{2,1,0:T(8,128)(2,1)S(1)} %get-tuple-element.15.refs_0_), channel_id=1, source_target_pairs={{6,0},{0,2},{2,4},{4,6},{7,1},{1,3},{3,5},{5,7},{14,8},{8,10},{10,... | collective-permute-start | bytes 1572872 | tf_op jit(solution)/shard_map/ppermute | solution.py:36
  78.1 16.0 %collective-permute-start.11 = (bf16[4,16,4096]{2,1,0:T(8,128)(2,1)S(1)}, bf16[4,16,4096]{2,1,0:T(8,128)(2,1)S(1)}, u32[]{:S(2)}, u32[]{:S(2)}) collective-permute-start(bf16[4,16,4096]{2,1,0:T(8,128)(2,1)S(1)} %get-tuple-element.15.refs_0_), channel_id=1, source_target_pairs={{2,0},{4,2},{6,4},{0,6},{3,1},{5,3},{7,5},{1,7},{10,8},{12,10},{14... | collective-permute-start | bytes 1572872 | tf_op jit(solution)/shard_map/ppermute | solution.py:36
  81.5 17.2 %collective-permute-start.7 = (bf16[2,16,4096]{2,1,0:T(8,128)(2,1)S(1)}, bf16[2,16,4096]{2,1,0:T(8,128)(2,1)S(1)}, u32[]{:S(2)}, u32[]{:S(2)}) collective-permute-start(bf16[2,16,4096]{2,1,0:T(8,128)(2,1)S(1)} %slice.21), channel_id=1, source_target_pairs={{6,0},{0,2},{2,4},{4,6},{7,1},{1,3},{3,5},{5,7},{14,8},{8,10},{10,... | collective-permute-start | bytes 786440 | tf_op jit(solution)/shard_map/ppermute | solution.py:36
  83.5 15.2 %collective-permute-start.8 = (bf16[2,16,4096]{2,1,0:T(8,128)(2,1)S(1)}, bf16[2,16,4096]{2,1,0:T(8,128)(2,1)S(1)}, u32[]{:S(2)}, u32[]{:S(2)}) collective-permute-start(bf16[2,16,4096]{2,1,0:T(8,128)(2,1)S(1)} %slice.22), channel_id=1, source_target_pairs={{2,0},{4,2},{6,4},{0,6},{3,1},{5,3},{7,5},{1,7},{10,8},{12,10},{14... | collective-permute-start | bytes 786440 | tf_op jit(solution)/shard_map/ppermute | solution.py:36
  92.1 11.3 %collective-permute-start.13 = (bf16[2,16,4096]{2,1,0:T(8,128)(2,1)S(1)}, bf16[2,16,4096]{2,1,0:T(8,128)(2,1)S(1)}, u32[]{:S(2)}, u32[]{:S(2)}) collective-permute-start(bf16[2,16,4096]{2,1,0:T(8,128)(2,1)S(1)} %slice.23), channel_id=1, source_target_pairs={{6,0},{0,2},{2,4},{4,6},{7,1},{1,3},{3,5},{5,7},{14,8},{8,10},{10,... | collective-permute-start | bytes 786440 | tf_op jit(solution)/shard_map/ppermute | solution.py:36
  94.1 9.3 %collective-permute-start.14 = (bf16[2,16,4096]{2,1,0:T(8,128)(2,1)S(1)}, bf16[2,16,4096]{2,1,0:T(8,128)(2,1)S(1)}, u32[]{:S(2)}, u32[]{:S(2)}) collective-permute-start(bf16[2,16,4096]{2,1,0:T(8,128)(2,1)S(1)} %slice.24), channel_id=1, source_target_pairs={{2,0},{4,2},{6,4},{0,6},{3,1},{5,3},{7,5},{1,7},{10,8},{12,10},{14... | collective-permute-start | bytes 786440 | tf_op jit(solution)/shard_map/ppermute | solution.py:36
  106.2 0.7 copy-start.4
  106.9 0.8 copy-start.7
  107.7 24.6 %all-to-all-start.1 = ((f32[16,8,256]{2,1,0:T(8,128)}), f32[16,8,256]{2,1,0:T(8,128)S(1)}, u32[]{:S(2)}, u32[]{:S(2)}) async-start(f32[16,8,256]{2,1,0:T(8,128)} %get-tuple-element.21), calls=%async_computation.1 | async-start | bytes 262144 | tf_op jit(solution)/shard_map/all_to_all | solution.py:279
  120.3 3.9 %collective-permute-start.15 = (bf16[512,384]{1,0:T(8,128)(2,1)}, bf16[512,384]{1,0:T(8,128)(2,1)}, u32[]{:S(2)}, u32[]{:S(2)}) collective-permute-start(bf16[512,384]{1,0:T(8,128)(2,1)} %copy-done.7), channel_id=1, source_target_pairs={{0,1},{1,0},{2,3},{3,2},{4,5},{5,4},{6,7},{7,6},{8,9},{9,8},{10,11... | collective-permute-start | bytes 1179656 | tf_op jit(solution)/shard_map/ppermute | solution.py:44
  124.2 1.0 copy-start.5

commit v8 on v7

--- a/solution.py
+++ b/solution.py
@@ -107,7 +107,7 @@
         for c in (0, 1):
             block = (z * 8 + y0 * 2 + c - owner[z0]) & 63
             row = slot_of(block >> 1, z0, y0) * ROWS + (block & 1) * 8
-            blocks[2 * z + c] = held[pl.ds(pl.multiple_of(row, 8), 8), :]
+            blocks[2 * z + c] = held[pl.ds(pl.multiple_of(row, 8), 8), :].astype(BF)
 
 
 def spread_kernel(kv, out, sems):
@@ -135,7 +135,7 @@
 
 def decode_kernel(got, tables, out):
     for g in range(NZ):
-        raw = (got[2 * g] + got[2 * g + 1]).astype(BF)
+        raw = (got[2 * g].astype(F32) + got[2 * g + 1].astype(F32)).astype(BF)
         out[g, :, :HD] = turn(
             raw[:, :HD].astype(F32), tables[g, :, :HD], tables[g, :, HD:]
         ).astype(BF)
@@ -161,10 +161,9 @@
     old = jnp.exp(old - top)
     new = jnp.exp(new - top)
     total = jnp.sum(old, axis=1, keepdims=True) + jnp.sum(new, axis=1, keepdims=True)
-    scale = 1.0 / total
-    att = jnp.dot((old * scale).astype(BF), resident[:, HD:], preferred_element_type=F32)
-    att = att + jnp.dot((new * scale).astype(BF), raw[:, HD:], preferred_element_type=F32)
-    att = att.astype(BF)
+    att = jnp.dot(old.astype(BF), resident[:, HD:], preferred_element_type=F32)
+    att = att + jnp.dot(new.astype(BF), raw[:, HD:], preferred_element_type=F32)
+    att = (att * (1.0 / total)).astype(BF)
     for slot in range(32):
         to = pl.multiple_of(place(slot, z0, y0) * ROWS, ROWS)
         out[pl.ds(to, ROWS), :] = att[slot * ROWS : (slot + 1) * ROWS]
@@ -269,7 +268,7 @@
     )(where, *everywhere(batch1), query_weight[0], wq_other, wkv)
     own2, send, blocks = call(
         second_kernel,
-        (projected[0], shaped(TOKENS, 3 * HD), shaped(NZ * 2, 8, 2 * HD, dtype=F32)),
+        (projected[0], shaped(TOKENS, 3 * HD), shaped(NZ * 2, 8, 2 * HD)),
         [SMEM, SMEM] + [HBM] * 5 + [VMEM] * 4,
         scratch=[scratch, pltpu.VMEM((TOKENS, 2 * HD), F32), pltpu.SemaphoreType.DMA((5,))],
         flops=2 * rows * half * 512,

time: 134 us -> 138 us (1.030)
  waiting for transfers between devices: 22.3 us -> 26.7 us
    all_to_all x1, waiting for transfers between devices: 3.73 us -> 10 us  [body(): blocks = lax.all_to_all(blocks, ('z', 'c'), 0, 0)]
    ppermute x2, starting transfers between devices: 4.85 us -> 9.94 us  [swap_core(): return lax.ppermute(value, 'c', [(0, 1), (1, 0)])]
    all_to_all x1, starting transfers between devices: 12.6 us -> 7.48 us  [body(): blocks = lax.all_to_all(blocks, ('z', 'c'), 0, 0)]
    ppermute x2, waiting for transfers between devices: 1.89 us -> 0.01 us  [swap_core(): return lax.ppermute(value, 'c', [(0, 1), (1, 0)])]
    unnamed x19 -> x17, local copies, waits for them, and re-layouts: 5.52 us -> 4.75 us
  transfers between devices with their start and end apart: 18 -> 18, of which waited for: 7 -> 6; matrix products, arithmetic and copies ran while one was open for 4% -> 4% of each run, Pallas kernels for 7% -> 4%
where the time goes in v8:
time: 138 us; the launch traced here: 137 us
  starting transfers between devices  82.9 us (60%)
  waiting for transfers between devices  26.7 us (19%)
  Pallas kernels  12.1 us (9%)
  local copies, waits for them, and re-layouts  7.9 us (6%)
  other arithmetic  4.02 us (3%)
  between operations  2.99 us (2%)
    ppermute x8, starting transfers between devices, along_y(): return lax.ppermute(value, 'y', [((i + k) % NY, i) for i in range(NY)])  26.1 us
    ppermute x4, starting transfers between devices, across_z(): return lax.ppermute(value, 'z', [(i, i ^ k) for i in range(NZ)])  18.6 us
    ppermute x1, starting transfers between devices, body(): same = lax.ppermute(kept, ('s', 'z', 'c'), steps[0])  13.3 us
    ppermute x4, waiting for transfers between devices, across_z(): return lax.ppermute(value, 'z', [(i, i ^ k) for i in range(NZ)])  10.4 us
    all_to_all x1, waiting for transfers between devices, body(): blocks = lax.all_to_all(blocks, ('z', 'c'), 0, 0)  10 us
    ppermute x2, starting transfers between devices, swap_core(): return lax.ppermute(value, 'c', [(0, 1), (1, 0)])  9.94 us
    all_to_all x1, starting transfers between devices, body(): blocks = lax.all_to_all(blocks, ('z', 'c'), 0, 0)  7.48 us
    all_to_all x1, starting transfers between devices, body(): wkv = lax.all_to_all(kv_halves, ('y', 'c'), 0, 0).reshape(256, half)  4.99 us
  transfers between devices with their start and end apart: 18, of which 6 were waited for; matrix products, arithmetic and copies ran while one was open for 4% of the time, Pallas kernels for 4%

profile of v8, /device:TPU:1, one launch (start us, length us, event | category | flops | bytes accessed | tf_op | source)
XLA Modules:
  0.0 136.5 jit_solution(17271393803993256603)
XLA Ops:
  0.6 0.0 copy-start
  0.7 1.2 fusion.4
  1.9 1.0 fusion.5
  2.9 13.3 %collective-permute-start = (bf16[8,4096]{1,0:T(8,128)(2,1)S(1)}, bf16[8,4096]{1,0:T(8,128)(2,1)S(1)}, u32[]{:S(2)}, u32[]{:S(2)}) collective-permute-start(bf16[8,4096]{1,0:T(8,128)(2,1)S(1)} %get-tuple-element.25), channel_id=1, source_target_pairs={{0,96},{1,97},{8,104},{9,105},{16,112},{17,113},{24,120},{25,121},... | collective-permute-start | bytes 196616 | tf_op jit(solution)/shard_map/ppermute | solution.py:214
  16.2 2.5 %collective-permute-start.1 = (bf16[8,4096]{1,0:T(8,128)(2,1)S(1)}, bf16[8,4096]{1,0:T(8,128)(2,1)S(1)}, u32[]{:S(2)}, u32[]{:S(2)}) collective-permute-start(bf16[8,4096]{1,0:T(8,128)(2,1)S(1)} %get-tuple-element.24), channel_id=1, source_target_pairs={{0,97},{1,96},{8,105},{9,104},{16,113},{17,112},{24,121},{25,120},... | collective-permute-start | bytes 196616 | tf_op jit(solution)/shard_map/ppermute | solution.py:215
  18.7 0.0 copy-start.2
  18.7 1.0 copy-done.2
  19.7 0.2 shard_map.86
  20.0 1.3 copy-done.1
  21.3 5.0 %all-to-all-start = ((bf16[8,32,4096]{2,1,0:T(8,128)(2,1)}), bf16[8,32,4096]{2,1,0:T(8,128)(2,1)}, u32[]{:S(2)}, u32[]{:S(2)}) async-start(bf16[8,32,4096]{2,1,0:T(8,128)(2,1)} %copy-done.1), calls=%async_computation | async-start | bytes 4194304 | tf_op jit(solution)/shard_map/all_to_all | solution.py:226
  26.3 2.3 %collective-permute-done.1 = bf16[8,4096]{1,0:T(8,128)(2,1)S(1)} collective-permute-done((bf16[8,4096]{1,0:T(8,128)(2,1)S(1)}, bf16[8,4096]{1,0:T(8,128)(2,1)S(1)}, u32[]{:S(2)}, u32[]{:S(2)}) %collective-permute-start.1) | collective-permute-done | bytes 65568 | tf_op jit(solution)/shard_map/ppermute | solution.py:215
  28.6 9.3 %collective-permute-start.2 = (bf16[16,4096]{1,0:T(8,128)(2,1)S(1)}, bf16[16,4096]{1,0:T(8,128)(2,1)S(1)}, u32[]{:S(2)}, u32[]{:S(2)}) collective-permute-start(bf16[16,4096]{1,0:T(8,128)(2,1)S(1)} %fusion.3), channel_id=1, source_target_pairs={{0,32},{8,40},{16,48},{24,56},{32,0},{40,8},{48,16},{56,24},{1,33}... | collective-permute-start | bytes 393224 | tf_op jit(solution)/shard_map/ppermute | solution.py:40
  38.0 0.5 slice.20
  39.2 2.5 %dynamic-slice_bitcast_fusion = bf16[4096,128]{1,0:T(8,128)(2,1)} fusion(bf16[1,8192,128]{2,1,0:T(8,128)(2,1)} %param.9, s32[]{:T(128)S(6)} %select_n.65), kind=kLoop, calls=%fused_computation | loop fusion | bytes 2097156 | tf_op jit(solution)/shard_map/dynamic_slice | solution.py:222
  41.7 2.8 %collective-permute-start.4 = (bf16[4096,128]{1,0:T(8,128)(2,1)}, bf16[4096,128]{1,0:T(8,128)(2,1)}, u32[]{:S(2)}, u32[]{:S(2)}) collective-permute-start(bf16[4096,128]{1,0:T(8,128)(2,1)} %dynamic-slice_bitcast_fusion), channel_id=1, source_target_pairs={{0,1},{1,0},{2,3},{3,2},{4,5},{5,4},{6,7},{7,6},{8,9},{9,8},{10,11... | collective-permute-start | bytes 3145736 | tf_op jit(solution)/shard_map/ppermute | solution.py:44
  44.6 5.6 %collective-permute-done.2 = bf16[16,4096]{1,0:T(8,128)(2,1)S(1)} collective-permute-done((bf16[16,4096]{1,0:T(8,128)(2,1)S(1)}, bf16[16,4096]{1,0:T(8,128)(2,1)S(1)}, u32[]{:S(2)}, u32[]{:S(2)}) %collective-permute-start.2) | collective-permute-done | bytes 131104 | tf_op jit(solution)/shard_map/ppermute | solution.py:40
  50.2 1.9 %collective-permute-start.3 = (bf16[2,16,4096]{2,1,0:T(8,128)(2,1)S(1)}, bf16[2,16,4096]{2,1,0:T(8,128)(2,1)S(1)}, u32[]{:S(2)}, u32[]{:S(2)}) collective-permute-start(bf16[2,16,4096]{2,1,0:T(8,128)(2,1)S(1)} %pad_maximum_fusion.one), channel_id=1, source_target_pairs={{0,8},{8,0},{16,24},{24,16},{32,40},{40,32},{48,56},{56,48},{1,9},... | collective-permute-start | bytes 786440 | tf_op jit(solution)/shard_map/ppermute | solution.py:40
  52.9 1.9 %collective-permute-start.9 = (bf16[2,16,4096]{2,1,0:T(8,128)(2,1)S(1)}, bf16[2,16,4096]{2,1,0:T(8,128)(2,1)S(1)}, u32[]{:S(2)}, u32[]{:S(2)}) collective-permute-start(bf16[2,16,4096]{2,1,0:T(8,128)(2,1)S(1)} %pad_maximum_fusion.one), channel_id=1, source_target_pairs={{0,16},{8,24},{16,0},{24,8},{32,48},{40,56},{48,32},{56,40},{1,17}... | collective-permute-start | bytes 786440 | tf_op jit(solution)/shard_map/ppermute | solution.py:40
  54.8 5.4 %collective-permute-start.10 = (bf16[2,16,4096]{2,1,0:T(8,128)(2,1)S(1)}, bf16[2,16,4096]{2,1,0:T(8,128)(2,1)S(1)}, u32[]{:S(2)}, u32[]{:S(2)}) collective-permute-start(bf16[2,16,4096]{2,1,0:T(8,128)(2,1)S(1)} %pad_maximum_fusion.one), channel_id=1, source_target_pairs={{0,24},{8,16},{16,8},{24,0},{32,56},{40,48},{48,40},{56,32},{1,25}... | collective-permute-start | bytes 786440 | tf_op jit(solution)/shard_map/ppermute | solution.py:40
  60.2 0.5 collective-permute-done.3.two
  60.7 0.6 shard_map.87
  61.3 4.6 %collective-permute-start.5 = (bf16[4,16,4096]{2,1,0:T(8,128)(2,1)S(1)}, bf16[4,16,4096]{2,1,0:T(8,128)(2,1)S(1)}, u32[]{:S(2)}, u32[]{:S(2)}) collective-permute-start(bf16[4,16,4096]{2,1,0:T(8,128)(2,1)S(1)} %get-tuple-element.12.refs_0_), channel_id=1, source_target_pairs={{2,0},{4,2},{6,4},{0,6},{3,1},{5,3},{7,5},{1,7},{10,8},{12,10},{14... | collective-permute-start | bytes 1572872 | tf_op jit(solution)/shard_map/ppermute | solution.py:36
  66.0 1.9 %collective-permute-start.6 = (bf16[4,16,4096]{2,1,0:T(8,128)(2,1)S(1)}, bf16[4,16,4096]{2,1,0:T(8,128)(2,1)S(1)}, u32[]{:S(2)}, u32[]{:S(2)}) collective-permute-start(bf16[4,16,4096]{2,1,0:T(8,128)(2,1)S(1)} %get-tuple-element.12.refs_0_), channel_id=1, source_target_pairs={{6,0},{0,2},{2,4},{4,6},{7,1},{1,3},{3,5},{5,7},{14,8},{8,10},{10,... | collective-permute-start | bytes 1572872 | tf_op jit(solution)/shard_map/ppermute | solution.py:36
  68.5 0.1 add_convert_fusion
  68.6 1.0 fusion.6
  69.6 0.2 multiply_cosine_fusion.1
  69.8 0.1 pad_maximum_fusion.3.rest_2_.tables
  69.9 0.2 pad_maximum_fusion.1
  70.1 4.2 %collective-permute-done.9.one = bf16[2,16,4096]{2,1,0:T(8,128)(2,1)S(1)} collective-permute-done((bf16[2,16,4096]{2,1,0:T(8,128)(2,1)S(1)}, bf16[2,16,4096]{2,1,0:T(8,128)(2,1)S(1)}, u32[]{:S(2)}, u32[]{:S(2)}) %collective-permute-start.9) | collective-permute-done | bytes 262176 | tf_op jit(solution)/shard_map/ppermute | solution.py:40
  74.3 0.6 shard_map.89
  74.9 3.2 %collective-permute-start.12 = (bf16[4,16,4096]{2,1,0:T(8,128)(2,1)S(1)}, bf16[4,16,4096]{2,1,0:T(8,128)(2,1)S(1)}, u32[]{:S(2)}, u32[]{:S(2)}) collective-permute-start(bf16[4,16,4096]{2,1,0:T(8,128)(2,1)S(1)} %get-tuple-element.15.refs_0_), channel_id=1, source_target_pairs={{6,0},{0,2},{2,4},{4,6},{7,1},{1,3},{3,5},{5,7},{14,8},{8,10},{10,... | collective-permute-start | bytes 1572872 | tf_op jit(solution)/shard_map/ppermute | solution.py:36
  78.1 3.4 %collective-permute-start.11 = (bf16[4,16,4096]{2,1,0:T(8,128)(2,1)S(1)}, bf16[4,16,4096]{2,1,0:T(8,128)(2,1)S(1)}, u32[]{:S(2)}, u32[]{:S(2)}) collective-permute-start(bf16[4,16,4096]{2,1,0:T(8,128)(2,1)S(1)} %get-tuple-element.15.refs_0_), channel_id=1, source_target_pairs={{2,0},{4,2},{6,4},{0,6},{3,1},{5,3},{7,5},{1,7},{10,8},{12,10},{14... | collective-permute-start | bytes 1572872 | tf_op jit(solution)/shard_map/ppermute | solution.py:36
  81.5 1.9 %collective-permute-start.7 = (bf16[2,16,4096]{2,1,0:T(8,128)(2,1)S(1)}, bf16[2,16,4096]{2,1,0:T(8,128)(2,1)S(1)}, u32[]{:S(2)}, u32[]{:S(2)}) collective-permute-start(bf16[2,16,4096]{2,1,0:T(8,128)(2,1)S(1)} %slice.21), channel_id=1, source_target_pairs={{6,0},{0,2},{2,4},{4,6},{7,1},{1,3},{3,5},{5,7},{14,8},{8,10},{10,... | collective-permute-start | bytes 786440 | tf_op jit(solution)/shard_map/ppermute | solution.py:36
  83.5 4.6 %collective-permute-start.8 = (bf16[2,16,4096]{2,1,0:T(8,128)(2,1)S(1)}, bf16[2,16,4096]{2,1,0:T(8,128)(2,1)S(1)}, u32[]{:S(2)}, u32[]{:S(2)}) collective-permute-start(bf16[2,16,4096]{2,1,0:T(8,128)(2,1)S(1)} %slice.22), channel_id=1, source_target_pairs={{2,0},{4,2},{6,4},{0,6},{3,1},{5,3},{7,5},{1,7},{10,8},{12,10},{14... | collective-permute-start | bytes 786440 | tf_op jit(solution)/shard_map/ppermute | solution.py:36
  88.1 0.1 pad_add_fusion.where
  88.1 4.0 %collective-permute-done.12.refs_4_ = bf16[4,16,4096]{2,1,0:T(8,128)(2,1)S(1)} collective-permute-done((bf16[4,16,4096]{2,1,0:T(8,128)(2,1)S(1)}, bf16[4,16,4096]{2,1,0:T(8,128)(2,1)S(1)}, u32[]{:S(2)}, u32[]{:S(2)}) %collective-permute-start.12) | collective-permute-done | bytes 524320 | tf_op jit(solution)/shard_map/ppermute | solution.py:36
  92.1 1.9 %collective-permute-start.13 = (bf16[2,16,4096]{2,1,0:T(8,128)(2,1)S(1)}, bf16[2,16,4096]{2,1,0:T(8,128)(2,1)S(1)}, u32[]{:S(2)}, u32[]{:S(2)}) collective-permute-start(bf16[2,16,4096]{2,1,0:T(8,128)(2,1)S(1)} %slice.23), channel_id=1, source_target_pairs={{6,0},{0,2},{2,4},{4,6},{7,1},{1,3},{3,5},{5,7},{14,8},{8,10},{10,... | collective-permute-start | bytes 786440 | tf_op jit(solution)/shard_map/ppermute | solution.py:36
  94.1 4.6 %collective-permute-start.14 = (bf16[2,16,4096]{2,1,0:T(8,128)(2,1)S(1)}, bf16[2,16,4096]{2,1,0:T(8,128)(2,1)S(1)}, u32[]{:S(2)}, u32[]{:S(2)}) collective-permute-start(bf16[2,16,4096]{2,1,0:T(8,128)(2,1)S(1)} %slice.24), channel_id=1, source_target_pairs={{2,0},{4,2},{6,4},{0,6},{3,1},{5,3},{7,5},{1,7},{10,8},{12,10},{14... | collective-permute-start | bytes 786440 | tf_op jit(solution)/shard_map/ppermute | solution.py:36
  98.7 4.7 %shard_map.88 = (f32[256,384]{1,0:T(8,128)S(1)}, bf16[256,384]{1,0:T(8,128)(2,1)S(1)}, bf16[4096,256]{1,0:T(8,128)(2,1)S(1)}, bf16[256,4096]{1,0:T(8,128)(2,1)S(1)}) custom-call(s32[3]{0:T(128)S(1)} %pad_add_fusion.where, bf16[4,16,4096]{2,1,0:T(8,128)(2,1)S(1)} %get-tuple-element.12.refs_0_, bf16[4,16,4096]{2,1,0:T(8,128)(2,1)S(1)} %collective-permute-done.5.refs_1_, ...), custom_call_target="tpu_custom_call" | custom-call | flops 107374182400 | bytes 9437184 | tf_op jit(solution)/shard_map/pallas_call | solution.py:261
  103.4 2.8 %shard_map.90 = (f32[256,384]{1,0:T(8,128)S(1)}, bf16[512,384]{1,0:T(8,128)(2,1)}, bf16[16,8,256]{2,1,0:T(8,128)(2,1)}) custom-call(s32[3]{0:T(128)S(1)} %pad_add_fusion.where, s32[8]{0:T(128)S(1)} %bitcast.43, bf16[4,16,4096]{2,1,0:T(8,128)(2,1)S(1)} %get-tuple-element.15.refs_0_, bf16[4,16,4096]{2,1,0:T(8,128)(2,1)S(1)} %collective-permute-done.11.refs_1_, ...), custom_call_target="tpu_custom_call" | custom-call | flops 1073741824 | bytes 9437184 | tf_op jit(solution)/shard_map/pallas_call | solution.py:269
  106.3 0.8 copy-done.4
  107.0 7.1 %collective-permute-start.15 = (bf16[512,384]{1,0:T(8,128)(2,1)}, bf16[512,384]{1,0:T(8,128)(2,1)}, u32[]{:S(2)}, u32[]{:S(2)}) collective-permute-start(bf16[512,384]{1,0:T(8,128)(2,1)} %get-tuple-element.20), channel_id=1, source_target_pairs={{0,1},{1,0},{2,3},{3,2},{4,5},{5,4},{6,7},{7,6},{8,9},{9,8},{10,11... | collective-permute-start | bytes 1179656 | tf_op jit(solution)/shard_map/ppermute | solution.py:44
  114.1 7.5 %all-to-all-start.1 = ((bf16[16,8,256]{2,1,0:T(8,128)(2,1)}), bf16[16,8,256]{2,1,0:T(8,128)(2,1)S(1)}, u32[]{:S(2)}, u32[]{:S(2)}) async-start(bf16[16,8,256]{2,1,0:T(8,128)(2,1)} %get-tuple-element.21), calls=%async_computation.1 | async-start | bytes 131072 | tf_op jit(solution)/shard_map/all_to_all | solution.py:278
  121.6 10.0 %all-to-all-done.1.got = bf16[16,8,256]{2,1,0:T(8,128)(2,1)S(1)} async-done(((bf16[16,8,256]{2,1,0:T(8,128)(2,1)}), bf16[16,8,256]{2,1,0:T(8,128)(2,1)S(1)}, u32[]{:S(2)}, u32[]{:S(2)}) %all-to-all-start.1) | async-done | bytes 65568 | tf_op jit(solution)/shard_map/all_to_all | solution.py:278
  131.7 0.1 shard_map.92
  131.8 0.6 copy.9
  132.4 1.0 copy-done.5
  133.4 3.2 %shard_map.91 = bf16[512,128]{1,0:T(8,128)(2,1)} custom-call(s32[3]{0:T(128)S(1)} %pad_add_fusion.where, f32[256,384]{1,0:T(8,128)S(1)} %get-tuple-element.13.refs_7_.own1, f32[256,384]{1,0:T(8,128)S(1)} %copy-done.5, bf16[512,384]{1,0:T(8,128)(2,1)} %collective-permute-done.15.got, f32[512,128]{1,0:T(8,128)S(1)} %get-tuple-element.32.rest_0_.cosine, ...), custom_call_target="tpu_custom_call" | custom-call | flops 268435456 | bytes 2097152 | tf_op jit(solution)/shard_map/pallas_call | solution.py:284
  (36 shorter events, 0.3 us)
Async XLA Ops:
  0.6 121.0 %copy-start = (bf16[1,8,512,256]{3,2,1,0:T(8,128)(2,1)S(1)}, bf16[1,8,512,256]{3,2,1,0:T(8,128)(2,1)}, u32[]{:S(2)}) copy-start(bf16[1,8,512,256]{3,2,1,0:T(8,128)(2,1)} %param.11) | copy-start | bytes 6291460
  2.9 23.4 %collective-permute-start = (bf16[8,4096]{1,0:T(8,128)(2,1)S(1)}, bf16[8,4096]{1,0:T(8,128)(2,1)S(1)}, u32[]{:S(2)}, u32[]{:S(2)}) collective-permute-start(bf16[8,4096]{1,0:T(8,128)(2,1)S(1)} %get-tuple-element.25), channel_id=1, source_target_pairs={{0,96},{1,97},{8,104},{9,105},{16,112},{17,113},{24,120},{25,121},... | collective-permute-start | bytes 196616 | tf_op jit(solution)/shard_map/ppermute | solution.py:214
  16.2 12.4 %collective-permute-start.1 = (bf16[8,4096]{1,0:T(8,128)(2,1)S(1)}, bf16[8,4096]{1,0:T(8,128)(2,1)S(1)}, u32[]{:S(2)}, u32[]{:S(2)}) collective-permute-start(bf16[8,4096]{1,0:T(8,128)(2,1)S(1)} %get-tuple-element.24), channel_id=1, source_target_pairs={{0,97},{1,96},{8,105},{9,104},{16,113},{17,112},{24,121},{25,120},... | collective-permute-start | bytes 196616 | tf_op jit(solution)/shard_map/ppermute | solution.py:215
  18.7 1.0 copy-start.2
  20.0 1.3 copy-start.1
  21.3 5.0 %copy-start.7 = (f32[1,8192]{1,0:T(1,128)S(1)}, f32[1,8192]{1,0:T(1,128)}, u32[]{:S(2)}) copy-start(f32[1,8192]{1,0:T(1,128)} %param.8) | copy-start | bytes 98308
  21.3 39.4 %all-to-all-start = ((bf16[8,32,4096]{2,1,0:T(8,128)(2,1)}), bf16[8,32,4096]{2,1,0:T(8,128)(2,1)}, u32[]{:S(2)}, u32[]{:S(2)}) async-start(bf16[8,32,4096]{2,1,0:T(8,128)(2,1)} %copy-done.1), calls=%async_computation | async-start | bytes 4194304 | tf_op jit(solution)/shard_map/all_to_all | solution.py:226
  26.3 26.5 %copy-start.6 = (s32[1,8]{1,0:T(1,128)S(1)}, s32[1,8]{1,0:T(1,128)}, u32[]{:S(2)}) copy-start(s32[1,8]{1,0:T(1,128)} %param.13) | copy-start | bytes 100
  28.6 21.6 %collective-permute-start.2 = (bf16[16,4096]{1,0:T(8,128)(2,1)S(1)}, bf16[16,4096]{1,0:T(8,128)(2,1)S(1)}, u32[]{:S(2)}, u32[]{:S(2)}) collective-permute-start(bf16[16,4096]{1,0:T(8,128)(2,1)S(1)} %fusion.3), channel_id=1, source_target_pairs={{0,32},{8,40},{16,48},{24,56},{32,0},{40,8},{48,16},{56,24},{1,33}... | collective-permute-start | bytes 393224 | tf_op jit(solution)/shard_map/ppermute | solution.py:40
  41.7 19.1 %collective-permute-start.4 = (bf16[4096,128]{1,0:T(8,128)(2,1)}, bf16[4096,128]{1,0:T(8,128)(2,1)}, u32[]{:S(2)}, u32[]{:S(2)}) collective-permute-start(bf16[4096,128]{1,0:T(8,128)(2,1)} %dynamic-slice_bitcast_fusion), channel_id=1, source_target_pairs={{0,1},{1,0},{2,3},{3,2},{4,5},{5,4},{6,7},{7,6},{8,9},{9,8},{10,11... | collective-permute-start | bytes 3145736 | tf_op jit(solution)/shard_map/ppermute | solution.py:44
  50.2 10.5 %collective-permute-start.3 = (bf16[2,16,4096]{2,1,0:T(8,128)(2,1)S(1)}, bf16[2,16,4096]{2,1,0:T(8,128)(2,1)S(1)}, u32[]{:S(2)}, u32[]{:S(2)}) collective-permute-start(bf16[2,16,4096]{2,1,0:T(8,128)(2,1)S(1)} %pad_maximum_fusion.one), channel_id=1, source_target_pairs={{0,8},{8,0},{16,24},{24,16},{32,40},{40,32},{48,56},{56,48},{1,9},... | collective-permute-start | bytes 786440 | tf_op jit(solution)/shard_map/ppermute | solution.py:40
  52.9 21.5 %collective-permute-start.9 = (bf16[2,16,4096]{2,1,0:T(8,128)(2,1)S(1)}, bf16[2,16,4096]{2,1,0:T(8,128)(2,1)S(1)}, u32[]{:S(2)}, u32[]{:S(2)}) collective-permute-start(bf16[2,16,4096]{2,1,0:T(8,128)(2,1)S(1)} %pad_maximum_fusion.one), channel_id=1, source_target_pairs={{0,16},{8,24},{16,0},{24,8},{32,48},{40,56},{48,32},{56,40},{1,17}... | collective-permute-start | bytes 786440 | tf_op jit(solution)/shard_map/ppermute | solution.py:40
  54.8 19.6 %collective-permute-start.10 = (bf16[2,16,4096]{2,1,0:T(8,128)(2,1)S(1)}, bf16[2,16,4096]{2,1,0:T(8,128)(2,1)S(1)}, u32[]{:S(2)}, u32[]{:S(2)}) collective-permute-start(bf16[2,16,4096]{2,1,0:T(8,128)(2,1)S(1)} %pad_maximum_fusion.one), channel_id=1, source_target_pairs={{0,24},{8,16},{16,8},{24,0},{32,56},{40,48},{48,40},{56,32},{1,25}... | collective-permute-start | bytes 786440 | tf_op jit(solution)/shard_map/ppermute | solution.py:40
  61.3 22.1 %collective-permute-start.5 = (bf16[4,16,4096]{2,1,0:T(8,128)(2,1)S(1)}, bf16[4,16,4096]{2,1,0:T(8,128)(2,1)S(1)}, u32[]{:S(2)}, u32[]{:S(2)}) collective-permute-start(bf16[4,16,4096]{2,1,0:T(8,128)(2,1)S(1)} %get-tuple-element.12.refs_0_), channel_id=1, source_target_pairs={{2,0},{4,2},{6,4},{0,6},{3,1},{5,3},{7,5},{1,7},{10,8},{12,10},{14... | collective-permute-start | bytes 1572872 | tf_op jit(solution)/shard_map/ppermute | solution.py:36
  66.0 15.5 %collective-permute-start.6 = (bf16[4,16,4096]{2,1,0:T(8,128)(2,1)S(1)}, bf16[4,16,4096]{2,1,0:T(8,128)(2,1)S(1)}, u32[]{:S(2)}, u32[]{:S(2)}) collective-permute-start(bf16[4,16,4096]{2,1,0:T(8,128)(2,1)S(1)} %get-tuple-element.12.refs_0_), channel_id=1, source_target_pairs={{6,0},{0,2},{2,4},{4,6},{7,1},{1,3},{3,5},{5,7},{14,8},{8,10},{10,... | collective-permute-start | bytes 1572872 | tf_op jit(solution)/shard_map/ppermute | solution.py:36
  69.9 28.8 %copy-start.3 = (bf16[1,8192,128]{2,1,0:T(8,128)(2,1)S(1)}, bf16[1,8192,128]{2,1,0:T(8,128)(2,1)}, u32[]{:S(2)}) copy-start(bf16[1,8192,128]{2,1,0:T(8,128)(2,1)} %param.9) | copy-start | bytes 6291460
  74.9 17.2 %collective-permute-start.12 = (bf16[4,16,4096]{2,1,0:T(8,128)(2,1)S(1)}, bf16[4,16,4096]{2,1,0:T(8,128)(2,1)S(1)}, u32[]{:S(2)}, u32[]{:S(2)}) collective-permute-start(bf16[4,16,4096]{2,1,0:T(8,128)(2,1)S(1)} %get-tuple-element.15.refs_0_), channel_id=1, source_target_pairs={{6,0},{0,2},{2,4},{4,6},{7,1},{1,3},{3,5},{5,7},{14,8},{8,10},{10,... | collective-permute-start | bytes 1572872 | tf_op jit(solution)/shard_map/ppermute | solution.py:36
  78.1 16.0 %collective-permute-start.11 = (bf16[4,16,4096]{2,1,0:T(8,128)(2,1)S(1)}, bf16[4,16,4096]{2,1,0:T(8,128)(2,1)S(1)}, u32[]{:S(2)}, u32[]{:S(2)}) collective-permute-start(bf16[4,16,4096]{2,1,0:T(8,128)(2,1)S(1)} %get-tuple-element.15.refs_0_), channel_id=1, source_target_pairs={{2,0},{4,2},{6,4},{0,6},{3,1},{5,3},{7,5},{1,7},{10,8},{12,10},{14... | collective-permute-start | bytes 1572872 | tf_op jit(solution)/shard_map/ppermute | solution.py:36
  81.5 17.2 %collective-permute-start.7 = (bf16[2,16,4096]{2,1,0:T(8,128)(2,1)S(1)}, bf16[2,16,4096]{2,1,0:T(8,128)(2,1)S(1)}, u32[]{:S(2)}, u32[]{:S(2)}) collective-permute-start(bf16[2,16,4096]{2,1,0:T(8,128)(2,1)S(1)} %slice.21), channel_id=1, source_target_pairs={{6,0},{0,2},{2,4},{4,6},{7,1},{1,3},{3,5},{5,7},{14,8},{8,10},{10,... | collective-permute-start | bytes 786440 | tf_op jit(solution)/shard_map/ppermute | solution.py:36
  83.5 15.2 %collective-permute-start.8 = (bf16[2,16,4096]{2,1,0:T(8,128)(2,1)S(1)}, bf16[2,16,4096]{2,1,0:T(8,128)(2,1)S(1)}, u32[]{:S(2)}, u32[]{:S(2)}) collective-permute-start(bf16[2,16,4096]{2,1,0:T(8,128)(2,1)S(1)} %slice.22), channel_id=1, source_target_pairs={{2,0},{4,2},{6,4},{0,6},{3,1},{5,3},{7,5},{1,7},{10,8},{12,10},{14... | collective-permute-start | bytes 786440 | tf_op jit(solution)/shard_map/ppermute | solution.py:36
  92.1 11.3 %collective-permute-start.13 = (bf16[2,16,4096]{2,1,0:T(8,128)(2,1)S(1)}, bf16[2,16,4096]{2,1,0:T(8,128)(2,1)S(1)}, u32[]{:S(2)}, u32[]{:S(2)}) collective-permute-start(bf16[2,16,4096]{2,1,0:T(8,128)(2,1)S(1)} %slice.23), channel_id=1, source_target_pairs={{6,0},{0,2},{2,4},{4,6},{7,1},{1,3},{3,5},{5,7},{14,8},{8,10},{10,... | collective-permute-start | bytes 786440 | tf_op jit(solution)/shard_map/ppermute | solution.py:36
  94.1 9.3 %collective-permute-start.14 = (bf16[2,16,4096]{2,1,0:T(8,128)(2,1)S(1)}, bf16[2,16,4096]{2,1,0:T(8,128)(2,1)S(1)}, u32[]{:S(2)}, u32[]{:S(2)}) collective-permute-start(bf16[2,16,4096]{2,1,0:T(8,128)(2,1)S(1)} %slice.24), channel_id=1, source_target_pairs={{2,0},{4,2},{6,4},{0,6},{3,1},{5,3},{7,5},{1,7},{10,8},{12,10},{14... | collective-permute-start | bytes 786440 | tf_op jit(solution)/shard_map/ppermute | solution.py:36
  106.2 0.8 copy-start.4
  107.0 25.4 %collective-permute-start.15 = (bf16[512,384]{1,0:T(8,128)(2,1)}, bf16[512,384]{1,0:T(8,128)(2,1)}, u32[]{:S(2)}, u32[]{:S(2)}) collective-permute-start(bf16[512,384]{1,0:T(8,128)(2,1)} %get-tuple-element.20), channel_id=1, source_target_pairs={{0,1},{1,0},{2,3},{3,2},{4,5},{5,4},{6,7},{7,6},{8,9},{9,8},{10,11... | collective-permute-start | bytes 1179656 | tf_op jit(solution)/shard_map/ppermute | solution.py:44
  114.1 17.5 %all-to-all-start.1 = ((bf16[16,8,256]{2,1,0:T(8,128)(2,1)}), bf16[16,8,256]{2,1,0:T(8,128)(2,1)S(1)}, u32[]{:S(2)}, u32[]{:S(2)}) async-start(bf16[16,8,256]{2,1,0:T(8,128)(2,1)} %get-tuple-element.21), calls=%async_computation.1 | async-start | bytes 131072 | tf_op jit(solution)/shard_map/all_to_all | solution.py:278
  132.4 1.0 copy-start.5

commit v9 on v8

--- a/solution.py
+++ b/solution.py
@@ -133,7 +133,7 @@
     return v * cosine + pltpu.roll(v, HD // 2, 1) * sine
 
 
-def decode_kernel(got, tables, out):
+def decode_kernel(_, got, tables, out):
     for g in range(NZ):
         raw = (got[2 * g].astype(F32) + got[2 * g + 1].astype(F32)).astype(BF)
         out[g, :, :HD] = turn(
@@ -142,7 +142,8 @@
         out[g, :, HD:] = raw[:, HD:]
 
 
-def attend_kernel(where, own1, own2, got, cosine, sine, resident, out):
+def attend_kernel(where, own1, own2, got, cosine, sine, resident, out, zero):
+    zero[0] = 0
     z0, y0 = where[0], where[1]
     own = jnp.concatenate([own1[...], own2[...]])
     raw = (own[:, HD:] + got[:, HD:].astype(F32)).astype(BF)
@@ -276,19 +277,18 @@
     )(where, decode_owner[0], *everywhere(batch2), *weights, own1, send1)
     got = swap_core(send)
     blocks = lax.all_to_all(blocks, ("z", "c"), 0, 0)
-    decode_kv = call(decode_kernel, shaped(NZ, 8, 2 * HD), [VMEM] * 2, moved=2**18, limit=4)(
-        blocks, decode_tables
+    resident = lax.dynamic_index_in_dim(resident_cache[0], z0, 0, keepdims=False)
+    attn, done = call(
+        attend_kernel,
+        (shaped(TOKENS, HD), shaped(1, dtype=jnp.int32)),
+        [SMEM] + [VMEM] * 6,
+        flops=2**10,
+        moved=2**10,
+    )(where, own1, own2, got, cosine, sine, resident)
+    decode_kv = call(decode_kernel, shaped(NZ, 8, 2 * HD), [SMEM] + [VMEM] * 2, moved=2**18, limit=4, flops=2**40)(
+        done, blocks, decode_tables
     )
     decode_kv = jnp.transpose(decode_kv, (1, 0, 2))[None]
-    resident = lax.dynamic_index_in_dim(resident_cache[0], z0, 0, keepdims=False)
-    attn = call(
-        attend_kernel,
-        shaped(TOKENS, HD),
-        [SMEM] + [VMEM] * 6,
-        flops=4 * TOKENS * 1024 * HD,
-        moved=2**21,
-        exps=TOKENS * 1024,
-    )(where, own1, own2, got, cosine, sine, resident)
     return attn[None], decode_kv
 
 

time: 138 us -> 133 us (0.964)
  waiting for transfers between devices: 26.7 us -> 23.5 us
  local copies, waits for them, and re-layouts: 7.9 us -> 6.14 us
    all_to_all x1, waiting for transfers between devices: 10 us -> 6.83 us  [body(): blocks = lax.all_to_all(blocks, ('z', 'c'), 0, 0)]
    unnamed x17 -> x13, local copies, waits for them, and re-layouts: 4.75 us -> 3 us
  transfers between devices with their start and end apart: 18 -> 18, of which waited for: 6 -> 6; matrix products, arithmetic and copies ran while one was open for 4% -> 4% of each run, Pallas kernels for 4% -> 7%
where the time goes in v9:
time: 133 us; the launch traced here: 132 us
  starting transfers between devices  82.9 us (62%)
  waiting for transfers between devices  23.5 us (18%)
  Pallas kernels  12.8 us (10%)
  local copies, waits for them, and re-layouts  6.14 us (5%)
  other arithmetic  4.02 us (3%)
  between operations  2.93 us (2%)
    ppermute x8, starting transfers between devices, along_y(): return lax.ppermute(value, 'y', [((i + k) % NY, i) for i in range(NY)])  26.1 us
    ppermute x4, starting transfers between devices, across_z(): return lax.ppermute(value, 'z', [(i, i ^ k) for i in range(NZ)])  18.6 us
    ppermute x1, starting transfers between devices, body(): same = lax.ppermute(kept, ('s', 'z', 'c'), steps[0])  13.3 us
    ppermute x4, waiting for transfers between devices, across_z(): return lax.ppermute(value, 'z', [(i, i ^ k) for i in range(NZ)])  10.4 us
    ppermute x2, starting transfers between devices, swap_core(): return lax.ppermute(value, 'c', [(0, 1), (1, 0)])  9.96 us
    all_to_all x1, starting transfers between devices, body(): blocks = lax.all_to_all(blocks, ('z', 'c'), 0, 0)  7.48 us
    all_to_all x1, waiting for transfers between devices, body(): blocks = lax.all_to_all(blocks, ('z', 'c'), 0, 0)  6.83 us
    all_to_all x1, starting transfers between devices, body(): wkv = lax.all_to_all(kv_halves, ('y', 'c'), 0, 0).reshape(256, half)  4.99 us
  transfers between devices with their start and end apart: 18, of which 6 were waited for; matrix products, arithmetic and copies ran while one was open for 4% of the time, Pallas kernels for 7%

profile of v9, /device:TPU:1, one launch (start us, length us, event | category | flops | bytes accessed | tf_op | source)
XLA Modules:
  0.0 132.3 jit_solution(18189408969247843635)
XLA Ops:
  0.6 0.0 copy-start
  0.7 1.2 fusion.4
  1.9 1.0 fusion.5
  2.9 13.3 %collective-permute-start = (bf16[8,4096]{1,0:T(8,128)(2,1)S(1)}, bf16[8,4096]{1,0:T(8,128)(2,1)S(1)}, u32[]{:S(2)}, u32[]{:S(2)}) collective-permute-start(bf16[8,4096]{1,0:T(8,128)(2,1)S(1)} %get-tuple-element.29), channel_id=1, source_target_pairs={{0,96},{1,97},{8,104},{9,105},{16,112},{17,113},{24,120},{25,121},... | collective-permute-start | bytes 196616 | tf_op jit(solution)/shard_map/ppermute | solution.py:215
  16.2 2.5 %collective-permute-start.1 = (bf16[8,4096]{1,0:T(8,128)(2,1)S(1)}, bf16[8,4096]{1,0:T(8,128)(2,1)S(1)}, u32[]{:S(2)}, u32[]{:S(2)}) collective-permute-start(bf16[8,4096]{1,0:T(8,128)(2,1)S(1)} %get-tuple-element.28), channel_id=1, source_target_pairs={{0,97},{1,96},{8,105},{9,104},{16,113},{17,112},{24,121},{25,120},... | collective-permute-start | bytes 196616 | tf_op jit(solution)/shard_map/ppermute | solution.py:216
  18.7 0.0 copy-start.2
  18.7 1.0 copy-done.2
  19.7 0.2 shard_map.86
  20.0 1.3 copy-done.1
  21.3 5.0 %all-to-all-start = ((bf16[8,32,4096]{2,1,0:T(8,128)(2,1)}), bf16[8,32,4096]{2,1,0:T(8,128)(2,1)}, u32[]{:S(2)}, u32[]{:S(2)}) async-start(bf16[8,32,4096]{2,1,0:T(8,128)(2,1)} %copy-done.1), calls=%async_computation | async-start | bytes 4194304 | tf_op jit(solution)/shard_map/all_to_all | solution.py:227
  26.3 2.2 %collective-permute-done.1 = bf16[8,4096]{1,0:T(8,128)(2,1)S(1)} collective-permute-done((bf16[8,4096]{1,0:T(8,128)(2,1)S(1)}, bf16[8,4096]{1,0:T(8,128)(2,1)S(1)}, u32[]{:S(2)}, u32[]{:S(2)}) %collective-permute-start.1) | collective-permute-done | bytes 65568 | tf_op jit(solution)/shard_map/ppermute | solution.py:216
  28.6 9.3 %collective-permute-start.2 = (bf16[16,4096]{1,0:T(8,128)(2,1)S(1)}, bf16[16,4096]{1,0:T(8,128)(2,1)S(1)}, u32[]{:S(2)}, u32[]{:S(2)}) collective-permute-start(bf16[16,4096]{1,0:T(8,128)(2,1)S(1)} %fusion.3), channel_id=1, source_target_pairs={{0,32},{8,40},{16,48},{24,56},{32,0},{40,8},{48,16},{56,24},{1,33}... | collective-permute-start | bytes 393224 | tf_op jit(solution)/shard_map/ppermute | solution.py:40
  38.0 0.5 slice.20
  39.2 2.5 %dynamic-slice_bitcast_fusion = bf16[4096,128]{1,0:T(8,128)(2,1)} fusion(bf16[1,8192,128]{2,1,0:T(8,128)(2,1)} %param.9, s32[]{:T(128)S(6)} %select_n.65), kind=kLoop, calls=%fused_computation | loop fusion | bytes 2097156 | tf_op jit(solution)/shard_map/dynamic_slice | solution.py:223
  41.7 2.8 %collective-permute-start.4 = (bf16[4096,128]{1,0:T(8,128)(2,1)}, bf16[4096,128]{1,0:T(8,128)(2,1)}, u32[]{:S(2)}, u32[]{:S(2)}) collective-permute-start(bf16[4096,128]{1,0:T(8,128)(2,1)} %dynamic-slice_bitcast_fusion), channel_id=1, source_target_pairs={{0,1},{1,0},{2,3},{3,2},{4,5},{5,4},{6,7},{7,6},{8,9},{9,8},{10,11... | collective-permute-start | bytes 3145736 | tf_op jit(solution)/shard_map/ppermute | solution.py:44
  44.5 5.6 %collective-permute-done.2 = bf16[16,4096]{1,0:T(8,128)(2,1)S(1)} collective-permute-done((bf16[16,4096]{1,0:T(8,128)(2,1)S(1)}, bf16[16,4096]{1,0:T(8,128)(2,1)S(1)}, u32[]{:S(2)}, u32[]{:S(2)}) %collective-permute-start.2) | collective-permute-done | bytes 131104 | tf_op jit(solution)/shard_map/ppermute | solution.py:40
  50.2 1.9 %collective-permute-start.3 = (bf16[2,16,4096]{2,1,0:T(8,128)(2,1)S(1)}, bf16[2,16,4096]{2,1,0:T(8,128)(2,1)S(1)}, u32[]{:S(2)}, u32[]{:S(2)}) collective-permute-start(bf16[2,16,4096]{2,1,0:T(8,128)(2,1)S(1)} %pad_maximum_fusion.one), channel_id=1, source_target_pairs={{0,8},{8,0},{16,24},{24,16},{32,40},{40,32},{48,56},{56,48},{1,9},... | collective-permute-start | bytes 786440 | tf_op jit(solution)/shard_map/ppermute | solution.py:40
  52.9 1.9 %collective-permute-start.9 = (bf16[2,16,4096]{2,1,0:T(8,128)(2,1)S(1)}, bf16[2,16,4096]{2,1,0:T(8,128)(2,1)S(1)}, u32[]{:S(2)}, u32[]{:S(2)}) collective-permute-start(bf16[2,16,4096]{2,1,0:T(8,128)(2,1)S(1)} %pad_maximum_fusion.one), channel_id=1, source_target_pairs={{0,16},{8,24},{16,0},{24,8},{32,48},{40,56},{48,32},{56,40},{1,17}... | collective-permute-start | bytes 786440 | tf_op jit(solution)/shard_map/ppermute | solution.py:40
  54.8 5.4 %collective-permute-start.10 = (bf16[2,16,4096]{2,1,0:T(8,128)(2,1)S(1)}, bf16[2,16,4096]{2,1,0:T(8,128)(2,1)S(1)}, u32[]{:S(2)}, u32[]{:S(2)}) collective-permute-start(bf16[2,16,4096]{2,1,0:T(8,128)(2,1)S(1)} %pad_maximum_fusion.one), channel_id=1, source_target_pairs={{0,24},{8,16},{16,8},{24,0},{32,56},{40,48},{48,40},{56,32},{1,25}... | collective-permute-start | bytes 786440 | tf_op jit(solution)/shard_map/ppermute | solution.py:40
  60.2 0.5 collective-permute-done.3.two
  60.7 0.0 collective-permute-done.4.rest_0_.refs_6_
  60.7 0.6 shard_map.87
  61.3 4.6 %collective-permute-start.5 = (bf16[4,16,4096]{2,1,0:T(8,128)(2,1)S(1)}, bf16[4,16,4096]{2,1,0:T(8,128)(2,1)S(1)}, u32[]{:S(2)}, u32[]{:S(2)}) collective-permute-start(bf16[4,16,4096]{2,1,0:T(8,128)(2,1)S(1)} %get-tuple-element.14.refs_0_), channel_id=1, source_target_pairs={{2,0},{4,2},{6,4},{0,6},{3,1},{5,3},{7,5},{1,7},{10,8},{12,10},{14... | collective-permute-start | bytes 1572872 | tf_op jit(solution)/shard_map/ppermute | solution.py:36
  66.0 1.9 %collective-permute-start.6 = (bf16[4,16,4096]{2,1,0:T(8,128)(2,1)S(1)}, bf16[4,16,4096]{2,1,0:T(8,128)(2,1)S(1)}, u32[]{:S(2)}, u32[]{:S(2)}) collective-permute-start(bf16[4,16,4096]{2,1,0:T(8,128)(2,1)S(1)} %get-tuple-element.14.refs_0_), channel_id=1, source_target_pairs={{6,0},{0,2},{2,4},{4,6},{7,1},{1,3},{3,5},{5,7},{14,8},{8,10},{10,... | collective-permute-start | bytes 1572872 | tf_op jit(solution)/shard_map/ppermute | solution.py:36
  68.5 0.1 add_convert_fusion
  68.5 1.0 fusion.6
  69.5 0.2 multiply_cosine_fusion.1
  69.7 0.1 pad_maximum_fusion.3.rest_2_.tables
  69.8 0.0 copy-start.3
  69.8 0.2 pad_maximum_fusion.1
  70.1 4.3 %collective-permute-done.9.one = bf16[2,16,4096]{2,1,0:T(8,128)(2,1)S(1)} collective-permute-done((bf16[2,16,4096]{2,1,0:T(8,128)(2,1)S(1)}, bf16[2,16,4096]{2,1,0:T(8,128)(2,1)S(1)}, u32[]{:S(2)}, u32[]{:S(2)}) %collective-permute-start.9) | collective-permute-done | bytes 262176 | tf_op jit(solution)/shard_map/ppermute | solution.py:40
  74.3 0.6 shard_map.89
  74.9 3.2 %collective-permute-start.12 = (bf16[4,16,4096]{2,1,0:T(8,128)(2,1)S(1)}, bf16[4,16,4096]{2,1,0:T(8,128)(2,1)S(1)}, u32[]{:S(2)}, u32[]{:S(2)}) collective-permute-start(bf16[4,16,4096]{2,1,0:T(8,128)(2,1)S(1)} %get-tuple-element.17.refs_0_), channel_id=1, source_target_pairs={{6,0},{0,2},{2,4},{4,6},{7,1},{1,3},{3,5},{5,7},{14,8},{8,10},{10,... | collective-permute-start | bytes 1572872 | tf_op jit(solution)/shard_map/ppermute | solution.py:36
  78.1 3.4 %collective-permute-start.11 = (bf16[4,16,4096]{2,1,0:T(8,128)(2,1)S(1)}, bf16[4,16,4096]{2,1,0:T(8,128)(2,1)S(1)}, u32[]{:S(2)}, u32[]{:S(2)}) collective-permute-start(bf16[4,16,4096]{2,1,0:T(8,128)(2,1)S(1)} %get-tuple-element.17.refs_0_), channel_id=1, source_target_pairs={{2,0},{4,2},{6,4},{0,6},{3,1},{5,3},{7,5},{1,7},{10,8},{12,10},{14... | collective-permute-start | bytes 1572872 | tf_op jit(solution)/shard_map/ppermute | solution.py:36
  81.5 1.9 %collective-permute-start.7 = (bf16[2,16,4096]{2,1,0:T(8,128)(2,1)S(1)}, bf16[2,16,4096]{2,1,0:T(8,128)(2,1)S(1)}, u32[]{:S(2)}, u32[]{:S(2)}) collective-permute-start(bf16[2,16,4096]{2,1,0:T(8,128)(2,1)S(1)} %slice.21), channel_id=1, source_target_pairs={{6,0},{0,2},{2,4},{4,6},{7,1},{1,3},{3,5},{5,7},{14,8},{8,10},{10,... | collective-permute-start | bytes 786440 | tf_op jit(solution)/shard_map/ppermute | solution.py:36
  83.5 4.6 %collective-permute-start.8 = (bf16[2,16,4096]{2,1,0:T(8,128)(2,1)S(1)}, bf16[2,16,4096]{2,1,0:T(8,128)(2,1)S(1)}, u32[]{:S(2)}, u32[]{:S(2)}) collective-permute-start(bf16[2,16,4096]{2,1,0:T(8,128)(2,1)S(1)} %slice.22), channel_id=1, source_target_pairs={{2,0},{4,2},{6,4},{0,6},{3,1},{5,3},{7,5},{1,7},{10,8},{12,10},{14... | collective-permute-start | bytes 786440 | tf_op jit(solution)/shard_map/ppermute | solution.py:36
  88.1 0.1 pad_add_fusion.where
  88.1 4.0 %collective-permute-done.12.refs_4_ = bf16[4,16,4096]{2,1,0:T(8,128)(2,1)S(1)} collective-permute-done((bf16[4,16,4096]{2,1,0:T(8,128)(2,1)S(1)}, bf16[4,16,4096]{2,1,0:T(8,128)(2,1)S(1)}, u32[]{:S(2)}, u32[]{:S(2)}) %collective-permute-start.12) | collective-permute-done | bytes 524320 | tf_op jit(solution)/shard_map/ppermute | solution.py:36
  92.1 1.9 %collective-permute-start.13 = (bf16[2,16,4096]{2,1,0:T(8,128)(2,1)S(1)}, bf16[2,16,4096]{2,1,0:T(8,128)(2,1)S(1)}, u32[]{:S(2)}, u32[]{:S(2)}) collective-permute-start(bf16[2,16,4096]{2,1,0:T(8,128)(2,1)S(1)} %slice.23), channel_id=1, source_target_pairs={{6,0},{0,2},{2,4},{4,6},{7,1},{1,3},{3,5},{5,7},{14,8},{8,10},{10,... | collective-permute-start | bytes 786440 | tf_op jit(solution)/shard_map/ppermute | solution.py:36
  94.1 4.6 %collective-permute-start.14 = (bf16[2,16,4096]{2,1,0:T(8,128)(2,1)S(1)}, bf16[2,16,4096]{2,1,0:T(8,128)(2,1)S(1)}, u32[]{:S(2)}, u32[]{:S(2)}) collective-permute-start(bf16[2,16,4096]{2,1,0:T(8,128)(2,1)S(1)} %slice.24), channel_id=1, source_target_pairs={{2,0},{4,2},{6,4},{0,6},{3,1},{5,3},{7,5},{1,7},{10,8},{12,10},{14... | collective-permute-start | bytes 786440 | tf_op jit(solution)/shard_map/ppermute | solution.py:36
  98.7 4.7 %shard_map.88 = (f32[256,384]{1,0:T(8,128)S(1)}, bf16[256,384]{1,0:T(8,128)(2,1)S(1)}, bf16[4096,256]{1,0:T(8,128)(2,1)S(1)}, bf16[256,4096]{1,0:T(8,128)(2,1)S(1)}) custom-call(s32[3]{0:T(128)S(1)} %pad_add_fusion.where, bf16[4,16,4096]{2,1,0:T(8,128)(2,1)S(1)} %get-tuple-element.14.refs_0_, bf16[4,16,4096]{2,1,0:T(8,128)(2,1)S(1)} %collective-permute-done.5.refs_1_, ...), custom_call_target="tpu_custom_call" | custom-call | flops 107374182400 | bytes 9437184 | tf_op jit(solution)/shard_map/pallas_call | solution.py:262
  103.4 2.8 %shard_map.90 = (f32[256,384]{1,0:T(8,128)S(1)}, bf16[512,384]{1,0:T(8,128)(2,1)}, bf16[16,8,256]{2,1,0:T(8,128)(2,1)}) custom-call(s32[3]{0:T(128)S(1)} %pad_add_fusion.where, s32[8]{0:T(128)S(1)} %bitcast.43, bf16[4,16,4096]{2,1,0:T(8,128)(2,1)S(1)} %get-tuple-element.17.refs_0_, bf16[4,16,4096]{2,1,0:T(8,128)(2,1)S(1)} %collective-permute-done.11.refs_1_, ...), custom_call_target="tpu_custom_call" | custom-call | flops 1073741824 | bytes 9437184 | tf_op jit(solution)/shard_map/pallas_call | solution.py:270
  106.3 7.1 %collective-permute-start.15 = (bf16[512,384]{1,0:T(8,128)(2,1)}, bf16[512,384]{1,0:T(8,128)(2,1)}, u32[]{:S(2)}, u32[]{:S(2)}) collective-permute-start(bf16[512,384]{1,0:T(8,128)(2,1)} %get-tuple-element.22), channel_id=1, source_target_pairs={{0,1},{1,0},{2,3},{3,2},{4,5},{5,4},{6,7},{7,6},{8,9},{9,8},{10,11... | collective-permute-start | bytes 1179656 | tf_op jit(solution)/shard_map/ppermute | solution.py:44
  113.4 7.5 %all-to-all-start.1 = ((bf16[16,8,256]{2,1,0:T(8,128)(2,1)}), bf16[16,8,256]{2,1,0:T(8,128)(2,1)S(1)}, u32[]{:S(2)}, u32[]{:S(2)}) async-start(bf16[16,8,256]{2,1,0:T(8,128)(2,1)} %get-tuple-element.25), calls=%async_computation.1 | async-start | bytes 131072 | tf_op jit(solution)/shard_map/all_to_all | solution.py:279
  120.9 3.2 %shard_map.91 = (bf16[512,128]{1,0:T(8,128)(2,1)}, s32[1]{0:T(128)}) custom-call(s32[3]{0:T(128)S(1)} %pad_add_fusion.where, f32[256,384]{1,0:T(8,128)S(1)} %get-tuple-element.15.refs_7_.own1, f32[256,384]{1,0:T(8,128)S(1)} %get-tuple-element.21.own2, bf16[512,384]{1,0:T(8,128)(2,1)} %collective-permute-done.15.got, ...), custom_call_target="tpu_custom_call" | custom-call | flops 1024 | bytes 1024 | tf_op jit(solution)/shard_map/pallas_call | solution.py:281
  124.1 6.8 %all-to-all-done.1.got = bf16[16,8,256]{2,1,0:T(8,128)(2,1)S(1)} async-done(((bf16[16,8,256]{2,1,0:T(8,128)(2,1)}), bf16[16,8,256]{2,1,0:T(8,128)(2,1)S(1)}, u32[]{:S(2)}, u32[]{:S(2)}) %all-to-all-start.1) | async-done | bytes 65568 | tf_op jit(solution)/shard_map/all_to_all | solution.py:279
  130.9 0.7 shard_map.92
  131.7 0.6 copy.9
  (32 shorter events, 0.3 us)
Async XLA Ops:
  0.6 120.2 %copy-start = (bf16[1,8,512,256]{3,2,1,0:T(8,128)(2,1)S(1)}, bf16[1,8,512,256]{3,2,1,0:T(8,128)(2,1)}, u32[]{:S(2)}) copy-start(bf16[1,8,512,256]{3,2,1,0:T(8,128)(2,1)} %param.11) | copy-start | bytes 6291460
  2.9 23.4 %collective-permute-start = (bf16[8,4096]{1,0:T(8,128)(2,1)S(1)}, bf16[8,4096]{1,0:T(8,128)(2,1)S(1)}, u32[]{:S(2)}, u32[]{:S(2)}) collective-permute-start(bf16[8,4096]{1,0:T(8,128)(2,1)S(1)} %get-tuple-element.29), channel_id=1, source_target_pairs={{0,96},{1,97},{8,104},{9,105},{16,112},{17,113},{24,120},{25,121},... | collective-permute-start | bytes 196616 | tf_op jit(solution)/shard_map/ppermute | solution.py:215
  16.2 12.4 %collective-permute-start.1 = (bf16[8,4096]{1,0:T(8,128)(2,1)S(1)}, bf16[8,4096]{1,0:T(8,128)(2,1)S(1)}, u32[]{:S(2)}, u32[]{:S(2)}) collective-permute-start(bf16[8,4096]{1,0:T(8,128)(2,1)S(1)} %get-tuple-element.28), channel_id=1, source_target_pairs={{0,97},{1,96},{8,105},{9,104},{16,113},{17,112},{24,121},{25,120},... | collective-permute-start | bytes 196616 | tf_op jit(solution)/shard_map/ppermute | solution.py:216
  18.7 1.0 copy-start.2
  20.0 1.3 %copy-start.1 = (bf16[8,32,4096]{2,1,0:T(8,128)(2,1)}, bf16[8,32,4096]{2,1,0:T(8,128)(2,1)S(1)}, u32[]{:S(2)}) copy-start(bf16[8,32,4096]{2,1,0:T(8,128)(2,1)S(1)} %shard_map.86) | copy-start | bytes 6291460
  21.3 5.0 %copy-start.5 = (f32[1,8192]{1,0:T(1,128)S(1)}, f32[1,8192]{1,0:T(1,128)}, u32[]{:S(2)}) copy-start(f32[1,8192]{1,0:T(1,128)} %param.8) | copy-start | bytes 98308
  21.3 39.4 %all-to-all-start = ((bf16[8,32,4096]{2,1,0:T(8,128)(2,1)}), bf16[8,32,4096]{2,1,0:T(8,128)(2,1)}, u32[]{:S(2)}, u32[]{:S(2)}) async-start(bf16[8,32,4096]{2,1,0:T(8,128)(2,1)} %copy-done.1), calls=%async_computation | async-start | bytes 4194304 | tf_op jit(solution)/shard_map/all_to_all | solution.py:227
  26.3 26.5 %copy-start.4 = (s32[1,8]{1,0:T(1,128)S(1)}, s32[1,8]{1,0:T(1,128)}, u32[]{:S(2)}) copy-start(s32[1,8]{1,0:T(1,128)} %param.13) | copy-start | bytes 100
  28.6 21.6 %collective-permute-start.2 = (bf16[16,4096]{1,0:T(8,128)(2,1)S(1)}, bf16[16,4096]{1,0:T(8,128)(2,1)S(1)}, u32[]{:S(2)}, u32[]{:S(2)}) collective-permute-start(bf16[16,4096]{1,0:T(8,128)(2,1)S(1)} %fusion.3), channel_id=1, source_target_pairs={{0,32},{8,40},{16,48},{24,56},{32,0},{40,8},{48,16},{56,24},{1,33}... | collective-permute-start | bytes 393224 | tf_op jit(solution)/shard_map/ppermute | solution.py:40
  41.7 19.1 %collective-permute-start.4 = (bf16[4096,128]{1,0:T(8,128)(2,1)}, bf16[4096,128]{1,0:T(8,128)(2,1)}, u32[]{:S(2)}, u32[]{:S(2)}) collective-permute-start(bf16[4096,128]{1,0:T(8,128)(2,1)} %dynamic-slice_bitcast_fusion), channel_id=1, source_target_pairs={{0,1},{1,0},{2,3},{3,2},{4,5},{5,4},{6,7},{7,6},{8,9},{9,8},{10,11... | collective-permute-start | bytes 3145736 | tf_op jit(solution)/shard_map/ppermute | solution.py:44
  50.2 10.5 %collective-permute-start.3 = (bf16[2,16,4096]{2,1,0:T(8,128)(2,1)S(1)}, bf16[2,16,4096]{2,1,0:T(8,128)(2,1)S(1)}, u32[]{:S(2)}, u32[]{:S(2)}) collective-permute-start(bf16[2,16,4096]{2,1,0:T(8,128)(2,1)S(1)} %pad_maximum_fusion.one), channel_id=1, source_target_pairs={{0,8},{8,0},{16,24},{24,16},{32,40},{40,32},{48,56},{56,48},{1,9},... | collective-permute-start | bytes 786440 | tf_op jit(solution)/shard_map/ppermute | solution.py:40
  52.9 21.5 %collective-permute-start.9 = (bf16[2,16,4096]{2,1,0:T(8,128)(2,1)S(1)}, bf16[2,16,4096]{2,1,0:T(8,128)(2,1)S(1)}, u32[]{:S(2)}, u32[]{:S(2)}) collective-permute-start(bf16[2,16,4096]{2,1,0:T(8,128)(2,1)S(1)} %pad_maximum_fusion.one), channel_id=1, source_target_pairs={{0,16},{8,24},{16,0},{24,8},{32,48},{40,56},{48,32},{56,40},{1,17}... | collective-permute-start | bytes 786440 | tf_op jit(solution)/shard_map/ppermute | solution.py:40
  54.8 19.6 %collective-permute-start.10 = (bf16[2,16,4096]{2,1,0:T(8,128)(2,1)S(1)}, bf16[2,16,4096]{2,1,0:T(8,128)(2,1)S(1)}, u32[]{:S(2)}, u32[]{:S(2)}) collective-permute-start(bf16[2,16,4096]{2,1,0:T(8,128)(2,1)S(1)} %pad_maximum_fusion.one), channel_id=1, source_target_pairs={{0,24},{8,16},{16,8},{24,0},{32,56},{40,48},{48,40},{56,32},{1,25}... | collective-permute-start | bytes 786440 | tf_op jit(solution)/shard_map/ppermute | solution.py:40
  61.3 22.1 %collective-permute-start.5 = (bf16[4,16,4096]{2,1,0:T(8,128)(2,1)S(1)}, bf16[4,16,4096]{2,1,0:T(8,128)(2,1)S(1)}, u32[]{:S(2)}, u32[]{:S(2)}) collective-permute-start(bf16[4,16,4096]{2,1,0:T(8,128)(2,1)S(1)} %get-tuple-element.14.refs_0_), channel_id=1, source_target_pairs={{2,0},{4,2},{6,4},{0,6},{3,1},{5,3},{7,5},{1,7},{10,8},{12,10},{14... | collective-permute-start | bytes 1572872 | tf_op jit(solution)/shard_map/ppermute | solution.py:36
  66.0 15.5 %collective-permute-start.6 = (bf16[4,16,4096]{2,1,0:T(8,128)(2,1)S(1)}, bf16[4,16,4096]{2,1,0:T(8,128)(2,1)S(1)}, u32[]{:S(2)}, u32[]{:S(2)}) collective-permute-start(bf16[4,16,4096]{2,1,0:T(8,128)(2,1)S(1)} %get-tuple-element.14.refs_0_), channel_id=1, source_target_pairs={{6,0},{0,2},{2,4},{4,6},{7,1},{1,3},{3,5},{5,7},{14,8},{8,10},{10,... | collective-permute-start | bytes 1572872 | tf_op jit(solution)/shard_map/ppermute | solution.py:36
  69.8 28.9 %copy-start.3 = (bf16[1,8192,128]{2,1,0:T(8,128)(2,1)S(1)}, bf16[1,8192,128]{2,1,0:T(8,128)(2,1)}, u32[]{:S(2)}) copy-start(bf16[1,8192,128]{2,1,0:T(8,128)(2,1)} %param.9) | copy-start | bytes 6291460
  74.9 17.2 %collective-permute-start.12 = (bf16[4,16,4096]{2,1,0:T(8,128)(2,1)S(1)}, bf16[4,16,4096]{2,1,0:T(8,128)(2,1)S(1)}, u32[]{:S(2)}, u32[]{:S(2)}) collective-permute-start(bf16[4,16,4096]{2,1,0:T(8,128)(2,1)S(1)} %get-tuple-element.17.refs_0_), channel_id=1, source_target_pairs={{6,0},{0,2},{2,4},{4,6},{7,1},{1,3},{3,5},{5,7},{14,8},{8,10},{10,... | collective-permute-start | bytes 1572872 | tf_op jit(solution)/shard_map/ppermute | solution.py:36
  78.1 16.0 %collective-permute-start.11 = (bf16[4,16,4096]{2,1,0:T(8,128)(2,1)S(1)}, bf16[4,16,4096]{2,1,0:T(8,128)(2,1)S(1)}, u32[]{:S(2)}, u32[]{:S(2)}) collective-permute-start(bf16[4,16,4096]{2,1,0:T(8,128)(2,1)S(1)} %get-tuple-element.17.refs_0_), channel_id=1, source_target_pairs={{2,0},{4,2},{6,4},{0,6},{3,1},{5,3},{7,5},{1,7},{10,8},{12,10},{14... | collective-permute-start | bytes 1572872 | tf_op jit(solution)/shard_map/ppermute | solution.py:36
  81.5 17.2 %collective-permute-start.7 = (bf16[2,16,4096]{2,1,0:T(8,128)(2,1)S(1)}, bf16[2,16,4096]{2,1,0:T(8,128)(2,1)S(1)}, u32[]{:S(2)}, u32[]{:S(2)}) collective-permute-start(bf16[2,16,4096]{2,1,0:T(8,128)(2,1)S(1)} %slice.21), channel_id=1, source_target_pairs={{6,0},{0,2},{2,4},{4,6},{7,1},{1,3},{3,5},{5,7},{14,8},{8,10},{10,... | collective-permute-start | bytes 786440 | tf_op jit(solution)/shard_map/ppermute | solution.py:36
  83.5 15.2 %collective-permute-start.8 = (bf16[2,16,4096]{2,1,0:T(8,128)(2,1)S(1)}, bf16[2,16,4096]{2,1,0:T(8,128)(2,1)S(1)}, u32[]{:S(2)}, u32[]{:S(2)}) collective-permute-start(bf16[2,16,4096]{2,1,0:T(8,128)(2,1)S(1)} %slice.22), channel_id=1, source_target_pairs={{2,0},{4,2},{6,4},{0,6},{3,1},{5,3},{7,5},{1,7},{10,8},{12,10},{14... | collective-permute-start | bytes 786440 | tf_op jit(solution)/shard_map/ppermute | solution.py:36
  92.1 11.3 %collective-permute-start.13 = (bf16[2,16,4096]{2,1,0:T(8,128)(2,1)S(1)}, bf16[2,16,4096]{2,1,0:T(8,128)(2,1)S(1)}, u32[]{:S(2)}, u32[]{:S(2)}) collective-permute-start(bf16[2,16,4096]{2,1,0:T(8,128)(2,1)S(1)} %slice.23), channel_id=1, source_target_pairs={{6,0},{0,2},{2,4},{4,6},{7,1},{1,3},{3,5},{5,7},{14,8},{8,10},{10,... | collective-permute-start | bytes 786440 | tf_op jit(solution)/shard_map/ppermute | solution.py:36
  94.1 9.3 %collective-permute-start.14 = (bf16[2,16,4096]{2,1,0:T(8,128)(2,1)S(1)}, bf16[2,16,4096]{2,1,0:T(8,128)(2,1)S(1)}, u32[]{:S(2)}, u32[]{:S(2)}) collective-permute-start(bf16[2,16,4096]{2,1,0:T(8,128)(2,1)S(1)} %slice.24), channel_id=1, source_target_pairs={{2,0},{4,2},{6,4},{0,6},{3,1},{5,3},{7,5},{1,7},{10,8},{12,10},{14... | collective-permute-start | bytes 786440 | tf_op jit(solution)/shard_map/ppermute | solution.py:36
  106.3 14.6 %collective-permute-start.15 = (bf16[512,384]{1,0:T(8,128)(2,1)}, bf16[512,384]{1,0:T(8,128)(2,1)}, u32[]{:S(2)}, u32[]{:S(2)}) collective-permute-start(bf16[512,384]{1,0:T(8,128)(2,1)} %get-tuple-element.22), channel_id=1, source_target_pairs={{0,1},{1,0},{2,3},{3,2},{4,5},{5,4},{6,7},{7,6},{8,9},{9,8},{10,11... | collective-permute-start | bytes 1179656 | tf_op jit(solution)/shard_map/ppermute | solution.py:44
  113.4 17.5 %all-to-all-start.1 = ((bf16[16,8,256]{2,1,0:T(8,128)(2,1)}), bf16[16,8,256]{2,1,0:T(8,128)(2,1)S(1)}, u32[]{:S(2)}, u32[]{:S(2)}) async-start(bf16[16,8,256]{2,1,0:T(8,128)(2,1)} %get-tuple-element.25), calls=%async_computation.1 | async-start | bytes 131072 | tf_op jit(solution)/shard_map/all_to_all | solution.py:279
